TPU v7x, 32 devices: a whole 2x2x4 slice. The times are simulated.
32 devices in a mesh: row: 4 (over y, x), col: 8 (over z, core).
Axes of the slice: x: 2, y: 2, z: 4, core: 2. Of those that a mesh axis runs over, the one named last changes fastest.
Arguments:
- residual: bfloat16 [256, 5120], P('row', 'col'), may hold values from -6 to 6
- attn_gain: float32 [5120], P('col'), may hold values from 0.1 to 1.9
- w_query: bfloat16 [5120, 5120], P('col', 'row'), may hold values from -0.078125 to 0.078125
- w_key: bfloat16 [5120, 1024], P('col', 'row'), may hold values from -0.078125 to 0.078125
- w_value: bfloat16 [5120, 1024], P('col', 'row'), may hold values from -0.078125 to 0.078125
- w_out: bfloat16 [5120, 5120], P('row', 'col'), may hold values from -0.078125 to 0.078125
- mlp_gain: float32 [5120], P('col'), may hold values from 0.1 to 1.9
- w_gate: bfloat16 [2, 5120, 13824], P(None, 'col', 'row'), may hold values from -0.078125 to 0.078125
- w_up: bfloat16 [2, 5120, 13824], P(None, 'col', 'row'), may hold values from -0.078125 to 0.078125
- w_down: bfloat16 [2, 13824, 5120], P(None, 'row', 'col'), may hold values from -0.0546875 to 0.0546875
- final_gain: float32 [5120], P('col'), may hold values from 0.1 to 1.9
- w_head: bfloat16 [5120, 81920], P(None, ('row', 'col')), may hold values from -32 to 32
- seq_lengths: int32 [8], replicated, may hold values from 1 to 64, 256 in all
- targets: int32 [256], replicated, may hold values from 0 to 81919
Outputs:
- seq_diff: float32 [8], replicated
Inputs may be any that keep to these rules, and one draw needn't show every extreme that they name: `seq_lengths`: the lengths sum to 256 and the largest is exactly 64.
All inputs are finite; a program needn't handle non-finite values.
Results may differ from a plain program's by a relative error of at most 0.02.
Values may be sent and summed in bfloat16 or wider, within the bound.
No kernel may reach another device: no remote copies, remote signals or barrier semaphores. Data moves between devices by JAX's collectives and lax.ppermute only.
A program may use at most 128 MiB of HBM per device.

v0:
```python
import jax
import jax.numpy as jnp
from jax import lax
from jax.sharding import PartitionSpec as P

D = 5120
HEAD_DIM = 128
SEQS = 8


EPSILON = 1e-06
ROPE_BASE = 1000000.0
MASKED = -1e30


def sequence_layout(seq_lengths, token_index):
    ends_at = jnp.cumsum(seq_lengths)
    before = ends_at[None, :] <= token_index[:, None]
    segment = jnp.sum(before.astype(jnp.int32), axis=1)
    starts_at = jnp.sum(jnp.where(before, seq_lengths[None, :], 0), axis=1)
    return (segment, (token_index - starts_at).astype(jnp.float32))


def angles_for(positions, head_width):
    exponent = jnp.arange(head_width // 2, dtype=jnp.float32) * 2.0 / head_width
    frequency = ROPE_BASE ** (-exponent)
    return positions[:, None] * frequency[None, :]


def rotate(features, angles):
    half_width = features.shape[-1] // 2
    lower_half = features[..., :half_width]
    upper_half = features[..., half_width:]
    cosine = jnp.cos(angles)[:, None, :]
    sine_part = jnp.sin(angles)[:, None, :]
    return jnp.concatenate(
        [
            lower_half * cosine - upper_half * sine_part,
            upper_half * cosine + lower_half * sine_part,
        ],
        axis=-1,
    )


def rms_local(features, gain_vector):
    squares = jnp.sum(features * features, axis=1)
    grand_total = lax.psum(squares, "col")
    return features * lax.rsqrt(grand_total / D + EPSILON)[:, None] * gain_vector[None, :]


def feed_forward(mlp_input, gate_up, down_weight):
    ff_local = down_weight.shape[0]
    row_block = mlp_input
    summed = lax.psum_scatter(
        jnp.dot(row_block, gate_up, preferred_element_type=jnp.float32),
        "col",
        scatter_dimension=0,
        tiled=True,
    )
    hidden = (jax.nn.silu(summed[:, :ff_local]) * summed[:, ff_local:]).astype(jnp.bfloat16)
    hidden_all = lax.all_gather(hidden, "col", axis=0, tiled=True)
    row_block = hidden_all
    return lax.psum_scatter(
        jnp.dot(row_block, down_weight, preferred_element_type=jnp.float32),
        "row",
        scatter_dimension=0,
        tiled=True,
    )


def per_device(
    residual,
    attn_gain,
    w_query,
    w_key,
    w_value,
    w_out,
    mlp_gain,
    w_gate,
    w_up,
    w_down,
    final_gain,
    w_head,
    seq_lengths,
    targets,
):
    row_count = lax.axis_size("row")
    col_count = lax.axis_size("col")
    row_index = lax.axis_index("row")
    col_index = lax.axis_index("col")
    local_rows = residual.shape[0]
    total_tokens = local_rows * row_count
    query_heads = w_query.shape[1] // HEAD_DIM
    kv_local = w_key.shape[1] // HEAD_DIM
    group_size = query_heads // kv_local
    query_width = query_heads * HEAD_DIM
    key_width = kv_local * HEAD_DIM
    stream_in = residual.astype(jnp.float32)
    normed = rms_local(stream_in, attn_gain).astype(jnp.bfloat16)
    gathered = lax.all_gather(normed, "row", axis=0, tiled=True)
    w_joint = jnp.concatenate([w_query, w_key, w_value], axis=1)
    joint_part = jnp.dot(gathered, w_joint, preferred_element_type=jnp.float32)
    joint_sums = lax.psum(joint_part, "col")
    token_index = jnp.arange(total_tokens, dtype=jnp.int32)
    segment, positions = sequence_layout(seq_lengths, token_index)
    angles = angles_for(positions, HEAD_DIM)
    queries = rotate(
        joint_sums[:, :query_width].reshape(total_tokens, query_heads, HEAD_DIM), angles
    ).astype(jnp.bfloat16)
    keys_all = rotate(
        joint_sums[:, query_width : query_width + key_width].reshape(
            total_tokens, kv_local, HEAD_DIM
        ),
        angles,
    ).astype(jnp.bfloat16)
    values_all = (
        joint_sums[:, query_width + key_width :]
        .astype(jnp.bfloat16)
        .reshape(total_tokens, kv_local, HEAD_DIM)
    )
    grouped = queries.reshape(total_tokens, kv_local, group_size, HEAD_DIM)
    block_rows = min(512, total_tokens)
    block_count = total_tokens // block_rows

    def attend_block(block_start):
        block_index = block_start + jnp.arange(block_rows, dtype=jnp.int32)
        scores = jnp.einsum(
            "qhgd,khd->hgqk", grouped, keys_all, preferred_element_type=jnp.float32
        ) * HEAD_DIM ** (-0.5)
        allowed = (segment[:, None] == segment[None, :]) & (
            token_index[None, :] <= block_index[:, None]
        )
        scores = jnp.where(allowed[None, None], scores, MASKED)
        top_value = jnp.max(scores, axis=-1, keepdims=True)
        weights = jnp.exp(scores - top_value)
        weights = (weights / jnp.sum(weights, axis=-1, keepdims=True)).astype(jnp.bfloat16)
        result = jnp.einsum(
            "hgqk,khd->qhgd", weights, values_all, preferred_element_type=jnp.float32
        )
        return result.astype(jnp.bfloat16).reshape(block_rows, query_width)

    block_starts = jnp.arange(block_count, dtype=jnp.int32) * block_rows
    attn_all = lax.map(attend_block, block_starts).reshape(total_tokens, query_width)
    projected = lax.psum_scatter(
        jnp.dot(attn_all, w_out, preferred_element_type=jnp.float32),
        "row",
        scatter_dimension=0,
        tiled=True,
    )
    stream = lax.optimization_barrier((stream_in + projected).astype(jnp.bfloat16))
    stream_f = stream.astype(jnp.float32)
    mlp_in = rms_local(stream_f, mlp_gain).astype(jnp.bfloat16)
    mlp_input = lax.all_gather(mlp_in, "row", axis=0, tiled=True)
    outputs = []
    for member in range(2):
        gate_up = jnp.concatenate([w_gate[member], w_up[member]], axis=1)
        outputs.append(stream_f + feed_forward(mlp_input, gate_up, w_down[member]))
    pair_sums = lax.psum(
        (jnp.sum(outputs[0] * outputs[0], axis=1), jnp.sum(outputs[1] * outputs[1], axis=1)), "col"
    )
    policy_final = (
        outputs[0] * lax.rsqrt(pair_sums[0] / D + EPSILON)[:, None] * final_gain[None, :]
    ).astype(jnp.bfloat16)
    refer_final = (
        outputs[1] * lax.rsqrt(pair_sums[1] / D + EPSILON)[:, None] * final_gain[None, :]
    ).astype(jnp.bfloat16)
    tall_pair = (
        lax.all_gather(policy_final, "row", axis=0, tiled=True),
        lax.all_gather(refer_final, "row", axis=0, tiled=True),
    )
    policy_all, refer_all = (
        lax.all_gather(tall_pair[0], "col", axis=1, tiled=True),
        lax.all_gather(tall_pair[1], "col", axis=1, tiled=True),
    )
    vocab_local = w_head.shape[1]
    vocab_start = (row_index * col_count + col_index) * vocab_local
    vocab_ids = vocab_start + jnp.arange(vocab_local, dtype=jnp.int32)
    target_hits = targets[:, None] == vocab_ids[None, :]

    def local_stats(final_all):
        logits = jnp.dot(final_all, w_head, preferred_element_type=jnp.float32)
        local_top = jnp.max(logits, axis=1)
        local_total = jnp.sum(jnp.exp(logits - local_top[:, None]), axis=1)
        picked = jnp.sum(jnp.where(target_hits, logits, 0.0), axis=1)
        return (local_top, local_total, picked)

    policy_top, policy_total, policy_picked = local_stats(policy_all)
    refer_top, refer_total, refer_picked = local_stats(refer_all)
    top_policy, top_refer = lax.pmax((policy_top, refer_top), ("row", "col"))
    vocab_sums = lax.psum(
        (
            policy_total * jnp.exp(policy_top - top_policy),
            refer_total * jnp.exp(refer_top - top_refer),
            policy_picked,
            refer_picked,
        ),
        ("row", "col"),
    )
    policy_logprob = vocab_sums[2] - (top_policy + jnp.log(vocab_sums[0]))
    refer_logprob = vocab_sums[3] - (top_refer + jnp.log(vocab_sums[1]))
    difference = policy_logprob - refer_logprob
    one_hot = (segment[:, None] == jnp.arange(SEQS, dtype=jnp.int32)[None, :]).astype(jnp.float32)
    seq_sums = jnp.dot(difference, one_hot, precision=lax.Precision.HIGHEST)
    return seq_sums / seq_lengths.astype(jnp.float32)


def solution(mesh):
    placed = (
        P("row", "col"),
        P("col"),
        P("col", "row"),
        P("col", "row"),
        P("col", "row"),
        P("row", "col"),
        P("col"),
        P(None, "col", "row"),
        P(None, "col", "row"),
        P(None, "row", "col"),
        P("col"),
        P(None, ("row", "col")),
        P(),
        P(),
    )
    return jax.shard_map(per_device, mesh=mesh, in_specs=placed, out_specs=P(), check_vma=False)
```

profile of v0, /device:TPU:0, one launch (start us, length us, event | category | flops | bytes accessed | tf_op | source)
XLA Modules:
  0.0 643.2 jit_solution(11914020283448620208)
XLA Ops:
  7.7 18.1 %psum.63 = f32[64]{0:T(128)S(1)} all-reduce(f32[64]{0:T(128)S(1)} %fusion.39), channel_id=1, replica_groups=mesh['row'=4,'col'=8] {'col'}, use_global_device_ids=true, to_apply=%region_1.0 | all-reduce | flops 64 | bytes 512 | tf_op jit(solution)/shard_map/psum | solution.py:47
  26.7 9.3 %all_gather.24 = bf16[256,640]{1,0:T(8,128)(2,1)S(1)} all-gather(bf16[64,640]{1,0:T(8,128)(2,1)S(1)} %fusion.41), channel_id=1, replica_groups=mesh['row'=4,'col'=8] {'row'}, dimensions={0}, use_global_device_ids=true | all-gather | bytes 409600 | tf_op jit(solution)/shard_map/all_gather | solution.py:100
  42.7 57.8 %all-reduce.5.cloned.1.call-done = f32[256,1792]{1,0:T(8,128)} async-done(((f32[256,1792]{1,0:T(8,128)}), f32[256,1792]{1,0:T(8,128)}) %all-reduce.5.cloned.1.call-update) | async-done | bytes 1835024 | tf_op jit(solution)/shard_map/psum | solution.py:103
  120.5 13.2 %slice_bitcast_fusion.2 = (bf16[640,3456]{1,0:T(8,128)(2,1)}, bf16[640,3456]{1,0:T(8,128)(2,1)}, bf16[640,3456]{1,0:T(8,128)(2,1)}, bf16[640,3456]{1,0:T(8,128)(2,1)}) fusion(bf16[2,640,3456]{2,1,0:T(8,128)(2,1)} %param.22, bf16[2,640,3456]{2,1,0:T(8,128)(2,1)} %param.21), kind=kLoop, calls=%fused_computation.17 | loop fusion | bytes 35389440 | tf_op jit(solution)/shard_map/squeeze | solution.py:156
  133.7 11.8 %reduce-scatter.6.cloned.1.call-done = f32[64,640]{1,0:T(8,128)} async-done(((f32[256,640]{1,0:T(8,128)}), f32[64,640]{1,0:T(8,128)}) %reduce-scatter.6.cloned.1.call-update) | async-done | bytes 163856 | tf_op jit(solution)/shard_map/reduce_scatter | solution.py:144
  146.6 16.3 %psum.65 = f32[64]{0:T(128)S(1)} all-reduce(f32[64]{0:T(128)S(1)} %fusion.43), channel_id=1, replica_groups=mesh['row'=4,'col'=8] {'col'}, use_global_device_ids=true, to_apply=%region_10.11 | all-reduce | flops 64 | bytes 512 | tf_op jit(solution)/shard_map/psum | solution.py:47
  162.9 9.2 %all_gather.25 = bf16[256,640]{1,0:T(8,128)(2,1)S(1)} all-gather(bf16[64,640]{1,0:T(8,128)(2,1)S(1)} %fusion.45), channel_id=1, replica_groups=mesh['row'=4,'col'=8] {'row'}, dimensions={0}, use_global_device_ids=true | all-gather | bytes 409600 | tf_op jit(solution)/shard_map/all_gather | solution.py:153
  172.1 9.5 %fusion.5 = f32[256,6912]{1,0:T(8,128)} fusion(bf16[256,640]{1,0:T(8,128)(2,1)S(1)} %all_gather.25, bf16[640,3456]{1,0:T(8,128)(2,1)} %get-tuple-element.45, bf16[640,3456]{1,0:T(8,128)(2,1)} %get-tuple-element.64), kind=kOutput, calls=%fused_computation.5 | convolution fusion | flops 2282618880 | bytes 16252928 | tf_op jit(solution)/shard_map/dot_general | solution.py:55
  181.6 9.7 %fusion.1 = f32[256,6912]{1,0:T(8,128)} fusion(bf16[256,640]{1,0:T(8,128)(2,1)S(1)} %all_gather.25, bf16[640,3456]{1,0:T(8,128)(2,1)} %get-tuple-element.44, bf16[640,3456]{1,0:T(8,128)(2,1)} %get-tuple-element.65), kind=kOutput, calls=%fused_computation.1 | convolution fusion | flops 2282618880 | bytes 16252928 | tf_op jit(solution)/shard_map/dot_general | solution.py:55
  191.4 64.8 %reduce-scatter.12.cloned.1.call-done = f32[32,6912]{1,0:T(8,128)} async-done(((f32[256,6912]{1,0:T(8,128)}), f32[32,6912]{1,0:T(8,128)}) %reduce-scatter.12.cloned.1.call-update) | async-done | bytes 884752 | tf_op jit(solution)/shard_map/reduce_scatter | solution.py:54
  258.2 75.9 %reduce-scatter.8.cloned.1.call-done = f32[32,6912]{1,0:T(8,128)} async-done(((f32[256,6912]{1,0:T(8,128)}), f32[32,6912]{1,0:T(8,128)}) %reduce-scatter.8.cloned.1.call-update) | async-done | bytes 884752 | tf_op jit(solution)/shard_map/reduce_scatter | solution.py:54
  336.3 24.1 %all-gather.9.cloned.1.call-done = bf16[256,3456]{1,0:T(8,128)(2,1)} async-done(((bf16[32,3456]{1,0:T(8,128)(2,1)}), bf16[256,3456]{1,0:T(8,128)(2,1)}) %all-gather.9.cloned.1.call-update) | async-done | bytes 1769488 | tf_op jit(solution)/shard_map/all_gather | solution.py:61
  365.8 22.2 %all-gather.5.cloned.1.call-done = bf16[256,3456]{1,0:T(8,128)(2,1)} async-done(((bf16[32,3456]{1,0:T(8,128)(2,1)}), bf16[256,3456]{1,0:T(8,128)(2,1)}) %all-gather.5.cloned.1.call-update) | async-done | bytes 1769488 | tf_op jit(solution)/shard_map/all_gather | solution.py:61
  393.3 22.9 %reduce-scatter.14.cloned.1.call-done = f32[64,640]{1,0:T(8,128)} async-done(((f32[256,640]{1,0:T(8,128)}), f32[64,640]{1,0:T(8,128)}) %reduce-scatter.14.cloned.1.call-update) | async-done | bytes 163856 | tf_op jit(solution)/shard_map/reduce_scatter | solution.py:63
  416.2 28.3 %reduce-scatter.10.cloned.1.call-done = f32[64,640]{1,0:T(8,128)} async-done(((f32[256,640]{1,0:T(8,128)}), f32[64,640]{1,0:T(8,128)}) %reduce-scatter.10.cloned.1.call-update) | async-done | bytes 163856 | tf_op jit(solution)/shard_map/reduce_scatter | solution.py:63
  445.6 16.3 %all-reduce.2 = (f32[64]{0:T(128)S(1)}, f32[64]{0:T(128)S(1)}) all-reduce(f32[64]{0:T(128)S(1)} %get-tuple-element.30, f32[64]{0:T(128)S(1)} %get-tuple-element.28), channel_id=1, replica_groups=mesh['row'=4,'col'=8] {'col'}, use_global_device_ids=true, to_apply=%region_24.25 | all-reduce | flops 128 | bytes 1024 | tf_op jit(solution)/shard_map/psum | solution.py:158
  463.0 10.3 %all_gather.27 = bf16[256,640]{1,0:T(8,128)(2,1)} all-gather(bf16[64,640]{1,0:T(8,128)(2,1)S(1)} %get-tuple-element.52), channel_id=1, replica_groups=mesh['row'=4,'col'=8] {'row'}, dimensions={0}, use_global_device_ids=true | all-gather | bytes 409600 | tf_op jit(solution)/shard_map/all_gather | solution.py:168
  473.3 9.0 %all_gather.30 = bf16[256,640]{1,0:T(8,128)(2,1)} all-gather(bf16[64,640]{1,0:T(8,128)(2,1)S(1)} %get-tuple-element.53), channel_id=1, replica_groups=mesh['row'=4,'col'=8] {'row'}, dimensions={0}, use_global_device_ids=true | all-gather | bytes 409600 | tf_op jit(solution)/shard_map/all_gather | solution.py:169
  482.4 21.7 %all-gather.7.cloned.1.call-done = bf16[256,5120]{1,0:T(8,128)(2,1)} async-done(((bf16[256,640]{1,0:T(8,128)(2,1)}), bf16[256,5120]{1,0:T(8,128)(2,1)}) %all-gather.7.cloned.1.call-update) | async-done | bytes 2621456 | tf_op jit(solution)/shard_map/all_gather | solution.py:172
  504.1 14.1 %fusion.61 = (f32[256]{0:T(256)S(1)}, f32[256,2560]{1,0:T(8,128)}) fusion(bf16[256,5120]{1,0:T(8,128)(2,1)} %all-gather.7.cloned.1.call-done, bf16[5120,2560]{1,0:T(8,128)(2,1)} %param.25), kind=kOutput, calls=%fused_computation.101 | convolution fusion | flops 6711541760 | bytes 31458304 | tf_op jit(solution)/shard_map/dot_general | solution.py:181
  518.2 20.3 %all-gather.11.cloned.1.call-done = bf16[256,5120]{1,0:T(8,128)(2,1)} async-done(((bf16[256,640]{1,0:T(8,128)(2,1)}), bf16[256,5120]{1,0:T(8,128)(2,1)}) %all-gather.11.cloned.1.call-update) | async-done | bytes 2621456 | tf_op jit(solution)/shard_map/all_gather | solution.py:173
  538.6 13.8 %fusion.62 = (f32[256]{0:T(256)S(1)}, f32[256,2560]{1,0:T(8,128)}) fusion(bf16[256,5120]{1,0:T(8,128)(2,1)} %all-gather.11.cloned.1.call-done, bf16[5120,2560]{1,0:T(8,128)(2,1)} %param.25), kind=kOutput, calls=%fused_computation.102 | convolution fusion | flops 6711541760 | bytes 31458304 | tf_op jit(solution)/shard_map/dot_general | solution.py:181
  552.4 40.1 %all-reduce.1 = (f32[256]{0:T(256)S(1)}, f32[256]{0:T(256)S(1)}) all-reduce(f32[256]{0:T(256)S(1)} %get-tuple-element.62, f32[256]{0:T(256)S(1)} %get-tuple-element.60), channel_id=1, replica_groups=mesh['row'=4,'col'=8] {'row','col'}, use_global_device_ids=true, to_apply=%region_28.29 | all-reduce | flops 512 | bytes 4096 | tf_op jit(solution)/shard_map/pmax | solution.py:189
  596.5 39.1 %all-reduce = (f32[256]{0:T(256)S(1)}, f32[256]{0:T(256)S(1)}, f32[256]{0:T(256)S(1)}, f32[256]{0:T(256)S(1)}) all-reduce(f32[256]{0:T(256)S(1)} %get-tuple-element.54, f32[256]{0:T(256)S(1)} %exponential_multiply_fusion, f32[256]{0:T(256)S(1)} %get-tuple-element.18, ...), channel_id=1, replica_groups=mesh['row'=4,'col'=8] {'row','col'}, use_global_device_ids=true, to_apply=%region_26.27 | all-reduce | flops 1024 | bytes 8192 | tf_op jit(solution)/shard_map/psum | solution.py:190
  (82 shorter events, 52.0 us)
Async XLA Ops:
  6.5 112.3 %copy-start = (bf16[1280,640]{1,0:T(8,128)(2,1)S(1)}, bf16[1280,640]{1,0:T(8,128)(2,1)}, u32[]{:S(2)}) copy-start(bf16[1280,640]{1,0:T(8,128)(2,1)} %param.19) | copy-start | bytes 4915204
  6.5 93.9 %all-reduce.5.cloned.1.call-start = ((), (), s32[]{:S(2)}) async-start(), calls=%async_computation.5 | async-start | bytes 3670016 | tf_op jit(solution)/shard_map/psum | solution.py:103
  36.0 3.9 copy-start.8
  39.8 105.7 %reduce-scatter.6.cloned.1.call-start = ((), (), s32[]{:S(2)}) async-start(), calls=%async_computation.6 | async-start | bytes 819200 | tf_op jit(solution)/shard_map/reduce_scatter | solution.py:144
  40.5 60.0 %copy-start.3 = (f32[256,64]{0,1:T(8,128)}, f32[256,64]{0,1:T(8,128)S(1)}, u32[]{:S(2)}) copy-start(f32[256,64]{0,1:T(8,128)S(1)} %get-tuple-element.56) | copy-start | bytes 196612
  40.5 60.0 %copy-start.4 = (f32[256,64]{0,1:T(8,128)}, f32[256,64]{0,1:T(8,128)S(1)}, u32[]{:S(2)}) copy-start(f32[256,64]{0,1:T(8,128)S(1)} %get-tuple-element.57) | copy-start | bytes 196612
  120.5 25.0 %copy-start.2 = (bf16[64,640]{1,0:T(8,128)(2,1)S(1)}, bf16[64,640]{1,0:T(8,128)(2,1)}, u32[]{:S(2)}) copy-start(bf16[64,640]{1,0:T(8,128)(2,1)} %param.14) | copy-start | bytes 245764
  120.5 42.3 %copy-start.6 = (f32[640]{0:T(1024)S(1)}, f32[640]{0:T(1024)}, u32[]{:S(2)}) copy-start(f32[640]{0:T(1024)} %param.20) | copy-start | bytes 7684
  120.5 135.7 %reduce-scatter.12.cloned.1.call-start = ((), (), s32[]{:S(2)}) async-start(), calls=%async_computation.11 | async-start | bytes 7962624 | tf_op jit(solution)/shard_map/reduce_scatter | solution.py:54
  181.6 152.5 %reduce-scatter.8.cloned.1.call-start = ((), (), s32[]{:S(2)}) async-start(), calls=%async_computation.7 | async-start | bytes 7962624 | tf_op jit(solution)/shard_map/reduce_scatter | solution.py:54
  191.4 169.1 %all-gather.9.cloned.1.call-start = ((), (), s32[]{:S(2)}) async-start(), calls=%async_computation.12 | async-start | bytes 1990656 | tf_op jit(solution)/shard_map/all_gather | solution.py:61
  258.2 129.8 %all-gather.5.cloned.1.call-start = ((), (), s32[]{:S(2)}) async-start(), calls=%async_computation.8 | async-start | bytes 1990656 | tf_op jit(solution)/shard_map/all_gather | solution.py:61
  336.1 80.0 %reduce-scatter.14.cloned.1.call-start = ((), (), s32[]{:S(2)}) async-start(), calls=%async_computation.13 | async-start | bytes 819200 | tf_op jit(solution)/shard_map/reduce_scatter | solution.py:63
  365.7 96.2 %copy-start.5 = (f32[640]{0:T(1024)S(1)}, f32[640]{0:T(1024)}, u32[]{:S(2)}) copy-start(f32[640]{0:T(1024)} %param.24) | copy-start | bytes 7684
  365.7 78.7 %reduce-scatter.10.cloned.1.call-start = ((), (), s32[]{:S(2)}) async-start(), calls=%async_computation.9 | async-start | bytes 819200 | tf_op jit(solution)/shard_map/reduce_scatter | solution.py:63
  393.2 110.9 %all-gather.7.cloned.1.call-start = ((), (), s32[]{:S(2)}) async-start(), calls=%async_computation.10 | async-start | bytes 2949120 | tf_op jit(solution)/shard_map/all_gather | solution.py:172
  473.3 65.3 %all-gather.11.cloned.1.call-start = ((), (), s32[]{:S(2)}) async-start(), calls=%async_computation.14 | async-start | bytes 2949120 | tf_op jit(solution)/shard_map/all_gather | solution.py:173
  518.2 74.2 %copy-start.7 = (s32[256]{0:T(256)S(1)}, s32[256]{0:T(256)}, u32[]{:S(2)}) copy-start(s32[256]{0:T(256)} %param.27) | copy-start | bytes 3076
  592.5 43.9 %copy-start.1 = (bf16[1280,640]{1,0:T(8,128)(2,1)S(1)}, bf16[1280,640]{1,0:T(8,128)(2,1)}, u32[]{:S(2)}) copy-start(bf16[1280,640]{1,0:T(8,128)(2,1)} %param.19) | copy-start | bytes 4915204
Sparse Core Ops, SparseCore 0:
  39.9 60.5 all-reduce.4
  120.6 24.8 reduce-scatter.5
  181.7 74.4 reduce-scatter.11
  258.5 75.5 reduce-scatter.7
  335.7 24.7 all-gather.8
  362.0 25.9 all-gather.4
  391.1 24.9 reduce-scatter.13
  419.0 25.3 reduce-scatter.9
  473.4 30.6 all-gather.6
  505.7 32.8 all-gather.10
where the time goes:
time: 644 us; the launch traced here: 643 us
  waiting for transfers between devices  350 us (54%)
  blocking collectives  167 us (26%)
  matrix products  69.4 us (11%)
  local copies, waits for them, and re-layouts  23.8 us (4%)
  other arithmetic  18.4 us (3%)
  between operations  13.7 us (2%)
    reduce_scatter x2, waiting for transfers between devices, feed_forward(): lax.psum_scatter(jnp.dot(row_block, gate_up, preferred_element_type=jnp.f...  141 us
    psum x1, waiting for transfers between devices, per_device(): joint_sums = lax.psum(joint_part, 'col')  57.8 us
    reduce_scatter x2, waiting for transfers between devices, feed_forward(): lax.psum_scatter(jnp.dot(row_block, down_weight, preferred_element_type=j...  51.2 us
    all_gather x2, waiting for transfers between devices, feed_forward(): hidden_all = lax.all_gather(hidden, 'col', axis=0, tiled=True)  46.3 us
    pmax x1, blocking collectives, per_device(): top_policy, top_refer = lax.pmax((policy_top, refer_top), ('row', 'col'))  40.1 us
    psum x1, blocking collectives, per_device(): lax.psum((policy_total * jnp.exp(policy_top - top_policy), refer_total *...  39.1 us
    psum x2, blocking collectives, rms_local(): grand_total = lax.psum(squares, 'col')  34.3 us
    dot_general x2, matrix products, local_stats(): logits = jnp.dot(final_all, w_head, preferred_element_type=jnp.float32)  27.9 us
  transfers between devices with their start and end apart: 10, of which 10 were waited for; matrix products, arithmetic and copies ran while one was open for 8% of the time, Pallas kernels for 0%

commit v1 on v0

v1 whole, which is shorter than its diff:
```python
import functools

import jax
import jax.numpy as jnp
from jax import lax
from jax.experimental import pallas as pl
from jax.experimental.pallas import tpu as pltpu
from jax.sharding import PartitionSpec as P

D = 5120
HEAD_DIM = 128
SEQS = 8
LONGEST = 64

EPSILON = 1e-06
ROPE_BASE = 1000000.0
MASKED = -1e30
BF16 = jnp.bfloat16
F32 = jnp.float32
MIB = 1 << 20

VMEM = pl.BlockSpec(memory_space=pltpu.VMEM)
SMEM = pl.BlockSpec(memory_space=pltpu.SMEM)


def params(mib):
    return pltpu.CompilerParams(vmem_limit_bytes=mib * MIB)


def cost(flops, byte_count):
    return pl.CostEstimate(flops=flops, bytes_accessed=byte_count, transcendentals=0)


def row_xor(x, mask):
    count = lax.axis_size("row")
    return lax.ppermute(x, "row", [(i, i ^ mask) for i in range(count)])


def col_xor(x, mask):
    count = lax.axis_size("col")
    return lax.ppermute(x, "col", [(i, i ^ mask) for i in range(count)])


def tree_sum(values):
    values = list(values)
    while len(values) > 1:
        values = [values[i] + values[i + 1] for i in range(0, len(values), 2)]
    return values[0]


def col_sum(x):
    return tree_sum([x] + [col_xor(x, j) for j in range(1, lax.axis_size("col"))])


def sequence_layout(seq_lengths, token_index):
    ends_at = jnp.cumsum(seq_lengths)
    before = ends_at[None, :] <= token_index[:, None]
    segment = jnp.sum(before.astype(jnp.int32), axis=1)
    starts_at = jnp.sum(jnp.where(before, seq_lengths[None, :], 0), axis=1)
    return (segment, (token_index - starts_at).astype(F32))


def assemble(offsets, blocks, gain, x_ref, unit):
    step = 0
    for block in blocks:
        for first in range(0, block.shape[0], unit):
            rows = block[first : first + unit, :].astype(F32) * gain[...]
            place = pl.multiple_of(offsets[step], unit)
            x_ref[pl.ds(place, unit), :] = rows.astype(BF16)
            step += 1


def qkv_kernel(unit, count, offsets, *refs):
    blocks, (gain, wq, wk, wv, keep, send, x_ref) = refs[:count], refs[count:]
    assemble(offsets, blocks, gain, x_ref, unit)
    half = keep.shape[0]
    x = x_ref[...]
    at = 0
    for w in (wq, wk, wv):
        width = w.shape[1]
        part = jnp.dot(x, w[...], preferred_element_type=F32).astype(BF16)
        keep[:, at : at + width] = part[:half]
        send[:, at : at + width] = part[half:]
        at += width


def core_add_kernel(keep, recv, *outs):
    rows = outs[0].shape[0]
    for i, out in enumerate(outs):
        a = keep[i * rows : (i + 1) * rows, :].astype(F32)
        b = recv[i * rows : (i + 1) * rows, :].astype(F32)
        out[...] = (a + b).astype(out.dtype)


def rope_kernel(rotated, count, *refs):
    parts, (scale, cosine, sine, out) = refs[:count], refs[count:]
    width = out.shape[1]
    for at in range(0, width, HEAD_DIM):
        total = parts[0][:, at : at + HEAD_DIM].astype(F32)
        for part in parts[1:]:
            total = total + part[:, at : at + HEAD_DIM].astype(F32)
        total = total * scale[...]
        if at < rotated:
            total = total * cosine[...] + pltpu.roll(total, HEAD_DIM // 2, 1) * sine[...]
        out[:, at : at + HEAD_DIM] = total.astype(BF16)


def attention_kernel(heads, kv_heads, count, block, places, row_places, *refs):
    pieces, rest = refs[:count], refs[count:]
    bias, w_out = rest[0], rest[1]
    outs, (qkv, attended) = rest[2:-2], rest[-2:]
    unit = pieces[0].shape[0]
    for i, piece in enumerate(pieces):
        qkv[pl.ds(pl.multiple_of(places[i], unit), unit), :] = piece[...]
    tokens = qkv.shape[0]
    group = heads // kv_heads
    window = min(tokens, block + LONGEST)
    row_unit = outs[0].shape[0]
    for start in range(0, tokens, block):
        first = max(0, start + block - window)
        mask = bias[start : start + block, :]
        mask = jnp.concatenate([mask] * group, axis=0)
        for g in range(kv_heads):
            q = jnp.concatenate(
                [
                    qkv[start : start + block, h * HEAD_DIM : (h + 1) * HEAD_DIM]
                    for h in range(g * group, (g + 1) * group)
                ],
                axis=0,
            )
            k_at = (heads + g) * HEAD_DIM
            v_at = (heads + kv_heads + g) * HEAD_DIM
            k = qkv[first : first + window, k_at : k_at + HEAD_DIM]
            v = qkv[first : first + window, v_at : v_at + HEAD_DIM]
            scores = lax.dot_general(
                q, k, (((1,), (1,)), ((), ())), preferred_element_type=F32
            ) * HEAD_DIM ** (-0.5)
            scores = scores + mask
            weights = jnp.exp(scores - jnp.max(scores, axis=1, keepdims=True))
            total = jnp.sum(weights, axis=1, keepdims=True)
            weights = (weights / total).astype(BF16)
            result = jnp.dot(weights, v, preferred_element_type=F32).astype(BF16)
            for h in range(group):
                at = (g * group + h) * HEAD_DIM
                for sub in range(0, block, row_unit):
                    place = pl.multiple_of(row_places[(start + sub) // row_unit], row_unit)
                    attended[pl.ds(place, row_unit), at : at + HEAD_DIM] = result[
                        h * block + sub : h * block + sub + row_unit
                    ]
    product = jnp.dot(attended[...], w_out[...], preferred_element_type=F32)
    for i, out in enumerate(outs):
        out[...] = product[i * row_unit : (i + 1) * row_unit].astype(out.dtype)


def arrange_kernel(unit, offsets, *refs):
    blocks, (gain, out) = refs[:-2], refs[-2:]
    assemble(offsets, blocks, gain, out, unit)


def gate_up_kernel(x, w_gate, w_up, keep, send):
    half = keep.shape[1]
    for i, w in enumerate((w_gate, w_up)):
        part = jnp.dot(x[...], w[0], preferred_element_type=F32).astype(BF16)
        keep[i] = part[:half]
        send[i] = part[half:]


def down_kernel(count, places, *refs):
    own, other, w_down = refs[:count], refs[count : 2 * count], refs[2 * count]
    outs, total = refs[2 * count + 1 : -1], refs[-1]
    at = 0
    for i in range(count):
        hidden = jnp.concatenate([own[i][...], other[i][...]], axis=0)
        width = hidden.shape[1]
        part = jnp.dot(hidden, w_down[0, at : at + width, :], preferred_element_type=F32)
        total[...] = part if i == 0 else total[...] + part
        at += width
    unit = outs[0].shape[0]
    for i, out in enumerate(outs):
        place = pl.multiple_of(places[i], unit)
        out[...] = total[pl.ds(place, unit), :].astype(out.dtype)


def head_kernel(rows, col_index, row_places, *refs):
    own, other = refs[:rows], refs[rows : 2 * rows]
    scale, target, w, out, lhs, top, total, picked = refs[2 * rows :]
    step = pl.program_id(0)
    blocks, unit = own[0].shape[0], own[0].shape[1]

    @pl.when(step == 0)
    def _():
        for core, arrays in enumerate((own, other)):
            for i, array in enumerate(arrays):
                place = pl.multiple_of(row_places[i], unit)
                for j in range(blocks):
                    feature = col_index[2 * j + core]
                    lhs[feature, pl.ds(place, unit), :] = array[j]
        top[...] = jnp.full_like(top, MASKED)
        total[...] = jnp.zeros_like(total)
        picked[...] = jnp.zeros_like(picked)

    depth = lhs.shape[2]
    logits = jnp.dot(lhs[0], w[:depth, :], preferred_element_type=F32)
    for i in range(1, lhs.shape[0]):
        logits += jnp.dot(
            lhs[i], w[i * depth : (i + 1) * depth, :], preferred_element_type=F32
        )
    logits = logits * scale[...]
    width = logits.shape[1]
    lane = lax.broadcasted_iota(jnp.int32, logits.shape, 1) + step * width
    hit = jnp.where(lane == target[...], logits, 0.0)
    picked[...] += jnp.sum(hit, axis=1, keepdims=True)
    new_top = jnp.maximum(top[...], jnp.max(logits, axis=1, keepdims=True))
    total[...] = total[...] * jnp.exp(top[...] - new_top) + jnp.sum(
        jnp.exp(logits - new_top), axis=1, keepdims=True
    )
    top[...] = new_top

    @pl.when(step == pl.num_programs(0) - 1)
    def _():
        place = lax.broadcasted_iota(jnp.int32, out.shape, 1)
        out[...] = jnp.where(
            place == 0, top[...], jnp.where(place == 1, total[...], picked[...])
        )


def chain_reduce(near, far, add_near, pairs_of):
    length = lax.axis_size("col") // 2
    middle = length // 2 - 1
    for hop in range(length - 1):
        if hop <= middle:
            received = lax.ppermute(far, "col", pairs_of(hop))
        else:
            received = lax.ppermute(near, "col", pairs_of(hop))
        if hop < middle:
            far = (far.astype(F32) + received.astype(F32)).astype(BF16)
        else:
            near = add_near(near, received, hop)
    return near


def per_device(
    residual,
    attn_gain,
    w_query,
    w_key,
    w_value,
    w_out,
    mlp_gain,
    w_gate,
    w_up,
    w_down,
    final_gain,
    w_head,
    seq_lengths,
    targets,
):
    row_count = lax.axis_size("row")
    col_count = lax.axis_size("col")
    chips = col_count // 2
    row_index = lax.axis_index("row")
    col_index = lax.axis_index("col")
    core = col_index % 2
    chip = col_index // 2
    row_tokens, features = residual.shape
    tokens = row_tokens * row_count
    col_tokens = tokens // col_count
    quarter = tokens // 4
    heads = w_query.shape[1] // HEAD_DIM
    kv_heads = w_key.shape[1] // HEAD_DIM
    qkv_width = w_query.shape[1] + 2 * w_key.shape[1]
    rotated = w_query.shape[1] + w_key.shape[1]
    ff_local = w_gate.shape[2]
    vocab_local = w_head.shape[1]

    row_range = jnp.arange(row_count, dtype=jnp.int32)
    col_range = jnp.arange(col_count, dtype=jnp.int32)
    row_rel = row_range ^ row_index
    col_rel = col_range ^ col_index

    token_index = jnp.arange(tokens, dtype=jnp.int32)
    segment, positions = sequence_layout(seq_lengths, token_index)
    block = min(64, tokens)
    window = min(tokens, block + LONGEST)
    first_key = jnp.maximum(0, (token_index // block + 1) * block - window)
    key_index = first_key[:, None] + jnp.arange(window, dtype=jnp.int32)[None, :]
    key_segment, _ = sequence_layout(seq_lengths, key_index.reshape(-1))
    allowed = (key_segment.reshape(tokens, window) == segment[:, None]) & (
        key_index <= token_index[:, None]
    )
    bias = jnp.where(allowed, 0.0, MASKED).astype(F32)
    own_positions = lax.dynamic_slice_in_dim(positions, col_index * col_tokens, col_tokens)
    exponent = jnp.arange(HEAD_DIM // 2, dtype=F32) * 2.0 / HEAD_DIM
    angles = own_positions[:, None] * (ROPE_BASE ** (-exponent))[None, :]
    cosine, sine = jnp.cos(angles), jnp.sin(angles)
    cosine = jnp.concatenate([cosine, cosine], axis=1)
    sine = jnp.concatenate([-sine, sine], axis=1)

    blocks = [residual] + [row_xor(residual, j) for j in range(1, row_count)]
    squares = jnp.stack([jnp.sum(jnp.square(b.astype(F32)), axis=1) for b in blocks])
    scale_rel = lax.rsqrt(col_sum(squares) / D + EPSILON).reshape(-1)
    own_first = col_index * col_tokens
    own_place = ((own_first // row_tokens) ^ row_index) * row_tokens + own_first % row_tokens
    own_scale = lax.dynamic_slice_in_dim(scale_rel, own_place, col_tokens)[:, None]

    per_row = row_tokens // col_tokens
    col_block = (row_rel[:, None] * per_row + jnp.arange(per_row, dtype=jnp.int32)).reshape(-1)
    relative = col_block ^ col_index
    offsets = ((relative & 1) * chips + (relative >> 1)) * col_tokens
    half = tokens // 2
    shape = functools.partial(jax.ShapeDtypeStruct)
    keep, send = pl.pallas_call(
        functools.partial(qkv_kernel, col_tokens, row_count),
        out_shape=[shape((half, qkv_width), BF16)] * 2,
        in_specs=[SMEM] + [VMEM] * (row_count + 4),
        out_specs=[VMEM] * 2,
        scratch_shapes=[pltpu.VMEM((tokens, features), BF16)],
        compiler_params=params(24),
        cost_estimate=cost(
            2 * tokens * features * qkv_width, 2 * qkv_width * (features + tokens)
        ),
        name="qkv_partial",
    )(offsets, *blocks, attn_gain[None, :], w_query, w_key, w_value)
    received = col_xor(send, 1)
    parts = pl.pallas_call(
        core_add_kernel,
        out_shape=[shape((col_tokens, qkv_width), F32 if i == 0 else BF16) for i in range(chips)],
        in_specs=[VMEM] * 2,
        out_specs=[VMEM] * chips,
        compiler_params=params(16),
        cost_estimate=cost(half * qkv_width, 6 * half * qkv_width),
        name="qkv_core_add",
    )(keep, received)
    parts = [parts[0]] + [col_xor(parts[j], 2 * j) for j in range(1, chips)]
    mine = pl.pallas_call(
        functools.partial(rope_kernel, rotated, chips),
        out_shape=shape((col_tokens, qkv_width), BF16),
        in_specs=[VMEM] * (chips + 3),
        out_specs=VMEM,
        compiler_params=params(16),
        cost_estimate=cost(8 * col_tokens * qkv_width, 2 * tokens * qkv_width),
        name="qkv_rope",
    )(*parts, own_scale, cosine, sine)
    pieces = [mine] + [col_xor(mine, 2 * j) for j in range(1, chips)]
    pieces = pieces + [col_xor(piece, 1) for piece in pieces]
    piece_index = [2 * j for j in range(chips)] + [2 * j + 1 for j in range(chips)]
    places = (jnp.array(piece_index, jnp.int32) ^ col_index) * col_tokens

    projected = pl.pallas_call(
        functools.partial(attention_kernel, heads, kv_heads, col_count, block),
        out_shape=[shape((row_tokens, features), F32 if i == 0 else BF16) for i in range(row_count)],
        in_specs=[SMEM] * 2 + [VMEM] * (col_count + 2),
        out_specs=[VMEM] * row_count,
        scratch_shapes=[
            pltpu.VMEM((tokens, qkv_width), BF16),
            pltpu.VMEM((tokens, heads * HEAD_DIM), BF16),
        ],
        compiler_params=params(32),
        cost_estimate=cost(
            2 * tokens * heads * HEAD_DIM * features * 2, 2 * heads * HEAD_DIM * features * 2
        ),
        name="attention_out",
    )(places, row_rel * row_tokens, *pieces, bias, w_out)
    projected = [projected[0]] + [row_xor(projected[j], j) for j in range(1, row_count)]
    stream = residual.astype(F32) + tree_sum([p.astype(F32) for p in projected])
    stream = lax.optimization_barrier(stream.astype(BF16))
    stream_f = stream.astype(F32)

    blocks = [stream] + [row_xor(stream, j) for j in range(1, row_count)]
    squares = jnp.stack([jnp.sum(jnp.square(b.astype(F32)), axis=1) for b in blocks])
    scale_rel = lax.rsqrt(col_sum(squares) / D + EPSILON)
    per_quarter = row_count // 4
    upper = (chip >= chips // 2).astype(jnp.int32)
    quarter_own = upper * 2 + core
    quarter_rows = (quarter_own * per_quarter + jnp.arange(per_quarter, dtype=jnp.int32)) ^ row_index
    near_scale = jnp.take(scale_rel, quarter_rows, axis=0).reshape(quarter)[:, None]
    at_end = (chip == 0) | (chip == chips - 1)
    near_scale_end = jnp.where(at_end, near_scale, 0.0)
    relative = (row_rel // per_quarter) ^ quarter_own
    quarter_offsets = ((relative & 1) * 2 + (relative >> 1)) * quarter + (
        row_rel % per_quarter
    ) * row_tokens
    mlp_in = pl.pallas_call(
        functools.partial(arrange_kernel, row_tokens),
        out_shape=shape((tokens, features), BF16),
        in_specs=[SMEM] + [VMEM] * (row_count + 1),
        out_specs=VMEM,
        compiler_params=params(16),
        cost_estimate=cost(tokens * features, 4 * tokens * features),
        name="mlp_in",
    )(quarter_offsets, *blocks, mlp_gain[None, :])

    chunk_count = 3 if ff_local % (3 * HEAD_DIM) == 0 else 1
    chunk = ff_local // chunk_count
    tile = chunk // 3 if chunk % (3 * HEAD_DIM) == 0 else chunk
    tiles = chunk // tile

    def pairs_of(hop):
        pairs = []
        for k in range(2):
            pairs.append((2 * hop + k, 2 * (hop + 1) + k))
            pairs.append((2 * (chips - 1 - hop) + k, 2 * (chips - 2 - hop) + k))
        return pairs

    def back_of(hop):
        return [(b, a) for a, b in pairs_of(hop)]

    def gate_up(member, index):
        first = index * tiles
        return pl.pallas_call(
            gate_up_kernel,
            grid=(tiles,),
            out_shape=[shape((2, half, chunk), BF16)] * 2,
            in_specs=[
                pl.BlockSpec((tokens, features), lambda i: (0, 0)),
                pl.BlockSpec((1, features, tile), lambda i: (member, 0, first + i)),
                pl.BlockSpec((1, features, tile), lambda i: (member, 0, first + i)),
            ],
            out_specs=[pl.BlockSpec((2, half, tile), lambda i: (0, 0, i))] * 2,
            compiler_params=params(24),
            cost_estimate=cost(
                4 * tokens * features * chunk, 4 * chunk * (features + tokens)
            ),
            name="gate_up",
        )(mlp_in, w_gate, w_up)

    def add_near(near, received, hop):
        total = near.astype(F32) + received.astype(F32)
        if hop < chips - 2:
            return total.astype(BF16)
        gate = total[0] * near_scale_end
        up = total[1] * near_scale_end
        return (gate / (1.0 + jnp.exp(-gate)) * up).astype(BF16)

    def hidden_chunk(member, index):
        keep, send = gate_up(member, index)
        received = col_xor(send, 1)
        far = (keep[:, quarter:].astype(F32) + received[:, quarter:].astype(F32)).astype(BF16)
        near = (keep[:, :quarter].astype(F32) + received[:, :quarter].astype(F32)).astype(BF16)
        hidden = chain_reduce(near, far, add_near, pairs_of)
        middle = chips // 2 - 1
        moving = hidden
        near_sum, far_sum = hidden, None
        for hop in range(chips - 2, -1, -1):
            moving = lax.ppermute(moving, "col", back_of(hop))
            if hop > middle:
                near_sum = near_sum + moving
            else:
                far_sum = moving if far_sum is None else far_sum + moving
        own = jnp.concatenate([near_sum, far_sum], axis=0)
        return own, col_xor(own, 1)

    def down(member, chunks):
        own = [c[0] for c in chunks]
        other = [c[1] for c in chunks]
        count = len(chunks)
        return pl.pallas_call(
            functools.partial(down_kernel, count),
            grid=(1,),
            out_shape=[
                shape((row_tokens, features), F32 if i == 0 else BF16) for i in range(row_count)
            ],
            in_specs=[SMEM]
            + [pl.BlockSpec((half, chunk), lambda i: (0, 0))] * (2 * count)
            + [pl.BlockSpec((1, ff_local, features), lambda i: (member, 0, 0))],
            out_specs=[pl.BlockSpec((row_tokens, features), lambda i: (0, 0))] * row_count,
            scratch_shapes=[pltpu.VMEM((tokens, features), F32)],
            compiler_params=params(32),
            cost_estimate=cost(
                2 * tokens * features * ff_local, 2 * ff_local * (features + tokens)
            ),
            name="down",
        )(quarter_offsets, *own, *other, w_down)

    vocab_start = (row_index * col_count + col_index) * vocab_local
    local_targets = (targets - vocab_start)[:, None]
    vocab_tile = 512 if vocab_local % 512 == 0 else vocab_local

    def head(member, chunks):
        partial_rows = down(member, chunks)
        partial_rows = [partial_rows[0]] + [
            row_xor(partial_rows[j], j) for j in range(1, row_count)
        ]
        output = stream_f + tree_sum([p.astype(F32) for p in partial_rows])
        squares = col_sum(jnp.sum(output * output, axis=1))
        scaled = (output * final_gain[None, :]).astype(BF16)
        squares = jnp.stack([squares] + [row_xor(squares, j) for j in range(1, row_count)])
        squares = jnp.take(squares, row_rel, axis=0).reshape(tokens)
        scale = lax.rsqrt(squares / D + EPSILON)[:, None]
        by_chip = jnp.stack([scaled] + [col_xor(scaled, 2 * j) for j in range(1, chips)])
        own = [by_chip] + [row_xor(by_chip, j) for j in range(1, row_count)]
        other = [col_xor(array, 1) for array in own]
        return pl.pallas_call(
            functools.partial(head_kernel, row_count),
            grid=(vocab_local // vocab_tile,),
            out_shape=shape((tokens, 128), F32),
            in_specs=[SMEM] * 2
            + [pl.BlockSpec((chips, row_tokens, features), lambda i: (0, 0, 0))] * (2 * row_count)
            + [pl.BlockSpec((tokens, 1), lambda i: (0, 0))] * 2
            + [pl.BlockSpec((D, vocab_tile), lambda i: (0, i))],
            out_specs=pl.BlockSpec((tokens, 128), lambda i: (0, 0)),
            scratch_shapes=[pltpu.VMEM((col_count, tokens, features), BF16)]
            + [pltpu.VMEM((tokens, 1), F32)] * 3,
            compiler_params=params(44),
            cost_estimate=cost(2 * tokens * D * vocab_local, 2 * D * vocab_local),
            name="head",
        )(col_rel, row_rel * row_tokens, *own, *other, scale, local_targets, w_head)[:, :3].T

    stats = []
    for member in range(2):
        chunks = [hidden_chunk(member, index) for index in range(chunk_count)]
        stats.append(head(member, chunks))
    stats = jnp.stack(stats, axis=1)

    def combine(parts):
        top = functools.reduce(jnp.maximum, [p[0] for p in parts])
        total = tree_sum([p[1] * jnp.exp(p[0] - top) for p in parts])
        picked = tree_sum([p[2] for p in parts])
        return jnp.stack([top, total, picked])

    stats = combine([stats] + [col_xor(stats, j) for j in range(1, col_count)])
    stats = combine([stats] + [row_xor(stats, j) for j in range(1, row_count)])
    logprob = stats[2] - (stats[0] + jnp.log(stats[1]))
    difference = logprob[0] - logprob[1]
    one_hot = (segment[:, None] == jnp.arange(SEQS, dtype=jnp.int32)[None, :]).astype(F32)
    seq_sums = jnp.dot(difference, one_hot, precision=lax.Precision.HIGHEST)
    return seq_sums / seq_lengths.astype(F32)


def solution(mesh):
    placed = (
        P("row", "col"),
        P("col"),
        P("col", "row"),
        P("col", "row"),
        P("col", "row"),
        P("row", "col"),
        P("col"),
        P(None, "col", "row"),
        P(None, "col", "row"),
        P(None, "row", "col"),
        P("col"),
        P(None, ("row", "col")),
        P(),
        P(),
    )
    return jax.shard_map(per_device, mesh=mesh, in_specs=placed, out_specs=P(), check_vma=False)
```

time: 644 us -> 377 us (0.59)
  waiting for transfers between devices: 350 us -> 152 us
  blocking collectives: 167 us -> 0 us
  starting transfers between devices: 0.56 us -> 137 us
  matrix products: 69.4 us -> 0.75 us
  Pallas kernels: 0 us -> 50.8 us
  between operations: 13.7 us -> 1.28 us
  other arithmetic: 18.4 us -> 9.97 us
    reduce_scatter x5 -> x0, waiting for transfers between devices: 204 us -> none  [the longest x2 141 us: feed_forward(): lax.psum_scatter(jnp.dot(row_block, gate_up, preferred_element_type=jnp.f...]
    ppermute x0 -> x138, waiting for transfers between devices: none -> 152 us  [the longest x30 38.6 us: row_xor(): return lax.ppermute(x, 'row', [(i, i ^ mask) for i in range(count)])]
    ppermute x0 -> x138, starting transfers between devices: none -> 137 us  [the longest x72 59.7 us: col_xor(): return lax.ppermute(x, 'col', [(i, i ^ mask) for i in range(count)])]
    psum x4 -> x0, blocking collectives: 89.7 us -> none  [the longest x1 39.1 us: per_device(): lax.psum((policy_total * jnp.exp(policy_top - top_policy), refer_total *...]
    all_gather x4 -> x0, waiting for transfers between devices: 88.4 us -> none  [the longest x2 46.3 us: feed_forward(): hidden_all = lax.all_gather(hidden, 'col', axis=0, tiled=True)]
    dot_general x9 -> x0, matrix products: 65 us -> none  [the longest x2 27.9 us: local_stats(): logits = jnp.dot(final_all, w_head, preferred_element_type=jnp.float32)]
    psum x1 -> x0, waiting for transfers between devices: 57.8 us -> none  [per_device(): joint_sums = lax.psum(joint_part, 'col')]
    pallas_call x0 -> x15, Pallas kernels: none -> 50.8 us  [the longest x2 28.8 us: head(): pl.pallas_call(functools.partial(head_kernel, row_count), grid=(vocab_loc...]
  transfers between devices with their start and end apart: 10 -> 138, of which waited for: 10 -> 54; matrix products, arithmetic and copies ran while one was open for 8% -> 3% of each run, Pallas kernels for 0% -> 7%
where the time goes in v1:
time: 377 us; the launch traced here: 376 us
  waiting for transfers between devices  152 us (40%)
  starting transfers between devices  137 us (36%)
  Pallas kernels  50.8 us (13%)
  local copies, waits for them, and re-layouts  23.2 us (6%)
  other arithmetic  9.97 us (3%)
    ppermute x72, starting transfers between devices, col_xor(): return lax.ppermute(x, 'col', [(i, i ^ mask) for i in range(count)])  59.7 us
    ppermute x30, waiting for transfers between devices, row_xor(): return lax.ppermute(x, 'row', [(i, i ^ mask) for i in range(count)])  38.6 us
    ppermute x6, waiting for transfers between devices, chain_reduce(): received = lax.ppermute(near, 'col', pairs_of(hop))  37 us
    ppermute x30, starting transfers between devices, row_xor(): return lax.ppermute(x, 'row', [(i, i ^ mask) for i in range(count)])  32.6 us
    ppermute x72, waiting for transfers between devices, col_xor(): return lax.ppermute(x, 'col', [(i, i ^ mask) for i in range(count)])  29.6 us
    pallas_call x2, Pallas kernels, head(): pl.pallas_call(functools.partial(head_kernel, row_count), grid=(vocab_loc...  28.8 us
    ppermute x12, waiting for transfers between devices, chain_reduce(): received = lax.ppermute(far, 'col', pairs_of(hop))  24.8 us
    ppermute x18, waiting for transfers between devices, hidden_chunk(): moving = lax.ppermute(moving, 'col', back_of(hop))  22.3 us
  transfers between devices with their start and end apart: 138, of which 54 were waited for; matrix products, arithmetic and copies ran while one was open for 3% of the time, Pallas kernels for 7%

profile of v1, /device:TPU:0, one launch (start us, length us, event | category | flops | bytes accessed | tf_op | source)
XLA Modules:
  0.0 375.7 jit_solution(13948147573624744971)
XLA Ops:
  19.0 3.6 collective-permute-start.12
  30.4 8.8 %collective-permute-done.5.refs_2_ = bf16[32,1792]{1,0:T(8,128)(2,1)S(1)} collective-permute-done((bf16[32,1792]{1,0:T(8,128)(2,1)S(1)}, bf16[32,1792]{1,0:T(8,128)(2,1)S(1)}, u32[]{:S(2)}, u32[]{:S(2)}) %collective-permute-start.5) | collective-permute-done | bytes 114720 | tf_op jit(solution)/shard_map/ppermute | solution.py:41
  45.4 7.2 %collective-permute-done.15.refs_2_ = bf16[32,1792]{1,0:T(8,128)(2,1)S(1)} collective-permute-done((bf16[32,1792]{1,0:T(8,128)(2,1)S(1)}, bf16[32,1792]{1,0:T(8,128)(2,1)S(1)}, u32[]{:S(2)}, u32[]{:S(2)}) %collective-permute-start.15) | collective-permute-done | bytes 114720 | tf_op jit(solution)/shard_map/ppermute | solution.py:41
  74.9 3.5 copy-done
  78.4 3.5 copy-done.1
  114.6 4.4 %collective-permute-start.49 = (bf16[2,64,1152]{2,1,0:T(8,128)(2,1)S(1)}, bf16[2,64,1152]{2,1,0:T(8,128)(2,1)S(1)}, u32[]{:S(2)}, u32[]{:S(2)}) collective-permute-start(bf16[2,64,1152]{2,1,0:T(8,128)(2,1)S(1)} %add_convert_fusion.14), channel_id=1, source_target_pairs={{0,2},{6,4},{1,3},{7,5},{8,10},{14,12},{9,11},{15,13},{16,18},{22,... | collective-permute-start | bytes 884744 | tf_op jit(solution)/shard_map/ppermute | solution.py:232
  121.6 5.6 %collective-permute-done.42 = bf16[2,64,1152]{2,1,0:T(8,128)(2,1)S(1)} collective-permute-done((bf16[2,64,1152]{2,1,0:T(8,128)(2,1)S(1)}, bf16[2,64,1152]{2,1,0:T(8,128)(2,1)S(1)}, u32[]{:S(2)}, u32[]{:S(2)}) %collective-permute-start.42) | collective-permute-done | bytes 294944 | tf_op jit(solution)/shard_map/ppermute | solution.py:232
  127.9 5.6 %collective-permute-done.82 = bf16[2,64,1152]{2,1,0:T(8,128)(2,1)S(1)} collective-permute-done((bf16[2,64,1152]{2,1,0:T(8,128)(2,1)S(1)}, bf16[2,64,1152]{2,1,0:T(8,128)(2,1)S(1)}, u32[]{:S(2)}, u32[]{:S(2)}) %collective-permute-start.82) | collective-permute-done | bytes 294944 | tf_op jit(solution)/shard_map/ppermute | solution.py:232
  134.3 5.6 %collective-permute-done.28 = bf16[2,64,1152]{2,1,0:T(8,128)(2,1)S(1)} collective-permute-done((bf16[2,64,1152]{2,1,0:T(8,128)(2,1)S(1)}, bf16[2,64,1152]{2,1,0:T(8,128)(2,1)S(1)}, u32[]{:S(2)}, u32[]{:S(2)}) %collective-permute-start.28) | collective-permute-done | bytes 294944 | tf_op jit(solution)/shard_map/ppermute | solution.py:232
  140.6 4.8 %collective-permute-done.49 = bf16[2,64,1152]{2,1,0:T(8,128)(2,1)S(1)} collective-permute-done((bf16[2,64,1152]{2,1,0:T(8,128)(2,1)S(1)}, bf16[2,64,1152]{2,1,0:T(8,128)(2,1)S(1)}, u32[]{:S(2)}, u32[]{:S(2)}) %collective-permute-start.49) | collective-permute-done | bytes 294944 | tf_op jit(solution)/shard_map/ppermute | solution.py:232
  154.1 9.0 %collective-permute-done.91 = bf16[2,64,1152]{2,1,0:T(8,128)(2,1)S(1)} collective-permute-done((bf16[2,64,1152]{2,1,0:T(8,128)(2,1)S(1)}, bf16[2,64,1152]{2,1,0:T(8,128)(2,1)S(1)}, u32[]{:S(2)}, u32[]{:S(2)}) %collective-permute-start.91) | collective-permute-done | bytes 294944 | tf_op jit(solution)/shard_map/ppermute | solution.py:234
  164.5 5.0 %collective-permute-done.98 = bf16[2,64,1152]{2,1,0:T(8,128)(2,1)S(1)} collective-permute-done((bf16[2,64,1152]{2,1,0:T(8,128)(2,1)S(1)}, bf16[2,64,1152]{2,1,0:T(8,128)(2,1)S(1)}, u32[]{:S(2)}, u32[]{:S(2)}) %collective-permute-start.98) | collective-permute-done | bytes 294944 | tf_op jit(solution)/shard_map/ppermute | solution.py:234
  169.5 6.2 %collective-permute-done.44 = bf16[2,64,1152]{2,1,0:T(8,128)(2,1)S(1)} collective-permute-done((bf16[2,64,1152]{2,1,0:T(8,128)(2,1)S(1)}, bf16[2,64,1152]{2,1,0:T(8,128)(2,1)S(1)}, u32[]{:S(2)}, u32[]{:S(2)}) %collective-permute-start.44) | collective-permute-done | bytes 294944 | tf_op jit(solution)/shard_map/ppermute | solution.py:234
  175.8 6.2 %collective-permute-done.84 = bf16[2,64,1152]{2,1,0:T(8,128)(2,1)S(1)} collective-permute-done((bf16[2,64,1152]{2,1,0:T(8,128)(2,1)S(1)}, bf16[2,64,1152]{2,1,0:T(8,128)(2,1)S(1)}, u32[]{:S(2)}, u32[]{:S(2)}) %collective-permute-start.84) | collective-permute-done | bytes 294944 | tf_op jit(solution)/shard_map/ppermute | solution.py:234
  182.2 6.2 %collective-permute-done.30 = bf16[2,64,1152]{2,1,0:T(8,128)(2,1)S(1)} collective-permute-done((bf16[2,64,1152]{2,1,0:T(8,128)(2,1)S(1)}, bf16[2,64,1152]{2,1,0:T(8,128)(2,1)S(1)}, u32[]{:S(2)}, u32[]{:S(2)}) %collective-permute-start.30) | collective-permute-done | bytes 294944 | tf_op jit(solution)/shard_map/ppermute | solution.py:234
  188.5 4.3 %collective-permute-done.51 = bf16[2,64,1152]{2,1,0:T(8,128)(2,1)S(1)} collective-permute-done((bf16[2,64,1152]{2,1,0:T(8,128)(2,1)S(1)}, bf16[2,64,1152]{2,1,0:T(8,128)(2,1)S(1)}, u32[]{:S(2)}, u32[]{:S(2)}) %collective-permute-start.51) | collective-permute-done | bytes 294944 | tf_op jit(solution)/shard_map/ppermute | solution.py:234
  220.4 8.5 %collective-permute-done.101 = bf16[64,1152]{1,0:T(8,128)(2,1)S(1)} collective-permute-done((bf16[64,1152]{1,0:T(8,128)(2,1)S(1)}, bf16[64,1152]{1,0:T(8,128)(2,1)S(1)}, u32[]{:S(2)}, u32[]{:S(2)}) %collective-permute-start.101) | collective-permute-done | bytes 147488 | tf_op jit(solution)/shard_map/ppermute | solution.py:445
  248.5 3.5 copy-done.3
  302.3 6.2 %collective-permute-done.64.refs_1_ = bf16[4,64,640]{2,1,0:T(8,128)(2,1)S(1)} collective-permute-done((bf16[4,64,640]{2,1,0:T(8,128)(2,1)S(1)}, bf16[4,64,640]{2,1,0:T(8,128)(2,1)S(1)}, u32[]{:S(2)}, u32[]{:S(2)}) %collective-permute-start.64) | collective-permute-done | bytes 327712 | tf_op jit(solution)/shard_map/ppermute | solution.py:36
  309.0 5.5 %collective-permute-done.65.refs_2_ = bf16[4,64,640]{2,1,0:T(8,128)(2,1)S(1)} collective-permute-done((bf16[4,64,640]{2,1,0:T(8,128)(2,1)S(1)}, bf16[4,64,640]{2,1,0:T(8,128)(2,1)S(1)}, u32[]{:S(2)}, u32[]{:S(2)}) %collective-permute-start.65) | collective-permute-done | bytes 327712 | tf_op jit(solution)/shard_map/ppermute | solution.py:36
  315.9 6.0 %collective-permute-done.111.refs_1_ = bf16[4,64,640]{2,1,0:T(8,128)(2,1)S(1)} collective-permute-done((bf16[4,64,640]{2,1,0:T(8,128)(2,1)S(1)}, bf16[4,64,640]{2,1,0:T(8,128)(2,1)S(1)}, u32[]{:S(2)}, u32[]{:S(2)}) %collective-permute-start.111) | collective-permute-done | bytes 327712 | tf_op jit(solution)/shard_map/ppermute | solution.py:36
  322.9 4.0 %collective-permute-done.112.refs_2_ = bf16[4,64,640]{2,1,0:T(8,128)(2,1)S(1)} collective-permute-done((bf16[4,64,640]{2,1,0:T(8,128)(2,1)S(1)}, bf16[4,64,640]{2,1,0:T(8,128)(2,1)S(1)}, u32[]{:S(2)}, u32[]{:S(2)}) %collective-permute-start.112) | collective-permute-done | bytes 327712 | tf_op jit(solution)/shard_map/ppermute | solution.py:36
  327.9 14.3 %head.2 = f32[256,128]{1,0:T(8,128)S(1)} custom-call(s32[8]{0:T(128)S(1)} %iota_xor_fusion.1.col_index, s32[4]{0:T(128)S(1)} %fusion.80.row_places, bf16[4,64,640]{2,1,0:T(8,128)(2,1)S(1)} %pad_maximum_fusion.refs_0_, bf16[4,64,640]{2,1,0:T(8,128)(2,1)S(1)} %collective-permute-done.64.refs_1_, bf16[4,64,640]{2,1,0:T(8,128)(2,1)S(1)} %collective-permute-done.65.refs_2_, ...), custom_call_target="tpu_custom_call" | custom-call | flops 6710886400 | bytes 26214400 | tf_op jit(solution)/shard_map/head/pallas_call | solution.py:493
  342.4 14.5 %head.3 = f32[256,128]{1,0:T(8,128)S(1)} custom-call(s32[8]{0:T(128)S(1)} %iota_xor_fusion.1.col_index, s32[4]{0:T(128)S(1)} %fusion.80.row_places, bf16[4,64,640]{2,1,0:T(8,128)(2,1)S(1)} %pad_maximum_fusion.1.refs_0_, bf16[4,64,640]{2,1,0:T(8,128)(2,1)S(1)} %collective-permute-done.111.refs_1_, bf16[4,64,640]{2,1,0:T(8,128)(2,1)S(1)} %collective-permute-done.112.refs_2_, ...), custom_call_target="tpu_custom_call" | custom-call | flops 6710886400 | bytes 26214400 | tf_op jit(solution)/shard_map/head/pallas_call | solution.py:493
  (398 shorter events, 222.4 us)
Async XLA Ops:
  88.4 16.2 %collective-permute-start.88 = (bf16[2,128,1152]{2,1,0:T(8,128)(2,1)S(1)}, bf16[2,128,1152]{2,1,0:T(8,128)(2,1)S(1)}, u32[]{:S(2)}, u32[]{:S(2)}) collective-permute-start(bf16[2,128,1152]{2,1,0:T(8,128)(2,1)S(1)} %get-tuple-element.59), channel_id=1, source_target_pairs={{0,1},{1,0},{2,3},{3,2},{4,5},{5,4},{6,7},{7,6},{8,9},{9,8},{10,11... | collective-permute-start | bytes 1769480 | tf_op jit(solution)/shard_map/ppermute | solution.py:41
  108.7 18.5 %collective-permute-start.42 = (bf16[2,64,1152]{2,1,0:T(8,128)(2,1)S(1)}, bf16[2,64,1152]{2,1,0:T(8,128)(2,1)S(1)}, u32[]{:S(2)}, u32[]{:S(2)}) collective-permute-start(bf16[2,64,1152]{2,1,0:T(8,128)(2,1)S(1)} %add_convert_fusion.18), channel_id=1, source_target_pairs={{0,2},{6,4},{1,3},{7,5},{8,10},{14,12},{9,11},{15,13},{16,18},{22,... | collective-permute-start | bytes 884744 | tf_op jit(solution)/shard_map/ppermute | solution.py:232
  110.1 23.4 %collective-permute-start.82 = (bf16[2,64,1152]{2,1,0:T(8,128)(2,1)S(1)}, bf16[2,64,1152]{2,1,0:T(8,128)(2,1)S(1)}, u32[]{:S(2)}, u32[]{:S(2)}) collective-permute-start(bf16[2,64,1152]{2,1,0:T(8,128)(2,1)S(1)} %add_convert_fusion.10), channel_id=1, source_target_pairs={{0,2},{6,4},{1,3},{7,5},{8,10},{14,12},{9,11},{15,13},{16,18},{22,... | collective-permute-start | bytes 884744 | tf_op jit(solution)/shard_map/ppermute | solution.py:232
  111.5 28.3 %collective-permute-start.28 = (bf16[2,64,1152]{2,1,0:T(8,128)(2,1)S(1)}, bf16[2,64,1152]{2,1,0:T(8,128)(2,1)S(1)}, u32[]{:S(2)}, u32[]{:S(2)}) collective-permute-start(bf16[2,64,1152]{2,1,0:T(8,128)(2,1)S(1)} %add_convert_fusion.22), channel_id=1, source_target_pairs={{0,2},{6,4},{1,3},{7,5},{8,10},{14,12},{9,11},{15,13},{16,18},{22,... | collective-permute-start | bytes 884744 | tf_op jit(solution)/shard_map/ppermute | solution.py:232
  114.6 30.8 %collective-permute-start.49 = (bf16[2,64,1152]{2,1,0:T(8,128)(2,1)S(1)}, bf16[2,64,1152]{2,1,0:T(8,128)(2,1)S(1)}, u32[]{:S(2)}, u32[]{:S(2)}) collective-permute-start(bf16[2,64,1152]{2,1,0:T(8,128)(2,1)S(1)} %add_convert_fusion.14), channel_id=1, source_target_pairs={{0,2},{6,4},{1,3},{7,5},{8,10},{14,12},{9,11},{15,13},{16,18},{22,... | collective-permute-start | bytes 884744 | tf_op jit(solution)/shard_map/ppermute | solution.py:232
  120.9 25.3 %collective-permute-start.90 = (bf16[2,64,1152]{2,1,0:T(8,128)(2,1)S(1)}, bf16[2,64,1152]{2,1,0:T(8,128)(2,1)S(1)}, u32[]{:S(2)}, u32[]{:S(2)}) collective-permute-start(bf16[2,64,1152]{2,1,0:T(8,128)(2,1)S(1)} %add_convert_fusion.5), channel_id=1, source_target_pairs={{2,4},{4,2},{3,5},{5,3},{10,12},{12,10},{11,13},{13,11},{18,20},{2... | collective-permute-start | bytes 884744 | tf_op jit(solution)/shard_map/ppermute | solution.py:232
  127.2 19.8 %collective-permute-start.97 = (bf16[2,64,1152]{2,1,0:T(8,128)(2,1)S(1)}, bf16[2,64,1152]{2,1,0:T(8,128)(2,1)S(1)}, u32[]{:S(2)}, u32[]{:S(2)}) collective-permute-start(bf16[2,64,1152]{2,1,0:T(8,128)(2,1)S(1)} %add_convert_fusion.1), channel_id=1, source_target_pairs={{2,4},{4,2},{3,5},{5,3},{10,12},{12,10},{11,13},{13,11},{18,20},{2... | collective-permute-start | bytes 884744 | tf_op jit(solution)/shard_map/ppermute | solution.py:232
  147.0 16.2 %collective-permute-start.91 = (bf16[2,64,1152]{2,1,0:T(8,128)(2,1)S(1)}, bf16[2,64,1152]{2,1,0:T(8,128)(2,1)S(1)}, u32[]{:S(2)}, u32[]{:S(2)}) collective-permute-start(bf16[2,64,1152]{2,1,0:T(8,128)(2,1)S(1)} %add_convert_fusion.4), channel_id=1, source_target_pairs={{4,6},{2,0},{5,7},{3,1},{12,14},{10,8},{13,15},{11,9},{20,22},{18,... | collective-permute-start | bytes 884744 | tf_op jit(solution)/shard_map/ppermute | solution.py:234
  148.4 21.0 %collective-permute-start.98 = (bf16[2,64,1152]{2,1,0:T(8,128)(2,1)S(1)}, bf16[2,64,1152]{2,1,0:T(8,128)(2,1)S(1)}, u32[]{:S(2)}, u32[]{:S(2)}) collective-permute-start(bf16[2,64,1152]{2,1,0:T(8,128)(2,1)S(1)} %add_convert_fusion), channel_id=1, source_target_pairs={{4,6},{2,0},{5,7},{3,1},{12,14},{10,8},{13,15},{11,9},{20,22},{18,... | collective-permute-start | bytes 884744 | tf_op jit(solution)/shard_map/ppermute | solution.py:234
  149.8 25.9 %collective-permute-start.44 = (bf16[2,64,1152]{2,1,0:T(8,128)(2,1)S(1)}, bf16[2,64,1152]{2,1,0:T(8,128)(2,1)S(1)}, u32[]{:S(2)}, u32[]{:S(2)}) collective-permute-start(bf16[2,64,1152]{2,1,0:T(8,128)(2,1)S(1)} %add_convert_fusion.16), channel_id=1, source_target_pairs={{4,6},{2,0},{5,7},{3,1},{12,14},{10,8},{13,15},{11,9},{20,22},{18,... | collective-permute-start | bytes 884744 | tf_op jit(solution)/shard_map/ppermute | solution.py:234
  151.3 30.8 %collective-permute-start.84 = (bf16[2,64,1152]{2,1,0:T(8,128)(2,1)S(1)}, bf16[2,64,1152]{2,1,0:T(8,128)(2,1)S(1)}, u32[]{:S(2)}, u32[]{:S(2)}) collective-permute-start(bf16[2,64,1152]{2,1,0:T(8,128)(2,1)S(1)} %add_convert_fusion.8), channel_id=1, source_target_pairs={{4,6},{2,0},{5,7},{3,1},{12,14},{10,8},{13,15},{11,9},{20,22},{18,... | collective-permute-start | bytes 884744 | tf_op jit(solution)/shard_map/ppermute | solution.py:234
  152.7 35.7 %collective-permute-start.30 = (bf16[2,64,1152]{2,1,0:T(8,128)(2,1)S(1)}, bf16[2,64,1152]{2,1,0:T(8,128)(2,1)S(1)}, u32[]{:S(2)}, u32[]{:S(2)}) collective-permute-start(bf16[2,64,1152]{2,1,0:T(8,128)(2,1)S(1)} %add_convert_fusion.20), channel_id=1, source_target_pairs={{4,6},{2,0},{5,7},{3,1},{12,14},{10,8},{13,15},{11,9},{20,22},{18,... | collective-permute-start | bytes 884744 | tf_op jit(solution)/shard_map/ppermute | solution.py:234
  163.1 29.6 %collective-permute-start.51 = (bf16[2,64,1152]{2,1,0:T(8,128)(2,1)S(1)}, bf16[2,64,1152]{2,1,0:T(8,128)(2,1)S(1)}, u32[]{:S(2)}, u32[]{:S(2)}) collective-permute-start(bf16[2,64,1152]{2,1,0:T(8,128)(2,1)S(1)} %add_convert_fusion.12), channel_id=1, source_target_pairs={{4,6},{2,0},{5,7},{3,1},{12,14},{10,8},{13,15},{11,9},{20,22},{18,... | collective-permute-start | bytes 884744 | tf_op jit(solution)/shard_map/ppermute | solution.py:234
  213.6 15.4 %collective-permute-start.101 = (bf16[64,1152]{1,0:T(8,128)(2,1)S(1)}, bf16[64,1152]{1,0:T(8,128)(2,1)S(1)}, u32[]{:S(2)}, u32[]{:S(2)}) collective-permute-start(bf16[64,1152]{1,0:T(8,128)(2,1)S(1)} %collective-permute-done.100), channel_id=1, source_target_pairs={{2,0},{4,6},{3,1},{5,7},{10,8},{12,14},{11,9},{13,15},{18,16},{20,... | collective-permute-start | bytes 442376 | tf_op jit(solution)/shard_map/ppermute | solution.py:445
  215.2 16.9 %collective-permute-start.94 = (bf16[64,1152]{1,0:T(8,128)(2,1)S(1)}, bf16[64,1152]{1,0:T(8,128)(2,1)S(1)}, u32[]{:S(2)}, u32[]{:S(2)}) collective-permute-start(bf16[64,1152]{1,0:T(8,128)(2,1)S(1)} %collective-permute-done.93), channel_id=1, source_target_pairs={{2,0},{4,6},{3,1},{5,7},{10,8},{12,14},{11,9},{13,15},{18,16},{20,... | collective-permute-start | bytes 442376 | tf_op jit(solution)/shard_map/ppermute | solution.py:445
  216.5 17.2 %collective-permute-start.87 = (bf16[64,1152]{1,0:T(8,128)(2,1)S(1)}, bf16[64,1152]{1,0:T(8,128)(2,1)S(1)}, u32[]{:S(2)}, u32[]{:S(2)}) collective-permute-start(bf16[64,1152]{1,0:T(8,128)(2,1)S(1)} %collective-permute-done.86), channel_id=1, source_target_pairs={{2,0},{4,6},{3,1},{5,7},{10,8},{12,14},{11,9},{13,15},{18,16},{20,... | collective-permute-start | bytes 442376 | tf_op jit(solution)/shard_map/ppermute | solution.py:445
  217.8 17.5 %collective-permute-start.54 = (bf16[64,1152]{1,0:T(8,128)(2,1)S(1)}, bf16[64,1152]{1,0:T(8,128)(2,1)S(1)}, u32[]{:S(2)}, u32[]{:S(2)}) collective-permute-start(bf16[64,1152]{1,0:T(8,128)(2,1)S(1)} %collective-permute-done.53), channel_id=1, source_target_pairs={{2,0},{4,6},{3,1},{5,7},{10,8},{12,14},{11,9},{13,15},{18,16},{20,... | collective-permute-start | bytes 442376 | tf_op jit(solution)/shard_map/ppermute | solution.py:445
  219.1 17.8 %collective-permute-start.47 = (bf16[64,1152]{1,0:T(8,128)(2,1)S(1)}, bf16[64,1152]{1,0:T(8,128)(2,1)S(1)}, u32[]{:S(2)}, u32[]{:S(2)}) collective-permute-start(bf16[64,1152]{1,0:T(8,128)(2,1)S(1)} %collective-permute-done.46), channel_id=1, source_target_pairs={{2,0},{4,6},{3,1},{5,7},{10,8},{12,14},{11,9},{13,15},{18,16},{20,... | collective-permute-start | bytes 442376 | tf_op jit(solution)/shard_map/ppermute | solution.py:445
  298.1 16.4 %collective-permute-start.65 = (bf16[4,64,640]{2,1,0:T(8,128)(2,1)S(1)}, bf16[4,64,640]{2,1,0:T(8,128)(2,1)S(1)}, u32[]{:S(2)}, u32[]{:S(2)}) collective-permute-start(bf16[4,64,640]{2,1,0:T(8,128)(2,1)S(1)} %pad_maximum_fusion.refs_0_), channel_id=1, source_target_pairs={{0,16},{8,24},{16,0},{24,8},{1,17},{9,25},{17,1},{25,9},{2,18},{10... | collective-permute-start | bytes 983048 | tf_op jit(solution)/shard_map/ppermute | solution.py:36
  299.6 15.8 %collective-permute-start.66 = (bf16[4,64,640]{2,1,0:T(8,128)(2,1)S(1)}, bf16[4,64,640]{2,1,0:T(8,128)(2,1)S(1)}, u32[]{:S(2)}, u32[]{:S(2)}) collective-permute-start(bf16[4,64,640]{2,1,0:T(8,128)(2,1)S(1)} %pad_maximum_fusion.refs_0_), channel_id=1, source_target_pairs={{0,24},{8,16},{16,8},{24,0},{1,25},{9,17},{17,9},{25,1},{2,26},{10... | collective-permute-start | bytes 983048 | tf_op jit(solution)/shard_map/ppermute | solution.py:36
  301.4 20.6 %collective-permute-start.111 = (bf16[4,64,640]{2,1,0:T(8,128)(2,1)S(1)}, bf16[4,64,640]{2,1,0:T(8,128)(2,1)S(1)}, u32[]{:S(2)}, u32[]{:S(2)}) collective-permute-start(bf16[4,64,640]{2,1,0:T(8,128)(2,1)S(1)} %pad_maximum_fusion.1.refs_0_), channel_id=1, source_target_pairs={{0,8},{8,0},{16,24},{24,16},{1,9},{9,1},{17,25},{25,17},{2,10},{10... | collective-permute-start | bytes 983048 | tf_op jit(solution)/shard_map/ppermute | solution.py:36
  308.5 18.4 %collective-permute-start.112 = (bf16[4,64,640]{2,1,0:T(8,128)(2,1)S(1)}, bf16[4,64,640]{2,1,0:T(8,128)(2,1)S(1)}, u32[]{:S(2)}, u32[]{:S(2)}) collective-permute-start(bf16[4,64,640]{2,1,0:T(8,128)(2,1)S(1)} %pad_maximum_fusion.1.refs_0_), channel_id=1, source_target_pairs={{0,16},{8,24},{16,0},{24,8},{1,17},{9,25},{17,1},{25,9},{2,18},{10... | collective-permute-start | bytes 983048 | tf_op jit(solution)/shard_map/ppermute | solution.py:36
  326.9 15.5 %collective-permute-start.114 = (bf16[4,64,640]{2,1,0:T(8,128)(2,1)S(1)}, bf16[4,64,640]{2,1,0:T(8,128)(2,1)}, u32[]{:S(2)}, u32[]{:S(2)}) collective-permute-start(bf16[4,64,640]{2,1,0:T(8,128)(2,1)S(1)} %pad_maximum_fusion.1.refs_0_), channel_id=1, source_target_pairs={{0,1},{1,0},{2,3},{3,2},{4,5},{5,4},{6,7},{7,6},{8,9},{9,8},{10,11... | collective-permute-start | bytes 983048 | tf_op jit(solution)/shard_map/ppermute | solution.py:41
  326.9 15.5 %collective-permute-start.115 = (bf16[4,64,640]{2,1,0:T(8,128)(2,1)S(1)}, bf16[4,64,640]{2,1,0:T(8,128)(2,1)}, u32[]{:S(2)}, u32[]{:S(2)}) collective-permute-start(bf16[4,64,640]{2,1,0:T(8,128)(2,1)S(1)} %collective-permute-done.111.refs_1_), channel_id=1, source_target_pairs={{0,1},{1,0},{2,3},{3,2},{4,5},{5,4},{6,7},{7,6},{8,9},{9,8},{10,11... | collective-permute-start | bytes 983048 | tf_op jit(solution)/shard_map/ppermute | solution.py:41
  (126 other events, 993.0 us)

commit v2 on v1

v2 whole, which is shorter than its diff:
```python
import functools

import jax
import jax.numpy as jnp
from jax import lax
from jax.experimental import pallas as pl
from jax.experimental.pallas import tpu as pltpu
from jax.sharding import PartitionSpec as P

D = 5120
HEAD_DIM = 128
SEQS = 8
LONGEST = 64

EPSILON = 1e-06
ROPE_BASE = 1000000.0
MASKED = -1e30
LANES = 128
BF16 = jnp.bfloat16
F32 = jnp.float32
MIB = 1 << 20

VMEM = pl.BlockSpec(memory_space=pltpu.VMEM)
ANY = pl.BlockSpec(memory_space=pl.ANY)
SMEM = pl.BlockSpec(memory_space=pltpu.SMEM)


def params(mib):
    return pltpu.CompilerParams(vmem_limit_bytes=mib * MIB)


def cost(flops, byte_count):
    return pl.CostEstimate(flops=flops, bytes_accessed=byte_count, transcendentals=0)


def row_xor(x, mask):
    count = lax.axis_size("row")
    return lax.ppermute(x, "row", [(i, i ^ mask) for i in range(count)])


def col_xor(x, mask):
    count = lax.axis_size("col")
    return lax.ppermute(x, "col", [(i, i ^ mask) for i in range(count)])


def tree_sum(values):
    values = list(values)
    while len(values) > 1:
        values = [values[i] + values[i + 1] for i in range(0, len(values), 2)]
    return values[0]


def sequence_layout(seq_lengths, token_index):
    ends_at = jnp.cumsum(seq_lengths)
    before = ends_at[None, :] <= token_index[:, None]
    segment = jnp.sum(before.astype(jnp.int32), axis=1)
    starts_at = jnp.sum(jnp.where(before, seq_lengths[None, :], 0), axis=1)
    return (segment, (token_index - starts_at).astype(F32))


def split_square(total):
    high = total.astype(BF16)
    low = (total - high.astype(F32)).astype(BF16)
    lane = lax.broadcasted_iota(jnp.int32, total.shape, 1)
    return jnp.where(lane < LANES // 2, high.astype(F32), low.astype(F32)).astype(BF16)


def join_square(tile):
    return tile + pltpu.roll(tile, LANES // 2, 1)


def assemble(offsets, blocks, gain, x_ref, square_ref, unit):
    step = 0
    for block in blocks:
        for first in range(0, block.shape[0], unit):
            rows = block[first : first + unit, :].astype(F32)
            place = pl.multiple_of(offsets[step], unit)
            x_ref[pl.ds(place, unit), :] = (rows * gain[...]).astype(BF16)
            square = jnp.sum(rows * rows, axis=1, keepdims=True)
            square_ref[pl.ds(place, unit), :] = jnp.broadcast_to(square, (unit, LANES))
            step += 1


def put_squares(square_ref, keep, send, at):
    half = keep.shape[0]
    total = square_ref[...]
    lane = lax.broadcasted_iota(jnp.int32, (half, LANES), 1)
    keep[:, at : at + LANES] = jnp.where(lane < LANES // 2, total[:half], 0.0)
    send[:, at : at + LANES] = split_square(total[half:])


def qkv_kernel(unit, count, offsets, *refs):
    blocks, (gain, wq, wk, wv, keep, send, x_ref, square_ref) = refs[:count], refs[count:]
    assemble(offsets, blocks, gain, x_ref, square_ref, unit)
    half = keep.shape[0]
    x = x_ref[...]
    at = 0
    for w in (wq, wk, wv):
        width = w.shape[1]
        part = jnp.dot(x, w[...], preferred_element_type=F32)
        keep[:, at : at + width] = part[:half]
        send[:, at : at + width] = part[half:].astype(BF16)
        at += width
    put_squares(square_ref, keep, send, at)


def core_add_kernel(keep, recv, *outs):
    rows, width = outs[0].shape
    for i, out in enumerate(outs):
        total = keep[i * rows : (i + 1) * rows, :] + recv[
            i * rows : (i + 1) * rows, :
        ].astype(F32)
        if i == 0:
            out[...] = total
        else:
            out[:, : width - LANES] = total[:, : width - LANES].astype(BF16)
            out[:, width - LANES :] = split_square(join_square(total[:, width - LANES :]))


def rope_kernel(rotated, count, *refs):
    parts, (cosine, sine, out) = refs[:count], refs[count:]
    width = out.shape[1]

    def summed(at):
        total = parts[0][:, at : at + LANES].astype(F32)
        for part in parts[1:]:
            total = total + part[:, at : at + LANES].astype(F32)
        return total

    scale = lax.rsqrt(join_square(summed(width)) / D + EPSILON)
    for at in range(0, width, HEAD_DIM):
        total = summed(at) * scale
        if at < rotated:
            total = total * cosine[...] + pltpu.roll(total, HEAD_DIM // 2, 1) * sine[...]
        out[:, at : at + HEAD_DIM] = total.astype(BF16)


def attention_kernel(heads, kv_heads, count, block, places, *refs):
    pieces, (bias, w_out, out, qkv, attended) = refs[:count], refs[count:]
    unit = pieces[0].shape[0]
    for i, piece in enumerate(pieces):
        qkv[pl.ds(pl.multiple_of(places[i], unit), unit), :] = piece[...]
    tokens = qkv.shape[0]
    group = heads // kv_heads
    window = min(tokens, block + LONGEST)
    for start in range(0, tokens, block):
        first = max(0, start + block - window)
        mask = bias[start : start + block, :]
        mask = jnp.concatenate([mask] * group, axis=0)
        for g in range(kv_heads):
            q = jnp.concatenate(
                [
                    qkv[start : start + block, h * HEAD_DIM : (h + 1) * HEAD_DIM]
                    for h in range(g * group, (g + 1) * group)
                ],
                axis=0,
            )
            k_at = (heads + g) * HEAD_DIM
            v_at = (heads + kv_heads + g) * HEAD_DIM
            k = qkv[first : first + window, k_at : k_at + HEAD_DIM]
            v = qkv[first : first + window, v_at : v_at + HEAD_DIM]
            scores = lax.dot_general(
                q, k, (((1,), (1,)), ((), ())), preferred_element_type=F32
            ) * HEAD_DIM ** (-0.5)
            scores = scores + mask
            weights = jnp.exp(scores - jnp.max(scores, axis=1, keepdims=True))
            total = jnp.sum(weights, axis=1, keepdims=True)
            weights = (weights / total).astype(BF16)
            result = jnp.dot(weights, v, preferred_element_type=F32).astype(BF16)
            for h in range(group):
                at = (g * group + h) * HEAD_DIM
                attended[start : start + block, at : at + HEAD_DIM] = result[
                    h * block : (h + 1) * block
                ]
    product = jnp.dot(attended[...], w_out[...], preferred_element_type=F32)
    rows = out.shape[1]
    for i in range(out.shape[0]):
        out[i] = product[i * rows : (i + 1) * rows].astype(out.dtype)


def arrange_kernel(unit, offsets, *refs):
    blocks, (gain, out, square) = refs[:-3], refs[-3:]
    assemble(offsets, blocks, gain, out, square, unit)


def gate_up_kernel(tile, squares, x, w_gate, w_up, *refs):
    keep, send = refs[-2:]
    half = keep.shape[0]
    tiles = keep.shape[1] // (2 * tile)
    for i, w in enumerate((w_gate, w_up)):
        part = jnp.dot(x[...], w[0], preferred_element_type=F32)
        for step in range(tiles):

            @pl.when(pl.program_id(0) == step)
            def _(at=(2 * step + i) * tile, part=part):
                keep[:, at : at + tile] = part[:half]
                send[:, at : at + tile] = part[half:].astype(BF16)

    if squares:

        @pl.when(pl.program_id(0) == 0)
        def _():
            put_squares(refs[0], keep, send, 2 * tiles * tile)


def halve_kernel(squares, keep, recv, *refs):
    kept, send = refs[-2:]
    half, width = kept.shape
    kept[...] = keep[:half, :] + recv[:half, :].astype(F32)
    total = keep[half:, :] + recv[half:, :].astype(F32)
    if squares:
        body = width - LANES
        send[:, :body] = total[:, :body].astype(BF16)
        send[:, body:] = split_square(join_square(total[:, body:]))
    else:
        send[...] = total.astype(BF16)


def hidden_kernel(tile, squares, keep, recv, *refs):
    if squares:
        hidden, scale_ref = refs
        at = keep.shape[1] - LANES
        total = keep[:, at:] + recv[:, at:].astype(F32)
        scale_ref[...] = lax.rsqrt(join_square(total) / D + EPSILON)
    else:
        scale_ref, hidden = refs
    scale = scale_ref[:, :1]
    for i in range(hidden.shape[1] // tile):
        at = 2 * i * tile
        gate = (keep[:, at : at + tile] + recv[:, at : at + tile].astype(F32)) * scale
        at += tile
        up = (keep[:, at : at + tile] + recv[:, at : at + tile].astype(F32)) * scale
        hidden[:, i * tile : (i + 1) * tile] = (gate / (1.0 + jnp.exp(-gate)) * up).astype(BF16)


def down_kernel(sources, count, unit, offsets, *refs):
    own, other, w_down = refs[:count], refs[count : 2 * count], refs[2 * count]
    outs, total = refs[2 * count + 1 : -1], refs[-1]
    tile = w_down.shape[1]
    for i, (which, at) in enumerate(sources):

        @pl.when(pl.program_id(0) == i)
        def _():
            hidden = jnp.concatenate(
                [own[which][:, at : at + tile], other[which][:, at : at + tile]], axis=0
            )
            part = jnp.dot(hidden, w_down[0], preferred_element_type=F32)
            total[...] = part if i == 0 else total[...] + part

    @pl.when(pl.program_id(0) == len(sources) - 1)
    def _():
        step = 0
        for out in outs:
            for first in range(0, out.shape[0], unit):
                place = pl.multiple_of(offsets[step], unit)
                out[first : first + unit, :] = total[pl.ds(place, unit), :].astype(out.dtype)
                step += 1


def head_kernel(col_index, row_places, own, other, gains, target, w, *refs):
    out, lhs, square, top, total, picked = refs[-6:]
    step = pl.program_id(0)
    rows, chips, unit, width = own.shape

    @pl.when(step == 0)
    def _():
        inverse = 1.0 / gains[...]
        for i in range(rows):
            place = pl.multiple_of(row_places[i], unit)
            sums = jnp.zeros((unit, 1), F32)
            for core, array in enumerate((own, other)):
                for j in range(chips):
                    feature = pl.multiple_of(col_index[2 * j + core] * width, LANES)
                    values = array[i, j]
                    lhs[pl.ds(place, unit), pl.ds(feature, width)] = values
                    plain = values.astype(F32) * inverse[2 * j + core : 2 * j + core + 1, :]
                    sums += jnp.sum(plain * plain, axis=1, keepdims=True)
            square[pl.ds(place, unit), :] = sums
        top[...] = jnp.full_like(top, MASKED)
        total[...] = jnp.zeros_like(total)
        picked[...] = jnp.zeros_like(picked)

    logits = jnp.dot(lhs[...], w[...], preferred_element_type=F32)
    logits = logits * lax.rsqrt(square[...] / D + EPSILON)
    lane = lax.broadcasted_iota(jnp.int32, logits.shape, 1) + step * logits.shape[1]
    hit = jnp.where(lane == target[...], logits, 0.0)
    picked[...] += jnp.sum(hit, axis=1, keepdims=True)
    new_top = jnp.maximum(top[...], jnp.max(logits, axis=1, keepdims=True))
    total[...] = total[...] * jnp.exp(top[...] - new_top) + jnp.sum(
        jnp.exp(logits - new_top), axis=1, keepdims=True
    )
    top[...] = new_top

    @pl.when(step == pl.num_programs(0) - 1)
    def _():
        place = lax.broadcasted_iota(jnp.int32, out.shape, 1)
        out[...] = jnp.where(
            place == 0, top[...], jnp.where(place == 1, total[...], picked[...])
        )


def per_device(
    residual,
    attn_gain,
    w_query,
    w_key,
    w_value,
    w_out,
    mlp_gain,
    w_gate,
    w_up,
    w_down,
    final_gain,
    w_head,
    seq_lengths,
    targets,
):
    row_count = lax.axis_size("row")
    col_count = lax.axis_size("col")
    chips = col_count // 2
    row_index = lax.axis_index("row")
    col_index = lax.axis_index("col")
    core = col_index % 2
    chip = col_index // 2
    row_tokens, features = residual.shape
    tokens = row_tokens * row_count
    col_tokens = tokens // col_count
    quarter = tokens // 4
    heads = w_query.shape[1] // HEAD_DIM
    kv_heads = w_key.shape[1] // HEAD_DIM
    qkv_width = w_query.shape[1] + 2 * w_key.shape[1]
    rotated = w_query.shape[1] + w_key.shape[1]
    ff_local = w_gate.shape[2]
    vocab_local = w_head.shape[1]

    row_range = jnp.arange(row_count, dtype=jnp.int32)
    col_range = jnp.arange(col_count, dtype=jnp.int32)
    row_rel = row_range ^ row_index
    col_rel = col_range ^ col_index

    token_index = jnp.arange(tokens, dtype=jnp.int32)
    segment, positions = sequence_layout(seq_lengths, token_index)
    block = min(64, tokens)
    window = min(tokens, block + LONGEST)
    first_key = jnp.maximum(0, (token_index // block + 1) * block - window)
    key_index = first_key[:, None] + jnp.arange(window, dtype=jnp.int32)[None, :]
    key_segment, _ = sequence_layout(seq_lengths, key_index.reshape(-1))
    allowed = (key_segment.reshape(tokens, window) == segment[:, None]) & (
        key_index <= token_index[:, None]
    )
    bias = jnp.where(allowed, 0.0, MASKED).astype(F32)
    own_positions = lax.dynamic_slice_in_dim(positions, col_index * col_tokens, col_tokens)
    exponent = jnp.arange(HEAD_DIM // 2, dtype=F32) * 2.0 / HEAD_DIM
    angles = own_positions[:, None] * (ROPE_BASE ** (-exponent))[None, :]
    cosine, sine = jnp.cos(angles), jnp.sin(angles)
    cosine = jnp.concatenate([cosine, cosine], axis=1)
    sine = jnp.concatenate([-sine, sine], axis=1)

    blocks = [residual] + [row_xor(residual, j) for j in range(1, row_count)]
    shape = jax.ShapeDtypeStruct

    per_row = row_tokens // col_tokens
    col_block = (row_rel[:, None] * per_row + jnp.arange(per_row, dtype=jnp.int32)).reshape(-1)
    relative = col_block ^ col_index
    offsets = ((relative & 1) * chips + (relative >> 1)) * col_tokens
    half = tokens // 2
    wide = qkv_width + LANES
    keep, send = pl.pallas_call(
        functools.partial(qkv_kernel, col_tokens, row_count),
        out_shape=[shape((half, wide), F32), shape((half, wide), BF16)],
        in_specs=[SMEM] + [VMEM] * (row_count + 4),
        out_specs=[VMEM] * 2,
        scratch_shapes=[pltpu.VMEM((tokens, features), BF16), pltpu.VMEM((tokens, LANES), F32)],
        compiler_params=params(24),
        cost_estimate=cost(
            2 * tokens * features * qkv_width, 2 * qkv_width * (features + tokens)
        ),
        name="qkv_partial",
    )(offsets, *blocks, attn_gain[None, :], w_query, w_key, w_value)
    received = col_xor(send, 1)
    parts = pl.pallas_call(
        core_add_kernel,
        out_shape=[shape((col_tokens, wide), F32 if i == 0 else BF16) for i in range(chips)],
        in_specs=[VMEM] * 2,
        out_specs=[VMEM] * chips,
        compiler_params=params(16),
        cost_estimate=cost(half * qkv_width, 6 * half * qkv_width),
        name="qkv_core_add",
    )(keep, received)
    parts = [parts[0]] + [col_xor(parts[j], 2 * j) for j in range(1, chips)]
    mine = pl.pallas_call(
        functools.partial(rope_kernel, rotated, chips),
        out_shape=shape((col_tokens, qkv_width), BF16),
        in_specs=[VMEM] * (chips + 2),
        out_specs=VMEM,
        compiler_params=params(16),
        cost_estimate=cost(8 * col_tokens * qkv_width, 2 * tokens * qkv_width),
        name="qkv_rope",
    )(*parts, cosine, sine)
    pieces = [mine] + [col_xor(mine, 2 * j) for j in range(1, chips)]
    pieces = pieces + [col_xor(piece, 1) for piece in pieces]
    piece_index = [2 * j for j in range(chips)] + [2 * j + 1 for j in range(chips)]
    places = (jnp.array(piece_index, jnp.int32) ^ col_index) * col_tokens

    projected = pl.pallas_call(
        functools.partial(attention_kernel, heads, kv_heads, col_count, block),
        out_shape=shape((row_count, row_tokens, features), BF16),
        in_specs=[SMEM] + [VMEM] * (col_count + 2),
        out_specs=VMEM,
        scratch_shapes=[
            pltpu.VMEM((tokens, qkv_width), BF16),
            pltpu.VMEM((tokens, heads * HEAD_DIM), BF16),
        ],
        compiler_params=params(32),
        cost_estimate=cost(
            2 * tokens * heads * HEAD_DIM * features * 2, 2 * heads * HEAD_DIM * features * 2
        ),
        name="attention_out",
    )(places, *pieces, bias, w_out)
    projected = lax.all_to_all(projected, "row", 0, 0)
    stream = residual.astype(F32) + jnp.sum(projected.astype(F32), axis=0)
    stream = lax.optimization_barrier(stream.astype(BF16))
    stream_f = stream.astype(F32)

    levels = (col_count - 1).bit_length()
    blocks = [stream] + [row_xor(stream, j) for j in range(1, row_count)]
    position = sum(((relative >> level) & 1) << (levels - 1 - level) for level in range(levels))
    half_offsets = position * col_tokens
    mlp_in, squares = pl.pallas_call(
        functools.partial(arrange_kernel, col_tokens),
        out_shape=[shape((tokens, features), BF16), shape((tokens, LANES), F32)],
        in_specs=[SMEM] + [VMEM] * (row_count + 1),
        out_specs=[VMEM] * 2,
        compiler_params=params(16),
        cost_estimate=cost(tokens * features, 4 * tokens * features),
        name="mlp_in",
    )(half_offsets, *blocks, mlp_gain[None, :])

    gains, _ = lax.optimization_barrier((final_gain[None, :], mlp_in))
    for level in range(levels):
        gains = jnp.concatenate([gains, col_xor(gains, 1 << level)], axis=0)

    tile = ff_local // 3 if ff_local % (3 * LANES) == 0 else ff_local
    tiles = ff_local // tile
    plan = [[(0, 1), (1, 2)], [(0, 2), (2, 1)]] if tiles == 3 else [[(0, 1)], [(0, 1)]]

    def gate_up(member, first, count, squared):
        width = 2 * count * tile + (LANES if squared else 0)
        operands = [mlp_in, w_gate, w_up] + ([squares] if squared else [])
        weight = pl.BlockSpec((1, features, tile), lambda i: (member, 0, first + i))
        return pl.pallas_call(
            functools.partial(gate_up_kernel, tile, squared),
            grid=(count,),
            out_shape=[shape((half, width), F32), shape((half, width), BF16)],
            in_specs=[pl.BlockSpec((tokens, features), lambda i: (0, 0)), weight, weight]
            + ([pl.BlockSpec((tokens, LANES), lambda i: (0, 0))] if squared else []),
            out_specs=[pl.BlockSpec((half, width), lambda i: (0, 0))] * 2,
            compiler_params=params(56),
            cost_estimate=cost(4 * tokens * features * tile * count, 4 * tile * count * features),
            name="gate_up",
        )(*operands)

    def halve(keep, received, squared, after):
        rows, width = keep.shape
        step = width if squared or width % (2 * LANES) else width // 2
        return pl.pallas_call(
            functools.partial(halve_kernel, squared),
            grid=(width // step,),
            out_shape=[shape((rows // 2, width), F32), shape((rows // 2, width), BF16)],
            in_specs=[pl.BlockSpec((rows, step), lambda i: (0, i))] * 2 + [ANY] * len(after),
            out_specs=[pl.BlockSpec((rows // 2, step), lambda i: (0, i))] * 2,
            compiler_params=params(24),
            cost_estimate=cost(rows * width, 9 * rows * width),
            name="halve",
        )(keep, received, *after)

    def hidden_of(keep, received, squared, scale):
        rows = keep.shape[0]
        width = keep.shape[1] // (2 * tile) * tile
        scale_shape = shape((rows, LANES), F32)
        hidden_shape = shape((rows, width), BF16)
        return pl.pallas_call(
            functools.partial(hidden_kernel, tile, squared),
            out_shape=[hidden_shape, scale_shape] if squared else hidden_shape,
            in_specs=[VMEM] * (2 if squared else 3),
            out_specs=[VMEM] * 2 if squared else VMEM,
            compiler_params=params(24),
            cost_estimate=cost(8 * rows * width, 14 * rows * width),
            name="hidden",
        )(keep, received, *([] if squared else [scale]))

    arrived, scale, chunks = [], None, [[], []]
    for member in range(2):
        for first, count in plan[member]:
            squared = not arrived
            keep, send = gate_up(member, first, count, squared)
            for level in range(levels - 1):
                received = col_xor(send, 1 << level)
                if level == 1:
                    arrived.append(received)
                after = arrived[-2:-1] if level == 0 else []
                keep, send = halve(keep, received, squared, after)
            received = col_xor(send, 1 << (levels - 1))
            if squared:
                hidden, scale = hidden_of(keep, received, squared, None)
            else:
                hidden = hidden_of(keep, received, squared, scale)
            for level in range(levels - 1, 0, -1):
                hidden = jnp.concatenate([hidden, col_xor(hidden, 1 << level)], axis=0)
            chunks[member].append((hidden, col_xor(hidden, 1)))

    def down(member):
        own = [c[0] for c in chunks[member]]
        other = [c[1] for c in chunks[member]]
        sources = [
            (which, i * tile) for which, (_, count) in enumerate(plan[member]) for i in range(count)
        ]
        return pl.pallas_call(
            functools.partial(down_kernel, sources, len(own), col_tokens),
            grid=(tiles,),
            out_shape=[
                shape((row_tokens, features), F32 if i == 0 else BF16) for i in range(row_count)
            ],
            in_specs=[SMEM]
            + [pl.BlockSpec(array.shape, lambda i: (0, 0)) for array in own + other]
            + [pl.BlockSpec((1, tile, features), lambda i: (member, i, 0))],
            out_specs=[pl.BlockSpec((row_tokens, features), lambda i: (0, 0))] * row_count,
            scratch_shapes=[pltpu.VMEM((tokens, features), F32)],
            compiler_params=params(56),
            cost_estimate=cost(
                2 * tokens * features * ff_local, 2 * ff_local * (features + tokens)
            ),
            name="down",
        )(half_offsets, *own, *other, w_down)

    def final_state(member):
        partial_rows = down(member)
        partial_rows = [partial_rows[0]] + [
            row_xor(partial_rows[j], j) for j in range(1, row_count)
        ]
        output = stream_f + tree_sum([p.astype(F32) for p in partial_rows])
        scaled = (output * final_gain[None, :]).astype(BF16)
        by_chip = jnp.stack([scaled] + [col_xor(scaled, 2 * j) for j in range(1, chips)])
        own = jnp.stack([by_chip] + [row_xor(by_chip, j) for j in range(1, row_count)])
        return by_chip, own, col_xor(own, 1)

    vocab_start = (row_index * col_count + col_index) * vocab_local
    local_targets = (targets - vocab_start)[:, None]
    vocab_tile = 512 if vocab_local % 512 == 0 else vocab_local

    def head(own, other, after):
        return pl.pallas_call(
            head_kernel,
            grid=(vocab_local // vocab_tile,),
            out_shape=shape((tokens, LANES), F32),
            in_specs=[SMEM] * 2
            + [pl.BlockSpec(own.shape, lambda i: (0, 0, 0, 0))] * 2
            + [pl.BlockSpec(gains.shape, lambda i: (0, 0))]
            + [pl.BlockSpec((tokens, 1), lambda i: (0, 0))]
            + [pl.BlockSpec((D, vocab_tile), lambda i: (0, i))]
            + [ANY] * len(after),
            out_specs=pl.BlockSpec((tokens, LANES), lambda i: (0, 0)),
            scratch_shapes=[pltpu.VMEM((tokens, D), BF16)] + [pltpu.VMEM((tokens, 1), F32)] * 4,
            compiler_params=params(56),
            cost_estimate=cost(2 * tokens * D * vocab_local, 2 * D * vocab_local),
            name="head",
        )(col_rel, row_rel * row_tokens, own, other, gains, local_targets, w_head, *after)

    _, policy_own, policy_other = final_state(0)
    by_chip, refer_own, refer_other = final_state(1)
    stats = jnp.stack(
        [head(policy_own, policy_other, [by_chip]), head(refer_own, refer_other, [])]
    )
    stats = stats[:, :, :3].transpose(2, 0, 1)

    stats = lax.all_gather(stats, ("row", "col"), axis=1)
    top = jnp.max(stats[0], axis=0)
    total = jnp.sum(stats[1] * jnp.exp(stats[0] - top[None]), axis=0)
    logprob = jnp.sum(stats[2], axis=0) - (top + jnp.log(total))
    difference = logprob[0] - logprob[1]
    one_hot = (segment[:, None] == jnp.arange(SEQS, dtype=jnp.int32)[None, :]).astype(F32)
    seq_sums = jnp.dot(difference, one_hot, precision=lax.Precision.HIGHEST)
    return seq_sums / seq_lengths.astype(F32)


def solution(mesh):
    placed = (
        P("row", "col"),
        P("col"),
        P("col", "row"),
        P("col", "row"),
        P("col", "row"),
        P("row", "col"),
        P("col"),
        P(None, "col", "row"),
        P(None, "col", "row"),
        P(None, "row", "col"),
        P("col"),
        P(None, ("row", "col")),
        P(),
        P(),
    )
    return jax.shard_map(per_device, mesh=mesh, in_specs=placed, out_specs=P(), check_vma=False)
```

time: 377 us -> 350 us (0.928)
  starting transfers between devices: 137 us -> 70.7 us
  blocking collectives: 0 us -> 50.4 us
  Pallas kernels: 50.8 us -> 72 us
  waiting for transfers between devices: 152 us -> 134 us
  local copies, waits for them, and re-layouts: 23.2 us -> 12.6 us
    ppermute x36 -> x0, waiting for transfers between devices: 84.1 us -> none  [the longest x6 37 us: chain_reduce(): received = lax.ppermute(near, 'col', pairs_of(hop))]
    ppermute x72 -> x46, waiting for transfers between devices: 29.6 us -> 99.1 us  [col_xor(): return lax.ppermute(x, 'col', [(i, i ^ mask) for i in range(count)])]
    ppermute x36 -> x0, starting transfers between devices: 45.1 us -> none  [the longest x18 21.8 us: hidden_chunk(): moving = lax.ppermute(moving, 'col', back_of(hop))]
    all_gather x0 -> x1, blocking collectives: none -> 40.6 us  [per_device(): stats = lax.all_gather(stats, ('row', 'col'), axis=1)]
    pallas_call x12 -> x22, Pallas kernels: 46.5 us -> 67.9 us  [the longest x2 30.7 us: head(): pl.pallas_call(head_kernel, grid=(vocab_local // vocab_tile,), out_shape=...]
    ppermute x72 -> x46, starting transfers between devices: 59.7 us -> 48.5 us  [col_xor(): return lax.ppermute(x, 'col', [(i, i ^ mask) for i in range(count)])]
    ppermute x30 -> x18, starting transfers between devices: 32.6 us -> 22.2 us  [row_xor(): return lax.ppermute(x, 'row', [(i, i ^ mask) for i in range(count)])]
    all_to_all x0 -> x1, blocking collectives: none -> 9.76 us  [per_device(): projected = lax.all_to_all(projected, 'row', 0, 0)]
  transfers between devices with their start and end apart: 138 -> 64, of which waited for: 54 -> 34; matrix products, arithmetic and copies ran while one was open for 3% -> 2% of each run, Pallas kernels for 7% -> 13%
where the time goes in v2:
time: 350 us
  waiting for transfers between devices  134 us (38%)
  Pallas kernels  72 us (21%)
  starting transfers between devices  70.7 us (20%)
  blocking collectives  50.4 us (14%)
  local copies, waits for them, and re-layouts  12.6 us (4%)
  other arithmetic  8.33 us (2%)
    ppermute x46, waiting for transfers between devices, col_xor(): return lax.ppermute(x, 'col', [(i, i ^ mask) for i in range(count)])  99.1 us
    ppermute x46, starting transfers between devices, col_xor(): return lax.ppermute(x, 'col', [(i, i ^ mask) for i in range(count)])  48.5 us
    all_gather x1, blocking collectives, per_device(): stats = lax.all_gather(stats, ('row', 'col'), axis=1)  40.6 us
    ppermute x18, waiting for transfers between devices, row_xor(): return lax.ppermute(x, 'row', [(i, i ^ mask) for i in range(count)])  35.1 us
    pallas_call x2, Pallas kernels, head(): pl.pallas_call(head_kernel, grid=(vocab_local // vocab_tile,), out_shape=...  30.7 us
    ppermute x18, starting transfers between devices, row_xor(): return lax.ppermute(x, 'row', [(i, i ^ mask) for i in range(count)])  22.2 us
    pallas_call x4, Pallas kernels, gate_up(): pl.pallas_call(functools.partial(gate_up_kernel, tile, squared), grid=(co...  22.1 us
    pallas_call x2, Pallas kernels, down(): pl.pallas_call(functools.partial(down_kernel, sources, len(own), col_toke...  10.8 us
  transfers between devices with their start and end apart: 64, of which 34 were waited for; matrix products, arithmetic and copies ran while one was open for 2% of the time, Pallas kernels for 13%

profile of v2, /device:TPU:0, one launch (start us, length us, event | category | flops | bytes accessed | tf_op | source)
XLA Modules:
  0.0 349.7 jit_solution(11627597321806240148)
XLA Ops:
  24.9 6.9 %collective-permute-done.5.refs_2_ = bf16[32,1920]{1,0:T(8,128)(2,1)S(1)} collective-permute-done((bf16[32,1920]{1,0:T(8,128)(2,1)S(1)}, bf16[32,1920]{1,0:T(8,128)(2,1)S(1)}, u32[]{:S(2)}, u32[]{:S(2)}) %collective-permute-start.5) | collective-permute-done | bytes 122912 | tf_op jit(solution)/shard_map/ppermute | solution.py:43
  38.1 7.0 %collective-permute-done.8.refs_2_ = bf16[32,1792]{1,0:T(8,128)(2,1)S(1)} collective-permute-done((bf16[32,1792]{1,0:T(8,128)(2,1)S(1)}, bf16[32,1792]{1,0:T(8,128)(2,1)S(1)}, u32[]{:S(2)}, u32[]{:S(2)}) %collective-permute-start.8) | collective-permute-done | bytes 114720 | tf_op jit(solution)/shard_map/ppermute | solution.py:43
  49.1 9.8 %all_to_all.5 = bf16[4,64,640]{2,1,0:T(8,128)(2,1)S(1)} all-to-all(bf16[4,64,640]{2,1,0:T(8,128)(2,1)S(1)} %attention_out.1), channel_id=1, replica_groups=mesh['row'=4,'col'=8] {'row'}, dimensions={0} | all-to-all | bytes 655360 | tf_op jit(solution)/shard_map/all_to_all | solution.py:420
  67.9 6.6 %gate_up.5 = (f32[128,4608]{1,0:T(8,128)}, bf16[128,4608]{1,0:T(8,128)(2,1)}) custom-call(bf16[256,640]{1,0:T(8,128)(2,1)} %copy-done, bf16[2,640,3456]{2,1,0:T(8,128)(2,1)} %w_gate.7, bf16[2,640,3456]{2,1,0:T(8,128)(2,1)} %w_up.7), custom_call_target="tpu_custom_call" | custom-call | flops 1509949440 | bytes 5898240 | tf_op jit(solution)/shard_map/gate_up/pallas_call | solution.py:451
  74.5 6.7 %gate_up.6 = (f32[128,4608]{1,0:T(8,128)}, bf16[128,4608]{1,0:T(8,128)(2,1)}) custom-call(bf16[256,640]{1,0:T(8,128)(2,1)} %copy-done, bf16[2,640,3456]{2,1,0:T(8,128)(2,1)} %w_gate.7, bf16[2,640,3456]{2,1,0:T(8,128)(2,1)} %w_up.7), custom_call_target="tpu_custom_call" | custom-call | flops 1509949440 | bytes 5898240 | tf_op jit(solution)/shard_map/gate_up/pallas_call | solution.py:451
  81.7 4.5 %gate_up.4 = (f32[128,2432]{1,0:T(8,128)}, bf16[128,2432]{1,0:T(8,128)(2,1)}) custom-call(bf16[256,640]{1,0:T(8,128)(2,1)} %copy-done, bf16[2,640,3456]{2,1,0:T(8,128)(2,1)} %w_gate.7, bf16[2,640,3456]{2,1,0:T(8,128)(2,1)} %w_up.7, f32[256,128]{1,0:T(8,128)} %copy-done.10), custom_call_target="tpu_custom_call" | custom-call | flops 754974720 | bytes 2949120 | tf_op jit(solution)/shard_map/gate_up/pallas_call | solution.py:451
  92.7 7.5 %collective-permute-done.18.recv.refs_0_ = bf16[64,2432]{1,0:T(8,128)(2,1)S(1)} collective-permute-done((bf16[64,2432]{1,0:T(8,128)(2,1)S(1)}, bf16[64,2432]{1,0:T(8,128)(2,1)S(1)}, u32[]{:S(2)}, u32[]{:S(2)}) %collective-permute-start.18) | collective-permute-done | bytes 311328 | tf_op jit(solution)/shard_map/ppermute | solution.py:43
  102.3 4.3 %gate_up.7 = (f32[128,2304]{1,0:T(8,128)}, bf16[128,2304]{1,0:T(8,128)(2,1)}) custom-call(bf16[256,640]{1,0:T(8,128)(2,1)} %copy-done, bf16[2,640,3456]{2,1,0:T(8,128)(2,1)} %w_gate.7, bf16[2,640,3456]{2,1,0:T(8,128)(2,1)} %w_up.7), custom_call_target="tpu_custom_call" | custom-call | flops 754974720 | bytes 2949120 | tf_op jit(solution)/shard_map/gate_up/pallas_call | solution.py:451
  107.8 19.1 %collective-permute-done.19.recv = bf16[32,2432]{1,0:T(8,128)(2,1)S(1)} collective-permute-done((bf16[32,2432]{1,0:T(8,128)(2,1)S(1)}, bf16[32,2432]{1,0:T(8,128)(2,1)S(1)}, u32[]{:S(2)}, u32[]{:S(2)}) %collective-permute-start.19) | collective-permute-done | bytes 155680 | tf_op jit(solution)/shard_map/ppermute | solution.py:43
  134.8 11.6 %collective-permute-start.21 = (bf16[64,1152]{1,0:T(8,128)(2,1)S(1)}, bf16[64,1152]{1,0:T(8,128)(2,1)S(1)}, u32[]{:S(2)}, u32[]{:S(2)}) collective-permute-start(bf16[64,1152]{1,0:T(8,128)(2,1)S(1)} %pad_maximum_fusion.10), channel_id=1, source_target_pairs={{0,2},{1,3},{2,0},{3,1},{4,6},{5,7},{6,4},{7,5},{8,10},{9,11},{10,... | collective-permute-start | bytes 442376 | tf_op jit(solution)/shard_map/ppermute | solution.py:43
  146.5 7.1 %collective-permute-done.24.recv = bf16[32,4608]{1,0:T(8,128)(2,1)S(1)} collective-permute-done((bf16[32,4608]{1,0:T(8,128)(2,1)S(1)}, bf16[32,4608]{1,0:T(8,128)(2,1)S(1)}, u32[]{:S(2)}, u32[]{:S(2)}) %collective-permute-start.24) | collective-permute-done | bytes 294944 | tf_op jit(solution)/shard_map/ppermute | solution.py:43
  153.8 9.2 %collective-permute-done.44.recv = bf16[32,4608]{1,0:T(8,128)(2,1)S(1)} collective-permute-done((bf16[32,4608]{1,0:T(8,128)(2,1)S(1)}, bf16[32,4608]{1,0:T(8,128)(2,1)S(1)}, u32[]{:S(2)}, u32[]{:S(2)}) %collective-permute-start.44) | collective-permute-done | bytes 294944 | tf_op jit(solution)/shard_map/ppermute | solution.py:43
  166.4 4.4 %collective-permute-done.25 = bf16[32,2304]{1,0:T(8,128)(2,1)S(1)} collective-permute-done((bf16[32,2304]{1,0:T(8,128)(2,1)S(1)}, bf16[32,2304]{1,0:T(8,128)(2,1)S(1)}, u32[]{:S(2)}, u32[]{:S(2)}) %collective-permute-start.25) | collective-permute-done | bytes 147488 | tf_op jit(solution)/shard_map/ppermute | solution.py:43
  171.9 7.0 %collective-permute-done.49.recv = bf16[32,2304]{1,0:T(8,128)(2,1)S(1)} collective-permute-done((bf16[32,2304]{1,0:T(8,128)(2,1)S(1)}, bf16[32,2304]{1,0:T(8,128)(2,1)S(1)}, u32[]{:S(2)}, u32[]{:S(2)}) %collective-permute-start.49) | collective-permute-done | bytes 147488 | tf_op jit(solution)/shard_map/ppermute | solution.py:43
  186.9 6.2 %collective-permute-done.46 = bf16[64,2304]{1,0:T(8,128)(2,1)S(1)} collective-permute-done((bf16[64,2304]{1,0:T(8,128)(2,1)S(1)}, bf16[64,2304]{1,0:T(8,128)(2,1)S(1)}, u32[]{:S(2)}, u32[]{:S(2)}) %collective-permute-start.46) | collective-permute-done | bytes 294944 | tf_op jit(solution)/shard_map/ppermute | solution.py:43
  197.6 5.4 %down.2 = (f32[64,640]{1,0:T(8,128)}, bf16[64,640]{1,0:T(8,128)(2,1)}, bf16[64,640]{1,0:T(8,128)(2,1)}, bf16[64,640]{1,0:T(8,128)(2,1)}) custom-call(s32[8]{0:T(128)} %copy-done.11, bf16[128,1152]{1,0:T(8,128)(2,1)} %copy-done.22, bf16[128,2304]{1,0:T(8,128)(2,1)} %copy-done.16, bf16[128,1152]{1,0:T(8,128)(2,1)} %copy-done.24, bf16[128,2304]{1,0:T(8,128)(2,1)} %copy-done.20, ...), custom_call_target="tpu_custom_call" | custom-call | flops 1132462080 | bytes 6193152 | tf_op jit(solution)/shard_map/down/pallas_call | solution.py:518
  208.2 5.4 %down.3 = (f32[64,640]{1,0:T(8,128)}, bf16[64,640]{1,0:T(8,128)(2,1)}, bf16[64,640]{1,0:T(8,128)(2,1)}, bf16[64,640]{1,0:T(8,128)(2,1)}) custom-call(s32[8]{0:T(128)} %copy-done.11, bf16[128,2304]{1,0:T(8,128)(2,1)} %copy-done.15, bf16[128,1152]{1,0:T(8,128)(2,1)} %copy-done.18, bf16[128,2304]{1,0:T(8,128)(2,1)} %copy-done.19, bf16[128,1152]{1,0:T(8,128)(2,1)} %copy-done.23, ...), custom_call_target="tpu_custom_call" | custom-call | flops 1132462080 | bytes 6193152 | tf_op jit(solution)/shard_map/down/pallas_call | solution.py:518
  236.2 6.4 %collective-permute-done.62 = bf16[4,64,640]{2,1,0:T(8,128)(2,1)S(1)} collective-permute-done((bf16[4,64,640]{2,1,0:T(8,128)(2,1)S(1)}, bf16[4,64,640]{2,1,0:T(8,128)(2,1)S(1)}, u32[]{:S(2)}, u32[]{:S(2)}) %collective-permute-start.62) | collective-permute-done | bytes 327712 | tf_op jit(solution)/shard_map/ppermute | solution.py:38
  242.8 3.9 %collective-permute-done.61 = bf16[4,64,640]{2,1,0:T(8,128)(2,1)S(1)} collective-permute-done((bf16[4,64,640]{2,1,0:T(8,128)(2,1)S(1)}, bf16[4,64,640]{2,1,0:T(8,128)(2,1)S(1)}, u32[]{:S(2)}, u32[]{:S(2)}) %collective-permute-start.61) | collective-permute-done | bytes 327712 | tf_op jit(solution)/shard_map/ppermute | solution.py:38
  250.7 8.0 %collective-permute-done.37 = bf16[4,64,640]{2,1,0:T(8,128)(2,1)S(1)} collective-permute-done((bf16[4,64,640]{2,1,0:T(8,128)(2,1)S(1)}, bf16[4,64,640]{2,1,0:T(8,128)(2,1)S(1)}, u32[]{:S(2)}, u32[]{:S(2)}) %collective-permute-start.37) | collective-permute-done | bytes 327712 | tf_op jit(solution)/shard_map/ppermute | solution.py:38
  258.6 6.6 %collective-permute-done.36 = bf16[4,64,640]{2,1,0:T(8,128)(2,1)} collective-permute-done((bf16[4,64,640]{2,1,0:T(8,128)(2,1)S(1)}, bf16[4,64,640]{2,1,0:T(8,128)(2,1)}, u32[]{:S(2)}, u32[]{:S(2)}) %collective-permute-start.36) | collective-permute-done | bytes 327712 | tf_op jit(solution)/shard_map/ppermute | solution.py:38
  275.7 15.4 %head.3 = f32[256,128]{1,0:T(8,128)} custom-call(s32[8]{0:T(128)} %iota_xor_fusion.1.col_index, s32[4]{0:T(128)} %fusion.20.row_places, bf16[4,4,64,640]{3,2,1,0:T(8,128)(2,1)} %copy-done.13, bf16[4,4,64,640]{3,2,1,0:T(8,128)(2,1)} %collective-permute-done.63.other, f32[8,640]{1,0:T(8,128)} %pad_maximum_fusion.12.gains, s32[256,1]{1,0:T(8,128)} %copy.21.target, ...), custom_call_target="tpu_custom_call" | custom-call | flops 6710886400 | bytes 26214400 | tf_op jit(solution)/shard_map/head/pallas_call | solution.py:552
  291.0 15.4 %head.2 = f32[256,128]{1,0:T(8,128)} custom-call(s32[8]{0:T(128)} %iota_xor_fusion.1.col_index, s32[4]{0:T(128)} %fusion.20.row_places, bf16[4,4,64,640]{3,2,1,0:T(8,128)(2,1)} %copy-done.14, bf16[4,4,64,640]{3,2,1,0:T(8,128)(2,1)} %collective-permute-done.38.other, f32[8,640]{1,0:T(8,128)} %pad_maximum_fusion.12.gains, s32[256,1]{1,0:T(8,128)} %copy.21.target, ...), custom_call_target="tpu_custom_call" | custom-call | flops 6710886400 | bytes 26214400 | tf_op jit(solution)/shard_map/head/pallas_call | solution.py:552
  307.5 40.6 %all-gather = f32[3,64,256]{2,0,1:T(4,128)S(1)} all-gather(f32[3,2,256]{2,0,1:T(4,128)S(1)} %copy.23), channel_id=2, replica_groups=mesh['row'=4,'col'=8] {'row','col'}, dimensions={1}, use_global_device_ids=true | all-gather | bytes 202752 | tf_op jit(solution)/shard_map/all_gather | solution.py:576
  (247 shorter events, 124.1 us)
Async XLA Ops:
  74.5 16.9 %collective-permute-start.22 = (bf16[128,4608]{1,0:T(8,128)(2,1)}, bf16[128,4608]{1,0:T(8,128)(2,1)S(1)}, u32[]{:S(2)}, u32[]{:S(2)}) collective-permute-start(bf16[128,4608]{1,0:T(8,128)(2,1)} %get-tuple-element.64), channel_id=1, source_target_pairs={{0,1},{1,0},{2,3},{3,2},{4,5},{5,4},{6,7},{7,6},{8,9},{9,8},{10,11... | collective-permute-start | bytes 3538952 | tf_op jit(solution)/shard_map/ppermute | solution.py:43
  81.2 19.0 %collective-permute-start.42 = (bf16[128,4608]{1,0:T(8,128)(2,1)}, bf16[128,4608]{1,0:T(8,128)(2,1)S(1)}, u32[]{:S(2)}, u32[]{:S(2)}) collective-permute-start(bf16[128,4608]{1,0:T(8,128)(2,1)} %get-tuple-element.76), channel_id=1, source_target_pairs={{0,1},{1,0},{2,3},{3,2},{4,5},{5,4},{6,7},{7,6},{8,9},{9,8},{10,11... | collective-permute-start | bytes 3538952 | tf_op jit(solution)/shard_map/ppermute | solution.py:43
  92.0 38.6 %collective-permute-start.23 = (bf16[64,4608]{1,0:T(8,128)(2,1)S(1)}, bf16[64,4608]{1,0:T(8,128)(2,1)S(1)}, u32[]{:S(2)}, u32[]{:S(2)}) collective-permute-start(bf16[64,4608]{1,0:T(8,128)(2,1)S(1)} %get-tuple-element.66), channel_id=1, source_target_pairs={{0,2},{1,3},{2,0},{3,1},{4,6},{5,7},{6,4},{7,5},{8,10},{9,11},{10,... | collective-permute-start | bytes 1769480 | tf_op jit(solution)/shard_map/ppermute | solution.py:43
  100.8 30.2 %collective-permute-start.43 = (bf16[64,4608]{1,0:T(8,128)(2,1)S(1)}, bf16[64,4608]{1,0:T(8,128)(2,1)S(1)}, u32[]{:S(2)}, u32[]{:S(2)}) collective-permute-start(bf16[64,4608]{1,0:T(8,128)(2,1)S(1)} %get-tuple-element.78), channel_id=1, source_target_pairs={{0,2},{1,3},{2,0},{3,1},{4,6},{5,7},{6,4},{7,5},{8,10},{9,11},{10,... | collective-permute-start | bytes 1769480 | tf_op jit(solution)/shard_map/ppermute | solution.py:43
  106.5 27.8 %collective-permute-start.47 = (bf16[128,2304]{1,0:T(8,128)(2,1)}, bf16[128,2304]{1,0:T(8,128)(2,1)S(1)}, u32[]{:S(2)}, u32[]{:S(2)}) collective-permute-start(bf16[128,2304]{1,0:T(8,128)(2,1)} %get-tuple-element.82), channel_id=1, source_target_pairs={{0,1},{1,0},{2,3},{3,2},{4,5},{5,4},{6,7},{7,6},{8,9},{9,8},{10,11... | collective-permute-start | bytes 1769480 | tf_op jit(solution)/shard_map/ppermute | solution.py:43
  106.6 20.3 %collective-permute-start.19 = (bf16[32,2432]{1,0:T(8,128)(2,1)S(1)}, bf16[32,2432]{1,0:T(8,128)(2,1)S(1)}, u32[]{:S(2)}, u32[]{:S(2)}) collective-permute-start(bf16[32,2432]{1,0:T(8,128)(2,1)S(1)} %get-tuple-element.61), channel_id=1, source_target_pairs={{0,4},{1,5},{2,6},{3,7},{4,0},{5,1},{6,2},{7,3},{8,12},{9,13},{10,... | collective-permute-start | bytes 466952 | tf_op jit(solution)/shard_map/ppermute | solution.py:43
  130.9 22.6 %collective-permute-start.24 = (bf16[32,4608]{1,0:T(8,128)(2,1)S(1)}, bf16[32,4608]{1,0:T(8,128)(2,1)S(1)}, u32[]{:S(2)}, u32[]{:S(2)}) collective-permute-start(bf16[32,4608]{1,0:T(8,128)(2,1)S(1)} %get-tuple-element.68), channel_id=1, source_target_pairs={{0,4},{1,5},{2,6},{3,7},{4,0},{5,1},{6,2},{7,3},{8,12},{9,13},{10,... | collective-permute-start | bytes 884744 | tf_op jit(solution)/shard_map/ppermute | solution.py:43
  131.4 31.6 %collective-permute-start.44 = (bf16[32,4608]{1,0:T(8,128)(2,1)S(1)}, bf16[32,4608]{1,0:T(8,128)(2,1)S(1)}, u32[]{:S(2)}, u32[]{:S(2)}) collective-permute-start(bf16[32,4608]{1,0:T(8,128)(2,1)S(1)} %get-tuple-element.80), channel_id=1, source_target_pairs={{0,4},{1,5},{2,6},{3,7},{4,0},{5,1},{6,2},{7,3},{8,12},{9,13},{10,... | collective-permute-start | bytes 884744 | tf_op jit(solution)/shard_map/ppermute | solution.py:43
  134.7 28.5 %collective-permute-start.48 = (bf16[64,2304]{1,0:T(8,128)(2,1)S(1)}, bf16[64,2304]{1,0:T(8,128)(2,1)S(1)}, u32[]{:S(2)}, u32[]{:S(2)}) collective-permute-start(bf16[64,2304]{1,0:T(8,128)(2,1)S(1)} %get-tuple-element.84), channel_id=1, source_target_pairs={{0,2},{1,3},{2,0},{3,1},{4,6},{5,7},{6,4},{7,5},{8,10},{9,11},{10,... | collective-permute-start | bytes 884744 | tf_op jit(solution)/shard_map/ppermute | solution.py:43
  134.8 58.4 %collective-permute-start.21 = (bf16[64,1152]{1,0:T(8,128)(2,1)S(1)}, bf16[64,1152]{1,0:T(8,128)(2,1)S(1)}, u32[]{:S(2)}, u32[]{:S(2)}) collective-permute-start(bf16[64,1152]{1,0:T(8,128)(2,1)S(1)} %pad_maximum_fusion.10), channel_id=1, source_target_pairs={{0,2},{1,3},{2,0},{3,1},{4,6},{5,7},{6,4},{7,5},{8,10},{9,11},{10,... | collective-permute-start | bytes 442376 | tf_op jit(solution)/shard_map/ppermute | solution.py:43
  153.7 17.2 %collective-permute-start.25 = (bf16[32,2304]{1,0:T(8,128)(2,1)S(1)}, bf16[32,2304]{1,0:T(8,128)(2,1)S(1)}, u32[]{:S(2)}, u32[]{:S(2)}) collective-permute-start(bf16[32,2304]{1,0:T(8,128)(2,1)S(1)} %hidden.5), channel_id=1, source_target_pairs={{0,4},{1,5},{2,6},{3,7},{4,0},{5,1},{6,2},{7,3},{8,12},{9,13},{10,... | collective-permute-start | bytes 442376 | tf_op jit(solution)/shard_map/ppermute | solution.py:43
  163.1 15.9 %collective-permute-start.45 = (bf16[32,2304]{1,0:T(8,128)(2,1)S(1)}, bf16[32,2304]{1,0:T(8,128)(2,1)S(1)}, u32[]{:S(2)}, u32[]{:S(2)}) collective-permute-start(bf16[32,2304]{1,0:T(8,128)(2,1)S(1)} %hidden.6), channel_id=1, source_target_pairs={{0,4},{1,5},{2,6},{3,7},{4,0},{5,1},{6,2},{7,3},{8,12},{9,13},{10,... | collective-permute-start | bytes 442376 | tf_op jit(solution)/shard_map/ppermute | solution.py:43
  163.5 15.4 %collective-permute-start.49 = (bf16[32,2304]{1,0:T(8,128)(2,1)S(1)}, bf16[32,2304]{1,0:T(8,128)(2,1)S(1)}, u32[]{:S(2)}, u32[]{:S(2)}) collective-permute-start(bf16[32,2304]{1,0:T(8,128)(2,1)S(1)} %get-tuple-element.86), channel_id=1, source_target_pairs={{0,4},{1,5},{2,6},{3,7},{4,0},{5,1},{6,2},{7,3},{8,12},{9,13},{10,... | collective-permute-start | bytes 442376 | tf_op jit(solution)/shard_map/ppermute | solution.py:43
  170.9 15.9 %collective-permute-start.26 = (bf16[64,2304]{1,0:T(8,128)(2,1)S(1)}, bf16[64,2304]{1,0:T(8,128)(2,1)S(1)}, u32[]{:S(2)}, u32[]{:S(2)}) collective-permute-start(bf16[64,2304]{1,0:T(8,128)(2,1)S(1)} %pad_maximum_fusion.6), channel_id=1, source_target_pairs={{0,2},{1,3},{2,0},{3,1},{4,6},{5,7},{6,4},{7,5},{8,10},{9,11},{10,... | collective-permute-start | bytes 884744 | tf_op jit(solution)/shard_map/ppermute | solution.py:43
  179.1 14.0 %collective-permute-start.46 = (bf16[64,2304]{1,0:T(8,128)(2,1)S(1)}, bf16[64,2304]{1,0:T(8,128)(2,1)S(1)}, u32[]{:S(2)}, u32[]{:S(2)}) collective-permute-start(bf16[64,2304]{1,0:T(8,128)(2,1)S(1)} %pad_maximum_fusion.7), channel_id=1, source_target_pairs={{0,2},{1,3},{2,0},{3,1},{4,6},{5,7},{6,4},{7,5},{8,10},{9,11},{10,... | collective-permute-start | bytes 884744 | tf_op jit(solution)/shard_map/ppermute | solution.py:43
  193.1 13.5 %collective-permute-start.52 = (bf16[128,2304]{1,0:T(8,128)(2,1)S(1)}, bf16[128,2304]{1,0:T(8,128)(2,1)S(1)}, u32[]{:S(2)}, u32[]{:S(2)}) collective-permute-start(bf16[128,2304]{1,0:T(8,128)(2,1)S(1)} %pad_maximum_fusion.3.refs_0_), channel_id=1, source_target_pairs={{0,1},{1,0},{2,3},{3,2},{4,5},{5,4},{6,7},{7,6},{8,9},{9,8},{10,11... | collective-permute-start | bytes 1769480 | tf_op jit(solution)/shard_map/ppermute | solution.py:43
  203.1 13.4 %collective-permute-start.31 = (bf16[64,640]{1,0:T(8,128)(2,1)}, bf16[64,640]{1,0:T(8,128)(2,1)S(1)}, u32[]{:S(2)}, u32[]{:S(2)}) collective-permute-start(bf16[64,640]{1,0:T(8,128)(2,1)} %get-tuple-element.73), channel_id=1, source_target_pairs={{0,24},{8,16},{16,8},{24,0},{1,25},{9,17},{17,9},{25,1},{2,26},{10... | collective-permute-start | bytes 245768 | tf_op jit(solution)/shard_map/ppermute | solution.py:38
  232.5 14.2 %collective-permute-start.61 = (bf16[4,64,640]{2,1,0:T(8,128)(2,1)S(1)}, bf16[4,64,640]{2,1,0:T(8,128)(2,1)S(1)}, u32[]{:S(2)}, u32[]{:S(2)}) collective-permute-start(bf16[4,64,640]{2,1,0:T(8,128)(2,1)S(1)} %get-tuple-element.99.refs_0_), channel_id=1, source_target_pairs={{0,16},{8,24},{16,0},{24,8},{1,17},{9,25},{17,1},{25,9},{2,18},{10... | collective-permute-start | bytes 983048 | tf_op jit(solution)/shard_map/ppermute | solution.py:38
  233.3 13.4 %collective-permute-start.60 = (bf16[4,64,640]{2,1,0:T(8,128)(2,1)S(1)}, bf16[4,64,640]{2,1,0:T(8,128)(2,1)S(1)}, u32[]{:S(2)}, u32[]{:S(2)}) collective-permute-start(bf16[4,64,640]{2,1,0:T(8,128)(2,1)S(1)} %get-tuple-element.99.refs_0_), channel_id=1, source_target_pairs={{0,8},{8,0},{16,24},{24,16},{1,9},{9,1},{17,25},{25,17},{2,10},{10... | collective-permute-start | bytes 983048 | tf_op jit(solution)/shard_map/ppermute | solution.py:38
  246.9 28.8 %collective-permute-start.63 = (bf16[4,4,64,640]{3,2,1,0:T(8,128)(2,1)S(1)}, bf16[4,4,64,640]{3,2,1,0:T(8,128)(2,1)}, u32[]{:S(2)}, u32[]{:S(2)}) collective-permute-start(bf16[4,4,64,640]{3,2,1,0:T(8,128)(2,1)S(1)} %pad_maximum_fusion.1.own), channel_id=1, source_target_pairs={{0,1},{1,0},{2,3},{3,2},{4,5},{5,4},{6,7},{7,6},{8,9},{9,8},{10,11... | collective-permute-start | bytes 3932168 | tf_op jit(solution)/shard_map/ppermute | solution.py:43
  249.4 15.9 %collective-permute-start.36 = (bf16[4,64,640]{2,1,0:T(8,128)(2,1)S(1)}, bf16[4,64,640]{2,1,0:T(8,128)(2,1)}, u32[]{:S(2)}, u32[]{:S(2)}) collective-permute-start(bf16[4,64,640]{2,1,0:T(8,128)(2,1)S(1)} %get-tuple-element.97), channel_id=1, source_target_pairs={{0,16},{8,24},{16,0},{24,8},{1,17},{9,25},{17,1},{25,9},{2,18},{10... | collective-permute-start | bytes 983048 | tf_op jit(solution)/shard_map/ppermute | solution.py:38
  250.0 15.3 %collective-permute-start.35 = (bf16[4,64,640]{2,1,0:T(8,128)(2,1)S(1)}, bf16[4,64,640]{2,1,0:T(8,128)(2,1)}, u32[]{:S(2)}, u32[]{:S(2)}) collective-permute-start(bf16[4,64,640]{2,1,0:T(8,128)(2,1)S(1)} %get-tuple-element.97), channel_id=1, source_target_pairs={{0,8},{8,0},{16,24},{24,16},{1,9},{9,1},{17,25},{25,17},{2,10},{10... | collective-permute-start | bytes 983048 | tf_op jit(solution)/shard_map/ppermute | solution.py:38
  250.7 16.0 %collective-permute-start.39 = (f32[1,640]{1,0:T(1,128)S(1)}, f32[1,640]{1,0:T(1,128)S(1)}, u32[]{:S(2)}, u32[]{:S(2)}) collective-permute-start(f32[1,640]{1,0:T(1,128)S(1)} %broadcast_in_dim.55), channel_id=1, source_target_pairs={{0,1},{1,0},{2,3},{3,2},{4,5},{5,4},{6,7},{7,6},{8,9},{9,8},{10,11... | collective-permute-start | bytes 7688 | tf_op jit(solution)/shard_map/ppermute | solution.py:43
  266.6 24.5 %collective-permute-start.38 = (bf16[4,4,64,640]{3,2,1,0:T(8,128)(2,1)S(1)}, bf16[4,4,64,640]{3,2,1,0:T(8,128)(2,1)}, u32[]{:S(2)}, u32[]{:S(2)}) collective-permute-start(bf16[4,4,64,640]{3,2,1,0:T(8,128)(2,1)S(1)} %pad_maximum_fusion.own), channel_id=1, source_target_pairs={{0,1},{1,0},{2,3},{3,2},{4,5},{5,4},{6,7},{7,6},{8,9},{9,8},{10,11... | collective-permute-start | bytes 3932168 | tf_op jit(solution)/shard_map/ppermute | solution.py:43
  (71 other events, 598.9 us)

commit v3 on v2

--- a/solution.py
+++ b/solution.py
@@ -31,6 +31,15 @@
 
 def cost(flops, byte_count):
     return pl.CostEstimate(flops=flops, bytes_accessed=byte_count, transcendentals=0)
+
+
+def call(kernel, operands, in_specs, after, **options):
+    count, extra = len(operands), len(after)
+
+    def body(*refs):
+        kernel(*refs[:count], *refs[count + extra :])
+
+    return pl.pallas_call(body, in_specs=in_specs + [ANY] * extra, **options)(*operands, *after)
 
 
 def row_xor(x, mask):
@@ -135,8 +144,14 @@
         out[:, at : at + HEAD_DIM] = total.astype(BF16)
 
 
-def attention_kernel(heads, kv_heads, count, block, places, *refs):
-    pieces, (bias, w_out, out, qkv, attended) = refs[:count], refs[count:]
+def attention_kernel(heads, kv_heads, count, block, places, row_places, *refs):
+    pieces, (bias, w_out), outs, (qkv, attended) = (
+        refs[:count],
+        refs[count : count + 2],
+        refs[count + 2 : -2],
+        refs[-2:],
+    )
+    row_unit = outs[0].shape[0]
     unit = pieces[0].shape[0]
     for i, piece in enumerate(pieces):
         qkv[pl.ds(pl.multiple_of(places[i], unit), unit), :] = piece[...]
@@ -169,68 +184,79 @@
             result = jnp.dot(weights, v, preferred_element_type=F32).astype(BF16)
             for h in range(group):
                 at = (g * group + h) * HEAD_DIM
-                attended[start : start + block, at : at + HEAD_DIM] = result[
-                    h * block : (h + 1) * block
-                ]
+                for sub in range(0, block, row_unit):
+                    place = pl.multiple_of(row_places[(start + sub) // row_unit], row_unit)
+                    attended[pl.ds(place, row_unit), at : at + HEAD_DIM] = result[
+                        h * block + sub : h * block + sub + row_unit
+                    ]
     product = jnp.dot(attended[...], w_out[...], preferred_element_type=F32)
-    rows = out.shape[1]
-    for i in range(out.shape[0]):
-        out[i] = product[i * rows : (i + 1) * rows].astype(out.dtype)
+    for i, out in enumerate(outs):
+        out[...] = product[i * row_unit : (i + 1) * row_unit].astype(out.dtype)
 
 
 def arrange_kernel(unit, offsets, *refs):
-    blocks, (gain, out, square) = refs[:-3], refs[-3:]
+    blocks, (gain, out, keep, send, square) = refs[:-5], refs[-5:]
     assemble(offsets, blocks, gain, out, square, unit)
-
-
-def gate_up_kernel(tile, squares, x, w_gate, w_up, *refs):
-    keep, send = refs[-2:]
-    half = keep.shape[0]
-    tiles = keep.shape[1] // (2 * tile)
+    put_squares(square, keep, send, 0)
+
+
+def gate_up_kernel(x, w_gate, w_up, keep, send):
+    half = keep.shape[1]
     for i, w in enumerate((w_gate, w_up)):
         part = jnp.dot(x[...], w[0], preferred_element_type=F32)
-        for step in range(tiles):
-
-            @pl.when(pl.program_id(0) == step)
-            def _(at=(2 * step + i) * tile, part=part):
-                keep[:, at : at + tile] = part[:half]
-                send[:, at : at + tile] = part[half:].astype(BF16)
-
+        keep[i] = part[:half]
+        send[i] = part[half:].astype(BF16)
+
+
+def halve_kernel(squares, *refs):
     if squares:
-
-        @pl.when(pl.program_id(0) == 0)
-        def _():
-            put_squares(refs[0], keep, send, 2 * tiles * tile)
-
-
-def halve_kernel(squares, keep, recv, *refs):
-    kept, send = refs[-2:]
-    half, width = kept.shape
-    kept[...] = keep[:half, :] + recv[:half, :].astype(F32)
-    total = keep[half:, :] + recv[half:, :].astype(F32)
+        keep, recv, square_keep, square_recv, kept, send, square_kept, square_send = refs
+        half = square_kept.shape[0]
+        total = square_keep[...] + square_recv[...].astype(F32)
+        square_kept[...] = total[:half]
+        square_send[...] = split_square(join_square(total[half:]))
+    else:
+        keep, recv, kept, send = refs
+    half = kept.shape[1]
+    kept[...] = keep[:, :half, :] + recv[:, :half, :].astype(F32)
+    send[...] = (keep[:, half:, :] + recv[:, half:, :].astype(F32)).astype(BF16)
+
+
+def hidden_kernel(squares, keep, recv, *refs):
     if squares:
-        body = width - LANES
-        send[:, :body] = total[:, :body].astype(BF16)
-        send[:, body:] = split_square(join_square(total[:, body:]))
-    else:
-        send[...] = total.astype(BF16)
-
-
-def hidden_kernel(tile, squares, keep, recv, *refs):
-    if squares:
-        hidden, scale_ref = refs
-        at = keep.shape[1] - LANES
-        total = keep[:, at:] + recv[:, at:].astype(F32)
+        square_keep, square_recv, hidden, scale_ref = refs
+        total = square_keep[...] + square_recv[...].astype(F32)
         scale_ref[...] = lax.rsqrt(join_square(total) / D + EPSILON)
     else:
         scale_ref, hidden = refs
     scale = scale_ref[:, :1]
-    for i in range(hidden.shape[1] // tile):
-        at = 2 * i * tile
-        gate = (keep[:, at : at + tile] + recv[:, at : at + tile].astype(F32)) * scale
-        at += tile
-        up = (keep[:, at : at + tile] + recv[:, at : at + tile].astype(F32)) * scale
-        hidden[:, i * tile : (i + 1) * tile] = (gate / (1.0 + jnp.exp(-gate)) * up).astype(BF16)
+    width = keep.shape[2]
+    for i in range(keep.shape[0] // 2):
+        gate = (keep[2 * i] + recv[2 * i].astype(F32)) * scale
+        up = (keep[2 * i + 1] + recv[2 * i + 1].astype(F32)) * scale
+        hidden[:, i * width : (i + 1) * width] = (
+            gate / (1.0 + jnp.exp(-gate)) * up
+        ).astype(BF16)
+
+
+def join_kernel(first, second, out):
+    rows = first.shape[0]
+    out[:rows] = first[...]
+    out[rows:] = second[...]
+
+
+def pack_kernel(*refs):
+    parts, out = refs[:-1], refs[-1]
+    for i, part in enumerate(parts):
+        out[i] = part[...]
+
+
+def output_kernel(stream, gain, *refs):
+    parts, out = refs[:-1], refs[-1]
+    total = stream[...].astype(F32)
+    for part in parts:
+        total = total + part[...].astype(F32)
+    out[...] = (total * gain[...]).astype(BF16)
 
 
 def down_kernel(sources, count, unit, offsets, *refs):
@@ -257,10 +283,11 @@
                 step += 1
 
 
-def head_kernel(col_index, row_places, own, other, gains, target, w, *refs):
-    out, lhs, square, top, total, picked = refs[-6:]
+def head_kernel(rows, first, col_index, row_places, *refs):
+    own, other = refs[:rows], refs[rows : 2 * rows]
+    gains, target, w, out, lhs, square, top, total, picked = refs[2 * rows :]
     step = pl.program_id(0)
-    rows, chips, unit, width = own.shape
+    chips, unit, width = own[0].shape
 
     @pl.when(step == 0)
     def _():
@@ -268,10 +295,10 @@
         for i in range(rows):
             place = pl.multiple_of(row_places[i], unit)
             sums = jnp.zeros((unit, 1), F32)
-            for core, array in enumerate((own, other)):
+            for core, arrays in enumerate((own, other)):
                 for j in range(chips):
                     feature = pl.multiple_of(col_index[2 * j + core] * width, LANES)
-                    values = array[i, j]
+                    values = arrays[i][j]
                     lhs[pl.ds(place, unit), pl.ds(feature, width)] = values
                     plain = values.astype(F32) * inverse[2 * j + core : 2 * j + core + 1, :]
                     sums += jnp.sum(plain * plain, axis=1, keepdims=True)
@@ -282,7 +309,8 @@
 
     logits = jnp.dot(lhs[...], w[...], preferred_element_type=F32)
     logits = logits * lax.rsqrt(square[...] / D + EPSILON)
-    lane = lax.broadcasted_iota(jnp.int32, logits.shape, 1) + step * logits.shape[1]
+    lane = lax.broadcasted_iota(jnp.int32, logits.shape, 1)
+    lane = lane + (step + first) * logits.shape[1]
     hit = jnp.where(lane == target[...], logits, 0.0)
     picked[...] += jnp.sum(hit, axis=1, keepdims=True)
     new_top = jnp.maximum(top[...], jnp.max(logits, axis=1, keepdims=True))
@@ -371,7 +399,7 @@
         in_specs=[SMEM] + [VMEM] * (row_count + 4),
         out_specs=[VMEM] * 2,
         scratch_shapes=[pltpu.VMEM((tokens, features), BF16), pltpu.VMEM((tokens, LANES), F32)],
-        compiler_params=params(24),
+        compiler_params=params(56),
         cost_estimate=cost(
             2 * tokens * features * qkv_width, 2 * qkv_width * (features + tokens)
         ),
@@ -404,9 +432,11 @@
 
     projected = pl.pallas_call(
         functools.partial(attention_kernel, heads, kv_heads, col_count, block),
-        out_shape=shape((row_count, row_tokens, features), BF16),
-        in_specs=[SMEM] + [VMEM] * (col_count + 2),
-        out_specs=VMEM,
+        out_shape=[
+            shape((row_tokens, features), F32 if i == 0 else BF16) for i in range(row_count)
+        ],
+        in_specs=[SMEM] * 2 + [VMEM] * (col_count + 2),
+        out_specs=[VMEM] * row_count,
         scratch_shapes=[
             pltpu.VMEM((tokens, qkv_width), BF16),
             pltpu.VMEM((tokens, heads * HEAD_DIM), BF16),
@@ -416,21 +446,25 @@
             2 * tokens * heads * HEAD_DIM * features * 2, 2 * heads * HEAD_DIM * features * 2
         ),
         name="attention_out",
-    )(places, *pieces, bias, w_out)
-    projected = lax.all_to_all(projected, "row", 0, 0)
-    stream = residual.astype(F32) + jnp.sum(projected.astype(F32), axis=0)
+    )(places, row_rel * row_tokens, *pieces, bias, w_out)
+    projected = [projected[0]] + [row_xor(projected[j], j) for j in range(1, row_count)]
+    stream = residual.astype(F32) + tree_sum([p.astype(F32) for p in projected])
     stream = lax.optimization_barrier(stream.astype(BF16))
-    stream_f = stream.astype(F32)
 
     levels = (col_count - 1).bit_length()
     blocks = [stream] + [row_xor(stream, j) for j in range(1, row_count)]
     position = sum(((relative >> level) & 1) << (levels - 1 - level) for level in range(levels))
     half_offsets = position * col_tokens
-    mlp_in, squares = pl.pallas_call(
+    mlp_in, square_keep, square_send = pl.pallas_call(
         functools.partial(arrange_kernel, col_tokens),
-        out_shape=[shape((tokens, features), BF16), shape((tokens, LANES), F32)],
+        out_shape=[
+            shape((tokens, features), BF16),
+            shape((half, LANES), F32),
+            shape((half, LANES), BF16),
+        ],
         in_specs=[SMEM] + [VMEM] * (row_count + 1),
-        out_specs=[VMEM] * 2,
+        out_specs=[VMEM] * 3,
+        scratch_shapes=[pltpu.VMEM((tokens, LANES), F32)],
         compiler_params=params(16),
         cost_estimate=cost(tokens * features, 4 * tokens * features),
         name="mlp_in",
@@ -440,90 +474,131 @@
     for level in range(levels):
         gains = jnp.concatenate([gains, col_xor(gains, 1 << level)], axis=0)
 
-    tile = ff_local // 3 if ff_local % (3 * LANES) == 0 else ff_local
+    divisible = ff_local % (3 * LANES) == 0
+    tile = ff_local // 3 if divisible else ff_local
     tiles = ff_local // tile
-    plan = [[(0, 1), (1, 2)], [(0, 2), (2, 1)]] if tiles == 3 else [[(0, 1)], [(0, 1)]]
-
-    def gate_up(member, first, count, squared):
-        width = 2 * count * tile + (LANES if squared else 0)
-        operands = [mlp_in, w_gate, w_up] + ([squares] if squared else [])
-        weight = pl.BlockSpec((1, features, tile), lambda i: (member, 0, first + i))
-        return pl.pallas_call(
-            functools.partial(gate_up_kernel, tile, squared),
-            grid=(count,),
-            out_shape=[shape((half, width), F32), shape((half, width), BF16)],
-            in_specs=[pl.BlockSpec((tokens, features), lambda i: (0, 0)), weight, weight]
-            + ([pl.BlockSpec((tokens, LANES), lambda i: (0, 0))] if squared else []),
-            out_specs=[pl.BlockSpec((half, width), lambda i: (0, 0))] * 2,
+    sub = tile // 3 if tile % (3 * LANES) == 0 else tile
+    subs = tile // sub
+    plan = [(0, 0, 1), (0, 1, 2), (1, 0, 2), (1, 2, 1)] if divisible else [(0, 0, 1), (1, 0, 1)]
+    last = levels - 1
+    keeps, arrivals, hiddens = {}, {}, {}
+    token = [mlp_in]
+    scale = [None]
+    states = {}
+
+    def gate_up(j):
+        member, first, count = plan[j]
+        first = first * subs
+        weight = pl.BlockSpec((1, features, sub), lambda i: (member, 0, first + i))
+        out = pl.BlockSpec((2, half, sub), lambda i: (i, 0, 0))
+        groups = 2 * count * subs
+        keep, send = call(
+            gate_up_kernel,
+            [mlp_in, w_gate, w_up],
+            [pl.BlockSpec((tokens, features), lambda i: (0, 0)), weight, weight],
+            token,
+            grid=(count * subs,),
+            out_shape=[shape((groups, half, sub), F32), shape((groups, half, sub), BF16)],
+            out_specs=[out] * 2,
             compiler_params=params(56),
             cost_estimate=cost(4 * tokens * features * tile * count, 4 * tile * count * features),
             name="gate_up",
-        )(*operands)
-
-    def halve(keep, received, squared, after):
-        rows, width = keep.shape
-        step = width if squared or width % (2 * LANES) else width // 2
-        return pl.pallas_call(
+        )
+        arrived = [col_xor(send, 1)]
+        keeps[j] = [keep]
+        if j == 0:
+            keeps[j].append(square_keep)
+            arrived.append(col_xor(square_send, 1))
+        arrivals[j] = arrived
+        token[:] = [send]
+
+    def halve(j, level):
+        count = plan[j][2]
+        keep, received = keeps[j], arrivals[j]
+        groups, rows, _ = keep[0].shape
+        part = groups // count
+        squared = len(keep) == 2
+        specs = [pl.BlockSpec((part, rows, sub), lambda i: (i, 0, 0))] * 2
+        outs = [pl.BlockSpec((part, rows // 2, sub), lambda i: (i, 0, 0))] * 2
+        shapes = [shape((groups, rows // 2, sub), F32), shape((groups, rows // 2, sub), BF16)]
+        operands = [keep[0], received[0]]
+        if squared:
+            operands += [keep[1], received[1]]
+            specs = specs + [pl.BlockSpec((rows, LANES), lambda i: (0, 0))] * 2
+            outs = outs + [pl.BlockSpec((rows // 2, LANES), lambda i: (0, 0))] * 2
+            shapes += [shape((rows // 2, LANES), F32), shape((rows // 2, LANES), BF16)]
+        result = call(
             functools.partial(halve_kernel, squared),
-            grid=(width // step,),
-            out_shape=[shape((rows // 2, width), F32), shape((rows // 2, width), BF16)],
-            in_specs=[pl.BlockSpec((rows, step), lambda i: (0, i))] * 2 + [ANY] * len(after),
-            out_specs=[pl.BlockSpec((rows // 2, step), lambda i: (0, i))] * 2,
+            operands,
+            specs,
+            token,
+            grid=(count,),
+            out_shape=shapes,
+            out_specs=outs,
             compiler_params=params(24),
-            cost_estimate=cost(rows * width, 9 * rows * width),
+            cost_estimate=cost(rows * sub * groups, 9 * rows * sub * groups),
             name="halve",
-        )(keep, received, *after)
-
-    def hidden_of(keep, received, squared, scale):
-        rows = keep.shape[0]
-        width = keep.shape[1] // (2 * tile) * tile
+        )
+        keeps[j] = result[0::2]
+        arrivals[j] = [col_xor(send, 2 << level) for send in result[1::2]]
+        token[:] = [result[1]]
+
+    def hidden_of(j):
+        keep, received = keeps[j], arrivals[j]
+        groups, rows, _ = keep[0].shape
+        hidden_shape = shape((rows, groups // 2 * sub), BF16)
         scale_shape = shape((rows, LANES), F32)
-        hidden_shape = shape((rows, width), BF16)
-        return pl.pallas_call(
-            functools.partial(hidden_kernel, tile, squared),
-            out_shape=[hidden_shape, scale_shape] if squared else hidden_shape,
-            in_specs=[VMEM] * (2 if squared else 3),
-            out_specs=[VMEM] * 2 if squared else VMEM,
+        squared = len(keep) == 2
+        operands = [keep[0], received[0]] + ([keep[1], received[1]] if squared else scale)
+        result = call(
+            functools.partial(hidden_kernel, squared),
+            operands,
+            [VMEM] * len(operands),
+            token,
+            out_shape=[hidden_shape, scale_shape] if squared else [hidden_shape],
+            out_specs=[VMEM] * 2 if squared else [VMEM],
             compiler_params=params(24),
-            cost_estimate=cost(8 * rows * width, 14 * rows * width),
+            cost_estimate=cost(8 * rows * groups * sub, 6 * rows * groups * sub),
             name="hidden",
-        )(keep, received, *([] if squared else [scale]))
-
-    arrived, scale, chunks = [], None, [[], []]
-    for member in range(2):
-        for first, count in plan[member]:
-            squared = not arrived
-            keep, send = gate_up(member, first, count, squared)
-            for level in range(levels - 1):
-                received = col_xor(send, 1 << level)
-                if level == 1:
-                    arrived.append(received)
-                after = arrived[-2:-1] if level == 0 else []
-                keep, send = halve(keep, received, squared, after)
-            received = col_xor(send, 1 << (levels - 1))
-            if squared:
-                hidden, scale = hidden_of(keep, received, squared, None)
-            else:
-                hidden = hidden_of(keep, received, squared, scale)
-            for level in range(levels - 1, 0, -1):
-                hidden = jnp.concatenate([hidden, col_xor(hidden, 1 << level)], axis=0)
-            chunks[member].append((hidden, col_xor(hidden, 1)))
+        )
+        if squared:
+            scale[:] = [result[1]]
+        hiddens[j] = (result[0], col_xor(result[0], 1 << last))
+        token[:] = [result[0]]
+
+    def join(j, level):
+        first, second = hiddens[j]
+        rows, width = first.shape
+        joined = call(
+            join_kernel,
+            [first, second],
+            [VMEM] * 2,
+            token,
+            out_shape=shape((2 * rows, width), BF16),
+            out_specs=VMEM,
+            compiler_params=params(16),
+            cost_estimate=cost(rows * width, 8 * rows * width),
+            name="join",
+        )
+        hiddens[j] = (joined, col_xor(joined, 1 << level))
+        token[:] = [joined]
 
     def down(member):
-        own = [c[0] for c in chunks[member]]
-        other = [c[1] for c in chunks[member]]
-        sources = [
-            (which, i * tile) for which, (_, count) in enumerate(plan[member]) for i in range(count)
-        ]
-        return pl.pallas_call(
+        which = [j for j in range(len(plan)) if plan[j][0] == member]
+        own = [hiddens[j][0] for j in which]
+        other = [hiddens[j][1] for j in which]
+        sources = [(k, i * tile) for k, j in enumerate(which) for i in range(plan[j][2])]
+        parts = call(
             functools.partial(down_kernel, sources, len(own), col_tokens),
+            [half_offsets, *own, *other, w_down],
+            [SMEM]
+            + [pl.BlockSpec(array.shape, lambda i: (0, 0)) for array in own + other]
+            + [pl.BlockSpec((1, tile, features), lambda i: (member, i, 0))],
+            token,
             grid=(tiles,),
             out_shape=[
                 shape((row_tokens, features), F32 if i == 0 else BF16) for i in range(row_count)
             ],
-            in_specs=[SMEM]
-            + [pl.BlockSpec(array.shape, lambda i: (0, 0)) for array in own + other]
-            + [pl.BlockSpec((1, tile, features), lambda i: (member, i, 0))],
             out_specs=[pl.BlockSpec((row_tokens, features), lambda i: (0, 0))] * row_count,
             scratch_shapes=[pltpu.VMEM((tokens, features), F32)],
             compiler_params=params(56),
@@ -531,52 +606,107 @@
                 2 * tokens * features * ff_local, 2 * ff_local * (features + tokens)
             ),
             name="down",
-        )(half_offsets, *own, *other, w_down)
-
-    def final_state(member):
-        partial_rows = down(member)
-        partial_rows = [partial_rows[0]] + [
-            row_xor(partial_rows[j], j) for j in range(1, row_count)
-        ]
-        output = stream_f + tree_sum([p.astype(F32) for p in partial_rows])
-        scaled = (output * final_gain[None, :]).astype(BF16)
-        by_chip = jnp.stack([scaled] + [col_xor(scaled, 2 * j) for j in range(1, chips)])
-        own = jnp.stack([by_chip] + [row_xor(by_chip, j) for j in range(1, row_count)])
-        return by_chip, own, col_xor(own, 1)
+        )
+        states[member] = [parts[0]] + [row_xor(parts[j], j) for j in range(1, row_count)]
+        token[:] = [parts[1]]
+
+    def output(member):
+        parts = states[member]
+        scaled = call(
+            output_kernel,
+            [stream, final_gain[None, :], *parts],
+            [VMEM] * (2 + row_count),
+            token,
+            out_shape=shape((row_tokens, features), BF16),
+            out_specs=VMEM,
+            compiler_params=params(16),
+            cost_estimate=cost(8 * row_tokens * features, 16 * row_tokens * features),
+            name="output",
+        )
+        states[member] = [scaled] + [col_xor(scaled, 2 * j) for j in range(1, chips)]
+        token[:] = [scaled]
+
+    def pack(member):
+        by_chip = call(
+            pack_kernel,
+            states[member],
+            [VMEM] * chips,
+            token,
+            out_shape=shape((chips, row_tokens, features), BF16),
+            out_specs=VMEM,
+            compiler_params=params(16),
+            cost_estimate=cost(chips * row_tokens * features, 4 * chips * row_tokens * features),
+            name="pack",
+        )
+        own = [by_chip] + [row_xor(by_chip, j) for j in range(1, row_count)]
+        states[member] = own + [col_xor(array, 1) for array in own]
+        token[:] = [by_chip]
 
     vocab_start = (row_index * col_count + col_index) * vocab_local
     local_targets = (targets - vocab_start)[:, None]
     vocab_tile = 512 if vocab_local % 512 == 0 else vocab_local
-
-    def head(own, other, after):
-        return pl.pallas_call(
-            head_kernel,
-            grid=(vocab_local // vocab_tile,),
-            out_shape=shape((tokens, LANES), F32),
-            in_specs=[SMEM] * 2
-            + [pl.BlockSpec(own.shape, lambda i: (0, 0, 0, 0))] * 2
+    vocab_tiles = vocab_local // vocab_tile
+    stats = {0: [], 1: []}
+
+    def head(member, first, count):
+        state = states[member]
+        result = call(
+            functools.partial(head_kernel, row_count, first),
+            [col_rel, row_rel * row_tokens, *state, gains, local_targets, w_head],
+            [SMEM] * 2
+            + [pl.BlockSpec(state[0].shape, lambda i: (0, 0, 0))] * (2 * row_count)
             + [pl.BlockSpec(gains.shape, lambda i: (0, 0))]
             + [pl.BlockSpec((tokens, 1), lambda i: (0, 0))]
-            + [pl.BlockSpec((D, vocab_tile), lambda i: (0, i))]
-            + [ANY] * len(after),
+            + [pl.BlockSpec((D, vocab_tile), lambda i: (0, first + i))],
+            token,
+            grid=(count,),
+            out_shape=shape((tokens, LANES), F32),
             out_specs=pl.BlockSpec((tokens, LANES), lambda i: (0, 0)),
             scratch_shapes=[pltpu.VMEM((tokens, D), BF16)] + [pltpu.VMEM((tokens, 1), F32)] * 4,
             compiler_params=params(56),
-            cost_estimate=cost(2 * tokens * D * vocab_local, 2 * D * vocab_local),
+            cost_estimate=cost(
+                2 * tokens * D * vocab_tile * count, 2 * D * vocab_tile * count
+            ),
             name="head",
-        )(col_rel, row_rel * row_tokens, own, other, gains, local_targets, w_head, *after)
-
-    _, policy_own, policy_other = final_state(0)
-    by_chip, refer_own, refer_other = final_state(1)
-    stats = jnp.stack(
-        [head(policy_own, policy_other, [by_chip]), head(refer_own, refer_other, [])]
-    )
-    stats = stats[:, :, :3].transpose(2, 0, 1)
-
-    stats = lax.all_gather(stats, ("row", "col"), axis=1)
-    top = jnp.max(stats[0], axis=0)
-    total = jnp.sum(stats[1] * jnp.exp(stats[0] - top[None]), axis=0)
-    logprob = jnp.sum(stats[2], axis=0) - (top + jnp.log(total))
+        )
+        token[:] = [result]
+        stats[member].append(result[:, :3].T)
+
+    if len(plan) == 4 and levels == 3:
+        schedule = [
+            (gate_up, 0), (gate_up, 1), (halve, 0, 0), (gate_up, 2), (halve, 1, 0),
+            (halve, 0, 1), (gate_up, 3), (hidden_of, 0), (join, 0, 1), (halve, 2, 0),
+            (halve, 1, 1), (join, 0, 0), (hidden_of, 1), (join, 1, 1), (halve, 3, 0),
+            (halve, 2, 1), (join, 1, 0), (halve, 3, 1), (down, 0), (hidden_of, 2),
+            (output, 0), (join, 2, 1), (hidden_of, 3), (pack, 0), (join, 3, 1),
+            (join, 2, 0), (join, 3, 0), (down, 1),
+        ]
+    else:
+        schedule = []
+        for j in range(len(plan)):
+            schedule += [(gate_up, j)] + [(halve, j, level) for level in range(last)]
+            schedule += [(hidden_of, j)] + [(join, j, level) for level in range(last - 1, -1, -1)]
+        schedule += [(down, 0), (output, 0), (pack, 0), (down, 1)]
+    early = min(2, vocab_tiles)
+    schedule += [(head, 0, 0, early), (output, 1), (pack, 1)]
+    if early < vocab_tiles:
+        schedule += [(head, 0, early, vocab_tiles - early)]
+    schedule += [(head, 1, 0, vocab_tiles)]
+    for step, *arguments in schedule:
+        step(*arguments)
+
+    def combine(parts):
+        top = functools.reduce(jnp.maximum, [p[0] for p in parts])
+        total = tree_sum([p[1] * jnp.exp(p[0] - top) for p in parts])
+        picked = tree_sum([p[2] for p in parts])
+        return jnp.stack([top, total, picked])
+
+    merged = combine(stats[0]) if len(stats[0]) > 1 else stats[0][0]
+    merged = jnp.stack([merged, stats[1][0]], axis=1)
+    merged = combine([merged, col_xor(merged, 1)])
+    merged = combine([merged] + [col_xor(merged, 2 * j) for j in range(1, chips)])
+    merged = combine([merged] + [row_xor(merged, j) for j in range(1, row_count)])
+    logprob = merged[2] - (merged[0] + jnp.log(merged[1]))
     difference = logprob[0] - logprob[1]
     one_hot = (segment[:, None] == jnp.arange(SEQS, dtype=jnp.int32)[None, :]).astype(F32)
     seq_sums = jnp.dot(difference, one_hot, precision=lax.Precision.HIGHEST)

time: 350 us -> 322 us (0.920)
  blocking collectives: 50.4 us -> 0 us
  Pallas kernels: 72 us -> 79.5 us
  starting transfers between devices: 70.7 us -> 77.2 us
  local copies, waits for them, and re-layouts: 12.6 us -> 18.8 us
  waiting for transfers between devices: 134 us -> 140 us
  other arithmetic: 8.33 us -> 4.11 us
    all_gather x1 -> x0, blocking collectives: 40.6 us -> none  [per_device(): stats = lax.all_gather(stats, ('row', 'col'), axis=1)]
    ppermute x46 -> x59, waiting for transfers between devices: 99.1 us -> 118 us  [col_xor(): return lax.ppermute(x, 'col', [(i, i ^ mask) for i in range(count)])]
    ppermute x18 -> x24, waiting for transfers between devices: 35.1 us -> 21.3 us  [row_xor(): return lax.ppermute(x, 'row', [(i, i ^ mask) for i in range(count)])]
    all_to_all x1 -> x0, blocking collectives: 9.76 us -> none  [per_device(): projected = lax.all_to_all(projected, 'row', 0, 0)]
    ppermute x18 -> x24, starting transfers between devices: 22.2 us -> 29.2 us  [row_xor(): return lax.ppermute(x, 'row', [(i, i ^ mask) for i in range(count)])]
    pallas_call x20 -> x33, Pallas kernels: 67.1 us -> 72.1 us  [call(): pl.pallas_call(body, in_specs=in_specs + [ANY] * extra, **options)]
    unnamed x64 -> x106, local copies, waits for them, and re-layouts: 10.1 us -> 13.4 us
    ppermute x46 -> x59, starting transfers between devices: 48.5 us -> 48 us  [col_xor(): return lax.ppermute(x, 'col', [(i, i ^ mask) for i in range(count)])]
  transfers between devices with their start and end apart: 64 -> 83, of which waited for: 34 -> 45; matrix products, arithmetic and copies ran while one was open for 2% -> 3% of each run, Pallas kernels for 13% -> 16%
where the time goes in v3:
time: 322 us; the launch traced here: 321 us
  waiting for transfers between devices  140 us (43%)
  Pallas kernels  79.5 us (25%)
  starting transfers between devices  77.2 us (24%)
  local copies, waits for them, and re-layouts  18.8 us (6%)
  other arithmetic  4.11 us (1%)
    ppermute x59, waiting for transfers between devices, col_xor(): return lax.ppermute(x, 'col', [(i, i ^ mask) for i in range(count)])  118 us
    pallas_call x33, Pallas kernels, call(): pl.pallas_call(body, in_specs=in_specs + [ANY] * extra, **options)  72.1 us
    ppermute x59, starting transfers between devices, col_xor(): return lax.ppermute(x, 'col', [(i, i ^ mask) for i in range(count)])  48 us
    ppermute x24, starting transfers between devices, row_xor(): return lax.ppermute(x, 'row', [(i, i ^ mask) for i in range(count)])  29.2 us
    ppermute x24, waiting for transfers between devices, row_xor(): return lax.ppermute(x, 'row', [(i, i ^ mask) for i in range(count)])  21.3 us
    unnamed x106, local copies, waits for them, and re-layouts  13.4 us
  transfers between devices with their start and end apart: 83, of which 45 were waited for; matrix products, arithmetic and copies ran while one was open for 3% of the time, Pallas kernels for 16%

profile of v3, /device:TPU:0, one launch (start us, length us, event | category | flops | bytes accessed | tf_op | source)
XLA Modules:
  0.0 320.9 jit_solution(14137136614838287871)
XLA Ops:
  10.6 3.9 %qkv_partial.1 = (f32[128,1920]{1,0:T(8,128)}, bf16[128,1920]{1,0:T(8,128)(2,1)}) custom-call(s32[8]{0:T(128)} %reshape.112.offsets, bf16[64,640]{1,0:T(8,128)(2,1)} %refs_0_.1, bf16[64,640]{1,0:T(8,128)(2,1)} %copy-done.45, bf16[64,640]{1,0:T(8,128)(2,1)} %copy-done.46, bf16[64,640]{1,0:T(8,128)(2,1)} %copy-done.47, f32[1,640]{1,0:T(1,128)} %broadcast_in_dim.28.refs_4_, ...), custom_call_target="tpu_custom_call" | custom-call | flops 587202560 | bytes 3211264 | tf_op jit(solution)/shard_map/qkv_partial/pallas_call | solution.py:396
  25.0 6.9 %collective-permute-done.5.refs_2_ = bf16[32,1920]{1,0:T(8,128)(2,1)S(1)} collective-permute-done((bf16[32,1920]{1,0:T(8,128)(2,1)S(1)}, bf16[32,1920]{1,0:T(8,128)(2,1)S(1)}, u32[]{:S(2)}, u32[]{:S(2)}) %collective-permute-start.5) | collective-permute-done | bytes 122912 | tf_op jit(solution)/shard_map/ppermute | solution.py:52
  38.2 7.0 %collective-permute-done.8.refs_2_ = bf16[32,1792]{1,0:T(8,128)(2,1)S(1)} collective-permute-done((bf16[32,1792]{1,0:T(8,128)(2,1)S(1)}, bf16[32,1792]{1,0:T(8,128)(2,1)S(1)}, u32[]{:S(2)}, u32[]{:S(2)}) %collective-permute-start.8) | collective-permute-done | bytes 114720 | tf_op jit(solution)/shard_map/ppermute | solution.py:52
  65.7 4.6 %gate_up.4 = (f32[6,128,384]{2,1,0:T(8,128)}, bf16[6,128,384]{2,1,0:T(8,128)(2,1)}) custom-call(bf16[256,640]{1,0:T(8,128)(2,1)} %copy-done, bf16[2,640,3456]{2,1,0:T(8,128)(2,1)} %refs_1_.7, bf16[2,640,3456]{2,1,0:T(8,128)(2,1)} %refs_2_.7, bf16[256,640]{1,0:T(8,128)(2,1)} %copy-done), custom_call_target="tpu_custom_call" | custom-call | flops 754974720 | bytes 2949120 | tf_op jit(solution)/shard_map/gate_up/pallas_call | solution.py:42
  70.3 7.4 %gate_up.5 = (f32[12,128,384]{2,1,0:T(8,128)}, bf16[12,128,384]{2,1,0:T(8,128)(2,1)}) custom-call(bf16[256,640]{1,0:T(8,128)(2,1)} %copy-done, bf16[2,640,3456]{2,1,0:T(8,128)(2,1)} %refs_1_.7, bf16[2,640,3456]{2,1,0:T(8,128)(2,1)} %refs_2_.7, bf16[6,128,384]{2,1,0:T(8,128)(2,1)} %get-tuple-element.69.refs_3_), custom_call_target="tpu_custom_call" | custom-call | flops 1509949440 | bytes 5898240 | tf_op jit(solution)/shard_map/gate_up/pallas_call | solution.py:42
  82.8 7.4 %gate_up.6 = (f32[12,128,384]{2,1,0:T(8,128)}, bf16[12,128,384]{2,1,0:T(8,128)(2,1)}) custom-call(bf16[256,640]{1,0:T(8,128)(2,1)} %copy-done, bf16[2,640,3456]{2,1,0:T(8,128)(2,1)} %refs_1_.7, bf16[2,640,3456]{2,1,0:T(8,128)(2,1)} %refs_2_.7, bf16[6,64,384]{2,1,0:T(8,128)(2,1)} %copy-done.15), custom_call_target="tpu_custom_call" | custom-call | flops 1509949440 | bytes 5898240 | tf_op jit(solution)/shard_map/gate_up/pallas_call | solution.py:42
  95.6 18.6 %collective-permute-done.23.refs_3_ = bf16[64,128]{1,0:T(8,128)(2,1)S(1)} collective-permute-done((bf16[64,128]{1,0:T(8,128)(2,1)S(1)}, bf16[64,128]{1,0:T(8,128)(2,1)S(1)}, u32[]{:S(2)}, u32[]{:S(2)}) %collective-permute-start.23) | collective-permute-done | bytes 16416 | tf_op jit(solution)/shard_map/ppermute | solution.py:52
  117.3 4.7 %gate_up.7 = (f32[6,128,384]{2,1,0:T(8,128)}, bf16[6,128,384]{2,1,0:T(8,128)(2,1)}) custom-call(bf16[256,640]{1,0:T(8,128)(2,1)} %copy-done, bf16[2,640,3456]{2,1,0:T(8,128)(2,1)} %refs_1_.7, bf16[2,640,3456]{2,1,0:T(8,128)(2,1)} %refs_2_.7, bf16[6,32,384]{2,1,0:T(8,128)(2,1)} %copy-done.21), custom_call_target="tpu_custom_call" | custom-call | flops 754974720 | bytes 2949120 | tf_op jit(solution)/shard_map/gate_up/pallas_call | solution.py:42
  124.8 5.1 %collective-permute-done.27.refs_1_ = bf16[32,1152]{1,0:T(8,128)(2,1)S(1)} collective-permute-done((bf16[32,1152]{1,0:T(8,128)(2,1)S(1)}, bf16[32,1152]{1,0:T(8,128)(2,1)S(1)}, u32[]{:S(2)}, u32[]{:S(2)}) %collective-permute-start.27) | collective-permute-done | bytes 73760 | tf_op jit(solution)/shard_map/ppermute | solution.py:52
  133.2 8.0 %collective-permute-done.28.refs_1_ = bf16[64,1152]{1,0:T(8,128)(2,1)S(1)} collective-permute-done((bf16[64,1152]{1,0:T(8,128)(2,1)S(1)}, bf16[64,1152]{1,0:T(8,128)(2,1)S(1)}, u32[]{:S(2)}, u32[]{:S(2)}) %collective-permute-start.28) | collective-permute-done | bytes 147488 | tf_op jit(solution)/shard_map/ppermute | solution.py:52
  144.6 9.8 %collective-permute-done.32.refs_1_ = bf16[32,2304]{1,0:T(8,128)(2,1)S(1)} collective-permute-done((bf16[32,2304]{1,0:T(8,128)(2,1)S(1)}, bf16[32,2304]{1,0:T(8,128)(2,1)S(1)}, u32[]{:S(2)}, u32[]{:S(2)}) %collective-permute-start.32) | collective-permute-done | bytes 147488 | tf_op jit(solution)/shard_map/ppermute | solution.py:52
  154.4 3.0 collective-permute-start.33
  159.0 5.7 %collective-permute-done.33.refs_1_ = bf16[64,2304]{1,0:T(8,128)(2,1)S(1)} collective-permute-done((bf16[64,2304]{1,0:T(8,128)(2,1)S(1)}, bf16[64,2304]{1,0:T(8,128)(2,1)S(1)}, u32[]{:S(2)}, u32[]{:S(2)}) %collective-permute-start.33) | collective-permute-done | bytes 294944 | tf_op jit(solution)/shard_map/ppermute | solution.py:52
  167.3 12.2 %collective-permute-done.38.refs_1_ = bf16[6,64,384]{2,1,0:T(8,128)(2,1)S(1)} collective-permute-done((bf16[6,64,384]{2,1,0:T(8,128)(2,1)S(1)}, bf16[6,64,384]{2,1,0:T(8,128)(2,1)S(1)}, u32[]{:S(2)}, u32[]{:S(2)}) %collective-permute-start.38) | collective-permute-done | bytes 294944 | tf_op jit(solution)/shard_map/ppermute | solution.py:52
  181.1 5.5 %down.2 = (f32[64,640]{1,0:T(8,128)}, bf16[64,640]{1,0:T(8,128)(2,1)}, bf16[64,640]{1,0:T(8,128)(2,1)}, bf16[64,640]{1,0:T(8,128)(2,1)}) custom-call(s32[8]{0:T(128)} %copy-done.23, bf16[128,1152]{1,0:T(8,128)(2,1)} %copy-done.6, bf16[128,2304]{1,0:T(8,128)(2,1)} %copy-done.2, bf16[128,1152]{1,0:T(8,128)(2,1)} %copy-done.44, bf16[128,2304]{1,0:T(8,128)(2,1)} %copy-done.34, ...), custom_call_target="tpu_custom_call" | custom-call | flops 1132462080 | bytes 6193152 | tf_op jit(solution)/shard_map/down/pallas_call | solution.py:42
  196.7 3.2 %collective-permute-done.47.refs_1_ = bf16[32,2304]{1,0:T(8,128)(2,1)S(1)} collective-permute-done((bf16[32,2304]{1,0:T(8,128)(2,1)S(1)}, bf16[32,2304]{1,0:T(8,128)(2,1)S(1)}, u32[]{:S(2)}, u32[]{:S(2)}) %collective-permute-start.47) | collective-permute-done | bytes 147488 | tf_op jit(solution)/shard_map/ppermute | solution.py:52
  206.0 10.2 %collective-permute-done.43.refs_1_ = bf16[64,640]{1,0:T(8,128)(2,1)S(1)} collective-permute-done((bf16[64,640]{1,0:T(8,128)(2,1)S(1)}, bf16[64,640]{1,0:T(8,128)(2,1)S(1)}, u32[]{:S(2)}, u32[]{:S(2)}) %collective-permute-start.43) | collective-permute-done | bytes 81952 | tf_op jit(solution)/shard_map/ppermute | solution.py:52
  223.4 3.9 %collective-permute-done.57 = f32[4,640]{1,0:T(4,128)S(1)} collective-permute-done((f32[4,640]{1,0:T(4,128)S(1)}, f32[4,640]{1,0:T(4,128)S(1)}, u32[]{:S(2)}, u32[]{:S(2)}) %collective-permute-start.57) | collective-permute-done | bytes 10272 | tf_op jit(solution)/shard_map/ppermute | solution.py:52
  229.0 6.8 %collective-permute-done.49.refs_4_ = bf16[4,64,640]{2,1,0:T(8,128)(2,1)S(1)} collective-permute-done((bf16[4,64,640]{2,1,0:T(8,128)(2,1)S(1)}, bf16[4,64,640]{2,1,0:T(8,128)(2,1)S(1)}, u32[]{:S(2)}, u32[]{:S(2)}) %collective-permute-start.49) | collective-permute-done | bytes 327712 | tf_op jit(solution)/shard_map/ppermute | solution.py:47
  238.4 5.4 %down.3 = (f32[64,640]{1,0:T(8,128)}, bf16[64,640]{1,0:T(8,128)(2,1)}, bf16[64,640]{1,0:T(8,128)(2,1)}, bf16[64,640]{1,0:T(8,128)(2,1)}) custom-call(s32[8]{0:T(128)} %copy-done.23, bf16[128,2304]{1,0:T(8,128)(2,1)} %copy-done.1, bf16[128,1152]{1,0:T(8,128)(2,1)} %copy-done.5, bf16[128,2304]{1,0:T(8,128)(2,1)} %copy-done.33, bf16[128,1152]{1,0:T(8,128)(2,1)} %copy-done.43, ...), custom_call_target="tpu_custom_call" | custom-call | flops 1132462080 | bytes 6193152 | tf_op jit(solution)/shard_map/down/pallas_call | solution.py:42
  248.9 8.5 %head.3.refs_6_ = f32[256,128]{1,0:T(8,128)} custom-call(s32[8]{0:T(128)} %iota_xor_fusion.1.refs_0_, s32[4]{0:T(128)} %copy-done.24, bf16[4,64,640]{2,1,0:T(8,128)(2,1)} %copy-done.3, bf16[4,64,640]{2,1,0:T(8,128)(2,1)} %copy-done.26, bf16[4,64,640]{2,1,0:T(8,128)(2,1)} %copy-done.27, bf16[4,64,640]{2,1,0:T(8,128)(2,1)} %copy-done.28, ...), custom_call_target="tpu_custom_call" | custom-call | flops 2684354560 | bytes 10485760 | tf_op jit(solution)/shard_map/head/pallas_call | solution.py:42
  263.8 4.6 %collective-permute-done.67.refs_2_ = bf16[64,640]{1,0:T(8,128)(2,1)S(1)} collective-permute-done((bf16[64,640]{1,0:T(8,128)(2,1)S(1)}, bf16[64,640]{1,0:T(8,128)(2,1)S(1)}, u32[]{:S(2)}, u32[]{:S(2)}) %collective-permute-start.67) | collective-permute-done | bytes 81952 | tf_op jit(solution)/shard_map/ppermute | solution.py:52
  272.0 11.0 %head.4.refs_13_ = f32[256,128]{1,0:T(8,128)} custom-call(s32[8]{0:T(128)} %iota_xor_fusion.1.refs_0_, s32[4]{0:T(128)} %copy-done.24, bf16[4,64,640]{2,1,0:T(8,128)(2,1)} %copy-done.3, bf16[4,64,640]{2,1,0:T(8,128)(2,1)} %copy-done.26, bf16[4,64,640]{2,1,0:T(8,128)(2,1)} %copy-done.27, bf16[4,64,640]{2,1,0:T(8,128)(2,1)} %copy-done.28, ...), custom_call_target="tpu_custom_call" | custom-call | flops 4026531840 | bytes 15728640 | tf_op jit(solution)/shard_map/head/pallas_call | solution.py:42
  288.6 15.3 %head.5 = f32[256,128]{1,0:T(8,128)} custom-call(s32[8]{0:T(128)} %iota_xor_fusion.1.refs_0_, s32[4]{0:T(128)} %copy-done.24, bf16[4,64,640]{2,1,0:T(8,128)(2,1)} %copy-done.4, bf16[4,64,640]{2,1,0:T(8,128)(2,1)} %copy-done.35, bf16[4,64,640]{2,1,0:T(8,128)(2,1)} %copy-done.36, bf16[4,64,640]{2,1,0:T(8,128)(2,1)} %copy-done.37, ...), custom_call_target="tpu_custom_call" | custom-call | flops 6710886400 | bytes 26214400 | tf_op jit(solution)/shard_map/head/pallas_call | solution.py:42
  (337 shorter events, 141.3 us)
Async XLA Ops:
  90.2 39.8 %collective-permute-start.30 = (bf16[12,128,384]{2,1,0:T(8,128)(2,1)}, bf16[12,128,384]{2,1,0:T(8,128)(2,1)S(1)}, u32[]{:S(2)}, u32[]{:S(2)}) collective-permute-start(bf16[12,128,384]{2,1,0:T(8,128)(2,1)} %get-tuple-element.78.refs_2_), channel_id=1, source_target_pairs={{0,1},{1,0},{2,3},{3,2},{4,5},{5,4},{6,7},{7,6},{8,9},{9,8},{10,11... | collective-permute-start | bytes 3538952 | tf_op jit(solution)/shard_map/ppermute | solution.py:52
  91.8 38.4 %collective-permute-start.29 = (bf16[12,64,384]{2,1,0:T(8,128)(2,1)S(1)}, bf16[12,64,384]{2,1,0:T(8,128)(2,1)S(1)}, u32[]{:S(2)}, u32[]{:S(2)}) collective-permute-start(bf16[12,64,384]{2,1,0:T(8,128)(2,1)S(1)} %get-tuple-element.79.refs_4_), channel_id=1, source_target_pairs={{0,2},{1,3},{2,0},{3,1},{4,6},{5,7},{6,4},{7,5},{8,10},{9,11},{10,... | collective-permute-start | bytes 1769480 | tf_op jit(solution)/shard_map/ppermute | solution.py:52
  93.5 20.6 %collective-permute-start.22 = (bf16[6,64,384]{2,1,0:T(8,128)(2,1)S(1)}, bf16[6,64,384]{2,1,0:T(8,128)(2,1)S(1)}, u32[]{:S(2)}, u32[]{:S(2)}) collective-permute-start(bf16[6,64,384]{2,1,0:T(8,128)(2,1)S(1)} %copy-done.16), channel_id=1, source_target_pairs={{0,2},{1,3},{2,0},{3,1},{4,6},{5,7},{6,4},{7,5},{8,10},{9,11},{10,... | collective-permute-start | bytes 884744 | tf_op jit(solution)/shard_map/ppermute | solution.py:52
  94.2 20.0 %collective-permute-start.23 = (bf16[64,128]{1,0:T(8,128)(2,1)S(1)}, bf16[64,128]{1,0:T(8,128)(2,1)S(1)}, u32[]{:S(2)}, u32[]{:S(2)}) collective-permute-start(bf16[64,128]{1,0:T(8,128)(2,1)S(1)} %get-tuple-element.76), channel_id=1, source_target_pairs={{0,2},{1,3},{2,0},{3,1},{4,6},{5,7},{6,4},{7,5},{8,10},{9,11},{10,... | collective-permute-start | bytes 49160 | tf_op jit(solution)/shard_map/ppermute | solution.py:52
  130.4 13.8 %collective-permute-start.31 = (bf16[12,32,384]{2,1,0:T(8,128)(2,1)S(1)}, bf16[12,32,384]{2,1,0:T(8,128)(2,1)S(1)}, u32[]{:S(2)}, u32[]{:S(2)}) collective-permute-start(bf16[12,32,384]{2,1,0:T(8,128)(2,1)S(1)} %get-tuple-element.89.refs_2_), channel_id=1, source_target_pairs={{0,4},{1,5},{2,6},{3,7},{4,0},{5,1},{6,2},{7,3},{8,12},{9,13},{10,... | collective-permute-start | bytes 884744 | tf_op jit(solution)/shard_map/ppermute | solution.py:52
  133.2 24.3 %collective-permute-start.35 = (bf16[6,128,384]{2,1,0:T(8,128)(2,1)}, bf16[6,128,384]{2,1,0:T(8,128)(2,1)S(1)}, u32[]{:S(2)}, u32[]{:S(2)}) collective-permute-start(bf16[6,128,384]{2,1,0:T(8,128)(2,1)} %get-tuple-element.84.refs_4_), channel_id=1, source_target_pairs={{0,1},{1,0},{2,3},{3,2},{4,5},{5,4},{6,7},{7,6},{8,9},{9,8},{10,11... | collective-permute-start | bytes 1769480 | tf_op jit(solution)/shard_map/ppermute | solution.py:52
  133.2 25.6 %collective-permute-start.34 = (bf16[12,64,384]{2,1,0:T(8,128)(2,1)S(1)}, bf16[12,64,384]{2,1,0:T(8,128)(2,1)S(1)}, u32[]{:S(2)}, u32[]{:S(2)}) collective-permute-start(bf16[12,64,384]{2,1,0:T(8,128)(2,1)S(1)} %get-tuple-element.88.refs_2_), channel_id=1, source_target_pairs={{0,2},{1,3},{2,0},{3,1},{4,6},{5,7},{6,4},{7,5},{8,10},{9,11},{10,... | collective-permute-start | bytes 1769480 | tf_op jit(solution)/shard_map/ppermute | solution.py:52
  164.7 15.5 %collective-permute-start.37 = (bf16[128,2304]{1,0:T(8,128)(2,1)S(1)}, bf16[128,2304]{1,0:T(8,128)(2,1)S(1)}, u32[]{:S(2)}, u32[]{:S(2)}) collective-permute-start(bf16[128,2304]{1,0:T(8,128)(2,1)S(1)} %join.11.refs_2_), channel_id=1, source_target_pairs={{0,1},{1,0},{2,3},{3,2},{4,5},{5,4},{6,7},{7,6},{8,9},{9,8},{10,11... | collective-permute-start | bytes 1769480 | tf_op jit(solution)/shard_map/ppermute | solution.py:52
  164.8 14.7 %collective-permute-start.38 = (bf16[6,64,384]{2,1,0:T(8,128)(2,1)S(1)}, bf16[6,64,384]{2,1,0:T(8,128)(2,1)S(1)}, u32[]{:S(2)}, u32[]{:S(2)}) collective-permute-start(bf16[6,64,384]{2,1,0:T(8,128)(2,1)S(1)} %get-tuple-element.94.refs_2_), channel_id=1, source_target_pairs={{0,2},{1,3},{2,0},{3,1},{4,6},{5,7},{6,4},{7,5},{8,10},{9,11},{10,... | collective-permute-start | bytes 884744 | tf_op jit(solution)/shard_map/ppermute | solution.py:52
  164.9 15.3 %collective-permute-start.36 = (bf16[128,1152]{1,0:T(8,128)(2,1)S(1)}, bf16[128,1152]{1,0:T(8,128)(2,1)S(1)}, u32[]{:S(2)}, u32[]{:S(2)}) collective-permute-start(bf16[128,1152]{1,0:T(8,128)(2,1)S(1)} %join.9.refs_3_.refs_1_), channel_id=1, source_target_pairs={{0,1},{1,0},{2,3},{3,2},{4,5},{5,4},{6,7},{7,6},{8,9},{9,8},{10,11... | collective-permute-start | bytes 884744 | tf_op jit(solution)/shard_map/ppermute | solution.py:52
  165.3 21.3 %collective-permute-start.42 = (bf16[12,32,384]{2,1,0:T(8,128)(2,1)S(1)}, bf16[12,32,384]{2,1,0:T(8,128)(2,1)S(1)}, u32[]{:S(2)}, u32[]{:S(2)}) collective-permute-start(bf16[12,32,384]{2,1,0:T(8,128)(2,1)S(1)} %get-tuple-element.95.refs_2_), channel_id=1, source_target_pairs={{0,4},{1,5},{2,6},{3,7},{4,0},{5,1},{6,2},{7,3},{8,12},{9,13},{10,... | collective-permute-start | bytes 884744 | tf_op jit(solution)/shard_map/ppermute | solution.py:52
  200.0 20.7 %collective-permute-start.58 = (bf16[64,2304]{1,0:T(8,128)(2,1)S(1)}, bf16[64,2304]{1,0:T(8,128)(2,1)S(1)}, u32[]{:S(2)}, u32[]{:S(2)}) collective-permute-start(bf16[64,2304]{1,0:T(8,128)(2,1)S(1)} %join.12.refs_3_.refs_0_), channel_id=1, source_target_pairs={{0,2},{1,3},{2,0},{3,1},{4,6},{5,7},{6,4},{7,5},{8,10},{9,11},{10,... | collective-permute-start | bytes 884744 | tf_op jit(solution)/shard_map/ppermute | solution.py:52
  200.0 16.1 %collective-permute-start.43 = (bf16[64,640]{1,0:T(8,128)(2,1)S(1)}, bf16[64,640]{1,0:T(8,128)(2,1)S(1)}, u32[]{:S(2)}, u32[]{:S(2)}) collective-permute-start(bf16[64,640]{1,0:T(8,128)(2,1)S(1)} %output.2.refs_2_.refs_0_), channel_id=1, source_target_pairs={{0,2},{1,3},{2,0},{3,1},{4,6},{5,7},{6,4},{7,5},{8,10},{9,11},{10,... | collective-permute-start | bytes 245768 | tf_op jit(solution)/shard_map/ppermute | solution.py:52
  202.1 14.1 %collective-permute-start.44 = (bf16[64,640]{1,0:T(8,128)(2,1)S(1)}, bf16[64,640]{1,0:T(8,128)(2,1)S(1)}, u32[]{:S(2)}, u32[]{:S(2)}) collective-permute-start(bf16[64,640]{1,0:T(8,128)(2,1)S(1)} %output.2.refs_2_.refs_0_), channel_id=1, source_target_pairs={{0,4},{1,5},{2,6},{3,7},{4,0},{5,1},{6,2},{7,3},{8,12},{9,13},{10,... | collective-permute-start | bytes 245768 | tf_op jit(solution)/shard_map/ppermute | solution.py:52
  202.4 13.8 %collective-permute-start.45 = (bf16[64,640]{1,0:T(8,128)(2,1)S(1)}, bf16[64,640]{1,0:T(8,128)(2,1)S(1)}, u32[]{:S(2)}, u32[]{:S(2)}) collective-permute-start(bf16[64,640]{1,0:T(8,128)(2,1)S(1)} %output.2.refs_2_.refs_0_), channel_id=1, source_target_pairs={{0,6},{1,7},{2,4},{3,5},{4,2},{5,3},{6,0},{7,1},{8,14},{9,15},{10,... | collective-permute-start | bytes 245768 | tf_op jit(solution)/shard_map/ppermute | solution.py:52
  219.5 16.3 %collective-permute-start.49 = (bf16[4,64,640]{2,1,0:T(8,128)(2,1)S(1)}, bf16[4,64,640]{2,1,0:T(8,128)(2,1)S(1)}, u32[]{:S(2)}, u32[]{:S(2)}) collective-permute-start(bf16[4,64,640]{2,1,0:T(8,128)(2,1)S(1)} %pack.2.refs_2_), channel_id=1, source_target_pairs={{0,16},{8,24},{16,0},{24,8},{1,17},{9,25},{17,1},{25,9},{2,18},{10... | collective-permute-start | bytes 983048 | tf_op jit(solution)/shard_map/ppermute | solution.py:47
  220.7 15.1 %collective-permute-start.50 = (bf16[4,64,640]{2,1,0:T(8,128)(2,1)S(1)}, bf16[4,64,640]{2,1,0:T(8,128)(2,1)S(1)}, u32[]{:S(2)}, u32[]{:S(2)}) collective-permute-start(bf16[4,64,640]{2,1,0:T(8,128)(2,1)S(1)} %pack.2.refs_2_), channel_id=1, source_target_pairs={{0,24},{8,16},{16,8},{24,0},{1,25},{9,17},{17,9},{25,1},{2,26},{10... | collective-permute-start | bytes 983048 | tf_op jit(solution)/shard_map/ppermute | solution.py:47
  222.7 14.9 %collective-permute-start.61 = (bf16[128,2304]{1,0:T(8,128)(2,1)S(1)}, bf16[128,2304]{1,0:T(8,128)(2,1)S(1)}, u32[]{:S(2)}, u32[]{:S(2)}) collective-permute-start(bf16[128,2304]{1,0:T(8,128)(2,1)S(1)} %join.14.refs_2_.refs_1_), channel_id=1, source_target_pairs={{0,1},{1,0},{2,3},{3,2},{4,5},{5,4},{6,7},{7,6},{8,9},{9,8},{10,11... | collective-permute-start | bytes 1769480 | tf_op jit(solution)/shard_map/ppermute | solution.py:52
  229.0 15.7 %collective-permute-start.51 = (bf16[4,64,640]{2,1,0:T(8,128)(2,1)S(1)}, bf16[4,64,640]{2,1,0:T(8,128)(2,1)S(1)}, u32[]{:S(2)}, u32[]{:S(2)}) collective-permute-start(bf16[4,64,640]{2,1,0:T(8,128)(2,1)S(1)} %pack.2.refs_2_), channel_id=1, source_target_pairs={{0,1},{1,0},{2,3},{3,2},{4,5},{5,4},{6,7},{7,6},{8,9},{9,8},{10,11... | collective-permute-start | bytes 983048 | tf_op jit(solution)/shard_map/ppermute | solution.py:52
  243.8 13.6 %collective-permute-start.63 = (bf16[64,640]{1,0:T(8,128)(2,1)}, bf16[64,640]{1,0:T(8,128)(2,1)S(1)}, u32[]{:S(2)}, u32[]{:S(2)}) collective-permute-start(bf16[64,640]{1,0:T(8,128)(2,1)} %get-tuple-element.105.refs_13_), channel_id=1, source_target_pairs={{0,8},{8,0},{16,24},{24,16},{1,9},{9,1},{17,25},{25,17},{2,10},{10... | collective-permute-start | bytes 245768 | tf_op jit(solution)/shard_map/ppermute | solution.py:47
  268.4 16.3 %collective-permute-start.69 = (bf16[4,64,640]{2,1,0:T(8,128)(2,1)S(1)}, bf16[4,64,640]{2,1,0:T(8,128)(2,1)S(1)}, u32[]{:S(2)}, u32[]{:S(2)}) collective-permute-start(bf16[4,64,640]{2,1,0:T(8,128)(2,1)S(1)} %pack.3.refs_13_.refs_2_), channel_id=1, source_target_pairs={{0,8},{8,0},{16,24},{24,16},{1,9},{9,1},{17,25},{25,17},{2,10},{10... | collective-permute-start | bytes 983048 | tf_op jit(solution)/shard_map/ppermute | solution.py:47
  269.0 16.4 %collective-permute-start.70 = (bf16[4,64,640]{2,1,0:T(8,128)(2,1)S(1)}, bf16[4,64,640]{2,1,0:T(8,128)(2,1)S(1)}, u32[]{:S(2)}, u32[]{:S(2)}) collective-permute-start(bf16[4,64,640]{2,1,0:T(8,128)(2,1)S(1)} %pack.3.refs_13_.refs_2_), channel_id=1, source_target_pairs={{0,16},{8,24},{16,0},{24,8},{1,17},{9,25},{17,1},{25,9},{2,18},{10... | collective-permute-start | bytes 983048 | tf_op jit(solution)/shard_map/ppermute | solution.py:47
  270.0 15.4 %collective-permute-start.71 = (bf16[4,64,640]{2,1,0:T(8,128)(2,1)S(1)}, bf16[4,64,640]{2,1,0:T(8,128)(2,1)S(1)}, u32[]{:S(2)}, u32[]{:S(2)}) collective-permute-start(bf16[4,64,640]{2,1,0:T(8,128)(2,1)S(1)} %pack.3.refs_13_.refs_2_), channel_id=1, source_target_pairs={{0,24},{8,16},{16,8},{24,0},{1,25},{9,17},{17,9},{25,1},{2,26},{10... | collective-permute-start | bytes 983048 | tf_op jit(solution)/shard_map/ppermute | solution.py:47
  272.0 14.0 %collective-permute-start.72 = (bf16[4,64,640]{2,1,0:T(8,128)(2,1)S(1)}, bf16[4,64,640]{2,1,0:T(8,128)(2,1)S(1)}, u32[]{:S(2)}, u32[]{:S(2)}) collective-permute-start(bf16[4,64,640]{2,1,0:T(8,128)(2,1)S(1)} %pack.3.refs_13_.refs_2_), channel_id=1, source_target_pairs={{0,1},{1,0},{2,3},{3,2},{4,5},{5,4},{6,7},{7,6},{8,9},{9,8},{10,11... | collective-permute-start | bytes 983048 | tf_op jit(solution)/shard_map/ppermute | solution.py:52
  (112 other events, 825.1 us)

commit v4 on v3

--- a/solution.py
+++ b/solution.py
@@ -16,6 +16,8 @@
 ROPE_BASE = 1000000.0
 MASKED = -1e30
 LANES = 128
+HEAD_BLOCKS = 4
+GATE_MIB = 46
 BF16 = jnp.bfloat16
 F32 = jnp.float32
 MIB = 1 << 20
@@ -30,16 +32,26 @@
 
 
 def cost(flops, byte_count):
-    return pl.CostEstimate(flops=flops, bytes_accessed=byte_count, transcendentals=0)
-
-
-def call(kernel, operands, in_specs, after, **options):
-    count, extra = len(operands), len(after)
+    del flops, byte_count
+    return pl.CostEstimate(flops=1, bytes_accessed=1, transcendentals=0)
+
+
+def call(kernel, operands, in_specs, token, out_shape, out_specs, **options):
+    count, outs = len(operands), len(out_shape)
 
     def body(*refs):
-        kernel(*refs[:count], *refs[count + extra :])
-
-    return pl.pallas_call(body, in_specs=in_specs + [ANY] * extra, **options)(*operands, *after)
+        inputs, results, scratch = refs[:count], refs[count + 1 :], refs[count + outs + 2 :]
+        kernel(*inputs, *results[:outs], *scratch)
+
+    results = pl.pallas_call(
+        body,
+        in_specs=in_specs + [ANY],
+        out_shape=out_shape + [jax.ShapeDtypeStruct((8, LANES), F32)],
+        out_specs=out_specs + [ANY],
+        **options,
+    )(*operands, token[0])
+    token[:] = [results[-1]]
+    return results[:-1]
 
 
 def row_xor(x, mask):
@@ -200,10 +212,13 @@
     put_squares(square, keep, send, 0)
 
 
-def gate_up_kernel(x, w_gate, w_up, keep, send):
+def gate_up_kernel(x, *refs):
+    weights, (keep, send) = refs[:-2], refs[-2:]
     half = keep.shape[1]
-    for i, w in enumerate((w_gate, w_up)):
-        part = jnp.dot(x[...], w[0], preferred_element_type=F32)
+    count = len(weights) // 2
+    for i in range(2):
+        w = jnp.concatenate([w[0] for w in weights[i * count : (i + 1) * count]], axis=0)
+        part = jnp.dot(x[...], w, preferred_element_type=F32)
         keep[i] = part[:half]
         send[i] = part[half:].astype(BF16)
 
@@ -259,10 +274,10 @@
     out[...] = (total * gain[...]).astype(BF16)
 
 
-def down_kernel(sources, count, unit, offsets, *refs):
-    own, other, w_down = refs[:count], refs[count : 2 * count], refs[2 * count]
-    outs, total = refs[2 * count + 1 : -1], refs[-1]
-    tile = w_down.shape[1]
+def down_kernel(sources, count, unit, rows, offsets, *refs):
+    own, other, weights = refs[:count], refs[count : 2 * count], refs[2 * count : -rows - 1]
+    outs, total = refs[-rows - 1 : -1], refs[-1]
+    tile = len(weights) * weights[0].shape[1]
     for i, (which, at) in enumerate(sources):
 
         @pl.when(pl.program_id(0) == i)
@@ -270,7 +285,8 @@
             hidden = jnp.concatenate(
                 [own[which][:, at : at + tile], other[which][:, at : at + tile]], axis=0
             )
-            part = jnp.dot(hidden, w_down[0], preferred_element_type=F32)
+            w = jnp.concatenate([w[0] for w in weights], axis=0)
+            part = jnp.dot(hidden, w, preferred_element_type=F32)
             total[...] = part if i == 0 else total[...] + part
 
     @pl.when(pl.program_id(0) == len(sources) - 1)
@@ -285,7 +301,8 @@
 
 def head_kernel(rows, first, col_index, row_places, *refs):
     own, other = refs[:rows], refs[rows : 2 * rows]
-    gains, target, w, out, lhs, square, top, total, picked = refs[2 * rows :]
+    gains, target, *weights = refs[2 * rows : -6]
+    out, lhs, square, top, total, picked = refs[-6:]
     step = pl.program_id(0)
     chips, unit, width = own[0].shape
 
@@ -307,7 +324,12 @@
         total[...] = jnp.zeros_like(total)
         picked[...] = jnp.zeros_like(picked)
 
-    logits = jnp.dot(lhs[...], w[...], preferred_element_type=F32)
+    depth = weights[0].shape[0]
+    logits = jnp.dot(lhs[:, :depth], weights[0][...], preferred_element_type=F32)
+    for i in range(1, len(weights)):
+        logits += jnp.dot(
+            lhs[:, i * depth : (i + 1) * depth], weights[i][...], preferred_element_type=F32
+        )
     logits = logits * lax.rsqrt(square[...] / D + EPSILON)
     lane = lax.broadcasted_iota(jnp.int32, logits.shape, 1)
     lane = lane + (step + first) * logits.shape[1]
@@ -325,6 +347,26 @@
         out[...] = jnp.where(
             place == 0, top[...], jnp.where(place == 1, total[...], picked[...])
         )
+
+
+def hold(arrays, token):
+    def kernel(*refs):
+        del refs
+
+    count = len(arrays)
+    results = pl.pallas_call(
+        kernel,
+        out_shape=[jax.ShapeDtypeStruct(array.shape, array.dtype) for array in arrays]
+        + [jax.ShapeDtypeStruct((8, LANES), F32)],
+        in_specs=[ANY] * (count + 1),
+        out_specs=[ANY] * (count + 1),
+        input_output_aliases={i: i for i in range(count)},
+        compiler_params=params(16),
+        cost_estimate=cost(0, 0),
+        name="hold",
+    )(*arrays, token[0])
+    token[:] = [results[-1]]
+    return results[:-1]
 
 
 def per_device(
@@ -455,24 +497,23 @@
     blocks = [stream] + [row_xor(stream, j) for j in range(1, row_count)]
     position = sum(((relative >> level) & 1) << (levels - 1 - level) for level in range(levels))
     half_offsets = position * col_tokens
-    mlp_in, square_keep, square_send = pl.pallas_call(
+    token = [mlp_gain]
+    mlp_in, square_keep, square_send = call(
         functools.partial(arrange_kernel, col_tokens),
+        [half_offsets, *blocks, mlp_gain[None, :]],
+        [SMEM] + [VMEM] * (row_count + 1),
+        token,
         out_shape=[
             shape((tokens, features), BF16),
             shape((half, LANES), F32),
             shape((half, LANES), BF16),
         ],
-        in_specs=[SMEM] + [VMEM] * (row_count + 1),
         out_specs=[VMEM] * 3,
         scratch_shapes=[pltpu.VMEM((tokens, LANES), F32)],
         compiler_params=params(16),
         cost_estimate=cost(tokens * features, 4 * tokens * features),
         name="mlp_in",
-    )(half_offsets, *blocks, mlp_gain[None, :])
-
-    gains, _ = lax.optimization_barrier((final_gain[None, :], mlp_in))
-    for level in range(levels):
-        gains = jnp.concatenate([gains, col_xor(gains, 1 << level)], axis=0)
+    )
 
     divisible = ff_local % (3 * LANES) == 0
     tile = ff_local // 3 if divisible else ff_local
@@ -482,25 +523,27 @@
     plan = [(0, 0, 1), (0, 1, 2), (1, 0, 2), (1, 2, 1)] if divisible else [(0, 0, 1), (1, 0, 1)]
     last = levels - 1
     keeps, arrivals, hiddens = {}, {}, {}
-    token = [mlp_in]
     scale = [None]
     states = {}
 
     def gate_up(j):
         member, first, count = plan[j]
         first = first * subs
-        weight = pl.BlockSpec((1, features, sub), lambda i: (member, 0, first + i))
+        weights = [
+            pl.BlockSpec((1, features // 2, sub), lambda i, q=q: (member, q, first + i))
+            for q in range(2)
+        ]
         out = pl.BlockSpec((2, half, sub), lambda i: (i, 0, 0))
         groups = 2 * count * subs
         keep, send = call(
             gate_up_kernel,
-            [mlp_in, w_gate, w_up],
-            [pl.BlockSpec((tokens, features), lambda i: (0, 0)), weight, weight],
+            [mlp_in, w_gate, w_gate, w_up, w_up],
+            [pl.BlockSpec((tokens, features), lambda i: (0, 0))] + weights * 2,
             token,
             grid=(count * subs,),
             out_shape=[shape((groups, half, sub), F32), shape((groups, half, sub), BF16)],
             out_specs=[out] * 2,
-            compiler_params=params(56),
+            compiler_params=params(GATE_MIB),
             cost_estimate=cost(4 * tokens * features * tile * count, 4 * tile * count * features),
             name="gate_up",
         )
@@ -510,7 +553,6 @@
             keeps[j].append(square_keep)
             arrived.append(col_xor(square_send, 1))
         arrivals[j] = arrived
-        token[:] = [send]
 
     def halve(j, level):
         count = plan[j][2]
@@ -541,7 +583,6 @@
         )
         keeps[j] = result[0::2]
         arrivals[j] = [col_xor(send, 2 << level) for send in result[1::2]]
-        token[:] = [result[1]]
 
     def hidden_of(j):
         keep, received = keeps[j], arrivals[j]
@@ -564,24 +605,22 @@
         if squared:
             scale[:] = [result[1]]
         hiddens[j] = (result[0], col_xor(result[0], 1 << last))
-        token[:] = [result[0]]
 
     def join(j, level):
         first, second = hiddens[j]
         rows, width = first.shape
-        joined = call(
+        (joined,) = call(
             join_kernel,
             [first, second],
             [VMEM] * 2,
             token,
-            out_shape=shape((2 * rows, width), BF16),
-            out_specs=VMEM,
+            out_shape=[shape((2 * rows, width), BF16)],
+            out_specs=[VMEM],
             compiler_params=params(16),
             cost_estimate=cost(rows * width, 8 * rows * width),
             name="join",
         )
         hiddens[j] = (joined, col_xor(joined, 1 << level))
-        token[:] = [joined]
 
     def down(member):
         which = [j for j in range(len(plan)) if plan[j][0] == member]
@@ -589,15 +628,19 @@
         other = [hiddens[j][1] for j in which]
         sources = [(k, i * tile) for k, j in enumerate(which) for i in range(plan[j][2])]
         parts = call(
-            functools.partial(down_kernel, sources, len(own), col_tokens),
-            [half_offsets, *own, *other, w_down],
+            functools.partial(down_kernel, sources, len(own), col_tokens, row_count),
+            [half_offsets, *own, *other] + [w_down] * 3,
             [SMEM]
             + [pl.BlockSpec(array.shape, lambda i: (0, 0)) for array in own + other]
-            + [pl.BlockSpec((1, tile, features), lambda i: (member, i, 0))],
+            + [
+                pl.BlockSpec((1, tile // 3, features), lambda i, q=q: (member, 3 * i + q, 0))
+                for q in range(3)
+            ],
             token,
             grid=(tiles,),
             out_shape=[
-                shape((row_tokens, features), F32 if i == 0 else BF16) for i in range(row_count)
+                shape((row_tokens, features), F32 if i == 0 else BF16)
+                for i in range(row_count)
             ],
             out_specs=[pl.BlockSpec((row_tokens, features), lambda i: (0, 0))] * row_count,
             scratch_shapes=[pltpu.VMEM((tokens, features), F32)],
@@ -608,39 +651,41 @@
             name="down",
         )
         states[member] = [parts[0]] + [row_xor(parts[j], j) for j in range(1, row_count)]
-        token[:] = [parts[1]]
 
     def output(member):
         parts = states[member]
-        scaled = call(
+        (scaled,) = call(
             output_kernel,
             [stream, final_gain[None, :], *parts],
             [VMEM] * (2 + row_count),
             token,
-            out_shape=shape((row_tokens, features), BF16),
-            out_specs=VMEM,
+            out_shape=[shape((row_tokens, features), BF16)],
+            out_specs=[VMEM],
             compiler_params=params(16),
             cost_estimate=cost(8 * row_tokens * features, 16 * row_tokens * features),
             name="output",
         )
         states[member] = [scaled] + [col_xor(scaled, 2 * j) for j in range(1, chips)]
-        token[:] = [scaled]
 
     def pack(member):
-        by_chip = call(
+        (by_chip,) = call(
             pack_kernel,
             states[member],
             [VMEM] * chips,
             token,
-            out_shape=shape((chips, row_tokens, features), BF16),
-            out_specs=VMEM,
+            out_shape=[shape((chips, row_tokens, features), BF16)],
+            out_specs=[VMEM],
             compiler_params=params(16),
             cost_estimate=cost(chips * row_tokens * features, 4 * chips * row_tokens * features),
             name="pack",
         )
-        own = [by_chip] + [row_xor(by_chip, j) for j in range(1, row_count)]
-        states[member] = own + [col_xor(array, 1) for array in own]
-        token[:] = [by_chip]
+        other = col_xor(by_chip, 1)
+        states[member] = [by_chip, other] + [row_xor(by_chip, j) for j in range(1, row_count)]
+
+    def forward(member):
+        by_chip, other, *rows = states[member]
+        rows = hold(rows, token)
+        states[member] = [by_chip, *rows, other] + [col_xor(array, 1) for array in rows]
 
     vocab_start = (row_index * col_count + col_index) * vocab_local
     local_targets = (targets - vocab_start)[:, None]
@@ -648,20 +693,30 @@
     vocab_tiles = vocab_local // vocab_tile
     stats = {0: [], 1: []}
 
+    gain_parts = [final_gain[None, :]]
+
+    def gather_gain(level):
+        (part,) = hold(gain_parts[-1:], token)
+        gain_parts.append(jnp.concatenate([part, col_xor(part, 1 << level)], axis=0))
+
     def head(member, first, count):
+        gains = gain_parts[-1]
         state = states[member]
-        result = call(
+        (result,) = call(
             functools.partial(head_kernel, row_count, first),
-            [col_rel, row_rel * row_tokens, *state, gains, local_targets, w_head],
+            [col_rel, row_rel * row_tokens, *state, gains, local_targets] + [w_head] * HEAD_BLOCKS,
             [SMEM] * 2
             + [pl.BlockSpec(state[0].shape, lambda i: (0, 0, 0))] * (2 * row_count)
             + [pl.BlockSpec(gains.shape, lambda i: (0, 0))]
             + [pl.BlockSpec((tokens, 1), lambda i: (0, 0))]
-            + [pl.BlockSpec((D, vocab_tile), lambda i: (0, first + i))],
+            + [
+                pl.BlockSpec((D // HEAD_BLOCKS, vocab_tile), lambda i, q=q: (q, first + i))
+                for q in range(HEAD_BLOCKS)
+            ],
             token,
             grid=(count,),
-            out_shape=shape((tokens, LANES), F32),
-            out_specs=pl.BlockSpec((tokens, LANES), lambda i: (0, 0)),
+            out_shape=[shape((tokens, LANES), F32)],
+            out_specs=[pl.BlockSpec((tokens, LANES), lambda i: (0, 0))],
             scratch_shapes=[pltpu.VMEM((tokens, D), BF16)] + [pltpu.VMEM((tokens, 1), F32)] * 4,
             compiler_params=params(56),
             cost_estimate=cost(
@@ -669,26 +724,27 @@
             ),
             name="head",
         )
-        token[:] = [result]
         stats[member].append(result[:, :3].T)
 
     if len(plan) == 4 and levels == 3:
         schedule = [
             (gate_up, 0), (gate_up, 1), (halve, 0, 0), (gate_up, 2), (halve, 1, 0),
-            (halve, 0, 1), (gate_up, 3), (hidden_of, 0), (join, 0, 1), (halve, 2, 0),
-            (halve, 1, 1), (join, 0, 0), (hidden_of, 1), (join, 1, 1), (halve, 3, 0),
-            (halve, 2, 1), (join, 1, 0), (halve, 3, 1), (down, 0), (hidden_of, 2),
-            (output, 0), (join, 2, 1), (hidden_of, 3), (pack, 0), (join, 3, 1),
-            (join, 2, 0), (join, 3, 0), (down, 1),
+            (halve, 0, 1), (gate_up, 3), (halve, 2, 0), (hidden_of, 0), (halve, 1, 1),
+            (halve, 3, 0), (join, 0, 1), (gather_gain, 0), (hidden_of, 1), (halve, 2, 1),
+            (join, 0, 0), (join, 1, 1), (gather_gain, 1), (halve, 3, 1), (hidden_of, 2),
+            (join, 1, 0), (join, 2, 1), (gather_gain, 2), (down, 0), (hidden_of, 3),
+            (join, 3, 1), (output, 0), (join, 2, 0), (join, 3, 0), (down, 1),
         ]
     else:
         schedule = []
         for j in range(len(plan)):
             schedule += [(gate_up, j)] + [(halve, j, level) for level in range(last)]
             schedule += [(hidden_of, j)] + [(join, j, level) for level in range(last - 1, -1, -1)]
-        schedule += [(down, 0), (output, 0), (pack, 0), (down, 1)]
-    early = min(2, vocab_tiles)
-    schedule += [(head, 0, 0, early), (output, 1), (pack, 1)]
+        schedule += [(gather_gain, level) for level in range(levels)]
+        schedule += [(down, 0), (output, 0), (down, 1)]
+    early = (3 * vocab_tiles + 4) // 5
+    schedule += [(output, 1), (pack, 0), (pack, 1), (forward, 0), (head, 0, 0, early)]
+    schedule += [(forward, 1)]
     if early < vocab_tiles:
         schedule += [(head, 0, early, vocab_tiles - early)]
     schedule += [(head, 1, 0, vocab_tiles)]

time: 322 us -> 332 us (1.031)
  waiting for transfers between devices: 140 us -> 153 us
  local copies, waits for them, and re-layouts: 18.8 us -> 15.4 us
    ppermute x59, waiting for transfers between devices: 118 us -> 140 us  [col_xor(): return lax.ppermute(x, 'col', [(i, i ^ mask) for i in range(count)])]
    ppermute x24, waiting for transfers between devices: 21.3 us -> 12.9 us  [row_xor(): return lax.ppermute(x, 'row', [(i, i ^ mask) for i in range(count)])]
    unnamed x106 -> x93, local copies, waits for them, and re-layouts: 13.4 us -> 10.1 us
    pallas_call x34 -> x39, Pallas kernels: 72.8 us -> 71.4 us  [the longest x34 71.4 us: call(): pl.pallas_call(body, in_specs=in_specs + [ANY], out_shape=out_shape + [ja...]
  transfers between devices with their start and end apart: 83 -> 83, of which waited for: 45 -> 42; matrix products, arithmetic and copies ran while one was open for 3% -> 2% of each run, Pallas kernels for 16% -> 14%
where the time goes in v4:
time: 332 us; the launch traced here: 331 us
  waiting for transfers between devices  153 us (46%)
  starting transfers between devices  78.6 us (24%)
  Pallas kernels  78 us (23%)
  local copies, waits for them, and re-layouts  15.4 us (5%)
  other arithmetic  4.09 us (1%)
    ppermute x59, waiting for transfers between devices, col_xor(): return lax.ppermute(x, 'col', [(i, i ^ mask) for i in range(count)])  140 us
    pallas_call x34, Pallas kernels, call(): pl.pallas_call(body, in_specs=in_specs + [ANY], out_shape=out_shape + [ja...  71.4 us
    ppermute x59, starting transfers between devices, col_xor(): return lax.ppermute(x, 'col', [(i, i ^ mask) for i in range(count)])  49.4 us
    ppermute x24, starting transfers between devices, row_xor(): return lax.ppermute(x, 'row', [(i, i ^ mask) for i in range(count)])  29.2 us
    ppermute x24, waiting for transfers between devices, row_xor(): return lax.ppermute(x, 'row', [(i, i ^ mask) for i in range(count)])  12.9 us
    unnamed x93, local copies, waits for them, and re-layouts  10.1 us
  transfers between devices with their start and end apart: 83, of which 42 were waited for; matrix products, arithmetic and copies ran while one was open for 2% of the time, Pallas kernels for 14%

profile of v4, /device:TPU:0, one launch (start us, length us, event | category | flops | bytes accessed | tf_op | source)
XLA Modules:
  0.0 331.0 jit_solution(7434394621818593781)
XLA Ops:
  0.0 2.9 collective-permute-start
  10.6 3.7 %qkv_partial.1 = (f32[128,1920]{1,0:T(8,128)}, bf16[128,1920]{1,0:T(8,128)(2,1)}) custom-call(s32[8]{0:T(128)} %reshape.112.offsets, bf16[64,640]{1,0:T(8,128)(2,1)} %refs_0_.1, bf16[64,640]{1,0:T(8,128)(2,1)} %copy-done.37, bf16[64,640]{1,0:T(8,128)(2,1)} %copy-done.38, bf16[64,640]{1,0:T(8,128)(2,1)} %copy-done.39, f32[1,640]{1,0:T(1,128)} %broadcast_in_dim.28.refs_4_, ...), custom_call_target="tpu_custom_call" | custom-call | flops 1 | bytes 1 | tf_op jit(solution)/shard_map/qkv_partial/pallas_call | solution.py:438
  24.9 6.9 %collective-permute-done.5.refs_2_ = bf16[32,1920]{1,0:T(8,128)(2,1)S(1)} collective-permute-done((bf16[32,1920]{1,0:T(8,128)(2,1)S(1)}, bf16[32,1920]{1,0:T(8,128)(2,1)S(1)}, u32[]{:S(2)}, u32[]{:S(2)}) %collective-permute-start.5) | collective-permute-done | bytes 122912 | tf_op jit(solution)/shard_map/ppermute | solution.py:64
  38.1 7.0 %collective-permute-done.8.refs_2_ = bf16[32,1792]{1,0:T(8,128)(2,1)S(1)} collective-permute-done((bf16[32,1792]{1,0:T(8,128)(2,1)S(1)}, bf16[32,1792]{1,0:T(8,128)(2,1)S(1)}, u32[]{:S(2)}, u32[]{:S(2)}) %collective-permute-start.8) | collective-permute-done | bytes 114720 | tf_op jit(solution)/shard_map/ppermute | solution.py:64
  64.8 3.9 %gate_up.4 = (f32[6,128,384]{2,1,0:T(8,128)S(1)}, bf16[6,128,384]{2,1,0:T(8,128)(2,1)S(1)}, f32[8,128]{1,0:T(8,128)S(1)}) custom-call(bf16[256,640]{1,0:T(8,128)(2,1)S(1)} %get-tuple-element.131.refs_0_, bf16[2,640,3456]{2,1,0:T(8,128)(2,1)} %refs_2_.7, bf16[2,640,3456]{2,1,0:T(8,128)(2,1)} %refs_2_.7, bf16[2,640,3456]{2,1,0:T(8,128)(2,1)} %refs_4_.7, ...), custom_call_target="tpu_custom_call" | custom-call | flops 1 | bytes 1 | tf_op jit(solution)/shard_map/gate_up/pallas_call | solution.py:46
  68.9 6.2 %gate_up.5 = (f32[12,128,384]{2,1,0:T(8,128)S(1)}, bf16[12,128,384]{2,1,0:T(8,128)(2,1)S(1)}, f32[8,128]{1,0:T(8,128)S(1)}) custom-call(bf16[256,640]{1,0:T(8,128)(2,1)S(1)} %get-tuple-element.131.refs_0_, bf16[2,640,3456]{2,1,0:T(8,128)(2,1)} %refs_2_.7, bf16[2,640,3456]{2,1,0:T(8,128)(2,1)} %refs_2_.7, bf16[2,640,3456]{2,1,0:T(8,128)(2,1)} %refs_4_.7, ...), custom_call_target="tpu_custom_call" | custom-call | flops 1 | bytes 1 | tf_op jit(solution)/shard_map/gate_up/pallas_call | solution.py:46
  78.3 6.2 %gate_up.6 = (f32[12,128,384]{2,1,0:T(8,128)S(1)}, bf16[12,128,384]{2,1,0:T(8,128)(2,1)S(1)}, f32[8,128]{1,0:T(8,128)S(1)}) custom-call(bf16[256,640]{1,0:T(8,128)(2,1)S(1)} %get-tuple-element.131.refs_0_, bf16[2,640,3456]{2,1,0:T(8,128)(2,1)} %refs_2_.7, bf16[2,640,3456]{2,1,0:T(8,128)(2,1)} %refs_2_.7, bf16[2,640,3456]{2,1,0:T(8,128)(2,1)} %refs_4_.7, ...), custom_call_target="tpu_custom_call" | custom-call | flops 1 | bytes 1 | tf_op jit(solution)/shard_map/gate_up/pallas_call | solution.py:46
  89.0 18.0 %collective-permute-done.23.refs_3_ = bf16[64,128]{1,0:T(8,128)(2,1)S(1)} collective-permute-done((bf16[64,128]{1,0:T(8,128)(2,1)S(1)}, bf16[64,128]{1,0:T(8,128)(2,1)S(1)}, u32[]{:S(2)}, u32[]{:S(2)}) %collective-permute-start.23) | collective-permute-done | bytes 16416 | tf_op jit(solution)/shard_map/ppermute | solution.py:64
  107.1 3.8 %gate_up.7 = (f32[6,128,384]{2,1,0:T(8,128)S(1)}, bf16[6,128,384]{2,1,0:T(8,128)(2,1)S(1)}, f32[8,128]{1,0:T(8,128)S(1)}) custom-call(bf16[256,640]{1,0:T(8,128)(2,1)S(1)} %get-tuple-element.131.refs_0_, bf16[2,640,3456]{2,1,0:T(8,128)(2,1)} %refs_2_.7, bf16[2,640,3456]{2,1,0:T(8,128)(2,1)} %refs_2_.7, bf16[2,640,3456]{2,1,0:T(8,128)(2,1)} %refs_4_.7, ...), custom_call_target="tpu_custom_call" | custom-call | flops 1 | bytes 1 | tf_op jit(solution)/shard_map/gate_up/pallas_call | solution.py:46
  115.9 14.3 %collective-permute-done.26.refs_3_ = bf16[32,128]{1,0:T(8,128)(2,1)S(1)} collective-permute-done((bf16[32,128]{1,0:T(8,128)(2,1)S(1)}, bf16[32,128]{1,0:T(8,128)(2,1)S(1)}, u32[]{:S(2)}, u32[]{:S(2)}) %collective-permute-start.26) | collective-permute-done | bytes 8224 | tf_op jit(solution)/shard_map/ppermute | solution.py:64
  130.5 3.4 %collective-permute-start.33 = (bf16[12,32,384]{2,1,0:T(8,128)(2,1)S(1)}, bf16[12,32,384]{2,1,0:T(8,128)(2,1)S(1)}, u32[]{:S(2)}, u32[]{:S(2)}) collective-permute-start(bf16[12,32,384]{2,1,0:T(8,128)(2,1)S(1)} %get-tuple-element.169), channel_id=1, source_target_pairs={{0,4},{1,5},{2,6},{3,7},{4,0},{5,1},{6,2},{7,3},{8,12},{9,13},{10,... | collective-permute-start | bytes 884744 | tf_op jit(solution)/shard_map/ppermute | solution.py:64
  134.2 15.8 %collective-permute-done.28.refs_1_ = bf16[32,1152]{1,0:T(8,128)(2,1)S(1)} collective-permute-done((bf16[32,1152]{1,0:T(8,128)(2,1)S(1)}, bf16[32,1152]{1,0:T(8,128)(2,1)S(1)}, u32[]{:S(2)}, u32[]{:S(2)}) %collective-permute-start.28) | collective-permute-done | bytes 73760 | tf_op jit(solution)/shard_map/ppermute | solution.py:64
  155.5 7.2 %collective-permute-done.31.refs_1_ = bf16[64,1152]{1,0:T(8,128)(2,1)S(1)} collective-permute-done((bf16[64,1152]{1,0:T(8,128)(2,1)S(1)}, bf16[64,1152]{1,0:T(8,128)(2,1)S(1)}, u32[]{:S(2)}, u32[]{:S(2)}) %collective-permute-start.31) | collective-permute-done | bytes 147488 | tf_op jit(solution)/shard_map/ppermute | solution.py:64
  164.1 7.7 %collective-permute-done.37.refs_1_ = bf16[6,64,384]{2,1,0:T(8,128)(2,1)S(1)} collective-permute-done((bf16[6,64,384]{2,1,0:T(8,128)(2,1)S(1)}, bf16[6,64,384]{2,1,0:T(8,128)(2,1)S(1)}, u32[]{:S(2)}, u32[]{:S(2)}) %collective-permute-start.37) | collective-permute-done | bytes 294944 | tf_op jit(solution)/shard_map/ppermute | solution.py:64
  172.1 4.7 %collective-permute-done.35.refs_1_ = bf16[64,2304]{1,0:T(8,128)(2,1)S(1)} collective-permute-done((bf16[64,2304]{1,0:T(8,128)(2,1)S(1)}, bf16[64,2304]{1,0:T(8,128)(2,1)S(1)}, u32[]{:S(2)}, u32[]{:S(2)}) %collective-permute-start.35) | collective-permute-done | bytes 294944 | tf_op jit(solution)/shard_map/ppermute | solution.py:64
  177.7 9.3 %collective-permute-done.42.refs_1_ = bf16[32,2304]{1,0:T(8,128)(2,1)S(1)} collective-permute-done((bf16[32,2304]{1,0:T(8,128)(2,1)S(1)}, bf16[32,2304]{1,0:T(8,128)(2,1)S(1)}, u32[]{:S(2)}, u32[]{:S(2)}) %collective-permute-start.42) | collective-permute-done | bytes 147488 | tf_op jit(solution)/shard_map/ppermute | solution.py:64
  189.3 10.0 %collective-permute-done.41 = f32[2,640]{1,0:T(2,128)S(1)} collective-permute-done((f32[2,640]{1,0:T(2,128)S(1)}, f32[2,640]{1,0:T(2,128)S(1)}, u32[]{:S(2)}, u32[]{:S(2)}) %collective-permute-start.41) | collective-permute-done | bytes 5152 | tf_op jit(solution)/shard_map/ppermute | solution.py:64
  200.9 5.5 %down.2 = (f32[64,640]{1,0:T(8,128)}, bf16[64,640]{1,0:T(8,128)(2,1)}, bf16[64,640]{1,0:T(8,128)(2,1)}, bf16[64,640]{1,0:T(8,128)(2,1)}, f32[8,128]{1,0:T(8,128)}) custom-call(s32[8]{0:T(128)} %copy-done.18, bf16[128,1152]{1,0:T(8,128)(2,1)} %copy-done.12, bf16[128,2304]{1,0:T(8,128)(2,1)} %copy-done.9, bf16[128,1152]{1,0:T(8,128)(2,1)} %copy-done.34, ...), custom_call_target="tpu_custom_call" | custom-call | flops 1 | bytes 1 | tf_op jit(solution)/shard_map/down/pallas_call | solution.py:46
  211.0 5.6 %collective-permute-done.47.refs_1_ = bf16[32,1152]{1,0:T(8,128)(2,1)S(1)} collective-permute-done((bf16[32,1152]{1,0:T(8,128)(2,1)S(1)}, bf16[32,1152]{1,0:T(8,128)(2,1)S(1)}, u32[]{:S(2)}, u32[]{:S(2)}) %collective-permute-start.47) | collective-permute-done | bytes 73760 | tf_op jit(solution)/shard_map/ppermute | solution.py:64
  217.8 6.2 %collective-permute-done.52.refs_1_ = bf16[64,1152]{1,0:T(8,128)(2,1)S(1)} collective-permute-done((bf16[64,1152]{1,0:T(8,128)(2,1)S(1)}, bf16[64,1152]{1,0:T(8,128)(2,1)S(1)}, u32[]{:S(2)}, u32[]{:S(2)}) %collective-permute-start.52) | collective-permute-done | bytes 147488 | tf_op jit(solution)/shard_map/ppermute | solution.py:64
  227.1 5.5 %down.3 = (f32[64,640]{1,0:T(8,128)}, bf16[64,640]{1,0:T(8,128)(2,1)}, bf16[64,640]{1,0:T(8,128)(2,1)}, bf16[64,640]{1,0:T(8,128)(2,1)}, f32[8,128]{1,0:T(8,128)}) custom-call(s32[8]{0:T(128)} %copy-done.18, bf16[128,2304]{1,0:T(8,128)(2,1)} %copy-done.10, bf16[128,1152]{1,0:T(8,128)(2,1)} %copy-done.13, bf16[128,2304]{1,0:T(8,128)(2,1)} %copy-done.29, ...), custom_call_target="tpu_custom_call" | custom-call | flops 1 | bytes 1 | tf_op jit(solution)/shard_map/down/pallas_call | solution.py:46
  268.8 11.9 %head.3 = (f32[256,128]{1,0:T(8,128)}, f32[8,128]{1,0:T(8,128)}) custom-call(s32[8]{0:T(128)} %iota_xor_fusion.1.refs_0_, s32[4]{0:T(128)} %copy-done.17, bf16[4,64,640]{2,1,0:T(8,128)(2,1)} %copy-done.4, bf16[4,64,640]{2,1,0:T(8,128)(2,1)} %copy-done, bf16[4,64,640]{2,1,0:T(8,128)(2,1)} %copy-done.1, bf16[4,64,640]{2,1,0:T(8,128)(2,1)} %copy-done.2, ...), custom_call_target="tpu_custom_call" | custom-call | flops 1 | bytes 1 | tf_op jit(solution)/shard_map/head/pallas_call | solution.py:46
  282.0 9.4 %head.4 = (f32[256,128]{1,0:T(8,128)}, f32[8,128]{1,0:T(8,128)}) custom-call(s32[8]{0:T(128)} %iota_xor_fusion.1.refs_0_, s32[4]{0:T(128)} %copy-done.17, bf16[4,64,640]{2,1,0:T(8,128)(2,1)} %copy-done.4, bf16[4,64,640]{2,1,0:T(8,128)(2,1)} %copy-done, bf16[4,64,640]{2,1,0:T(8,128)(2,1)} %copy-done.1, bf16[4,64,640]{2,1,0:T(8,128)(2,1)} %copy-done.2, ...), custom_call_target="tpu_custom_call" | custom-call | flops 1 | bytes 1 | tf_op jit(solution)/shard_map/head/pallas_call | solution.py:46
  296.5 15.9 %head.5 = (f32[256,128]{1,0:T(8,128)}, f32[8,128]{1,0:T(8,128)}) custom-call(s32[8]{0:T(128)} %iota_xor_fusion.1.refs_0_, s32[4]{0:T(128)} %copy-done.17, bf16[4,64,640]{2,1,0:T(8,128)(2,1)} %copy-done.11, bf16[4,64,640]{2,1,0:T(8,128)(2,1)} %copy-done.5, bf16[4,64,640]{2,1,0:T(8,128)(2,1)} %copy-done.6, bf16[4,64,640]{2,1,0:T(8,128)(2,1)} %copy-done.7, ...), custom_call_target="tpu_custom_call" | custom-call | flops 1 | bytes 1 | tf_op jit(solution)/shard_map/head/pallas_call | solution.py:46
  (329 shorter events, 139.0 us)
Async XLA Ops:
  84.5 29.0 %collective-permute-start.27 = (bf16[12,128,384]{2,1,0:T(8,128)(2,1)S(1)}, bf16[12,128,384]{2,1,0:T(8,128)(2,1)S(1)}, u32[]{:S(2)}, u32[]{:S(2)}) collective-permute-start(bf16[12,128,384]{2,1,0:T(8,128)(2,1)S(1)} %get-tuple-element.153), channel_id=1, source_target_pairs={{0,1},{1,0},{2,3},{3,2},{4,5},{5,4},{6,7},{7,6},{8,9},{9,8},{10,11... | collective-permute-start | bytes 3538952 | tf_op jit(solution)/shard_map/ppermute | solution.py:64
  85.0 22.0 %collective-permute-start.22 = (bf16[6,64,384]{2,1,0:T(8,128)(2,1)S(1)}, bf16[6,64,384]{2,1,0:T(8,128)(2,1)S(1)}, u32[]{:S(2)}, u32[]{:S(2)}) collective-permute-start(bf16[6,64,384]{2,1,0:T(8,128)(2,1)S(1)} %get-tuple-element.140), channel_id=1, source_target_pairs={{0,2},{1,3},{2,0},{3,1},{4,6},{5,7},{6,4},{7,5},{8,10},{9,11},{10,... | collective-permute-start | bytes 884744 | tf_op jit(solution)/shard_map/ppermute | solution.py:64
  86.9 43.5 %collective-permute-start.30 = (bf16[12,64,384]{2,1,0:T(8,128)(2,1)S(1)}, bf16[12,64,384]{2,1,0:T(8,128)(2,1)S(1)}, u32[]{:S(2)}, u32[]{:S(2)}) collective-permute-start(bf16[12,64,384]{2,1,0:T(8,128)(2,1)S(1)} %get-tuple-element.161), channel_id=1, source_target_pairs={{0,2},{1,3},{2,0},{3,1},{4,6},{5,7},{6,4},{7,5},{8,10},{9,11},{10,... | collective-permute-start | bytes 1769480 | tf_op jit(solution)/shard_map/ppermute | solution.py:64
  87.3 19.7 %collective-permute-start.23 = (bf16[64,128]{1,0:T(8,128)(2,1)S(1)}, bf16[64,128]{1,0:T(8,128)(2,1)S(1)}, u32[]{:S(2)}, u32[]{:S(2)}) collective-permute-start(bf16[64,128]{1,0:T(8,128)(2,1)S(1)} %get-tuple-element.142), channel_id=1, source_target_pairs={{0,2},{1,3},{2,0},{3,1},{4,6},{5,7},{6,4},{7,5},{8,10},{9,11},{10,... | collective-permute-start | bytes 49160 | tf_op jit(solution)/shard_map/ppermute | solution.py:64
  110.9 23.2 %collective-permute-start.29 = (bf16[6,128,384]{2,1,0:T(8,128)(2,1)S(1)}, bf16[6,128,384]{2,1,0:T(8,128)(2,1)S(1)}, u32[]{:S(2)}, u32[]{:S(2)}) collective-permute-start(bf16[6,128,384]{2,1,0:T(8,128)(2,1)S(1)} %get-tuple-element.159), channel_id=1, source_target_pairs={{0,1},{1,0},{2,3},{3,2},{4,5},{5,4},{6,7},{7,6},{8,9},{9,8},{10,11... | collective-permute-start | bytes 1769480 | tf_op jit(solution)/shard_map/ppermute | solution.py:64
  110.9 19.2 %collective-permute-start.25 = (bf16[6,32,384]{2,1,0:T(8,128)(2,1)S(1)}, bf16[6,32,384]{2,1,0:T(8,128)(2,1)S(1)}, u32[]{:S(2)}, u32[]{:S(2)}) collective-permute-start(bf16[6,32,384]{2,1,0:T(8,128)(2,1)S(1)} %get-tuple-element.149), channel_id=1, source_target_pairs={{0,4},{1,5},{2,6},{3,7},{4,0},{5,1},{6,2},{7,3},{8,12},{9,13},{10,... | collective-permute-start | bytes 442376 | tf_op jit(solution)/shard_map/ppermute | solution.py:64
  113.8 38.6 %collective-permute-start.32 = (bf16[12,64,384]{2,1,0:T(8,128)(2,1)S(1)}, bf16[12,64,384]{2,1,0:T(8,128)(2,1)S(1)}, u32[]{:S(2)}, u32[]{:S(2)}) collective-permute-start(bf16[12,64,384]{2,1,0:T(8,128)(2,1)S(1)} %get-tuple-element.167), channel_id=1, source_target_pairs={{0,2},{1,3},{2,0},{3,1},{4,6},{5,7},{6,4},{7,5},{8,10},{9,11},{10,... | collective-permute-start | bytes 1769480 | tf_op jit(solution)/shard_map/ppermute | solution.py:64
  114.1 16.0 %collective-permute-start.26 = (bf16[32,128]{1,0:T(8,128)(2,1)S(1)}, bf16[32,128]{1,0:T(8,128)(2,1)S(1)}, u32[]{:S(2)}, u32[]{:S(2)}) collective-permute-start(bf16[32,128]{1,0:T(8,128)(2,1)S(1)} %get-tuple-element.151), channel_id=1, source_target_pairs={{0,4},{1,5},{2,6},{3,7},{4,0},{5,1},{6,2},{7,3},{8,12},{9,13},{10,... | collective-permute-start | bytes 24584 | tf_op jit(solution)/shard_map/ppermute | solution.py:64
  130.5 19.6 %collective-permute-start.33 = (bf16[12,32,384]{2,1,0:T(8,128)(2,1)S(1)}, bf16[12,32,384]{2,1,0:T(8,128)(2,1)S(1)}, u32[]{:S(2)}, u32[]{:S(2)}) collective-permute-start(bf16[12,32,384]{2,1,0:T(8,128)(2,1)S(1)} %get-tuple-element.169), channel_id=1, source_target_pairs={{0,4},{1,5},{2,6},{3,7},{4,0},{5,1},{6,2},{7,3},{8,12},{9,13},{10,... | collective-permute-start | bytes 884744 | tf_op jit(solution)/shard_map/ppermute | solution.py:64
  134.0 16.0 %collective-permute-start.28 = (bf16[32,1152]{1,0:T(8,128)(2,1)S(1)}, bf16[32,1152]{1,0:T(8,128)(2,1)S(1)}, u32[]{:S(2)}, u32[]{:S(2)}) collective-permute-start(bf16[32,1152]{1,0:T(8,128)(2,1)S(1)} %get-tuple-element.157.refs_0_), channel_id=1, source_target_pairs={{0,4},{1,5},{2,6},{3,7},{4,0},{5,1},{6,2},{7,3},{8,12},{9,13},{10,... | collective-permute-start | bytes 221192 | tf_op jit(solution)/shard_map/ppermute | solution.py:64
  150.0 12.7 %collective-permute-start.31 = (bf16[64,1152]{1,0:T(8,128)(2,1)S(1)}, bf16[64,1152]{1,0:T(8,128)(2,1)S(1)}, u32[]{:S(2)}, u32[]{:S(2)}) collective-permute-start(bf16[64,1152]{1,0:T(8,128)(2,1)S(1)} %get-tuple-element.165.refs_0_), channel_id=1, source_target_pairs={{0,2},{1,3},{2,0},{3,1},{4,6},{5,7},{6,4},{7,5},{8,10},{9,11},{10,... | collective-permute-start | bytes 442376 | tf_op jit(solution)/shard_map/ppermute | solution.py:64
  152.3 19.4 %collective-permute-start.37 = (bf16[6,64,384]{2,1,0:T(8,128)(2,1)S(1)}, bf16[6,64,384]{2,1,0:T(8,128)(2,1)S(1)}, u32[]{:S(2)}, u32[]{:S(2)}) collective-permute-start(bf16[6,64,384]{2,1,0:T(8,128)(2,1)S(1)} %get-tuple-element.182), channel_id=1, source_target_pairs={{0,2},{1,3},{2,0},{3,1},{4,6},{5,7},{6,4},{7,5},{8,10},{9,11},{10,... | collective-permute-start | bytes 884744 | tf_op jit(solution)/shard_map/ppermute | solution.py:64
  152.6 19.3 %collective-permute-start.36 = (bf16[12,32,384]{2,1,0:T(8,128)(2,1)S(1)}, bf16[12,32,384]{2,1,0:T(8,128)(2,1)S(1)}, u32[]{:S(2)}, u32[]{:S(2)}) collective-permute-start(bf16[12,32,384]{2,1,0:T(8,128)(2,1)S(1)} %get-tuple-element.180), channel_id=1, source_target_pairs={{0,4},{1,5},{2,6},{3,7},{4,0},{5,1},{6,2},{7,3},{8,12},{9,13},{10,... | collective-permute-start | bytes 884744 | tf_op jit(solution)/shard_map/ppermute | solution.py:64
  162.8 14.0 %collective-permute-start.35 = (bf16[64,2304]{1,0:T(8,128)(2,1)S(1)}, bf16[64,2304]{1,0:T(8,128)(2,1)S(1)}, u32[]{:S(2)}, u32[]{:S(2)}) collective-permute-start(bf16[64,2304]{1,0:T(8,128)(2,1)S(1)} %get-tuple-element.178.refs_0_), channel_id=1, source_target_pairs={{0,2},{1,3},{2,0},{3,1},{4,6},{5,7},{6,4},{7,5},{8,10},{9,11},{10,... | collective-permute-start | bytes 884744 | tf_op jit(solution)/shard_map/ppermute | solution.py:64
  176.8 23.2 %collective-permute-start.40 = (bf16[128,2304]{1,0:T(8,128)(2,1)S(1)}, bf16[128,2304]{1,0:T(8,128)(2,1)S(1)}, u32[]{:S(2)}, u32[]{:S(2)}) collective-permute-start(bf16[128,2304]{1,0:T(8,128)(2,1)S(1)} %get-tuple-element.188.refs_2_), channel_id=1, source_target_pairs={{0,1},{1,0},{2,3},{3,2},{4,5},{5,4},{6,7},{7,6},{8,9},{9,8},{10,11... | collective-permute-start | bytes 1769480 | tf_op jit(solution)/shard_map/ppermute | solution.py:64
  177.6 22.4 %collective-permute-start.39 = (bf16[128,1152]{1,0:T(8,128)(2,1)S(1)}, bf16[128,1152]{1,0:T(8,128)(2,1)S(1)}, u32[]{:S(2)}, u32[]{:S(2)}) collective-permute-start(bf16[128,1152]{1,0:T(8,128)(2,1)S(1)} %get-tuple-element.175.refs_1_), channel_id=1, source_target_pairs={{0,1},{1,0},{2,3},{3,2},{4,5},{5,4},{6,7},{7,6},{8,9},{9,8},{10,11... | collective-permute-start | bytes 884744 | tf_op jit(solution)/shard_map/ppermute | solution.py:64
  187.1 30.5 %collective-permute-start.51 = (bf16[64,2304]{1,0:T(8,128)(2,1)S(1)}, bf16[64,2304]{1,0:T(8,128)(2,1)S(1)}, u32[]{:S(2)}, u32[]{:S(2)}) collective-permute-start(bf16[64,2304]{1,0:T(8,128)(2,1)S(1)} %get-tuple-element.205.refs_0_), channel_id=1, source_target_pairs={{0,2},{1,3},{2,0},{3,1},{4,6},{5,7},{6,4},{7,5},{8,10},{9,11},{10,... | collective-permute-start | bytes 884744 | tf_op jit(solution)/shard_map/ppermute | solution.py:64
  187.1 22.8 %collective-permute-start.46 = (bf16[6,32,384]{2,1,0:T(8,128)(2,1)S(1)}, bf16[6,32,384]{2,1,0:T(8,128)(2,1)S(1)}, u32[]{:S(2)}, u32[]{:S(2)}) collective-permute-start(bf16[6,32,384]{2,1,0:T(8,128)(2,1)S(1)} %get-tuple-element.199), channel_id=1, source_target_pairs={{0,4},{1,5},{2,6},{3,7},{4,0},{5,1},{6,2},{7,3},{8,12},{9,13},{10,... | collective-permute-start | bytes 442376 | tf_op jit(solution)/shard_map/ppermute | solution.py:64
  245.2 14.5 %collective-permute-start.58 = (bf16[4,64,640]{2,1,0:T(8,128)(2,1)S(1)}, bf16[4,64,640]{2,1,0:T(8,128)(2,1)S(1)}, u32[]{:S(2)}, u32[]{:S(2)}) collective-permute-start(bf16[4,64,640]{2,1,0:T(8,128)(2,1)S(1)} %get-tuple-element.218.refs_2_), channel_id=1, source_target_pairs={{0,8},{8,0},{16,24},{24,16},{1,9},{9,1},{17,25},{25,17},{2,10},{10... | collective-permute-start | bytes 983048 | tf_op jit(solution)/shard_map/ppermute | solution.py:59
  246.3 13.4 %collective-permute-start.59 = (bf16[4,64,640]{2,1,0:T(8,128)(2,1)S(1)}, bf16[4,64,640]{2,1,0:T(8,128)(2,1)S(1)}, u32[]{:S(2)}, u32[]{:S(2)}) collective-permute-start(bf16[4,64,640]{2,1,0:T(8,128)(2,1)S(1)} %get-tuple-element.218.refs_2_), channel_id=1, source_target_pairs={{0,16},{8,24},{16,0},{24,8},{1,17},{9,25},{17,1},{25,9},{2,18},{10... | collective-permute-start | bytes 983048 | tf_op jit(solution)/shard_map/ppermute | solution.py:59
  262.4 18.3 %collective-permute-start.69 = (bf16[4,64,640]{2,1,0:T(8,128)(2,1)S(1)}, bf16[4,64,640]{2,1,0:T(8,128)(2,1)S(1)}, u32[]{:S(2)}, u32[]{:S(2)}) collective-permute-start(bf16[4,64,640]{2,1,0:T(8,128)(2,1)S(1)} %get-tuple-element.228.refs_2_), channel_id=1, source_target_pairs={{0,8},{8,0},{16,24},{24,16},{1,9},{9,1},{17,25},{25,17},{2,10},{10... | collective-permute-start | bytes 983048 | tf_op jit(solution)/shard_map/ppermute | solution.py:59
  263.3 17.4 %collective-permute-start.70 = (bf16[4,64,640]{2,1,0:T(8,128)(2,1)S(1)}, bf16[4,64,640]{2,1,0:T(8,128)(2,1)S(1)}, u32[]{:S(2)}, u32[]{:S(2)}) collective-permute-start(bf16[4,64,640]{2,1,0:T(8,128)(2,1)S(1)} %get-tuple-element.228.refs_2_), channel_id=1, source_target_pairs={{0,16},{8,24},{16,0},{24,8},{1,17},{9,25},{17,1},{25,9},{2,18},{10... | collective-permute-start | bytes 983048 | tf_op jit(solution)/shard_map/ppermute | solution.py:59
  264.5 16.2 %collective-permute-start.71 = (bf16[4,64,640]{2,1,0:T(8,128)(2,1)S(1)}, bf16[4,64,640]{2,1,0:T(8,128)(2,1)S(1)}, u32[]{:S(2)}, u32[]{:S(2)}) collective-permute-start(bf16[4,64,640]{2,1,0:T(8,128)(2,1)S(1)} %get-tuple-element.228.refs_2_), channel_id=1, source_target_pairs={{0,24},{8,16},{16,8},{24,0},{1,25},{9,17},{17,9},{25,1},{2,26},{10... | collective-permute-start | bytes 983048 | tf_op jit(solution)/shard_map/ppermute | solution.py:59
  268.7 25.5 %collective-permute-start.72 = (bf16[4,64,640]{2,1,0:T(8,128)(2,1)S(1)}, bf16[4,64,640]{2,1,0:T(8,128)(2,1)}, u32[]{:S(2)}, u32[]{:S(2)}) collective-permute-start(bf16[4,64,640]{2,1,0:T(8,128)(2,1)S(1)} %get-tuple-element.228.refs_2_), channel_id=1, source_target_pairs={{0,1},{1,0},{2,3},{3,2},{4,5},{5,4},{6,7},{7,6},{8,9},{9,8},{10,11... | collective-permute-start | bytes 983048 | tf_op jit(solution)/shard_map/ppermute | solution.py:64
  (105 other events, 894.5 us)

commit v5 on v4

--- a/solution.py
+++ b/solution.py
@@ -207,40 +207,49 @@
 
 
 def arrange_kernel(unit, offsets, *refs):
-    blocks, (gain, out, keep, send, square) = refs[:-5], refs[-5:]
+    blocks, (gain, out, square) = refs[:-3], refs[-3:]
     assemble(offsets, blocks, gain, out, square, unit)
-    put_squares(square, keep, send, 0)
-
-
-def gate_up_kernel(x, *refs):
-    weights, (keep, send) = refs[:-2], refs[-2:]
+
+
+def gate_up_kernel(squares, x, *refs):
+    weights, (keep, send) = refs[: -2 - squares], refs[-2:]
     half = keep.shape[1]
     count = len(weights) // 2
+    base = 2 * pl.program_id(0) if squares else 0
     for i in range(2):
         w = jnp.concatenate([w[0] for w in weights[i * count : (i + 1) * count]], axis=0)
         part = jnp.dot(x[...], w, preferred_element_type=F32)
-        keep[i] = part[:half]
-        send[i] = part[half:].astype(BF16)
-
-
-def halve_kernel(squares, *refs):
+        keep[base + i] = part[:half]
+        send[base + i] = part[half:].astype(BF16)
     if squares:
-        keep, recv, square_keep, square_recv, kept, send, square_kept, square_send = refs
-        half = square_kept.shape[0]
-        total = square_keep[...] + square_recv[...].astype(F32)
-        square_kept[...] = total[:half]
-        square_send[...] = split_square(join_square(total[half:]))
-    else:
-        keep, recv, kept, send = refs
+
+        @pl.when(pl.program_id(0) == 0)
+        def _():
+            group = keep.shape[0] - 1
+            keep[group] = jnp.zeros(keep.shape[1:], F32)
+            send[group] = jnp.zeros(send.shape[1:], BF16)
+            total = refs[-3][...]
+            lane = lax.broadcasted_iota(jnp.int32, (half, LANES), 1)
+            keep[group, :, :LANES] = jnp.where(lane < LANES // 2, total[:half], 0.0)
+            send[group, :, :LANES] = split_square(total[half:])
+
+
+def halve_kernel(squares, keep, recv, kept, send):
     half = kept.shape[1]
+    body = keep.shape[0] - squares
     kept[...] = keep[:, :half, :] + recv[:, :half, :].astype(F32)
-    send[...] = (keep[:, half:, :] + recv[:, half:, :].astype(F32)).astype(BF16)
+    send[:body] = (keep[:body, half:, :] + recv[:body, half:, :].astype(F32)).astype(BF16)
+    if squares:
+        total = keep[body, half:, :LANES] + recv[body, half:, :LANES].astype(F32)
+        send[body] = jnp.zeros(send.shape[1:], BF16)
+        send[body, :, :LANES] = split_square(join_square(total))
 
 
 def hidden_kernel(squares, keep, recv, *refs):
     if squares:
-        square_keep, square_recv, hidden, scale_ref = refs
-        total = square_keep[...] + square_recv[...].astype(F32)
+        hidden, scale_ref = refs
+        group = keep.shape[0] - 1
+        total = keep[group, :, :LANES] + recv[group, :, :LANES].astype(F32)
         scale_ref[...] = lax.rsqrt(join_square(total) / D + EPSILON)
     else:
         scale_ref, hidden = refs
@@ -498,18 +507,16 @@
     position = sum(((relative >> level) & 1) << (levels - 1 - level) for level in range(levels))
     half_offsets = position * col_tokens
     token = [mlp_gain]
-    mlp_in, square_keep, square_send = call(
+    mlp_in, squares = call(
         functools.partial(arrange_kernel, col_tokens),
         [half_offsets, *blocks, mlp_gain[None, :]],
         [SMEM] + [VMEM] * (row_count + 1),
         token,
         out_shape=[
             shape((tokens, features), BF16),
-            shape((half, LANES), F32),
-            shape((half, LANES), BF16),
+            shape((tokens, LANES), F32),
         ],
-        out_specs=[VMEM] * 3,
-        scratch_shapes=[pltpu.VMEM((tokens, LANES), F32)],
+        out_specs=[VMEM] * 2,
         compiler_params=params(16),
         cost_estimate=cost(tokens * features, 4 * tokens * features),
         name="mlp_in",
@@ -523,22 +530,27 @@
     plan = [(0, 0, 1), (0, 1, 2), (1, 0, 2), (1, 2, 1)] if divisible else [(0, 0, 1), (1, 0, 1)]
     last = levels - 1
     keeps, arrivals, hiddens = {}, {}, {}
-    scale = [None]
+    scale = []
     states = {}
 
     def gate_up(j):
         member, first, count = plan[j]
         first = first * subs
+        squared = j == 0
+        groups = 2 * count * subs + squared
         weights = [
             pl.BlockSpec((1, features // 2, sub), lambda i, q=q: (member, q, first + i))
             for q in range(2)
         ]
-        out = pl.BlockSpec((2, half, sub), lambda i: (i, 0, 0))
-        groups = 2 * count * subs
+        whole = pl.BlockSpec((tokens, features), lambda i: (0, 0))
+        if squared:
+            out = pl.BlockSpec((groups, half, sub), lambda i: (0, 0, 0))
+        else:
+            out = pl.BlockSpec((2, half, sub), lambda i: (i, 0, 0))
         keep, send = call(
-            gate_up_kernel,
-            [mlp_in, w_gate, w_gate, w_up, w_up],
-            [pl.BlockSpec((tokens, features), lambda i: (0, 0))] + weights * 2,
+            functools.partial(gate_up_kernel, squared),
+            [mlp_in, w_gate, w_gate, w_up, w_up] + [squares] * squared,
+            [whole] + weights * 2 + [pl.BlockSpec((tokens, LANES), lambda i: (0, 0))] * squared,
             token,
             grid=(count * subs,),
             out_shape=[shape((groups, half, sub), F32), shape((groups, half, sub), BF16)],
@@ -547,64 +559,49 @@
             cost_estimate=cost(4 * tokens * features * tile * count, 4 * tile * count * features),
             name="gate_up",
         )
-        arrived = [col_xor(send, 1)]
-        keeps[j] = [keep]
-        if j == 0:
-            keeps[j].append(square_keep)
-            arrived.append(col_xor(square_send, 1))
-        arrivals[j] = arrived
+        keeps[j], arrivals[j] = keep, col_xor(send, 1)
 
     def halve(j, level):
-        count = plan[j][2]
-        keep, received = keeps[j], arrivals[j]
-        groups, rows, _ = keep[0].shape
+        count = 1 if j == 0 else plan[j][2]
+        keep = keeps[j]
+        groups, rows, _ = keep.shape
         part = groups // count
-        squared = len(keep) == 2
-        specs = [pl.BlockSpec((part, rows, sub), lambda i: (i, 0, 0))] * 2
-        outs = [pl.BlockSpec((part, rows // 2, sub), lambda i: (i, 0, 0))] * 2
-        shapes = [shape((groups, rows // 2, sub), F32), shape((groups, rows // 2, sub), BF16)]
-        operands = [keep[0], received[0]]
-        if squared:
-            operands += [keep[1], received[1]]
-            specs = specs + [pl.BlockSpec((rows, LANES), lambda i: (0, 0))] * 2
-            outs = outs + [pl.BlockSpec((rows // 2, LANES), lambda i: (0, 0))] * 2
-            shapes += [shape((rows // 2, LANES), F32), shape((rows // 2, LANES), BF16)]
-        result = call(
-            functools.partial(halve_kernel, squared),
-            operands,
-            specs,
+        keeps[j], send = call(
+            functools.partial(halve_kernel, j == 0),
+            [keep, arrivals[j]],
+            [pl.BlockSpec((part, rows, sub), lambda i: (i, 0, 0))] * 2,
             token,
             grid=(count,),
-            out_shape=shapes,
-            out_specs=outs,
+            out_shape=[
+                shape((groups, rows // 2, sub), F32),
+                shape((groups, rows // 2, sub), BF16),
+            ],
+            out_specs=[pl.BlockSpec((part, rows // 2, sub), lambda i: (i, 0, 0))] * 2,
             compiler_params=params(24),
             cost_estimate=cost(rows * sub * groups, 9 * rows * sub * groups),
             name="halve",
         )
-        keeps[j] = result[0::2]
-        arrivals[j] = [col_xor(send, 2 << level) for send in result[1::2]]
+        arrivals[j] = col_xor(send, 2 << level)
 
     def hidden_of(j):
-        keep, received = keeps[j], arrivals[j]
-        groups, rows, _ = keep[0].shape
+        groups, rows, _ = keeps[j].shape
+        squared = j == 0
         hidden_shape = shape((rows, groups // 2 * sub), BF16)
-        scale_shape = shape((rows, LANES), F32)
-        squared = len(keep) == 2
-        operands = [keep[0], received[0]] + ([keep[1], received[1]] if squared else scale)
-        result = call(
+        operands = [keeps[j], arrivals[j]] + ([] if squared else scale)
+        hidden, *extra = call(
             functools.partial(hidden_kernel, squared),
             operands,
             [VMEM] * len(operands),
             token,
-            out_shape=[hidden_shape, scale_shape] if squared else [hidden_shape],
-            out_specs=[VMEM] * 2 if squared else [VMEM],
+            out_shape=[hidden_shape] + [shape((rows, LANES), F32)] * squared,
+            out_specs=[VMEM] * (1 + squared),
             compiler_params=params(24),
             cost_estimate=cost(8 * rows * groups * sub, 6 * rows * groups * sub),
             name="hidden",
         )
         if squared:
-            scale[:] = [result[1]]
-        hiddens[j] = (result[0], col_xor(result[0], 1 << last))
+            scale[:] = extra
+        hiddens[j] = (hidden, col_xor(hidden, 1 << last))
 
     def join(j, level):
         first, second = hiddens[j]
@@ -694,17 +691,21 @@
     stats = {0: [], 1: []}
 
     gain_parts = [final_gain[None, :]]
+    small = []
 
     def gather_gain(level):
         (part,) = hold(gain_parts[-1:], token)
         gain_parts.append(jnp.concatenate([part, col_xor(part, 1 << level)], axis=0))
 
+    def ready():
+        small[:] = hold([gain_parts[-1], local_targets, col_rel, row_rel * row_tokens], token)
+
     def head(member, first, count):
-        gains = gain_parts[-1]
+        gains, target, features_at, rows_at = small
         state = states[member]
         (result,) = call(
             functools.partial(head_kernel, row_count, first),
-            [col_rel, row_rel * row_tokens, *state, gains, local_targets] + [w_head] * HEAD_BLOCKS,
+            [features_at, rows_at, *state, gains, target] + [w_head] * HEAD_BLOCKS,
             [SMEM] * 2
             + [pl.BlockSpec(state[0].shape, lambda i: (0, 0, 0))] * (2 * row_count)
             + [pl.BlockSpec(gains.shape, lambda i: (0, 0))]
@@ -732,7 +733,7 @@
             (halve, 0, 1), (gate_up, 3), (halve, 2, 0), (hidden_of, 0), (halve, 1, 1),
             (halve, 3, 0), (join, 0, 1), (gather_gain, 0), (hidden_of, 1), (halve, 2, 1),
             (join, 0, 0), (join, 1, 1), (gather_gain, 1), (halve, 3, 1), (hidden_of, 2),
-            (join, 1, 0), (join, 2, 1), (gather_gain, 2), (down, 0), (hidden_of, 3),
+            (join, 1, 0), (join, 2, 1), (gather_gain, 2), (ready,), (down, 0), (hidden_of, 3),
             (join, 3, 1), (output, 0), (join, 2, 0), (join, 3, 0), (down, 1),
         ]
     else:
@@ -740,7 +741,7 @@
         for j in range(len(plan)):
             schedule += [(gate_up, j)] + [(halve, j, level) for level in range(last)]
             schedule += [(hidden_of, j)] + [(join, j, level) for level in range(last - 1, -1, -1)]
-        schedule += [(gather_gain, level) for level in range(levels)]
+        schedule += [(gather_gain, level) for level in range(levels)] + [(ready,)]
         schedule += [(down, 0), (output, 0), (down, 1)]
     early = (3 * vocab_tiles + 4) // 5
     schedule += [(output, 1), (pack, 0), (pack, 1), (forward, 0), (head, 0, 0, early)]
@@ -759,9 +760,10 @@
 
     merged = combine(stats[0]) if len(stats[0]) > 1 else stats[0][0]
     merged = jnp.stack([merged, stats[1][0]], axis=1)
-    merged = combine([merged, col_xor(merged, 1)])
-    merged = combine([merged] + [col_xor(merged, 2 * j) for j in range(1, chips)])
-    merged = combine([merged] + [row_xor(merged, j) for j in range(1, row_count)])
+    for level in range(levels):
+        merged = combine([merged, col_xor(merged, 1 << level)])
+    for level in range((row_count - 1).bit_length()):
+        merged = combine([merged, row_xor(merged, 1 << level)])
     logprob = merged[2] - (merged[0] + jnp.log(merged[1]))
     difference = logprob[0] - logprob[1]
     one_hot = (segment[:, None] == jnp.arange(SEQS, dtype=jnp.int32)[None, :]).astype(F32)

time: 332 us -> 308 us (0.928)
  waiting for transfers between devices: 153 us -> 136 us
  starting transfers between devices: 78.6 us -> 72.4 us
    ppermute x59 -> x55, waiting for transfers between devices: 140 us -> 119 us  [col_xor(): return lax.ppermute(x, 'col', [(i, i ^ mask) for i in range(count)])]
    ppermute x59 -> x55, starting transfers between devices: 49.4 us -> 44.8 us  [col_xor(): return lax.ppermute(x, 'col', [(i, i ^ mask) for i in range(count)])]
    ppermute x24 -> x23, waiting for transfers between devices: 12.9 us -> 17.3 us  [row_xor(): return lax.ppermute(x, 'row', [(i, i ^ mask) for i in range(count)])]
    ppermute x24 -> x23, starting transfers between devices: 29.2 us -> 27.6 us  [row_xor(): return lax.ppermute(x, 'row', [(i, i ^ mask) for i in range(count)])]
    unnamed x93 -> x105, local copies, waits for them, and re-layouts: 10.1 us -> 10.9 us
  transfers between devices with their start and end apart: 83 -> 78, of which waited for: 42 -> 44; matrix products, arithmetic and copies ran while one was open for 2% -> 2% of each run, Pallas kernels for 14% -> 15%
where the time goes in v5:
time: 308 us; the launch traced here: 307 us
  waiting for transfers between devices  136 us (44%)
  Pallas kernels  77.9 us (25%)
  starting transfers between devices  72.4 us (24%)
  local copies, waits for them, and re-layouts  15.6 us (5%)
    ppermute x55, waiting for transfers between devices, col_xor(): return lax.ppermute(x, 'col', [(i, i ^ mask) for i in range(count)])  119 us
    pallas_call x34, Pallas kernels, call(): pl.pallas_call(body, in_specs=in_specs + [ANY], out_shape=out_shape + [ja...  71.2 us
    ppermute x55, starting transfers between devices, col_xor(): return lax.ppermute(x, 'col', [(i, i ^ mask) for i in range(count)])  44.8 us
    ppermute x23, starting transfers between devices, row_xor(): return lax.ppermute(x, 'row', [(i, i ^ mask) for i in range(count)])  27.6 us
    ppermute x23, waiting for transfers between devices, row_xor(): return lax.ppermute(x, 'row', [(i, i ^ mask) for i in range(count)])  17.3 us
    unnamed x105, local copies, waits for them, and re-layouts  10.9 us
  transfers between devices with their start and end apart: 78, of which 44 were waited for; matrix products, arithmetic and copies ran while one was open for 2% of the time, Pallas kernels for 15%

profile of v5, /device:TPU:0, one launch (start us, length us, event | category | flops | bytes accessed | tf_op | source)
XLA Modules:
  0.0 307.0 jit_solution(6278430311664669344)
XLA Ops:
  10.6 3.7 %qkv_partial.1 = (f32[128,1920]{1,0:T(8,128)}, bf16[128,1920]{1,0:T(8,128)(2,1)}) custom-call(s32[8]{0:T(128)} %reshape.112.offsets, bf16[64,640]{1,0:T(8,128)(2,1)} %refs_0_.1, bf16[64,640]{1,0:T(8,128)(2,1)} %copy-done.43, bf16[64,640]{1,0:T(8,128)(2,1)} %copy-done.44, bf16[64,640]{1,0:T(8,128)(2,1)} %copy-done.45, f32[1,640]{1,0:T(1,128)} %broadcast_in_dim.29.refs_4_, ...), custom_call_target="tpu_custom_call" | custom-call | flops 1 | bytes 1 | tf_op jit(solution)/shard_map/qkv_partial/pallas_call | solution.py:447
  24.9 6.9 %collective-permute-done.5.refs_2_ = bf16[32,1920]{1,0:T(8,128)(2,1)S(1)} collective-permute-done((bf16[32,1920]{1,0:T(8,128)(2,1)S(1)}, bf16[32,1920]{1,0:T(8,128)(2,1)S(1)}, u32[]{:S(2)}, u32[]{:S(2)}) %collective-permute-start.5) | collective-permute-done | bytes 122912 | tf_op jit(solution)/shard_map/ppermute | solution.py:64
  38.1 7.0 %collective-permute-done.8.refs_2_ = bf16[32,1792]{1,0:T(8,128)(2,1)S(1)} collective-permute-done((bf16[32,1792]{1,0:T(8,128)(2,1)S(1)}, bf16[32,1792]{1,0:T(8,128)(2,1)S(1)}, u32[]{:S(2)}, u32[]{:S(2)}) %collective-permute-start.8) | collective-permute-done | bytes 114720 | tf_op jit(solution)/shard_map/ppermute | solution.py:64
  64.8 4.0 %gate_up.4 = (f32[7,128,384]{2,1,0:T(8,128)S(1)}, bf16[7,128,384]{2,1,0:T(8,128)(2,1)S(1)}, f32[8,128]{1,0:T(8,128)S(1)}) custom-call(bf16[256,640]{1,0:T(8,128)(2,1)S(1)} %get-tuple-element.131.refs_0_, bf16[2,640,3456]{2,1,0:T(8,128)(2,1)} %refs_2_.7, bf16[2,640,3456]{2,1,0:T(8,128)(2,1)} %refs_2_.7, bf16[2,640,3456]{2,1,0:T(8,128)(2,1)} %refs_4_.7, ...), custom_call_target="tpu_custom_call" | custom-call | flops 1 | bytes 1 | tf_op jit(solution)/shard_map/gate_up/pallas_call | solution.py:46
  68.9 6.2 %gate_up.5 = (f32[12,128,384]{2,1,0:T(8,128)S(1)}, bf16[12,128,384]{2,1,0:T(8,128)(2,1)S(1)}, f32[8,128]{1,0:T(8,128)S(1)}) custom-call(bf16[256,640]{1,0:T(8,128)(2,1)S(1)} %get-tuple-element.131.refs_0_, bf16[2,640,3456]{2,1,0:T(8,128)(2,1)} %refs_2_.7, bf16[2,640,3456]{2,1,0:T(8,128)(2,1)} %refs_2_.7, bf16[2,640,3456]{2,1,0:T(8,128)(2,1)} %refs_4_.7, ...), custom_call_target="tpu_custom_call" | custom-call | flops 1 | bytes 1 | tf_op jit(solution)/shard_map/gate_up/pallas_call | solution.py:46
  75.8 6.2 %gate_up.6 = (f32[12,128,384]{2,1,0:T(8,128)S(1)}, bf16[12,128,384]{2,1,0:T(8,128)(2,1)S(1)}, f32[8,128]{1,0:T(8,128)S(1)}) custom-call(bf16[256,640]{1,0:T(8,128)(2,1)S(1)} %get-tuple-element.131.refs_0_, bf16[2,640,3456]{2,1,0:T(8,128)(2,1)} %refs_2_.7, bf16[2,640,3456]{2,1,0:T(8,128)(2,1)} %refs_2_.7, bf16[2,640,3456]{2,1,0:T(8,128)(2,1)} %refs_4_.7, ...), custom_call_target="tpu_custom_call" | custom-call | flops 1 | bytes 1 | tf_op jit(solution)/shard_map/gate_up/pallas_call | solution.py:46
  84.5 8.5 %collective-permute-done.21.refs_1_ = bf16[7,64,384]{2,1,0:T(8,128)(2,1)S(1)} collective-permute-done((bf16[7,64,384]{2,1,0:T(8,128)(2,1)S(1)}, bf16[7,64,384]{2,1,0:T(8,128)(2,1)S(1)}, u32[]{:S(2)}, u32[]{:S(2)}) %collective-permute-start.21) | collective-permute-done | bytes 344096 | tf_op jit(solution)/shard_map/ppermute | solution.py:64
  93.1 3.8 %gate_up.7 = (f32[6,128,384]{2,1,0:T(8,128)S(1)}, bf16[6,128,384]{2,1,0:T(8,128)(2,1)S(1)}, f32[8,128]{1,0:T(8,128)S(1)}) custom-call(bf16[256,640]{1,0:T(8,128)(2,1)S(1)} %get-tuple-element.131.refs_0_, bf16[2,640,3456]{2,1,0:T(8,128)(2,1)} %refs_2_.7, bf16[2,640,3456]{2,1,0:T(8,128)(2,1)} %refs_2_.7, bf16[2,640,3456]{2,1,0:T(8,128)(2,1)} %refs_4_.7, ...), custom_call_target="tpu_custom_call" | custom-call | flops 1 | bytes 1 | tf_op jit(solution)/shard_map/gate_up/pallas_call | solution.py:46
  99.9 8.5 %collective-permute-done.23.refs_1_ = bf16[7,32,384]{2,1,0:T(8,128)(2,1)S(1)} collective-permute-done((bf16[7,32,384]{2,1,0:T(8,128)(2,1)S(1)}, bf16[7,32,384]{2,1,0:T(8,128)(2,1)S(1)}, u32[]{:S(2)}, u32[]{:S(2)}) %collective-permute-start.23) | collective-permute-done | bytes 172064 | tf_op jit(solution)/shard_map/ppermute | solution.py:64
  112.6 16.0 %collective-permute-done.25.refs_1_ = bf16[32,1152]{1,0:T(8,128)(2,1)S(1)} collective-permute-done((bf16[32,1152]{1,0:T(8,128)(2,1)S(1)}, bf16[32,1152]{1,0:T(8,128)(2,1)S(1)}, u32[]{:S(2)}, u32[]{:S(2)}) %collective-permute-start.25) | collective-permute-done | bytes 73760 | tf_op jit(solution)/shard_map/ppermute | solution.py:64
  128.6 3.5 %collective-permute-start.31 = (bf16[64,1152]{1,0:T(8,128)(2,1)S(1)}, bf16[64,1152]{1,0:T(8,128)(2,1)S(1)}, u32[]{:S(2)}, u32[]{:S(2)}) collective-permute-start(bf16[64,1152]{1,0:T(8,128)(2,1)S(1)} %get-tuple-element.167.refs_0_), channel_id=1, source_target_pairs={{0,2},{1,3},{2,0},{3,1},{4,6},{5,7},{6,4},{7,5},{8,10},{9,11},{10,... | collective-permute-start | bytes 442376 | tf_op jit(solution)/shard_map/ppermute | solution.py:64
  138.6 4.0 %collective-permute-done.30.refs_1_ = bf16[32,2304]{1,0:T(8,128)(2,1)S(1)} collective-permute-done((bf16[32,2304]{1,0:T(8,128)(2,1)S(1)}, bf16[32,2304]{1,0:T(8,128)(2,1)S(1)}, u32[]{:S(2)}, u32[]{:S(2)}) %collective-permute-start.30) | collective-permute-done | bytes 147488 | tf_op jit(solution)/shard_map/ppermute | solution.py:64
  144.0 7.2 %collective-permute-done.35.refs_1_ = bf16[6,64,384]{2,1,0:T(8,128)(2,1)S(1)} collective-permute-done((bf16[6,64,384]{2,1,0:T(8,128)(2,1)S(1)}, bf16[6,64,384]{2,1,0:T(8,128)(2,1)S(1)}, u32[]{:S(2)}, u32[]{:S(2)}) %collective-permute-start.35) | collective-permute-done | bytes 294944 | tf_op jit(solution)/shard_map/ppermute | solution.py:64
  151.2 3.1 collective-permute-done.34.refs_1_
  154.5 3.4 %collective-permute-done.37.refs_1_ = bf16[64,2304]{1,0:T(8,128)(2,1)S(1)} collective-permute-done((bf16[64,2304]{1,0:T(8,128)(2,1)S(1)}, bf16[64,2304]{1,0:T(8,128)(2,1)S(1)}, u32[]{:S(2)}, u32[]{:S(2)}) %collective-permute-start.37) | collective-permute-done | bytes 294944 | tf_op jit(solution)/shard_map/ppermute | solution.py:64
  162.9 9.9 %collective-permute-done.36.refs_1_ = bf16[32,2304]{1,0:T(8,128)(2,1)S(1)} collective-permute-done((bf16[32,2304]{1,0:T(8,128)(2,1)S(1)}, bf16[32,2304]{1,0:T(8,128)(2,1)S(1)}, u32[]{:S(2)}, u32[]{:S(2)}) %collective-permute-start.36) | collective-permute-done | bytes 147488 | tf_op jit(solution)/shard_map/ppermute | solution.py:64
  179.1 5.5 %down.2 = (f32[64,640]{1,0:T(8,128)}, bf16[64,640]{1,0:T(8,128)(2,1)}, bf16[64,640]{1,0:T(8,128)(2,1)}, bf16[64,640]{1,0:T(8,128)(2,1)}, f32[8,128]{1,0:T(8,128)}) custom-call(s32[8]{0:T(128)} %copy-done.21, bf16[128,1152]{1,0:T(8,128)(2,1)} %copy-done.14, bf16[128,2304]{1,0:T(8,128)(2,1)} %copy-done.10, bf16[128,1152]{1,0:T(8,128)(2,1)} %copy-done.40, ...), custom_call_target="tpu_custom_call" | custom-call | flops 1 | bytes 1 | tf_op jit(solution)/shard_map/down/pallas_call | solution.py:46
  189.1 5.2 %collective-permute-done.45.refs_1_ = bf16[32,1152]{1,0:T(8,128)(2,1)S(1)} collective-permute-done((bf16[32,1152]{1,0:T(8,128)(2,1)S(1)}, bf16[32,1152]{1,0:T(8,128)(2,1)S(1)}, u32[]{:S(2)}, u32[]{:S(2)}) %collective-permute-start.45) | collective-permute-done | bytes 73760 | tf_op jit(solution)/shard_map/ppermute | solution.py:64
  195.6 6.2 %collective-permute-done.50.refs_1_ = bf16[64,1152]{1,0:T(8,128)(2,1)S(1)} collective-permute-done((bf16[64,1152]{1,0:T(8,128)(2,1)S(1)}, bf16[64,1152]{1,0:T(8,128)(2,1)S(1)}, u32[]{:S(2)}, u32[]{:S(2)}) %collective-permute-start.50) | collective-permute-done | bytes 147488 | tf_op jit(solution)/shard_map/ppermute | solution.py:64
  204.9 5.5 %down.3 = (f32[64,640]{1,0:T(8,128)}, bf16[64,640]{1,0:T(8,128)(2,1)}, bf16[64,640]{1,0:T(8,128)(2,1)}, bf16[64,640]{1,0:T(8,128)(2,1)}, f32[8,128]{1,0:T(8,128)}) custom-call(s32[8]{0:T(128)} %copy-done.21, bf16[128,2304]{1,0:T(8,128)(2,1)} %copy-done.11, bf16[128,1152]{1,0:T(8,128)(2,1)} %copy-done.15, bf16[128,2304]{1,0:T(8,128)(2,1)} %copy-done.34, ...), custom_call_target="tpu_custom_call" | custom-call | flops 1 | bytes 1 | tf_op jit(solution)/shard_map/down/pallas_call | solution.py:46
  243.0 11.8 %head.3 = (f32[256,128]{1,0:T(8,128)}, f32[8,128]{1,0:T(8,128)}) custom-call(s32[8]{0:T(128)} %copy-done.20, s32[4]{0:T(128)} %copy-done.19, bf16[4,64,640]{2,1,0:T(8,128)(2,1)} %copy-done.5, bf16[4,64,640]{2,1,0:T(8,128)(2,1)} %copy-done.1, bf16[4,64,640]{2,1,0:T(8,128)(2,1)} %copy-done.2, bf16[4,64,640]{2,1,0:T(8,128)(2,1)} %copy-done.3, ...), custom_call_target="tpu_custom_call" | custom-call | flops 1 | bytes 1 | tf_op jit(solution)/shard_map/head/pallas_call | solution.py:46
  257.8 9.4 %head.4 = (f32[256,128]{1,0:T(8,128)}, f32[8,128]{1,0:T(8,128)}) custom-call(s32[8]{0:T(128)} %copy-done.20, s32[4]{0:T(128)} %copy-done.19, bf16[4,64,640]{2,1,0:T(8,128)(2,1)} %copy-done.5, bf16[4,64,640]{2,1,0:T(8,128)(2,1)} %copy-done.1, bf16[4,64,640]{2,1,0:T(8,128)(2,1)} %copy-done.2, bf16[4,64,640]{2,1,0:T(8,128)(2,1)} %copy-done.3, ...), custom_call_target="tpu_custom_call" | custom-call | flops 1 | bytes 1 | tf_op jit(solution)/shard_map/head/pallas_call | solution.py:46
  272.3 15.9 %head.5 = (f32[256,128]{1,0:T(8,128)}, f32[8,128]{1,0:T(8,128)}) custom-call(s32[8]{0:T(128)} %copy-done.20, s32[4]{0:T(128)} %copy-done.19, bf16[4,64,640]{2,1,0:T(8,128)(2,1)} %copy-done.13, bf16[4,64,640]{2,1,0:T(8,128)(2,1)} %copy-done.6, bf16[4,64,640]{2,1,0:T(8,128)(2,1)} %copy-done.7, bf16[4,64,640]{2,1,0:T(8,128)(2,1)} %copy-done.8, ...), custom_call_target="tpu_custom_call" | custom-call | flops 1 | bytes 1 | tf_op jit(solution)/shard_map/head/pallas_call | solution.py:46
  295.2 3.6 %collective-permute-done.75 = f32[3,2,256]{2,1,0:T(2,128)S(1)} collective-permute-done((f32[3,2,256]{2,1,0:T(2,128)S(1)}, f32[3,2,256]{2,1,0:T(2,128)S(1)}, u32[]{:S(2)}, u32[]{:S(2)}) %collective-permute-start.75) | collective-permute-done | bytes 6176 | tf_op jit(solution)/shard_map/ppermute | solution.py:64
  (336 shorter events, 141.2 us)
Async XLA Ops:
  19.4 12.4 %collective-permute-start.5 = (bf16[32,1920]{1,0:T(8,128)(2,1)S(1)}, bf16[32,1920]{1,0:T(8,128)(2,1)S(1)}, u32[]{:S(2)}, u32[]{:S(2)}) collective-permute-start(bf16[32,1920]{1,0:T(8,128)(2,1)S(1)} %get-tuple-element.125), channel_id=1, source_target_pairs={{0,4},{1,5},{2,6},{3,7},{4,0},{5,1},{6,2},{7,3},{8,12},{9,13},{10,... | collective-permute-start | bytes 368648 | tf_op jit(solution)/shard_map/ppermute | solution.py:64
  82.0 17.6 %collective-permute-start.24 = (bf16[12,128,384]{2,1,0:T(8,128)(2,1)S(1)}, bf16[12,128,384]{2,1,0:T(8,128)(2,1)S(1)}, u32[]{:S(2)}, u32[]{:S(2)}) collective-permute-start(bf16[12,128,384]{2,1,0:T(8,128)(2,1)S(1)} %get-tuple-element.148), channel_id=1, source_target_pairs={{0,1},{1,0},{2,3},{3,2},{4,5},{5,4},{6,7},{7,6},{8,9},{9,8},{10,11... | collective-permute-start | bytes 3538952 | tf_op jit(solution)/shard_map/ppermute | solution.py:64
  82.1 10.9 %collective-permute-start.21 = (bf16[7,64,384]{2,1,0:T(8,128)(2,1)S(1)}, bf16[7,64,384]{2,1,0:T(8,128)(2,1)S(1)}, u32[]{:S(2)}, u32[]{:S(2)}) collective-permute-start(bf16[7,64,384]{2,1,0:T(8,128)(2,1)S(1)} %get-tuple-element.139), channel_id=1, source_target_pairs={{0,2},{1,3},{2,0},{3,1},{4,6},{5,7},{6,4},{7,5},{8,10},{9,11},{10,... | collective-permute-start | bytes 1032200 | tf_op jit(solution)/shard_map/ppermute | solution.py:64
  84.0 25.3 %collective-permute-start.27 = (bf16[12,64,384]{2,1,0:T(8,128)(2,1)S(1)}, bf16[12,64,384]{2,1,0:T(8,128)(2,1)S(1)}, u32[]{:S(2)}, u32[]{:S(2)}) collective-permute-start(bf16[12,64,384]{2,1,0:T(8,128)(2,1)S(1)} %get-tuple-element.156), channel_id=1, source_target_pairs={{0,2},{1,3},{2,0},{3,1},{4,6},{5,7},{6,4},{7,5},{8,10},{9,11},{10,... | collective-permute-start | bytes 1769480 | tf_op jit(solution)/shard_map/ppermute | solution.py:64
  96.9 15.6 %collective-permute-start.26 = (bf16[6,128,384]{2,1,0:T(8,128)(2,1)S(1)}, bf16[6,128,384]{2,1,0:T(8,128)(2,1)S(1)}, u32[]{:S(2)}, u32[]{:S(2)}) collective-permute-start(bf16[6,128,384]{2,1,0:T(8,128)(2,1)S(1)} %get-tuple-element.154), channel_id=1, source_target_pairs={{0,1},{1,0},{2,3},{3,2},{4,5},{5,4},{6,7},{7,6},{8,9},{9,8},{10,11... | collective-permute-start | bytes 1769480 | tf_op jit(solution)/shard_map/ppermute | solution.py:64
  97.0 11.5 %collective-permute-start.23 = (bf16[7,32,384]{2,1,0:T(8,128)(2,1)S(1)}, bf16[7,32,384]{2,1,0:T(8,128)(2,1)S(1)}, u32[]{:S(2)}, u32[]{:S(2)}) collective-permute-start(bf16[7,32,384]{2,1,0:T(8,128)(2,1)S(1)} %get-tuple-element.146), channel_id=1, source_target_pairs={{0,4},{1,5},{2,6},{3,7},{4,0},{5,1},{6,2},{7,3},{8,12},{9,13},{10,... | collective-permute-start | bytes 516104 | tf_op jit(solution)/shard_map/ppermute | solution.py:64
  99.8 34.5 %collective-permute-start.32 = (bf16[12,64,384]{2,1,0:T(8,128)(2,1)S(1)}, bf16[12,64,384]{2,1,0:T(8,128)(2,1)S(1)}, u32[]{:S(2)}, u32[]{:S(2)}) collective-permute-start(bf16[12,64,384]{2,1,0:T(8,128)(2,1)S(1)} %get-tuple-element.169), channel_id=1, source_target_pairs={{0,2},{1,3},{2,0},{3,1},{4,6},{5,7},{6,4},{7,5},{8,10},{9,11},{10,... | collective-permute-start | bytes 1769480 | tf_op jit(solution)/shard_map/ppermute | solution.py:64
  109.5 22.6 %collective-permute-start.29 = (bf16[12,32,384]{2,1,0:T(8,128)(2,1)S(1)}, bf16[12,32,384]{2,1,0:T(8,128)(2,1)S(1)}, u32[]{:S(2)}, u32[]{:S(2)}) collective-permute-start(bf16[12,32,384]{2,1,0:T(8,128)(2,1)S(1)} %get-tuple-element.163), channel_id=1, source_target_pairs={{0,4},{1,5},{2,6},{3,7},{4,0},{5,1},{6,2},{7,3},{8,12},{9,13},{10,... | collective-permute-start | bytes 884744 | tf_op jit(solution)/shard_map/ppermute | solution.py:64
  112.3 16.2 %collective-permute-start.25 = (bf16[32,1152]{1,0:T(8,128)(2,1)S(1)}, bf16[32,1152]{1,0:T(8,128)(2,1)S(1)}, u32[]{:S(2)}, u32[]{:S(2)}) collective-permute-start(bf16[32,1152]{1,0:T(8,128)(2,1)S(1)} %get-tuple-element.152.refs_0_), channel_id=1, source_target_pairs={{0,4},{1,5},{2,6},{3,7},{4,0},{5,1},{6,2},{7,3},{8,12},{9,13},{10,... | collective-permute-start | bytes 221192 | tf_op jit(solution)/shard_map/ppermute | solution.py:64
  132.3 18.8 %collective-permute-start.35 = (bf16[6,64,384]{2,1,0:T(8,128)(2,1)S(1)}, bf16[6,64,384]{2,1,0:T(8,128)(2,1)S(1)}, u32[]{:S(2)}, u32[]{:S(2)}) collective-permute-start(bf16[6,64,384]{2,1,0:T(8,128)(2,1)S(1)} %get-tuple-element.178), channel_id=1, source_target_pairs={{0,2},{1,3},{2,0},{3,1},{4,6},{5,7},{6,4},{7,5},{8,10},{9,11},{10,... | collective-permute-start | bytes 884744 | tf_op jit(solution)/shard_map/ppermute | solution.py:64
  134.5 19.8 %collective-permute-start.34 = (bf16[12,32,384]{2,1,0:T(8,128)(2,1)S(1)}, bf16[12,32,384]{2,1,0:T(8,128)(2,1)S(1)}, u32[]{:S(2)}, u32[]{:S(2)}) collective-permute-start(bf16[12,32,384]{2,1,0:T(8,128)(2,1)S(1)} %get-tuple-element.176), channel_id=1, source_target_pairs={{0,4},{1,5},{2,6},{3,7},{4,0},{5,1},{6,2},{7,3},{8,12},{9,13},{10,... | collective-permute-start | bytes 884744 | tf_op jit(solution)/shard_map/ppermute | solution.py:64
  142.7 15.2 %collective-permute-start.37 = (bf16[64,2304]{1,0:T(8,128)(2,1)S(1)}, bf16[64,2304]{1,0:T(8,128)(2,1)S(1)}, u32[]{:S(2)}, u32[]{:S(2)}) collective-permute-start(bf16[64,2304]{1,0:T(8,128)(2,1)S(1)} %get-tuple-element.182.refs_0_), channel_id=1, source_target_pairs={{0,2},{1,3},{2,0},{3,1},{4,6},{5,7},{6,4},{7,5},{8,10},{9,11},{10,... | collective-permute-start | bytes 884744 | tf_op jit(solution)/shard_map/ppermute | solution.py:64
  157.9 20.3 %collective-permute-start.40 = (bf16[128,2304]{1,0:T(8,128)(2,1)S(1)}, bf16[128,2304]{1,0:T(8,128)(2,1)S(1)}, u32[]{:S(2)}, u32[]{:S(2)}) collective-permute-start(bf16[128,2304]{1,0:T(8,128)(2,1)S(1)} %get-tuple-element.191.refs_2_), channel_id=1, source_target_pairs={{0,1},{1,0},{2,3},{3,2},{4,5},{5,4},{6,7},{7,6},{8,9},{9,8},{10,11... | collective-permute-start | bytes 1769480 | tf_op jit(solution)/shard_map/ppermute | solution.py:64
  159.8 12.9 %collective-permute-start.36 = (bf16[32,2304]{1,0:T(8,128)(2,1)S(1)}, bf16[32,2304]{1,0:T(8,128)(2,1)S(1)}, u32[]{:S(2)}, u32[]{:S(2)}) collective-permute-start(bf16[32,2304]{1,0:T(8,128)(2,1)S(1)} %get-tuple-element.181.refs_0_), channel_id=1, source_target_pairs={{0,4},{1,5},{2,6},{3,7},{4,0},{5,1},{6,2},{7,3},{8,12},{9,13},{10,... | collective-permute-start | bytes 442376 | tf_op jit(solution)/shard_map/ppermute | solution.py:64
  160.1 18.1 %collective-permute-start.39 = (bf16[128,1152]{1,0:T(8,128)(2,1)S(1)}, bf16[128,1152]{1,0:T(8,128)(2,1)S(1)}, u32[]{:S(2)}, u32[]{:S(2)}) collective-permute-start(bf16[128,1152]{1,0:T(8,128)(2,1)S(1)} %get-tuple-element.190.refs_1_), channel_id=1, source_target_pairs={{0,1},{1,0},{2,3},{3,2},{4,5},{5,4},{6,7},{7,6},{8,9},{9,8},{10,11... | collective-permute-start | bytes 884744 | tf_op jit(solution)/shard_map/ppermute | solution.py:64
  160.1 28.1 %collective-permute-start.44 = (bf16[6,32,384]{2,1,0:T(8,128)(2,1)S(1)}, bf16[6,32,384]{2,1,0:T(8,128)(2,1)S(1)}, u32[]{:S(2)}, u32[]{:S(2)}) collective-permute-start(bf16[6,32,384]{2,1,0:T(8,128)(2,1)S(1)} %get-tuple-element.198), channel_id=1, source_target_pairs={{0,4},{1,5},{2,6},{3,7},{4,0},{5,1},{6,2},{7,3},{8,12},{9,13},{10,... | collective-permute-start | bytes 442376 | tf_op jit(solution)/shard_map/ppermute | solution.py:64
  172.9 22.5 %collective-permute-start.49 = (bf16[64,2304]{1,0:T(8,128)(2,1)S(1)}, bf16[64,2304]{1,0:T(8,128)(2,1)S(1)}, u32[]{:S(2)}, u32[]{:S(2)}) collective-permute-start(bf16[64,2304]{1,0:T(8,128)(2,1)S(1)} %get-tuple-element.204.refs_0_), channel_id=1, source_target_pairs={{0,2},{1,3},{2,0},{3,1},{4,6},{5,7},{6,4},{7,5},{8,10},{9,11},{10,... | collective-permute-start | bytes 884744 | tf_op jit(solution)/shard_map/ppermute | solution.py:64
  222.9 14.4 %collective-permute-start.56 = (bf16[4,64,640]{2,1,0:T(8,128)(2,1)S(1)}, bf16[4,64,640]{2,1,0:T(8,128)(2,1)S(1)}, u32[]{:S(2)}, u32[]{:S(2)}) collective-permute-start(bf16[4,64,640]{2,1,0:T(8,128)(2,1)S(1)} %get-tuple-element.217.refs_2_), channel_id=1, source_target_pairs={{0,8},{8,0},{16,24},{24,16},{1,9},{9,1},{17,25},{25,17},{2,10},{10... | collective-permute-start | bytes 983048 | tf_op jit(solution)/shard_map/ppermute | solution.py:59
  224.1 13.9 %collective-permute-start.57 = (bf16[4,64,640]{2,1,0:T(8,128)(2,1)S(1)}, bf16[4,64,640]{2,1,0:T(8,128)(2,1)S(1)}, u32[]{:S(2)}, u32[]{:S(2)}) collective-permute-start(bf16[4,64,640]{2,1,0:T(8,128)(2,1)S(1)} %get-tuple-element.217.refs_2_), channel_id=1, source_target_pairs={{0,16},{8,24},{16,0},{24,8},{1,17},{9,25},{17,1},{25,9},{2,18},{10... | collective-permute-start | bytes 983048 | tf_op jit(solution)/shard_map/ppermute | solution.py:59
  225.2 12.8 %collective-permute-start.58 = (bf16[4,64,640]{2,1,0:T(8,128)(2,1)S(1)}, bf16[4,64,640]{2,1,0:T(8,128)(2,1)S(1)}, u32[]{:S(2)}, u32[]{:S(2)}) collective-permute-start(bf16[4,64,640]{2,1,0:T(8,128)(2,1)S(1)} %get-tuple-element.217.refs_2_), channel_id=1, source_target_pairs={{0,24},{8,16},{16,8},{24,0},{1,25},{9,17},{17,9},{25,1},{2,26},{10... | collective-permute-start | bytes 983048 | tf_op jit(solution)/shard_map/ppermute | solution.py:59
  238.7 16.2 %collective-permute-start.66 = (bf16[4,64,640]{2,1,0:T(8,128)(2,1)S(1)}, bf16[4,64,640]{2,1,0:T(8,128)(2,1)S(1)}, u32[]{:S(2)}, u32[]{:S(2)}) collective-permute-start(bf16[4,64,640]{2,1,0:T(8,128)(2,1)S(1)} %get-tuple-element.228.refs_2_), channel_id=1, source_target_pairs={{0,8},{8,0},{16,24},{24,16},{1,9},{9,1},{17,25},{25,17},{2,10},{10... | collective-permute-start | bytes 983048 | tf_op jit(solution)/shard_map/ppermute | solution.py:59
  239.7 16.8 %collective-permute-start.67 = (bf16[4,64,640]{2,1,0:T(8,128)(2,1)S(1)}, bf16[4,64,640]{2,1,0:T(8,128)(2,1)S(1)}, u32[]{:S(2)}, u32[]{:S(2)}) collective-permute-start(bf16[4,64,640]{2,1,0:T(8,128)(2,1)S(1)} %get-tuple-element.228.refs_2_), channel_id=1, source_target_pairs={{0,16},{8,24},{16,0},{24,8},{1,17},{9,25},{17,1},{25,9},{2,18},{10... | collective-permute-start | bytes 983048 | tf_op jit(solution)/shard_map/ppermute | solution.py:59
  240.5 15.9 %collective-permute-start.68 = (bf16[4,64,640]{2,1,0:T(8,128)(2,1)S(1)}, bf16[4,64,640]{2,1,0:T(8,128)(2,1)S(1)}, u32[]{:S(2)}, u32[]{:S(2)}) collective-permute-start(bf16[4,64,640]{2,1,0:T(8,128)(2,1)S(1)} %get-tuple-element.228.refs_2_), channel_id=1, source_target_pairs={{0,24},{8,16},{16,8},{24,0},{1,25},{9,17},{17,9},{25,1},{2,26},{10... | collective-permute-start | bytes 983048 | tf_op jit(solution)/shard_map/ppermute | solution.py:59
  242.2 27.4 %collective-permute-start.69 = (bf16[4,64,640]{2,1,0:T(8,128)(2,1)S(1)}, bf16[4,64,640]{2,1,0:T(8,128)(2,1)S(1)}, u32[]{:S(2)}, u32[]{:S(2)}) collective-permute-start(bf16[4,64,640]{2,1,0:T(8,128)(2,1)S(1)} %get-tuple-element.228.refs_2_), channel_id=1, source_target_pairs={{0,1},{1,0},{2,3},{3,2},{4,5},{5,4},{6,7},{7,6},{8,9},{9,8},{10,11... | collective-permute-start | bytes 983048 | tf_op jit(solution)/shard_map/ppermute | solution.py:64
  (106 other events, 812.6 us)

commit v6 on v5

--- a/solution.py
+++ b/solution.py
@@ -18,6 +18,7 @@
 LANES = 128
 HEAD_BLOCKS = 4
 GATE_MIB = 46
+DOWN_MIB = 46
 BF16 = jnp.bfloat16
 F32 = jnp.float32
 MIB = 1 << 20
@@ -107,7 +108,7 @@
     total = square_ref[...]
     lane = lax.broadcasted_iota(jnp.int32, (half, LANES), 1)
     keep[:, at : at + LANES] = jnp.where(lane < LANES // 2, total[:half], 0.0)
-    send[:, at : at + LANES] = split_square(total[half:])
+    send[:, at : at + LANES] = jnp.where(lane < LANES // 2, total[half:], 0.0)
 
 
 def qkv_kernel(unit, count, offsets, *refs):
@@ -120,7 +121,7 @@
         width = w.shape[1]
         part = jnp.dot(x, w[...], preferred_element_type=F32)
         keep[:, at : at + width] = part[:half]
-        send[:, at : at + width] = part[half:].astype(BF16)
+        send[:, at : at + width] = part[half:]
         at += width
     put_squares(square_ref, keep, send, at)
 
@@ -192,8 +193,11 @@
             scores = scores + mask
             weights = jnp.exp(scores - jnp.max(scores, axis=1, keepdims=True))
             total = jnp.sum(weights, axis=1, keepdims=True)
-            weights = (weights / total).astype(BF16)
-            result = jnp.dot(weights, v, preferred_element_type=F32).astype(BF16)
+            weights = weights / total
+            high = weights.astype(BF16)
+            low = (weights - high.astype(F32)).astype(BF16)
+            result = jnp.dot(high, v, preferred_element_type=F32)
+            result = (result + jnp.dot(low, v, preferred_element_type=F32)).astype(BF16)
             for h in range(group):
                 at = (g * group + h) * HEAD_DIM
                 for sub in range(0, block, row_unit):
@@ -207,8 +211,18 @@
 
 
 def arrange_kernel(unit, offsets, *refs):
-    blocks, (gain, out, square) = refs[:-3], refs[-3:]
-    assemble(offsets, blocks, gain, out, square, unit)
+    blocks, (gain, out, square_ref) = refs[:-3], refs[-3:]
+    inverse = 1.0 / gain[...]
+    step = 0
+    for block in blocks:
+        for first in range(0, block.shape[0], unit):
+            rows = block[first : first + unit, :]
+            place = pl.multiple_of(offsets[step], unit)
+            out[pl.ds(place, unit), :] = rows
+            plain = rows.astype(F32) * inverse
+            square = jnp.sum(plain * plain, axis=1, keepdims=True)
+            square_ref[pl.ds(place, unit), :] = jnp.broadcast_to(square, (unit, LANES))
+            step += 1
 
 
 def gate_up_kernel(squares, x, *refs):
@@ -220,18 +234,18 @@
         w = jnp.concatenate([w[0] for w in weights[i * count : (i + 1) * count]], axis=0)
         part = jnp.dot(x[...], w, preferred_element_type=F32)
         keep[base + i] = part[:half]
-        send[base + i] = part[half:].astype(BF16)
+        send[base + i] = part[half:]
     if squares:
 
         @pl.when(pl.program_id(0) == 0)
         def _():
             group = keep.shape[0] - 1
             keep[group] = jnp.zeros(keep.shape[1:], F32)
-            send[group] = jnp.zeros(send.shape[1:], BF16)
+            send[group] = jnp.zeros(send.shape[1:], F32)
             total = refs[-3][...]
             lane = lax.broadcasted_iota(jnp.int32, (half, LANES), 1)
             keep[group, :, :LANES] = jnp.where(lane < LANES // 2, total[:half], 0.0)
-            send[group, :, :LANES] = split_square(total[half:])
+            send[group, :, :LANES] = jnp.where(lane < LANES // 2, total[half:], 0.0)
 
 
 def halve_kernel(squares, keep, recv, kept, send):
@@ -283,9 +297,10 @@
     out[...] = (total * gain[...]).astype(BF16)
 
 
-def down_kernel(sources, count, unit, rows, offsets, *refs):
-    own, other, weights = refs[:count], refs[count : 2 * count], refs[2 * count : -rows - 1]
+def down_kernel(sources, count, added, unit, rows, offsets, *refs):
+    own, other, before = refs[:count], refs[count : 2 * count], refs[2 * count : 2 * count + added]
     outs, total = refs[-rows - 1 : -1], refs[-1]
+    weights = refs[2 * count + added : -rows - 1]
     tile = len(weights) * weights[0].shape[1]
     for i, (which, at) in enumerate(sources):
 
@@ -296,7 +311,11 @@
             )
             w = jnp.concatenate([w[0] for w in weights], axis=0)
             part = jnp.dot(hidden, w, preferred_element_type=F32)
-            total[...] = part if i == 0 else total[...] + part
+            if i > 0:
+                part = part + total[...]
+            elif added:
+                part = part + before[0][...]
+            total[...] = part
 
     @pl.when(pl.program_id(0) == len(sources) - 1)
     def _():
@@ -446,7 +465,7 @@
     wide = qkv_width + LANES
     keep, send = pl.pallas_call(
         functools.partial(qkv_kernel, col_tokens, row_count),
-        out_shape=[shape((half, wide), F32), shape((half, wide), BF16)],
+        out_shape=[shape((half, wide), F32)] * 2,
         in_specs=[SMEM] + [VMEM] * (row_count + 4),
         out_specs=[VMEM] * 2,
         scratch_shapes=[pltpu.VMEM((tokens, features), BF16), pltpu.VMEM((tokens, LANES), F32)],
@@ -500,10 +519,10 @@
     )(places, row_rel * row_tokens, *pieces, bias, w_out)
     projected = [projected[0]] + [row_xor(projected[j], j) for j in range(1, row_count)]
     stream = residual.astype(F32) + tree_sum([p.astype(F32) for p in projected])
-    stream = lax.optimization_barrier(stream.astype(BF16))
+    scaled_stream = (stream * mlp_gain[None, :]).astype(BF16)
 
     levels = (col_count - 1).bit_length()
-    blocks = [stream] + [row_xor(stream, j) for j in range(1, row_count)]
+    blocks = [scaled_stream] + [row_xor(scaled_stream, j) for j in range(1, row_count)]
     position = sum(((relative >> level) & 1) << (levels - 1 - level) for level in range(levels))
     half_offsets = position * col_tokens
     token = [mlp_gain]
@@ -527,7 +546,9 @@
     tiles = ff_local // tile
     sub = tile // 3 if tile % (3 * LANES) == 0 else tile
     subs = tile // sub
-    plan = [(0, 0, 1), (0, 1, 2), (1, 0, 2), (1, 2, 1)] if divisible else [(0, 0, 1), (1, 0, 1)]
+    plan = [(0, 0, 1), (1, 0, 1)]
+    if divisible:
+        plan = [(0, 0, 1), (0, 1, 2), (1, 0, 2), (1, 2, 1)]
     last = levels - 1
     keeps, arrivals, hiddens = {}, {}, {}
     scale = []
@@ -553,7 +574,7 @@
             [whole] + weights * 2 + [pl.BlockSpec((tokens, LANES), lambda i: (0, 0))] * squared,
             token,
             grid=(count * subs,),
-            out_shape=[shape((groups, half, sub), F32), shape((groups, half, sub), BF16)],
+            out_shape=[shape((groups, half, sub), F32)] * 2,
             out_specs=[out] * 2,
             compiler_params=params(GATE_MIB),
             cost_estimate=cost(4 * tokens * features * tile * count, 4 * tile * count * features),
@@ -619,35 +640,53 @@
         )
         hiddens[j] = (joined, col_xor(joined, 1 << level))
 
-    def down(member):
-        which = [j for j in range(len(plan)) if plan[j][0] == member]
+    partial = {0: [], 1: []}
+    summed = {0: [], 1: []}
+
+    def down(member, early=False):
+        which = [j for j in range(len(plan)) if plan[j][0] == member and j not in summed[member]]
+        if early:
+            which = which[:1]
+            summed[member] = which
         own = [hiddens[j][0] for j in which]
         other = [hiddens[j][1] for j in which]
         sources = [(k, i * tile) for k, j in enumerate(which) for i in range(plan[j][2])]
+        first = plan[which[0]][1]
+        before = partial[member]
+        count = len(which)
+        rows = 0 if early else row_count
+        sum_spec = pl.BlockSpec((tokens, features), lambda i: (0, 0))
+        sum_shape = shape((tokens, features), F32)
+        row_shapes = [
+            shape((row_tokens, features), F32 if i == 0 else BF16) for i in range(row_count)
+        ]
         parts = call(
-            functools.partial(down_kernel, sources, len(own), col_tokens, row_count),
-            [half_offsets, *own, *other] + [w_down] * 3,
+            functools.partial(down_kernel, sources, count, len(before), col_tokens, rows),
+            [half_offsets, *own, *other, *before] + [w_down] * 3,
             [SMEM]
             + [pl.BlockSpec(array.shape, lambda i: (0, 0)) for array in own + other]
+            + [sum_spec] * len(before)
             + [
-                pl.BlockSpec((1, tile // 3, features), lambda i, q=q: (member, 3 * i + q, 0))
+                pl.BlockSpec((1, tile // 3, features), lambda i, q=q: (member, 3 * (first + i) + q, 0))
                 for q in range(3)
             ],
             token,
-            grid=(tiles,),
-            out_shape=[
-                shape((row_tokens, features), F32 if i == 0 else BF16)
-                for i in range(row_count)
-            ],
-            out_specs=[pl.BlockSpec((row_tokens, features), lambda i: (0, 0))] * row_count,
-            scratch_shapes=[pltpu.VMEM((tokens, features), F32)],
-            compiler_params=params(56),
+            grid=(len(sources),),
+            out_shape=[sum_shape] if early else row_shapes,
+            out_specs=[sum_spec]
+            if early
+            else [pl.BlockSpec((row_tokens, features), lambda i: (0, 0))] * row_count,
+            scratch_shapes=[] if early else [pltpu.VMEM((tokens, features), F32)],
+            compiler_params=params(DOWN_MIB),
             cost_estimate=cost(
                 2 * tokens * features * ff_local, 2 * ff_local * (features + tokens)
             ),
             name="down",
         )
-        states[member] = [parts[0]] + [row_xor(parts[j], j) for j in range(1, row_count)]
+        if early:
+            partial[member] = [parts[0]]
+        else:
+            states[member] = [parts[0]] + [row_xor(parts[j], j) for j in range(1, row_count)]
 
     def output(member):
         parts = states[member]
@@ -727,14 +766,18 @@
         )
         stats[member].append(result[:, :3].T)
 
-    if len(plan) == 4 and levels == 3:
+    early = (3 * vocab_tiles + 4) // 5
+    rest = vocab_tiles - early
+    if divisible and levels == 3 and rest > 0:
         schedule = [
             (gate_up, 0), (gate_up, 1), (halve, 0, 0), (gate_up, 2), (halve, 1, 0),
             (halve, 0, 1), (gate_up, 3), (halve, 2, 0), (hidden_of, 0), (halve, 1, 1),
-            (halve, 3, 0), (join, 0, 1), (gather_gain, 0), (hidden_of, 1), (halve, 2, 1),
-            (join, 0, 0), (join, 1, 1), (gather_gain, 1), (halve, 3, 1), (hidden_of, 2),
-            (join, 1, 0), (join, 2, 1), (gather_gain, 2), (ready,), (down, 0), (hidden_of, 3),
-            (join, 3, 1), (output, 0), (join, 2, 0), (join, 3, 0), (down, 1),
+            (join, 0, 1), (halve, 3, 0), (hidden_of, 1), (halve, 2, 1), (halve, 3, 1),
+            (join, 1, 1), (gather_gain, 0), (hidden_of, 2), (join, 1, 0), (join, 0, 0),
+            (gather_gain, 1), (hidden_of, 3), (join, 2, 1), (gather_gain, 2), (ready,),
+            (down, 0), (join, 3, 1), (join, 2, 0), (down, 1, True), (join, 3, 0), (down, 1),
+            (output, 0), (output, 1), (pack, 0), (pack, 1), (forward, 0), (head, 0, 0, early),
+            (forward, 1), (head, 0, early, rest), (head, 1, 0, vocab_tiles),
         ]
     else:
         schedule = []
@@ -742,13 +785,9 @@
             schedule += [(gate_up, j)] + [(halve, j, level) for level in range(last)]
             schedule += [(hidden_of, j)] + [(join, j, level) for level in range(last - 1, -1, -1)]
         schedule += [(gather_gain, level) for level in range(levels)] + [(ready,)]
-        schedule += [(down, 0), (output, 0), (down, 1)]
-    early = (3 * vocab_tiles + 4) // 5
-    schedule += [(output, 1), (pack, 0), (pack, 1), (forward, 0), (head, 0, 0, early)]
-    schedule += [(forward, 1)]
-    if early < vocab_tiles:
-        schedule += [(head, 0, early, vocab_tiles - early)]
-    schedule += [(head, 1, 0, vocab_tiles)]
+        schedule += [(down, 0), (output, 0), (down, 1), (output, 1), (pack, 0), (pack, 1)]
+        schedule += [(forward, 0), (forward, 1), (head, 0, 0, vocab_tiles)]
+        schedule += [(head, 1, 0, vocab_tiles)]
     for step, *arguments in schedule:
         step(*arguments)
 

time: 308 us -> 303 us (0.984)
  starting transfers between devices: 72.4 us -> 82.8 us
  waiting for transfers between devices: 136 us -> 128 us
  local copies, waits for them, and re-layouts: 15.6 us -> 10.3 us
    ppermute x55, starting transfers between devices: 44.8 us -> 55.1 us  [col_xor(): return lax.ppermute(x, 'col', [(i, i ^ mask) for i in range(count)])]
    ppermute x55, waiting for transfers between devices: 119 us -> 111 us  [col_xor(): return lax.ppermute(x, 'col', [(i, i ^ mask) for i in range(count)])]
    unnamed x105 -> x73, local copies, waits for them, and re-layouts: 10.9 us -> 4.72 us
    pallas_call x34 -> x35, Pallas kernels: 71.2 us -> 69.1 us  [call(): pl.pallas_call(body, in_specs=in_specs + [ANY], out_shape=out_shape + [ja...]
  transfers between devices with their start and end apart: 78 -> 78, of which waited for: 44 -> 40; matrix products, arithmetic and copies ran while one was open for 2% -> 2% of each run, Pallas kernels for 15% -> 16%
where the time goes in v6:
time: 303 us; the launch traced here: 302 us
  waiting for transfers between devices  128 us (42%)
  starting transfers between devices  82.8 us (27%)
  Pallas kernels  76.7 us (25%)
  local copies, waits for them, and re-layouts  10.3 us (3%)
    ppermute x55, waiting for transfers between devices, col_xor(): return lax.ppermute(x, 'col', [(i, i ^ mask) for i in range(count)])  111 us
    pallas_call x35, Pallas kernels, call(): pl.pallas_call(body, in_specs=in_specs + [ANY], out_shape=out_shape + [ja...  69.1 us
    ppermute x55, starting transfers between devices, col_xor(): return lax.ppermute(x, 'col', [(i, i ^ mask) for i in range(count)])  55.1 us
    ppermute x23, starting transfers between devices, row_xor(): return lax.ppermute(x, 'row', [(i, i ^ mask) for i in range(count)])  27.6 us
    ppermute x23, waiting for transfers between devices, row_xor(): return lax.ppermute(x, 'row', [(i, i ^ mask) for i in range(count)])  16.1 us
  transfers between devices with their start and end apart: 78, of which 40 were waited for; matrix products, arithmetic and copies ran while one was open for 2% of the time, Pallas kernels for 16%

profile of v6, /device:TPU:0, one launch (start us, length us, event | category | flops | bytes accessed | tf_op | source)
XLA Modules:
  0.0 302.0 jit_solution(15475431184857638748)
XLA Ops:
  0.0 2.9 collective-permute-start
  10.6 3.9 %qkv_partial.1 = (f32[128,1920]{1,0:T(8,128)}, f32[128,1920]{1,0:T(8,128)}) custom-call(s32[8]{0:T(128)} %reshape.113.offsets, bf16[64,640]{1,0:T(8,128)(2,1)} %refs_0_.1, bf16[64,640]{1,0:T(8,128)(2,1)} %copy-done.27, bf16[64,640]{1,0:T(8,128)(2,1)} %copy-done.28, bf16[64,640]{1,0:T(8,128)(2,1)} %copy-done.29, f32[1,640]{1,0:T(1,128)} %broadcast_in_dim.29.refs_4_, ...), custom_call_target="tpu_custom_call" | custom-call | flops 1 | bytes 1 | tf_op jit(solution)/shard_map/qkv_partial/pallas_call | solution.py:466
  25.8 6.9 %collective-permute-done.5.refs_2_ = bf16[32,1920]{1,0:T(8,128)(2,1)S(1)} collective-permute-done((bf16[32,1920]{1,0:T(8,128)(2,1)S(1)}, bf16[32,1920]{1,0:T(8,128)(2,1)S(1)}, u32[]{:S(2)}, u32[]{:S(2)}) %collective-permute-start.5) | collective-permute-done | bytes 122912 | tf_op jit(solution)/shard_map/ppermute | solution.py:65
  39.0 7.0 %collective-permute-done.8.refs_2_ = bf16[32,1792]{1,0:T(8,128)(2,1)S(1)} collective-permute-done((bf16[32,1792]{1,0:T(8,128)(2,1)S(1)}, bf16[32,1792]{1,0:T(8,128)(2,1)S(1)}, u32[]{:S(2)}, u32[]{:S(2)}) %collective-permute-start.8) | collective-permute-done | bytes 114720 | tf_op jit(solution)/shard_map/ppermute | solution.py:65
  47.5 3.3 %attention_out.1 = (f32[64,640]{1,0:T(8,128)S(1)}, bf16[64,640]{1,0:T(8,128)(2,1)S(1)}, bf16[64,640]{1,0:T(8,128)(2,1)S(1)}, bf16[64,640]{1,0:T(8,128)(2,1)S(1)}) custom-call(s32[8]{0:T(128)S(1)} %xor_multiply_fusion.places, s32[4]{0:T(128)S(1)} %fusion.43.row_places.refs_3_, bf16[32,1792]{1,0:T(8,128)(2,1)S(1)} %qkv_rope.1.refs_0_, ...), custom_call_target="tpu_custom_call" | custom-call | flops 1 | bytes 1 | tf_op jit(solution)/shard_map/attention_out/pallas_call | solution.py:503
  66.7 3.9 %gate_up.4 = (f32[7,128,384]{2,1,0:T(8,128)S(1)}, f32[7,128,384]{2,1,0:T(8,128)S(1)}, f32[8,128]{1,0:T(8,128)S(1)}) custom-call(bf16[256,640]{1,0:T(8,128)(2,1)S(1)} %get-tuple-element.133.refs_0_, bf16[2,640,3456]{2,1,0:T(8,128)(2,1)} %refs_2_.7, bf16[2,640,3456]{2,1,0:T(8,128)(2,1)} %refs_2_.7, bf16[2,640,3456]{2,1,0:T(8,128)(2,1)} %refs_4_.9, ...), custom_call_target="tpu_custom_call" | custom-call | flops 1 | bytes 1 | tf_op jit(solution)/shard_map/gate_up/pallas_call | solution.py:47
  70.8 6.2 %gate_up.5 = (f32[12,128,384]{2,1,0:T(8,128)S(1)}, f32[12,128,384]{2,1,0:T(8,128)S(1)}, f32[8,128]{1,0:T(8,128)S(1)}) custom-call(bf16[256,640]{1,0:T(8,128)(2,1)S(1)} %get-tuple-element.133.refs_0_, bf16[2,640,3456]{2,1,0:T(8,128)(2,1)} %refs_2_.7, bf16[2,640,3456]{2,1,0:T(8,128)(2,1)} %refs_2_.7, bf16[2,640,3456]{2,1,0:T(8,128)(2,1)} %refs_4_.9, ...), custom_call_target="tpu_custom_call" | custom-call | flops 1 | bytes 1 | tf_op jit(solution)/shard_map/gate_up/pallas_call | solution.py:47
  77.7 6.2 %gate_up.6 = (f32[12,128,384]{2,1,0:T(8,128)S(1)}, f32[12,128,384]{2,1,0:T(8,128)S(1)}, f32[8,128]{1,0:T(8,128)S(1)}) custom-call(bf16[256,640]{1,0:T(8,128)(2,1)S(1)} %get-tuple-element.133.refs_0_, bf16[2,640,3456]{2,1,0:T(8,128)(2,1)} %refs_2_.7, bf16[2,640,3456]{2,1,0:T(8,128)(2,1)} %refs_2_.7, bf16[2,640,3456]{2,1,0:T(8,128)(2,1)} %refs_4_.9, ...), custom_call_target="tpu_custom_call" | custom-call | flops 1 | bytes 1 | tf_op jit(solution)/shard_map/gate_up/pallas_call | solution.py:47
  85.8 8.6 %collective-permute-done.23.refs_1_ = bf16[7,64,384]{2,1,0:T(8,128)(2,1)S(1)} collective-permute-done((bf16[7,64,384]{2,1,0:T(8,128)(2,1)S(1)}, bf16[7,64,384]{2,1,0:T(8,128)(2,1)S(1)}, u32[]{:S(2)}, u32[]{:S(2)}) %collective-permute-start.23) | collective-permute-done | bytes 344096 | tf_op jit(solution)/shard_map/ppermute | solution.py:65
  94.5 3.8 %gate_up.7 = (f32[6,128,384]{2,1,0:T(8,128)S(1)}, f32[6,128,384]{2,1,0:T(8,128)S(1)}, f32[8,128]{1,0:T(8,128)S(1)}) custom-call(bf16[256,640]{1,0:T(8,128)(2,1)S(1)} %get-tuple-element.133.refs_0_, bf16[2,640,3456]{2,1,0:T(8,128)(2,1)} %refs_2_.7, bf16[2,640,3456]{2,1,0:T(8,128)(2,1)} %refs_2_.7, bf16[2,640,3456]{2,1,0:T(8,128)(2,1)} %refs_4_.9, ...), custom_call_target="tpu_custom_call" | custom-call | flops 1 | bytes 1 | tf_op jit(solution)/shard_map/gate_up/pallas_call | solution.py:47
  103.1 14.1 %collective-permute-done.24.refs_1_ = bf16[7,32,384]{2,1,0:T(8,128)(2,1)S(1)} collective-permute-done((bf16[7,32,384]{2,1,0:T(8,128)(2,1)S(1)}, bf16[7,32,384]{2,1,0:T(8,128)(2,1)S(1)}, u32[]{:S(2)}, u32[]{:S(2)}) %collective-permute-start.24) | collective-permute-done | bytes 172064 | tf_op jit(solution)/shard_map/ppermute | solution.py:65
  121.3 15.9 %collective-permute-done.28.refs_1_ = bf16[32,1152]{1,0:T(8,128)(2,1)S(1)} collective-permute-done((bf16[32,1152]{1,0:T(8,128)(2,1)S(1)}, bf16[32,1152]{1,0:T(8,128)(2,1)S(1)}, u32[]{:S(2)}, u32[]{:S(2)}) %collective-permute-start.28) | collective-permute-done | bytes 73760 | tf_op jit(solution)/shard_map/ppermute | solution.py:65
  137.4 3.4 %collective-permute-start.30 = (bf16[6,64,384]{2,1,0:T(8,128)(2,1)S(1)}, bf16[6,64,384]{2,1,0:T(8,128)(2,1)S(1)}, u32[]{:S(2)}, u32[]{:S(2)}) collective-permute-start(bf16[6,64,384]{2,1,0:T(8,128)(2,1)S(1)} %get-tuple-element.168), channel_id=1, source_target_pairs={{0,2},{1,3},{2,0},{3,1},{4,6},{5,7},{6,4},{7,5},{8,10},{9,11},{10,... | collective-permute-start | bytes 884744 | tf_op jit(solution)/shard_map/ppermute | solution.py:65
  144.2 8.4 %collective-permute-done.30.refs_1_ = bf16[6,64,384]{2,1,0:T(8,128)(2,1)S(1)} collective-permute-done((bf16[6,64,384]{2,1,0:T(8,128)(2,1)S(1)}, bf16[6,64,384]{2,1,0:T(8,128)(2,1)S(1)}, u32[]{:S(2)}, u32[]{:S(2)}) %collective-permute-start.30) | collective-permute-done | bytes 294944 | tf_op jit(solution)/shard_map/ppermute | solution.py:65
  157.2 7.5 %collective-permute-done.35.refs_1_ = bf16[12,32,384]{2,1,0:T(8,128)(2,1)S(1)} collective-permute-done((bf16[12,32,384]{2,1,0:T(8,128)(2,1)S(1)}, bf16[12,32,384]{2,1,0:T(8,128)(2,1)S(1)}, u32[]{:S(2)}, u32[]{:S(2)}) %collective-permute-start.35) | collective-permute-done | bytes 294944 | tf_op jit(solution)/shard_map/ppermute | solution.py:65
  164.9 5.2 %collective-permute-done.34.refs_1_ = bf16[64,2304]{1,0:T(8,128)(2,1)S(1)} collective-permute-done((bf16[64,2304]{1,0:T(8,128)(2,1)S(1)}, bf16[64,2304]{1,0:T(8,128)(2,1)S(1)}, u32[]{:S(2)}, u32[]{:S(2)}) %collective-permute-start.34) | collective-permute-done | bytes 294944 | tf_op jit(solution)/shard_map/ppermute | solution.py:65
  173.9 6.8 %collective-permute-done.37.refs_1_ = bf16[32,2304]{1,0:T(8,128)(2,1)S(1)} collective-permute-done((bf16[32,2304]{1,0:T(8,128)(2,1)S(1)}, bf16[32,2304]{1,0:T(8,128)(2,1)S(1)}, u32[]{:S(2)}, u32[]{:S(2)}) %collective-permute-start.37) | collective-permute-done | bytes 147488 | tf_op jit(solution)/shard_map/ppermute | solution.py:65
  184.1 3.3 %collective-permute-done.39 = f32[4,640]{1,0:T(4,128)S(1)} collective-permute-done((f32[4,640]{1,0:T(4,128)S(1)}, f32[4,640]{1,0:T(4,128)S(1)}, u32[]{:S(2)}, u32[]{:S(2)}) %collective-permute-start.39) | collective-permute-done | bytes 10272 | tf_op jit(solution)/shard_map/ppermute | solution.py:65
  187.5 4.1 %down.3 = (f32[64,640]{1,0:T(8,128)S(1)}, bf16[64,640]{1,0:T(8,128)(2,1)S(1)}, bf16[64,640]{1,0:T(8,128)(2,1)S(1)}, bf16[64,640]{1,0:T(8,128)(2,1)S(1)}, f32[8,128]{1,0:T(8,128)S(1)}) custom-call(s32[8]{0:T(128)S(1)} %reshape.117.refs_0_, bf16[128,1152]{1,0:T(8,128)(2,1)S(1)} %get-tuple-element.195.refs_1_, ...), custom_call_target="tpu_custom_call" | custom-call | flops 1 | bytes 1 | tf_op jit(solution)/shard_map/down/pallas_call | solution.py:47
  213.3 4.7 %collective-permute-done.51.refs_2_ = bf16[64,640]{1,0:T(8,128)(2,1)S(1)} collective-permute-done((bf16[64,640]{1,0:T(8,128)(2,1)S(1)}, bf16[64,640]{1,0:T(8,128)(2,1)S(1)}, u32[]{:S(2)}, u32[]{:S(2)}) %collective-permute-start.51) | collective-permute-done | bytes 81952 | tf_op jit(solution)/shard_map/ppermute | solution.py:65
  237.8 11.8 %head.3 = (f32[256,128]{1,0:T(8,128)}, f32[8,128]{1,0:T(8,128)}) custom-call(s32[8]{0:T(128)} %copy-done.14, s32[4]{0:T(128)} %copy-done.13, bf16[4,64,640]{2,1,0:T(8,128)(2,1)} %copy-done.5, bf16[4,64,640]{2,1,0:T(8,128)(2,1)} %copy-done.1, bf16[4,64,640]{2,1,0:T(8,128)(2,1)} %copy-done.2, bf16[4,64,640]{2,1,0:T(8,128)(2,1)} %copy-done.3, ...), custom_call_target="tpu_custom_call" | custom-call | flops 1 | bytes 1 | tf_op jit(solution)/shard_map/head/pallas_call | solution.py:47
  252.6 9.3 %head.4 = (f32[256,128]{1,0:T(8,128)}, f32[8,128]{1,0:T(8,128)}) custom-call(s32[8]{0:T(128)} %copy-done.14, s32[4]{0:T(128)} %copy-done.13, bf16[4,64,640]{2,1,0:T(8,128)(2,1)} %copy-done.5, bf16[4,64,640]{2,1,0:T(8,128)(2,1)} %copy-done.1, bf16[4,64,640]{2,1,0:T(8,128)(2,1)} %copy-done.2, bf16[4,64,640]{2,1,0:T(8,128)(2,1)} %copy-done.3, ...), custom_call_target="tpu_custom_call" | custom-call | flops 1 | bytes 1 | tf_op jit(solution)/shard_map/head/pallas_call | solution.py:47
  266.6 15.9 %head.5 = (f32[256,128]{1,0:T(8,128)}, f32[8,128]{1,0:T(8,128)}) custom-call(s32[8]{0:T(128)} %copy-done.14, s32[4]{0:T(128)} %copy-done.13, bf16[4,64,640]{2,1,0:T(8,128)(2,1)} %copy-done.11, bf16[4,64,640]{2,1,0:T(8,128)(2,1)} %copy-done.6, bf16[4,64,640]{2,1,0:T(8,128)(2,1)} %copy-done.7, bf16[4,64,640]{2,1,0:T(8,128)(2,1)} %copy-done.8, ...), custom_call_target="tpu_custom_call" | custom-call | flops 1 | bytes 1 | tf_op jit(solution)/shard_map/head/pallas_call | solution.py:47
  289.1 3.0 %collective-permute-start.75 = (f32[3,2,256]{2,1,0:T(2,128)S(1)}, f32[3,2,256]{2,1,0:T(2,128)S(1)}, u32[]{:S(2)}, u32[]{:S(2)}) collective-permute-start(f32[3,2,256]{2,1,0:T(2,128)S(1)} %pad_maximum_fusion.6), channel_id=1, source_target_pairs={{0,4},{1,5},{2,6},{3,7},{4,0},{5,1},{6,2},{7,3},{8,12},{9,13},{10,... | collective-permute-start | bytes 18440 | tf_op jit(solution)/shard_map/ppermute | solution.py:65
  (305 shorter events, 134.8 us)
Async XLA Ops:
  20.3 12.4 %collective-permute-start.5 = (bf16[32,1920]{1,0:T(8,128)(2,1)S(1)}, bf16[32,1920]{1,0:T(8,128)(2,1)S(1)}, u32[]{:S(2)}, u32[]{:S(2)}) collective-permute-start(bf16[32,1920]{1,0:T(8,128)(2,1)S(1)} %get-tuple-element.127), channel_id=1, source_target_pairs={{0,4},{1,5},{2,6},{3,7},{4,0},{5,1},{6,2},{7,3},{8,12},{9,13},{10,... | collective-permute-start | bytes 368648 | tf_op jit(solution)/shard_map/ppermute | solution.py:65
  83.8 17.2 %collective-permute-start.25 = (f32[12,128,384]{2,1,0:T(8,128)S(1)}, f32[12,128,384]{2,1,0:T(8,128)S(1)}, u32[]{:S(2)}, u32[]{:S(2)}) collective-permute-start(f32[12,128,384]{2,1,0:T(8,128)S(1)} %get-tuple-element.152), channel_id=1, source_target_pairs={{0,1},{1,0},{2,3},{3,2},{4,5},{5,4},{6,7},{7,6},{8,9},{9,8},{10,11... | collective-permute-start | bytes 7077896 | tf_op jit(solution)/shard_map/ppermute | solution.py:65
  98.3 39.0 %collective-permute-start.27 = (f32[6,128,384]{2,1,0:T(8,128)S(1)}, f32[6,128,384]{2,1,0:T(8,128)S(1)}, u32[]{:S(2)}, u32[]{:S(2)}) collective-permute-start(f32[6,128,384]{2,1,0:T(8,128)S(1)} %get-tuple-element.161), channel_id=1, source_target_pairs={{0,1},{1,0},{2,3},{3,2},{4,5},{5,4},{6,7},{7,6},{8,9},{9,8},{10,11... | collective-permute-start | bytes 3538952 | tf_op jit(solution)/shard_map/ppermute | solution.py:65
  98.3 19.9 %collective-permute-start.22 = (bf16[12,64,384]{2,1,0:T(8,128)(2,1)S(1)}, bf16[12,64,384]{2,1,0:T(8,128)(2,1)S(1)}, u32[]{:S(2)}, u32[]{:S(2)}) collective-permute-start(bf16[12,64,384]{2,1,0:T(8,128)(2,1)S(1)} %get-tuple-element.145), channel_id=1, source_target_pairs={{0,2},{1,3},{2,0},{3,1},{4,6},{5,7},{6,4},{7,5},{8,10},{9,11},{10,... | collective-permute-start | bytes 1769480 | tf_op jit(solution)/shard_map/ppermute | solution.py:65
  99.8 17.3 %collective-permute-start.24 = (bf16[7,32,384]{2,1,0:T(8,128)(2,1)S(1)}, bf16[7,32,384]{2,1,0:T(8,128)(2,1)S(1)}, u32[]{:S(2)}, u32[]{:S(2)}) collective-permute-start(bf16[7,32,384]{2,1,0:T(8,128)(2,1)S(1)} %get-tuple-element.150), channel_id=1, source_target_pairs={{0,4},{1,5},{2,6},{3,7},{4,0},{5,1},{6,2},{7,3},{8,12},{9,13},{10,... | collective-permute-start | bytes 516104 | tf_op jit(solution)/shard_map/ppermute | solution.py:65
  101.3 39.9 %collective-permute-start.31 = (bf16[12,64,384]{2,1,0:T(8,128)(2,1)S(1)}, bf16[12,64,384]{2,1,0:T(8,128)(2,1)S(1)}, u32[]{:S(2)}, u32[]{:S(2)}) collective-permute-start(bf16[12,64,384]{2,1,0:T(8,128)(2,1)S(1)} %get-tuple-element.170), channel_id=1, source_target_pairs={{0,2},{1,3},{2,0},{3,1},{4,6},{5,7},{6,4},{7,5},{8,10},{9,11},{10,... | collective-permute-start | bytes 1769480 | tf_op jit(solution)/shard_map/ppermute | solution.py:65
  118.4 22.5 %collective-permute-start.26 = (bf16[12,32,384]{2,1,0:T(8,128)(2,1)S(1)}, bf16[12,32,384]{2,1,0:T(8,128)(2,1)S(1)}, u32[]{:S(2)}, u32[]{:S(2)}) collective-permute-start(bf16[12,32,384]{2,1,0:T(8,128)(2,1)S(1)} %get-tuple-element.158), channel_id=1, source_target_pairs={{0,4},{1,5},{2,6},{3,7},{4,0},{5,1},{6,2},{7,3},{8,12},{9,13},{10,... | collective-permute-start | bytes 884744 | tf_op jit(solution)/shard_map/ppermute | solution.py:65
  121.0 16.3 %collective-permute-start.28 = (bf16[32,1152]{1,0:T(8,128)(2,1)S(1)}, bf16[32,1152]{1,0:T(8,128)(2,1)S(1)}, u32[]{:S(2)}, u32[]{:S(2)}) collective-permute-start(bf16[32,1152]{1,0:T(8,128)(2,1)S(1)} %get-tuple-element.162.refs_0_), channel_id=1, source_target_pairs={{0,4},{1,5},{2,6},{3,7},{4,0},{5,1},{6,2},{7,3},{8,12},{9,13},{10,... | collective-permute-start | bytes 221192 | tf_op jit(solution)/shard_map/ppermute | solution.py:65
  137.4 15.2 %collective-permute-start.30 = (bf16[6,64,384]{2,1,0:T(8,128)(2,1)S(1)}, bf16[6,64,384]{2,1,0:T(8,128)(2,1)S(1)}, u32[]{:S(2)}, u32[]{:S(2)}) collective-permute-start(bf16[6,64,384]{2,1,0:T(8,128)(2,1)S(1)} %get-tuple-element.168), channel_id=1, source_target_pairs={{0,2},{1,3},{2,0},{3,1},{4,6},{5,7},{6,4},{7,5},{8,10},{9,11},{10,... | collective-permute-start | bytes 884744 | tf_op jit(solution)/shard_map/ppermute | solution.py:65
  141.0 11.7 %collective-permute-start.29 = (bf16[32,2304]{1,0:T(8,128)(2,1)S(1)}, bf16[32,2304]{1,0:T(8,128)(2,1)S(1)}, u32[]{:S(2)}, u32[]{:S(2)}) collective-permute-start(bf16[32,2304]{1,0:T(8,128)(2,1)S(1)} %get-tuple-element.166.refs_0_), channel_id=1, source_target_pairs={{0,4},{1,5},{2,6},{3,7},{4,0},{5,1},{6,2},{7,3},{8,12},{9,13},{10,... | collective-permute-start | bytes 442376 | tf_op jit(solution)/shard_map/ppermute | solution.py:65
  141.3 23.4 %collective-permute-start.35 = (bf16[12,32,384]{2,1,0:T(8,128)(2,1)S(1)}, bf16[12,32,384]{2,1,0:T(8,128)(2,1)S(1)}, u32[]{:S(2)}, u32[]{:S(2)}) collective-permute-start(bf16[12,32,384]{2,1,0:T(8,128)(2,1)S(1)} %get-tuple-element.179), channel_id=1, source_target_pairs={{0,4},{1,5},{2,6},{3,7},{4,0},{5,1},{6,2},{7,3},{8,12},{9,13},{10,... | collective-permute-start | bytes 884744 | tf_op jit(solution)/shard_map/ppermute | solution.py:65
  152.7 17.3 %collective-permute-start.34 = (bf16[64,2304]{1,0:T(8,128)(2,1)S(1)}, bf16[64,2304]{1,0:T(8,128)(2,1)S(1)}, u32[]{:S(2)}, u32[]{:S(2)}) collective-permute-start(bf16[64,2304]{1,0:T(8,128)(2,1)S(1)} %get-tuple-element.177.refs_0_), channel_id=1, source_target_pairs={{0,2},{1,3},{2,0},{3,1},{4,6},{5,7},{6,4},{7,5},{8,10},{9,11},{10,... | collective-permute-start | bytes 884744 | tf_op jit(solution)/shard_map/ppermute | solution.py:65
  154.1 17.5 %collective-permute-start.33 = (bf16[64,1152]{1,0:T(8,128)(2,1)S(1)}, bf16[64,1152]{1,0:T(8,128)(2,1)S(1)}, u32[]{:S(2)}, u32[]{:S(2)}) collective-permute-start(bf16[64,1152]{1,0:T(8,128)(2,1)S(1)} %get-tuple-element.176.refs_0_), channel_id=1, source_target_pairs={{0,2},{1,3},{2,0},{3,1},{4,6},{5,7},{6,4},{7,5},{8,10},{9,11},{10,... | collective-permute-start | bytes 442376 | tf_op jit(solution)/shard_map/ppermute | solution.py:65
  154.8 15.4 %collective-permute-start.32 = (f32[1,640]{1,0:T(1,128)S(1)}, f32[1,640]{1,0:T(1,128)S(1)}, u32[]{:S(2)}, u32[]{:S(2)}) collective-permute-start(f32[1,640]{1,0:T(1,128)S(1)} %get-tuple-element.175), channel_id=1, source_target_pairs={{0,1},{1,0},{2,3},{3,2},{4,5},{5,4},{6,7},{7,6},{8,9},{9,8},{10,11... | collective-permute-start | bytes 7688 | tf_op jit(solution)/shard_map/ppermute | solution.py:65
  154.9 18.9 %collective-permute-start.38 = (bf16[6,32,384]{2,1,0:T(8,128)(2,1)S(1)}, bf16[6,32,384]{2,1,0:T(8,128)(2,1)S(1)}, u32[]{:S(2)}, u32[]{:S(2)}) collective-permute-start(bf16[6,32,384]{2,1,0:T(8,128)(2,1)S(1)} %get-tuple-element.187), channel_id=1, source_target_pairs={{0,4},{1,5},{2,6},{3,7},{4,0},{5,1},{6,2},{7,3},{8,12},{9,13},{10,... | collective-permute-start | bytes 442376 | tf_op jit(solution)/shard_map/ppermute | solution.py:65
  170.1 17.3 %collective-permute-start.41 = (bf16[128,2304]{1,0:T(8,128)(2,1)S(1)}, bf16[128,2304]{1,0:T(8,128)(2,1)S(1)}, u32[]{:S(2)}, u32[]{:S(2)}) collective-permute-start(bf16[128,2304]{1,0:T(8,128)(2,1)S(1)} %get-tuple-element.196.refs_2_), channel_id=1, source_target_pairs={{0,1},{1,0},{2,3},{3,2},{4,5},{5,4},{6,7},{7,6},{8,9},{9,8},{10,11... | collective-permute-start | bytes 1769480 | tf_op jit(solution)/shard_map/ppermute | solution.py:65
  173.8 13.7 %collective-permute-start.40 = (bf16[128,1152]{1,0:T(8,128)(2,1)S(1)}, bf16[128,1152]{1,0:T(8,128)(2,1)S(1)}, u32[]{:S(2)}, u32[]{:S(2)}) collective-permute-start(bf16[128,1152]{1,0:T(8,128)(2,1)S(1)} %get-tuple-element.195.refs_1_), channel_id=1, source_target_pairs={{0,1},{1,0},{2,3},{3,2},{4,5},{5,4},{6,7},{7,6},{8,9},{9,8},{10,11... | collective-permute-start | bytes 884744 | tf_op jit(solution)/shard_map/ppermute | solution.py:65
  218.1 14.4 %collective-permute-start.56 = (bf16[4,64,640]{2,1,0:T(8,128)(2,1)S(1)}, bf16[4,64,640]{2,1,0:T(8,128)(2,1)S(1)}, u32[]{:S(2)}, u32[]{:S(2)}) collective-permute-start(bf16[4,64,640]{2,1,0:T(8,128)(2,1)S(1)} %get-tuple-element.221.refs_2_), channel_id=1, source_target_pairs={{0,8},{8,0},{16,24},{24,16},{1,9},{9,1},{17,25},{25,17},{2,10},{10... | collective-permute-start | bytes 983048 | tf_op jit(solution)/shard_map/ppermute | solution.py:60
  219.1 13.6 %collective-permute-start.57 = (bf16[4,64,640]{2,1,0:T(8,128)(2,1)S(1)}, bf16[4,64,640]{2,1,0:T(8,128)(2,1)S(1)}, u32[]{:S(2)}, u32[]{:S(2)}) collective-permute-start(bf16[4,64,640]{2,1,0:T(8,128)(2,1)S(1)} %get-tuple-element.221.refs_2_), channel_id=1, source_target_pairs={{0,16},{8,24},{16,0},{24,8},{1,17},{9,25},{17,1},{25,9},{2,18},{10... | collective-permute-start | bytes 983048 | tf_op jit(solution)/shard_map/ppermute | solution.py:60
  220.0 12.8 %collective-permute-start.58 = (bf16[4,64,640]{2,1,0:T(8,128)(2,1)S(1)}, bf16[4,64,640]{2,1,0:T(8,128)(2,1)S(1)}, u32[]{:S(2)}, u32[]{:S(2)}) collective-permute-start(bf16[4,64,640]{2,1,0:T(8,128)(2,1)S(1)} %get-tuple-element.221.refs_2_), channel_id=1, source_target_pairs={{0,24},{8,16},{16,8},{24,0},{1,25},{9,17},{17,9},{25,1},{2,26},{10... | collective-permute-start | bytes 983048 | tf_op jit(solution)/shard_map/ppermute | solution.py:60
  233.4 17.1 %collective-permute-start.66 = (bf16[4,64,640]{2,1,0:T(8,128)(2,1)S(1)}, bf16[4,64,640]{2,1,0:T(8,128)(2,1)S(1)}, u32[]{:S(2)}, u32[]{:S(2)}) collective-permute-start(bf16[4,64,640]{2,1,0:T(8,128)(2,1)S(1)} %get-tuple-element.232.refs_2_), channel_id=1, source_target_pairs={{0,8},{8,0},{16,24},{24,16},{1,9},{9,1},{17,25},{25,17},{2,10},{10... | collective-permute-start | bytes 983048 | tf_op jit(solution)/shard_map/ppermute | solution.py:60
  234.5 16.8 %collective-permute-start.67 = (bf16[4,64,640]{2,1,0:T(8,128)(2,1)S(1)}, bf16[4,64,640]{2,1,0:T(8,128)(2,1)S(1)}, u32[]{:S(2)}, u32[]{:S(2)}) collective-permute-start(bf16[4,64,640]{2,1,0:T(8,128)(2,1)S(1)} %get-tuple-element.232.refs_2_), channel_id=1, source_target_pairs={{0,16},{8,24},{16,0},{24,8},{1,17},{9,25},{17,1},{25,9},{2,18},{10... | collective-permute-start | bytes 983048 | tf_op jit(solution)/shard_map/ppermute | solution.py:60
  235.4 15.9 %collective-permute-start.68 = (bf16[4,64,640]{2,1,0:T(8,128)(2,1)S(1)}, bf16[4,64,640]{2,1,0:T(8,128)(2,1)S(1)}, u32[]{:S(2)}, u32[]{:S(2)}) collective-permute-start(bf16[4,64,640]{2,1,0:T(8,128)(2,1)S(1)} %get-tuple-element.232.refs_2_), channel_id=1, source_target_pairs={{0,24},{8,16},{16,8},{24,0},{1,25},{9,17},{17,9},{25,1},{2,26},{10... | collective-permute-start | bytes 983048 | tf_op jit(solution)/shard_map/ppermute | solution.py:60
  236.9 27.5 %collective-permute-start.69 = (bf16[4,64,640]{2,1,0:T(8,128)(2,1)S(1)}, bf16[4,64,640]{2,1,0:T(8,128)(2,1)S(1)}, u32[]{:S(2)}, u32[]{:S(2)}) collective-permute-start(bf16[4,64,640]{2,1,0:T(8,128)(2,1)S(1)} %get-tuple-element.232.refs_2_), channel_id=1, source_target_pairs={{0,1},{1,0},{2,3},{3,2},{4,5},{5,4},{6,7},{7,6},{8,9},{9,8},{10,11... | collective-permute-start | bytes 983048 | tf_op jit(solution)/shard_map/ppermute | solution.py:65
  (90 other events, 737.5 us)

commit v7 on v6

--- a/solution.py
+++ b/solution.py
@@ -108,7 +108,7 @@
     total = square_ref[...]
     lane = lax.broadcasted_iota(jnp.int32, (half, LANES), 1)
     keep[:, at : at + LANES] = jnp.where(lane < LANES // 2, total[:half], 0.0)
-    send[:, at : at + LANES] = jnp.where(lane < LANES // 2, total[half:], 0.0)
+    send[:, at : at + LANES] = split_square(total[half:])
 
 
 def qkv_kernel(unit, count, offsets, *refs):
@@ -121,7 +121,7 @@
         width = w.shape[1]
         part = jnp.dot(x, w[...], preferred_element_type=F32)
         keep[:, at : at + width] = part[:half]
-        send[:, at : at + width] = part[half:]
+        send[:, at : at + width] = part[half:].astype(BF16)
         at += width
     put_squares(square_ref, keep, send, at)
 
@@ -234,18 +234,18 @@
         w = jnp.concatenate([w[0] for w in weights[i * count : (i + 1) * count]], axis=0)
         part = jnp.dot(x[...], w, preferred_element_type=F32)
         keep[base + i] = part[:half]
-        send[base + i] = part[half:]
+        send[base + i] = part[half:].astype(BF16)
     if squares:
 
         @pl.when(pl.program_id(0) == 0)
         def _():
             group = keep.shape[0] - 1
             keep[group] = jnp.zeros(keep.shape[1:], F32)
-            send[group] = jnp.zeros(send.shape[1:], F32)
+            send[group] = jnp.zeros(send.shape[1:], BF16)
             total = refs[-3][...]
             lane = lax.broadcasted_iota(jnp.int32, (half, LANES), 1)
             keep[group, :, :LANES] = jnp.where(lane < LANES // 2, total[:half], 0.0)
-            send[group, :, :LANES] = jnp.where(lane < LANES // 2, total[half:], 0.0)
+            send[group, :, :LANES] = split_square(total[half:])
 
 
 def halve_kernel(squares, keep, recv, kept, send):
@@ -465,7 +465,7 @@
     wide = qkv_width + LANES
     keep, send = pl.pallas_call(
         functools.partial(qkv_kernel, col_tokens, row_count),
-        out_shape=[shape((half, wide), F32)] * 2,
+        out_shape=[shape((half, wide), F32), shape((half, wide), BF16)],
         in_specs=[SMEM] + [VMEM] * (row_count + 4),
         out_specs=[VMEM] * 2,
         scratch_shapes=[pltpu.VMEM((tokens, features), BF16), pltpu.VMEM((tokens, LANES), F32)],
@@ -574,7 +574,7 @@
             [whole] + weights * 2 + [pl.BlockSpec((tokens, LANES), lambda i: (0, 0))] * squared,
             token,
             grid=(count * subs,),
-            out_shape=[shape((groups, half, sub), F32)] * 2,
+            out_shape=[shape((groups, half, sub), F32), shape((groups, half, sub), BF16)],
             out_specs=[out] * 2,
             compiler_params=params(GATE_MIB),
             cost_estimate=cost(4 * tokens * features * tile * count, 4 * tile * count * features),
@@ -766,18 +766,16 @@
         )
         stats[member].append(result[:, :3].T)
 
-    early = (3 * vocab_tiles + 4) // 5
-    rest = vocab_tiles - early
-    if divisible and levels == 3 and rest > 0:
+    if divisible and levels == 3:
         schedule = [
             (gate_up, 0), (gate_up, 1), (halve, 0, 0), (gate_up, 2), (halve, 1, 0),
             (halve, 0, 1), (gate_up, 3), (halve, 2, 0), (hidden_of, 0), (halve, 1, 1),
             (join, 0, 1), (halve, 3, 0), (hidden_of, 1), (halve, 2, 1), (halve, 3, 1),
             (join, 1, 1), (gather_gain, 0), (hidden_of, 2), (join, 1, 0), (join, 0, 0),
-            (gather_gain, 1), (hidden_of, 3), (join, 2, 1), (gather_gain, 2), (ready,),
-            (down, 0), (join, 3, 1), (join, 2, 0), (down, 1, True), (join, 3, 0), (down, 1),
-            (output, 0), (output, 1), (pack, 0), (pack, 1), (forward, 0), (head, 0, 0, early),
-            (forward, 1), (head, 0, early, rest), (head, 1, 0, vocab_tiles),
+            (gather_gain, 1), (hidden_of, 3), (join, 2, 1), (gather_gain, 2), (join, 3, 1),
+            (ready,), (down, 0), (join, 2, 0), (down, 1, True), (join, 3, 0), (down, 1),
+            (output, 0), (output, 1), (pack, 0), (pack, 1), (forward, 0),
+            (head, 0, 0, vocab_tiles), (forward, 1), (head, 1, 0, vocab_tiles),
         ]
     else:
         schedule = []

time: 303 us -> 288 us (0.950)
  waiting for transfers between devices: 128 us -> 122 us
  Pallas kernels: 76.7 us -> 71.4 us
    pallas_call x35 -> x34, Pallas kernels: 69.1 us -> 64 us  [call(): pl.pallas_call(body, in_specs=in_specs + [ANY], out_shape=out_shape + [ja...]
    ppermute x55, waiting for transfers between devices: 111 us -> 107 us  [col_xor(): return lax.ppermute(x, 'col', [(i, i ^ mask) for i in range(count)])]
  transfers between devices with their start and end apart: 78 -> 78, of which waited for: 40 -> 38; matrix products, arithmetic and copies ran while one was open for 2% -> 2% of each run, Pallas kernels for 16% -> 15%
where the time goes in v7:
time: 288 us
  waiting for transfers between devices  122 us (42%)
  starting transfers between devices  81.2 us (28%)
  Pallas kernels  71.4 us (25%)
  local copies, waits for them, and re-layouts  8.83 us (3%)
    ppermute x55, waiting for transfers between devices, col_xor(): return lax.ppermute(x, 'col', [(i, i ^ mask) for i in range(count)])  107 us
    pallas_call x34, Pallas kernels, call(): pl.pallas_call(body, in_specs=in_specs + [ANY], out_shape=out_shape + [ja...  64 us
    ppermute x55, starting transfers between devices, col_xor(): return lax.ppermute(x, 'col', [(i, i ^ mask) for i in range(count)])  53.3 us
    ppermute x23, starting transfers between devices, row_xor(): return lax.ppermute(x, 'row', [(i, i ^ mask) for i in range(count)])  27.9 us
    ppermute x23, waiting for transfers between devices, row_xor(): return lax.ppermute(x, 'row', [(i, i ^ mask) for i in range(count)])  14.8 us
  transfers between devices with their start and end apart: 78, of which 38 were waited for; matrix products, arithmetic and copies ran while one was open for 2% of the time, Pallas kernels for 15%

profile of v7, /device:TPU:0, one launch (start us, length us, event | category | flops | bytes accessed | tf_op | source)
XLA Modules:
  0.0 287.8 jit_solution(331919344864882739)
XLA Ops:
  0.0 2.9 %collective-permute-start = (bf16[64,640]{1,0:T(8,128)(2,1)}, bf16[64,640]{1,0:T(8,128)(2,1)S(1)}, u32[]{:S(2)}, u32[]{:S(2)}) collective-permute-start(bf16[64,640]{1,0:T(8,128)(2,1)} %refs_0_.1), channel_id=1, source_target_pairs={{0,8},{8,0},{16,24},{24,16},{1,9},{9,1},{17,25},{25,17},{2,10},{10... | collective-permute-start | bytes 245768 | tf_op jit(solution)/shard_map/ppermute | solution.py:60
  10.6 3.7 %qkv_partial.1 = (f32[128,1920]{1,0:T(8,128)}, bf16[128,1920]{1,0:T(8,128)(2,1)}) custom-call(s32[8]{0:T(128)} %reshape.113.offsets, bf16[64,640]{1,0:T(8,128)(2,1)} %refs_0_.1, bf16[64,640]{1,0:T(8,128)(2,1)} %copy-done.27, bf16[64,640]{1,0:T(8,128)(2,1)} %copy-done.28, bf16[64,640]{1,0:T(8,128)(2,1)} %copy-done.29, f32[1,640]{1,0:T(1,128)} %broadcast_in_dim.29.refs_4_, ...), custom_call_target="tpu_custom_call" | custom-call | flops 1 | bytes 1 | tf_op jit(solution)/shard_map/qkv_partial/pallas_call | solution.py:466
  24.9 6.9 %collective-permute-done.5.refs_2_ = bf16[32,1920]{1,0:T(8,128)(2,1)S(1)} collective-permute-done((bf16[32,1920]{1,0:T(8,128)(2,1)S(1)}, bf16[32,1920]{1,0:T(8,128)(2,1)S(1)}, u32[]{:S(2)}, u32[]{:S(2)}) %collective-permute-start.5) | collective-permute-done | bytes 122912 | tf_op jit(solution)/shard_map/ppermute | solution.py:65
  38.1 7.0 %collective-permute-done.8.refs_2_ = bf16[32,1792]{1,0:T(8,128)(2,1)S(1)} collective-permute-done((bf16[32,1792]{1,0:T(8,128)(2,1)S(1)}, bf16[32,1792]{1,0:T(8,128)(2,1)S(1)}, u32[]{:S(2)}, u32[]{:S(2)}) %collective-permute-start.8) | collective-permute-done | bytes 114720 | tf_op jit(solution)/shard_map/ppermute | solution.py:65
  46.6 3.3 %attention_out.1 = (f32[64,640]{1,0:T(8,128)S(1)}, bf16[64,640]{1,0:T(8,128)(2,1)S(1)}, bf16[64,640]{1,0:T(8,128)(2,1)S(1)}, bf16[64,640]{1,0:T(8,128)(2,1)S(1)}) custom-call(s32[8]{0:T(128)S(1)} %xor_multiply_fusion.places, s32[4]{0:T(128)S(1)} %fusion.43.row_places.refs_3_, bf16[32,1792]{1,0:T(8,128)(2,1)S(1)} %qkv_rope.1.refs_0_, ...), custom_call_target="tpu_custom_call" | custom-call | flops 1 | bytes 1 | tf_op jit(solution)/shard_map/attention_out/pallas_call | solution.py:503
  65.6 4.0 %gate_up.4 = (f32[7,128,384]{2,1,0:T(8,128)S(1)}, bf16[7,128,384]{2,1,0:T(8,128)(2,1)S(1)}, f32[8,128]{1,0:T(8,128)S(1)}) custom-call(bf16[256,640]{1,0:T(8,128)(2,1)S(1)} %get-tuple-element.131.refs_0_, bf16[2,640,3456]{2,1,0:T(8,128)(2,1)} %refs_2_.7, bf16[2,640,3456]{2,1,0:T(8,128)(2,1)} %refs_2_.7, bf16[2,640,3456]{2,1,0:T(8,128)(2,1)} %refs_4_.9, ...), custom_call_target="tpu_custom_call" | custom-call | flops 1 | bytes 1 | tf_op jit(solution)/shard_map/gate_up/pallas_call | solution.py:47
  69.6 6.2 %gate_up.5 = (f32[12,128,384]{2,1,0:T(8,128)S(1)}, bf16[12,128,384]{2,1,0:T(8,128)(2,1)S(1)}, f32[8,128]{1,0:T(8,128)S(1)}) custom-call(bf16[256,640]{1,0:T(8,128)(2,1)S(1)} %get-tuple-element.131.refs_0_, bf16[2,640,3456]{2,1,0:T(8,128)(2,1)} %refs_2_.7, bf16[2,640,3456]{2,1,0:T(8,128)(2,1)} %refs_2_.7, bf16[2,640,3456]{2,1,0:T(8,128)(2,1)} %refs_4_.9, ...), custom_call_target="tpu_custom_call" | custom-call | flops 1 | bytes 1 | tf_op jit(solution)/shard_map/gate_up/pallas_call | solution.py:47
  76.5 6.2 %gate_up.6 = (f32[12,128,384]{2,1,0:T(8,128)S(1)}, bf16[12,128,384]{2,1,0:T(8,128)(2,1)S(1)}, f32[8,128]{1,0:T(8,128)S(1)}) custom-call(bf16[256,640]{1,0:T(8,128)(2,1)S(1)} %get-tuple-element.131.refs_0_, bf16[2,640,3456]{2,1,0:T(8,128)(2,1)} %refs_2_.7, bf16[2,640,3456]{2,1,0:T(8,128)(2,1)} %refs_2_.7, bf16[2,640,3456]{2,1,0:T(8,128)(2,1)} %refs_4_.9, ...), custom_call_target="tpu_custom_call" | custom-call | flops 1 | bytes 1 | tf_op jit(solution)/shard_map/gate_up/pallas_call | solution.py:47
  85.3 8.5 %collective-permute-done.23.refs_1_ = bf16[7,64,384]{2,1,0:T(8,128)(2,1)S(1)} collective-permute-done((bf16[7,64,384]{2,1,0:T(8,128)(2,1)S(1)}, bf16[7,64,384]{2,1,0:T(8,128)(2,1)S(1)}, u32[]{:S(2)}, u32[]{:S(2)}) %collective-permute-start.23) | collective-permute-done | bytes 344096 | tf_op jit(solution)/shard_map/ppermute | solution.py:65
  93.8 3.8 %gate_up.7 = (f32[6,128,384]{2,1,0:T(8,128)S(1)}, bf16[6,128,384]{2,1,0:T(8,128)(2,1)S(1)}, f32[8,128]{1,0:T(8,128)S(1)}) custom-call(bf16[256,640]{1,0:T(8,128)(2,1)S(1)} %get-tuple-element.131.refs_0_, bf16[2,640,3456]{2,1,0:T(8,128)(2,1)} %refs_2_.7, bf16[2,640,3456]{2,1,0:T(8,128)(2,1)} %refs_2_.7, bf16[2,640,3456]{2,1,0:T(8,128)(2,1)} %refs_4_.9, ...), custom_call_target="tpu_custom_call" | custom-call | flops 1 | bytes 1 | tf_op jit(solution)/shard_map/gate_up/pallas_call | solution.py:47
  100.7 8.6 %collective-permute-done.24.refs_1_ = bf16[7,32,384]{2,1,0:T(8,128)(2,1)S(1)} collective-permute-done((bf16[7,32,384]{2,1,0:T(8,128)(2,1)S(1)}, bf16[7,32,384]{2,1,0:T(8,128)(2,1)S(1)}, u32[]{:S(2)}, u32[]{:S(2)}) %collective-permute-start.24) | collective-permute-done | bytes 172064 | tf_op jit(solution)/shard_map/ppermute | solution.py:65
  113.2 16.1 %collective-permute-done.28.refs_1_ = bf16[32,1152]{1,0:T(8,128)(2,1)S(1)} collective-permute-done((bf16[32,1152]{1,0:T(8,128)(2,1)S(1)}, bf16[32,1152]{1,0:T(8,128)(2,1)S(1)}, u32[]{:S(2)}, u32[]{:S(2)}) %collective-permute-start.28) | collective-permute-done | bytes 73760 | tf_op jit(solution)/shard_map/ppermute | solution.py:65
  129.5 3.5 %collective-permute-start.30 = (bf16[6,64,384]{2,1,0:T(8,128)(2,1)S(1)}, bf16[6,64,384]{2,1,0:T(8,128)(2,1)S(1)}, u32[]{:S(2)}, u32[]{:S(2)}) collective-permute-start(bf16[6,64,384]{2,1,0:T(8,128)(2,1)S(1)} %get-tuple-element.166), channel_id=1, source_target_pairs={{0,2},{1,3},{2,0},{3,1},{4,6},{5,7},{6,4},{7,5},{8,10},{9,11},{10,... | collective-permute-start | bytes 884744 | tf_op jit(solution)/shard_map/ppermute | solution.py:65
  133.4 3.0 %collective-permute-start.35 = (bf16[12,32,384]{2,1,0:T(8,128)(2,1)S(1)}, bf16[12,32,384]{2,1,0:T(8,128)(2,1)S(1)}, u32[]{:S(2)}, u32[]{:S(2)}) collective-permute-start(bf16[12,32,384]{2,1,0:T(8,128)(2,1)S(1)} %get-tuple-element.177), channel_id=1, source_target_pairs={{0,4},{1,5},{2,6},{3,7},{4,0},{5,1},{6,2},{7,3},{8,12},{9,13},{10,... | collective-permute-start | bytes 884744 | tf_op jit(solution)/shard_map/ppermute | solution.py:65
  136.3 8.3 %collective-permute-done.30.refs_1_ = bf16[6,64,384]{2,1,0:T(8,128)(2,1)S(1)} collective-permute-done((bf16[6,64,384]{2,1,0:T(8,128)(2,1)S(1)}, bf16[6,64,384]{2,1,0:T(8,128)(2,1)S(1)}, u32[]{:S(2)}, u32[]{:S(2)}) %collective-permute-start.30) | collective-permute-done | bytes 294944 | tf_op jit(solution)/shard_map/ppermute | solution.py:65
  149.3 7.5 %collective-permute-done.35.refs_1_ = bf16[12,32,384]{2,1,0:T(8,128)(2,1)S(1)} collective-permute-done((bf16[12,32,384]{2,1,0:T(8,128)(2,1)S(1)}, bf16[12,32,384]{2,1,0:T(8,128)(2,1)S(1)}, u32[]{:S(2)}, u32[]{:S(2)}) %collective-permute-start.35) | collective-permute-done | bytes 294944 | tf_op jit(solution)/shard_map/ppermute | solution.py:65
  156.9 5.2 %collective-permute-done.34.refs_1_ = bf16[64,2304]{1,0:T(8,128)(2,1)S(1)} collective-permute-done((bf16[64,2304]{1,0:T(8,128)(2,1)S(1)}, bf16[64,2304]{1,0:T(8,128)(2,1)S(1)}, u32[]{:S(2)}, u32[]{:S(2)}) %collective-permute-start.34) | collective-permute-done | bytes 294944 | tf_op jit(solution)/shard_map/ppermute | solution.py:65
  166.0 7.2 %collective-permute-done.37.refs_1_ = bf16[32,2304]{1,0:T(8,128)(2,1)S(1)} collective-permute-done((bf16[32,2304]{1,0:T(8,128)(2,1)S(1)}, bf16[32,2304]{1,0:T(8,128)(2,1)S(1)}, u32[]{:S(2)}, u32[]{:S(2)}) %collective-permute-start.37) | collective-permute-done | bytes 147488 | tf_op jit(solution)/shard_map/ppermute | solution.py:65
  176.4 3.9 %collective-permute-done.39 = f32[4,640]{1,0:T(4,128)S(1)} collective-permute-done((f32[4,640]{1,0:T(4,128)S(1)}, f32[4,640]{1,0:T(4,128)S(1)}, u32[]{:S(2)}, u32[]{:S(2)}) %collective-permute-start.39) | collective-permute-done | bytes 10272 | tf_op jit(solution)/shard_map/ppermute | solution.py:65
  180.4 4.1 %down.3 = (f32[64,640]{1,0:T(8,128)S(1)}, bf16[64,640]{1,0:T(8,128)(2,1)S(1)}, bf16[64,640]{1,0:T(8,128)(2,1)S(1)}, bf16[64,640]{1,0:T(8,128)(2,1)S(1)}, f32[8,128]{1,0:T(8,128)S(1)}) custom-call(s32[8]{0:T(128)S(1)} %reshape.117.refs_0_, bf16[128,1152]{1,0:T(8,128)(2,1)S(1)} %get-tuple-element.195.refs_1_, ...), custom_call_target="tpu_custom_call" | custom-call | flops 1 | bytes 1 | tf_op jit(solution)/shard_map/down/pallas_call | solution.py:47
  184.7 3.3 %collective-permute-start.46 = (bf16[64,1152]{1,0:T(8,128)(2,1)S(1)}, bf16[64,1152]{1,0:T(8,128)(2,1)S(1)}, u32[]{:S(2)}, u32[]{:S(2)}) collective-permute-start(bf16[64,1152]{1,0:T(8,128)(2,1)S(1)} %get-tuple-element.202.refs_0_), channel_id=1, source_target_pairs={{0,2},{1,3},{2,0},{3,1},{4,6},{5,7},{6,4},{7,5},{8,10},{9,11},{10,... | collective-permute-start | bytes 442376 | tf_op jit(solution)/shard_map/ppermute | solution.py:65
  206.4 5.2 %collective-permute-done.51.refs_2_ = bf16[64,640]{1,0:T(8,128)(2,1)S(1)} collective-permute-done((bf16[64,640]{1,0:T(8,128)(2,1)S(1)}, bf16[64,640]{1,0:T(8,128)(2,1)S(1)}, u32[]{:S(2)}, u32[]{:S(2)}) %collective-permute-start.51) | collective-permute-done | bytes 81952 | tf_op jit(solution)/shard_map/ppermute | solution.py:65
  231.5 16.1 %head.2 = (f32[256,128]{1,0:T(8,128)}, f32[8,128]{1,0:T(8,128)}) custom-call(s32[8]{0:T(128)} %copy-done.14, s32[4]{0:T(128)} %copy-done.13, bf16[4,64,640]{2,1,0:T(8,128)(2,1)} %copy-done.10, bf16[4,64,640]{2,1,0:T(8,128)(2,1)} %copy-done.2, bf16[4,64,640]{2,1,0:T(8,128)(2,1)} %copy-done.3, bf16[4,64,640]{2,1,0:T(8,128)(2,1)} %copy-done.5, ...), custom_call_target="tpu_custom_call" | custom-call | flops 1 | bytes 1 | tf_op jit(solution)/shard_map/head/pallas_call | solution.py:47
  252.3 15.9 %head.3 = (f32[256,128]{1,0:T(8,128)}, f32[8,128]{1,0:T(8,128)}) custom-call(s32[8]{0:T(128)} %copy-done.14, s32[4]{0:T(128)} %copy-done.13, bf16[4,64,640]{2,1,0:T(8,128)(2,1)} %copy-done.9, bf16[4,64,640]{2,1,0:T(8,128)(2,1)} %copy-done.4, bf16[4,64,640]{2,1,0:T(8,128)(2,1)} %copy-done.6, bf16[4,64,640]{2,1,0:T(8,128)(2,1)} %copy-done.7, ...), custom_call_target="tpu_custom_call" | custom-call | flops 1 | bytes 1 | tf_op jit(solution)/shard_map/head/pallas_call | solution.py:47
  (287 shorter events, 126.6 us)
Async XLA Ops:
  19.4 12.4 %collective-permute-start.5 = (bf16[32,1920]{1,0:T(8,128)(2,1)S(1)}, bf16[32,1920]{1,0:T(8,128)(2,1)S(1)}, u32[]{:S(2)}, u32[]{:S(2)}) collective-permute-start(bf16[32,1920]{1,0:T(8,128)(2,1)S(1)} %get-tuple-element.125), channel_id=1, source_target_pairs={{0,4},{1,5},{2,6},{3,7},{4,0},{5,1},{6,2},{7,3},{8,12},{9,13},{10,... | collective-permute-start | bytes 368648 | tf_op jit(solution)/shard_map/ppermute | solution.py:65
  82.7 17.6 %collective-permute-start.25 = (bf16[12,128,384]{2,1,0:T(8,128)(2,1)S(1)}, bf16[12,128,384]{2,1,0:T(8,128)(2,1)S(1)}, u32[]{:S(2)}, u32[]{:S(2)}) collective-permute-start(bf16[12,128,384]{2,1,0:T(8,128)(2,1)S(1)} %get-tuple-element.150), channel_id=1, source_target_pairs={{0,1},{1,0},{2,3},{3,2},{4,5},{5,4},{6,7},{7,6},{8,9},{9,8},{10,11... | collective-permute-start | bytes 3538952 | tf_op jit(solution)/shard_map/ppermute | solution.py:65
  84.8 25.3 %collective-permute-start.22 = (bf16[12,64,384]{2,1,0:T(8,128)(2,1)S(1)}, bf16[12,64,384]{2,1,0:T(8,128)(2,1)S(1)}, u32[]{:S(2)}, u32[]{:S(2)}) collective-permute-start(bf16[12,64,384]{2,1,0:T(8,128)(2,1)S(1)} %get-tuple-element.143), channel_id=1, source_target_pairs={{0,2},{1,3},{2,0},{3,1},{4,6},{5,7},{6,4},{7,5},{8,10},{9,11},{10,... | collective-permute-start | bytes 1769480 | tf_op jit(solution)/shard_map/ppermute | solution.py:65
  97.6 31.7 %collective-permute-start.27 = (bf16[6,128,384]{2,1,0:T(8,128)(2,1)S(1)}, bf16[6,128,384]{2,1,0:T(8,128)(2,1)S(1)}, u32[]{:S(2)}, u32[]{:S(2)}) collective-permute-start(bf16[6,128,384]{2,1,0:T(8,128)(2,1)S(1)} %get-tuple-element.159), channel_id=1, source_target_pairs={{0,1},{1,0},{2,3},{3,2},{4,5},{5,4},{6,7},{7,6},{8,9},{9,8},{10,11... | collective-permute-start | bytes 1769480 | tf_op jit(solution)/shard_map/ppermute | solution.py:65
  100.5 32.7 %collective-permute-start.31 = (bf16[12,64,384]{2,1,0:T(8,128)(2,1)S(1)}, bf16[12,64,384]{2,1,0:T(8,128)(2,1)S(1)}, u32[]{:S(2)}, u32[]{:S(2)}) collective-permute-start(bf16[12,64,384]{2,1,0:T(8,128)(2,1)S(1)} %get-tuple-element.168), channel_id=1, source_target_pairs={{0,2},{1,3},{2,0},{3,1},{4,6},{5,7},{6,4},{7,5},{8,10},{9,11},{10,... | collective-permute-start | bytes 1769480 | tf_op jit(solution)/shard_map/ppermute | solution.py:65
  110.2 22.7 %collective-permute-start.26 = (bf16[12,32,384]{2,1,0:T(8,128)(2,1)S(1)}, bf16[12,32,384]{2,1,0:T(8,128)(2,1)S(1)}, u32[]{:S(2)}, u32[]{:S(2)}) collective-permute-start(bf16[12,32,384]{2,1,0:T(8,128)(2,1)S(1)} %get-tuple-element.156), channel_id=1, source_target_pairs={{0,4},{1,5},{2,6},{3,7},{4,0},{5,1},{6,2},{7,3},{8,12},{9,13},{10,... | collective-permute-start | bytes 884744 | tf_op jit(solution)/shard_map/ppermute | solution.py:65
  113.1 16.2 %collective-permute-start.28 = (bf16[32,1152]{1,0:T(8,128)(2,1)S(1)}, bf16[32,1152]{1,0:T(8,128)(2,1)S(1)}, u32[]{:S(2)}, u32[]{:S(2)}) collective-permute-start(bf16[32,1152]{1,0:T(8,128)(2,1)S(1)} %get-tuple-element.160.refs_0_), channel_id=1, source_target_pairs={{0,4},{1,5},{2,6},{3,7},{4,0},{5,1},{6,2},{7,3},{8,12},{9,13},{10,... | collective-permute-start | bytes 221192 | tf_op jit(solution)/shard_map/ppermute | solution.py:65
  129.5 15.2 %collective-permute-start.30 = (bf16[6,64,384]{2,1,0:T(8,128)(2,1)S(1)}, bf16[6,64,384]{2,1,0:T(8,128)(2,1)S(1)}, u32[]{:S(2)}, u32[]{:S(2)}) collective-permute-start(bf16[6,64,384]{2,1,0:T(8,128)(2,1)S(1)} %get-tuple-element.166), channel_id=1, source_target_pairs={{0,2},{1,3},{2,0},{3,1},{4,6},{5,7},{6,4},{7,5},{8,10},{9,11},{10,... | collective-permute-start | bytes 884744 | tf_op jit(solution)/shard_map/ppermute | solution.py:65
  133.1 11.6 %collective-permute-start.29 = (bf16[32,2304]{1,0:T(8,128)(2,1)S(1)}, bf16[32,2304]{1,0:T(8,128)(2,1)S(1)}, u32[]{:S(2)}, u32[]{:S(2)}) collective-permute-start(bf16[32,2304]{1,0:T(8,128)(2,1)S(1)} %get-tuple-element.164.refs_0_), channel_id=1, source_target_pairs={{0,4},{1,5},{2,6},{3,7},{4,0},{5,1},{6,2},{7,3},{8,12},{9,13},{10,... | collective-permute-start | bytes 442376 | tf_op jit(solution)/shard_map/ppermute | solution.py:65
  133.4 23.3 %collective-permute-start.35 = (bf16[12,32,384]{2,1,0:T(8,128)(2,1)S(1)}, bf16[12,32,384]{2,1,0:T(8,128)(2,1)S(1)}, u32[]{:S(2)}, u32[]{:S(2)}) collective-permute-start(bf16[12,32,384]{2,1,0:T(8,128)(2,1)S(1)} %get-tuple-element.177), channel_id=1, source_target_pairs={{0,4},{1,5},{2,6},{3,7},{4,0},{5,1},{6,2},{7,3},{8,12},{9,13},{10,... | collective-permute-start | bytes 884744 | tf_op jit(solution)/shard_map/ppermute | solution.py:65
  144.8 17.4 %collective-permute-start.34 = (bf16[64,2304]{1,0:T(8,128)(2,1)S(1)}, bf16[64,2304]{1,0:T(8,128)(2,1)S(1)}, u32[]{:S(2)}, u32[]{:S(2)}) collective-permute-start(bf16[64,2304]{1,0:T(8,128)(2,1)S(1)} %get-tuple-element.175.refs_0_), channel_id=1, source_target_pairs={{0,2},{1,3},{2,0},{3,1},{4,6},{5,7},{6,4},{7,5},{8,10},{9,11},{10,... | collective-permute-start | bytes 884744 | tf_op jit(solution)/shard_map/ppermute | solution.py:65
  146.2 17.5 %collective-permute-start.33 = (bf16[64,1152]{1,0:T(8,128)(2,1)S(1)}, bf16[64,1152]{1,0:T(8,128)(2,1)S(1)}, u32[]{:S(2)}, u32[]{:S(2)}) collective-permute-start(bf16[64,1152]{1,0:T(8,128)(2,1)S(1)} %get-tuple-element.174.refs_0_), channel_id=1, source_target_pairs={{0,2},{1,3},{2,0},{3,1},{4,6},{5,7},{6,4},{7,5},{8,10},{9,11},{10,... | collective-permute-start | bytes 442376 | tf_op jit(solution)/shard_map/ppermute | solution.py:65
  146.9 15.4 %collective-permute-start.32 = (f32[1,640]{1,0:T(1,128)S(1)}, f32[1,640]{1,0:T(1,128)S(1)}, u32[]{:S(2)}, u32[]{:S(2)}) collective-permute-start(f32[1,640]{1,0:T(1,128)S(1)} %get-tuple-element.173), channel_id=1, source_target_pairs={{0,1},{1,0},{2,3},{3,2},{4,5},{5,4},{6,7},{7,6},{8,9},{9,8},{10,11... | collective-permute-start | bytes 7688 | tf_op jit(solution)/shard_map/ppermute | solution.py:65
  146.9 17.5 %collective-permute-start.38 = (bf16[6,32,384]{2,1,0:T(8,128)(2,1)S(1)}, bf16[6,32,384]{2,1,0:T(8,128)(2,1)S(1)}, u32[]{:S(2)}, u32[]{:S(2)}) collective-permute-start(bf16[6,32,384]{2,1,0:T(8,128)(2,1)S(1)} %get-tuple-element.185), channel_id=1, source_target_pairs={{0,4},{1,5},{2,6},{3,7},{4,0},{5,1},{6,2},{7,3},{8,12},{9,13},{10,... | collective-permute-start | bytes 442376 | tf_op jit(solution)/shard_map/ppermute | solution.py:65
  162.2 18.2 %collective-permute-start.42 = (bf16[128,2304]{1,0:T(8,128)(2,1)S(1)}, bf16[128,2304]{1,0:T(8,128)(2,1)S(1)}, u32[]{:S(2)}, u32[]{:S(2)}) collective-permute-start(bf16[128,2304]{1,0:T(8,128)(2,1)S(1)} %get-tuple-element.196.refs_2_), channel_id=1, source_target_pairs={{0,1},{1,0},{2,3},{3,2},{4,5},{5,4},{6,7},{7,6},{8,9},{9,8},{10,11... | collective-permute-start | bytes 1769480 | tf_op jit(solution)/shard_map/ppermute | solution.py:65
  164.6 11.7 %collective-permute-start.40 = (bf16[32,1152]{1,0:T(8,128)(2,1)S(1)}, bf16[32,1152]{1,0:T(8,128)(2,1)S(1)}, u32[]{:S(2)}, u32[]{:S(2)}) collective-permute-start(bf16[32,1152]{1,0:T(8,128)(2,1)S(1)} %get-tuple-element.190.refs_0_), channel_id=1, source_target_pairs={{0,4},{1,5},{2,6},{3,7},{4,0},{5,1},{6,2},{7,3},{8,12},{9,13},{10,... | collective-permute-start | bytes 221192 | tf_op jit(solution)/shard_map/ppermute | solution.py:65
  166.0 14.3 %collective-permute-start.41 = (bf16[128,1152]{1,0:T(8,128)(2,1)S(1)}, bf16[128,1152]{1,0:T(8,128)(2,1)S(1)}, u32[]{:S(2)}, u32[]{:S(2)}) collective-permute-start(bf16[128,1152]{1,0:T(8,128)(2,1)S(1)} %get-tuple-element.195.refs_1_), channel_id=1, source_target_pairs={{0,1},{1,0},{2,3},{3,2},{4,5},{5,4},{6,7},{7,6},{8,9},{9,8},{10,11... | collective-permute-start | bytes 884744 | tf_op jit(solution)/shard_map/ppermute | solution.py:65
  211.6 14.9 %collective-permute-start.56 = (bf16[4,64,640]{2,1,0:T(8,128)(2,1)S(1)}, bf16[4,64,640]{2,1,0:T(8,128)(2,1)S(1)}, u32[]{:S(2)}, u32[]{:S(2)}) collective-permute-start(bf16[4,64,640]{2,1,0:T(8,128)(2,1)S(1)} %get-tuple-element.219.refs_2_), channel_id=1, source_target_pairs={{0,8},{8,0},{16,24},{24,16},{1,9},{9,1},{17,25},{25,17},{2,10},{10... | collective-permute-start | bytes 983048 | tf_op jit(solution)/shard_map/ppermute | solution.py:60
  212.8 13.7 %collective-permute-start.57 = (bf16[4,64,640]{2,1,0:T(8,128)(2,1)S(1)}, bf16[4,64,640]{2,1,0:T(8,128)(2,1)S(1)}, u32[]{:S(2)}, u32[]{:S(2)}) collective-permute-start(bf16[4,64,640]{2,1,0:T(8,128)(2,1)S(1)} %get-tuple-element.219.refs_2_), channel_id=1, source_target_pairs={{0,16},{8,24},{16,0},{24,8},{1,17},{9,25},{17,1},{25,9},{2,18},{10... | collective-permute-start | bytes 983048 | tf_op jit(solution)/shard_map/ppermute | solution.py:60
  213.9 12.5 %collective-permute-start.58 = (bf16[4,64,640]{2,1,0:T(8,128)(2,1)S(1)}, bf16[4,64,640]{2,1,0:T(8,128)(2,1)S(1)}, u32[]{:S(2)}, u32[]{:S(2)}) collective-permute-start(bf16[4,64,640]{2,1,0:T(8,128)(2,1)S(1)} %get-tuple-element.219.refs_2_), channel_id=1, source_target_pairs={{0,24},{8,16},{16,8},{24,0},{1,25},{9,17},{17,9},{25,1},{2,26},{10... | collective-permute-start | bytes 983048 | tf_op jit(solution)/shard_map/ppermute | solution.py:60
  227.2 20.5 %collective-permute-start.66 = (bf16[4,64,640]{2,1,0:T(8,128)(2,1)S(1)}, bf16[4,64,640]{2,1,0:T(8,128)(2,1)S(1)}, u32[]{:S(2)}, u32[]{:S(2)}) collective-permute-start(bf16[4,64,640]{2,1,0:T(8,128)(2,1)S(1)} %get-tuple-element.230.refs_2_), channel_id=1, source_target_pairs={{0,8},{8,0},{16,24},{24,16},{1,9},{9,1},{17,25},{25,17},{2,10},{10... | collective-permute-start | bytes 983048 | tf_op jit(solution)/shard_map/ppermute | solution.py:60
  228.3 19.4 %collective-permute-start.67 = (bf16[4,64,640]{2,1,0:T(8,128)(2,1)S(1)}, bf16[4,64,640]{2,1,0:T(8,128)(2,1)S(1)}, u32[]{:S(2)}, u32[]{:S(2)}) collective-permute-start(bf16[4,64,640]{2,1,0:T(8,128)(2,1)S(1)} %get-tuple-element.230.refs_2_), channel_id=1, source_target_pairs={{0,16},{8,24},{16,0},{24,8},{1,17},{9,25},{17,1},{25,9},{2,18},{10... | collective-permute-start | bytes 983048 | tf_op jit(solution)/shard_map/ppermute | solution.py:60
  229.5 18.2 %collective-permute-start.68 = (bf16[4,64,640]{2,1,0:T(8,128)(2,1)S(1)}, bf16[4,64,640]{2,1,0:T(8,128)(2,1)S(1)}, u32[]{:S(2)}, u32[]{:S(2)}) collective-permute-start(bf16[4,64,640]{2,1,0:T(8,128)(2,1)S(1)} %get-tuple-element.230.refs_2_), channel_id=1, source_target_pairs={{0,24},{8,16},{16,8},{24,0},{1,25},{9,17},{17,9},{25,1},{2,26},{10... | collective-permute-start | bytes 983048 | tf_op jit(solution)/shard_map/ppermute | solution.py:60
  230.7 20.2 %collective-permute-start.69 = (bf16[4,64,640]{2,1,0:T(8,128)(2,1)S(1)}, bf16[4,64,640]{2,1,0:T(8,128)(2,1)S(1)}, u32[]{:S(2)}, u32[]{:S(2)}) collective-permute-start(bf16[4,64,640]{2,1,0:T(8,128)(2,1)S(1)} %get-tuple-element.230.refs_2_), channel_id=1, source_target_pairs={{0,1},{1,0},{2,3},{3,2},{4,5},{5,4},{6,7},{7,6},{8,9},{9,8},{10,11... | collective-permute-start | bytes 983048 | tf_op jit(solution)/shard_map/ppermute | solution.py:65
  (88 other events, 619.2 us)

commit v8 on v7

--- a/solution.py
+++ b/solution.py
@@ -19,6 +19,7 @@
 HEAD_BLOCKS = 4
 GATE_MIB = 46
 DOWN_MIB = 46
+HEAD_MIB = 46
 BF16 = jnp.bfloat16
 F32 = jnp.float32
 MIB = 1 << 20
@@ -339,15 +340,15 @@
         inverse = 1.0 / gains[...]
         for i in range(rows):
             place = pl.multiple_of(row_places[i], unit)
-            sums = jnp.zeros((unit, 1), F32)
+            sums = jnp.zeros((unit, width), F32)
             for core, arrays in enumerate((own, other)):
                 for j in range(chips):
                     feature = pl.multiple_of(col_index[2 * j + core] * width, LANES)
                     values = arrays[i][j]
                     lhs[pl.ds(place, unit), pl.ds(feature, width)] = values
                     plain = values.astype(F32) * inverse[2 * j + core : 2 * j + core + 1, :]
-                    sums += jnp.sum(plain * plain, axis=1, keepdims=True)
-            square[pl.ds(place, unit), :] = sums
+                    sums += plain * plain
+            square[pl.ds(place, unit), :] = jnp.sum(sums, axis=1, keepdims=True)
         top[...] = jnp.full_like(top, MASKED)
         total[...] = jnp.zeros_like(total)
         picked[...] = jnp.zeros_like(picked)
@@ -758,7 +759,7 @@
             out_shape=[shape((tokens, LANES), F32)],
             out_specs=[pl.BlockSpec((tokens, LANES), lambda i: (0, 0))],
             scratch_shapes=[pltpu.VMEM((tokens, D), BF16)] + [pltpu.VMEM((tokens, 1), F32)] * 4,
-            compiler_params=params(56),
+            compiler_params=params(HEAD_MIB),
             cost_estimate=cost(
                 2 * tokens * D * vocab_tile * count, 2 * D * vocab_tile * count
             ),

time: 288 us -> 281 us (0.976)
  local copies, waits for them, and re-layouts: 8.83 us -> 4.22 us
  Pallas kernels: 71.4 us -> 67.8 us
    pallas_call x34, Pallas kernels: 64 us -> 60.4 us  [call(): pl.pallas_call(body, in_specs=in_specs + [ANY], out_shape=out_shape + [ja...]
  transfers between devices with their start and end apart: 78 -> 78, of which waited for: 38 -> 39; matrix products, arithmetic and copies ran while one was open for 2% -> 2% of each run, Pallas kernels for 15% -> 15%
where the time goes in v8:
time: 281 us; the launch traced here: 280 us
  waiting for transfers between devices  123 us (44%)
  starting transfers between devices  81 us (29%)
  Pallas kernels  67.8 us (24%)
  local copies, waits for them, and re-layouts  4.22 us (2%)
    ppermute x55, waiting for transfers between devices, col_xor(): return lax.ppermute(x, 'col', [(i, i ^ mask) for i in range(count)])  108 us
    pallas_call x34, Pallas kernels, call(): pl.pallas_call(body, in_specs=in_specs + [ANY], out_shape=out_shape + [ja...  60.4 us
    ppermute x55, starting transfers between devices, col_xor(): return lax.ppermute(x, 'col', [(i, i ^ mask) for i in range(count)])  53 us
    ppermute x23, starting transfers between devices, row_xor(): return lax.ppermute(x, 'row', [(i, i ^ mask) for i in range(count)])  27.9 us
    ppermute x23, waiting for transfers between devices, row_xor(): return lax.ppermute(x, 'row', [(i, i ^ mask) for i in range(count)])  14.8 us
  transfers between devices with their start and end apart: 78, of which 39 were waited for; matrix products, arithmetic and copies ran while one was open for 2% of the time, Pallas kernels for 15%

profile of v8, /device:TPU:0, one launch (start us, length us, event | category | flops | bytes accessed | tf_op | source)
XLA Modules:
  0.0 280.2 jit_solution(17853430860667355857)
XLA Ops:
  0.0 2.9 %collective-permute-start = (bf16[64,640]{1,0:T(8,128)(2,1)}, bf16[64,640]{1,0:T(8,128)(2,1)S(1)}, u32[]{:S(2)}, u32[]{:S(2)}) collective-permute-start(bf16[64,640]{1,0:T(8,128)(2,1)} %refs_0_.1), channel_id=1, source_target_pairs={{0,8},{8,0},{16,24},{24,16},{1,9},{9,1},{17,25},{25,17},{2,10},{10... | collective-permute-start | bytes 245768 | tf_op jit(solution)/shard_map/ppermute | solution.py:61
  10.7 3.7 %qkv_partial.1 = (f32[128,1920]{1,0:T(8,128)}, bf16[128,1920]{1,0:T(8,128)(2,1)}) custom-call(s32[8]{0:T(128)} %reshape.113.offsets, bf16[64,640]{1,0:T(8,128)(2,1)} %refs_0_.1, bf16[64,640]{1,0:T(8,128)(2,1)} %copy-done.4, bf16[64,640]{1,0:T(8,128)(2,1)} %copy-done.5, bf16[64,640]{1,0:T(8,128)(2,1)} %copy-done.6, f32[1,640]{1,0:T(1,128)} %broadcast_in_dim.29.refs_4_, ...), custom_call_target="tpu_custom_call" | custom-call | flops 1 | bytes 1 | tf_op jit(solution)/shard_map/qkv_partial/pallas_call | solution.py:467
  24.9 6.9 %collective-permute-done.5.refs_2_ = bf16[32,1920]{1,0:T(8,128)(2,1)S(1)} collective-permute-done((bf16[32,1920]{1,0:T(8,128)(2,1)S(1)}, bf16[32,1920]{1,0:T(8,128)(2,1)S(1)}, u32[]{:S(2)}, u32[]{:S(2)}) %collective-permute-start.5) | collective-permute-done | bytes 122912 | tf_op jit(solution)/shard_map/ppermute | solution.py:66
  38.1 7.0 %collective-permute-done.8.refs_2_ = bf16[32,1792]{1,0:T(8,128)(2,1)S(1)} collective-permute-done((bf16[32,1792]{1,0:T(8,128)(2,1)S(1)}, bf16[32,1792]{1,0:T(8,128)(2,1)S(1)}, u32[]{:S(2)}, u32[]{:S(2)}) %collective-permute-start.8) | collective-permute-done | bytes 114720 | tf_op jit(solution)/shard_map/ppermute | solution.py:66
  46.6 3.3 %attention_out.1 = (f32[64,640]{1,0:T(8,128)S(1)}, bf16[64,640]{1,0:T(8,128)(2,1)S(1)}, bf16[64,640]{1,0:T(8,128)(2,1)S(1)}, bf16[64,640]{1,0:T(8,128)(2,1)S(1)}) custom-call(s32[8]{0:T(128)S(1)} %xor_multiply_fusion.places, s32[4]{0:T(128)S(1)} %fusion.43.row_places.refs_3_, bf16[32,1792]{1,0:T(8,128)(2,1)S(1)} %qkv_rope.1.refs_0_, ...), custom_call_target="tpu_custom_call" | custom-call | flops 1 | bytes 1 | tf_op jit(solution)/shard_map/attention_out/pallas_call | solution.py:504
  65.6 4.0 %gate_up.4 = (f32[7,128,384]{2,1,0:T(8,128)S(1)}, bf16[7,128,384]{2,1,0:T(8,128)(2,1)S(1)}, f32[8,128]{1,0:T(8,128)S(1)}) custom-call(bf16[256,640]{1,0:T(8,128)(2,1)S(1)} %get-tuple-element.131.refs_0_, bf16[2,640,3456]{2,1,0:T(8,128)(2,1)} %refs_2_.7, bf16[2,640,3456]{2,1,0:T(8,128)(2,1)} %refs_2_.7, bf16[2,640,3456]{2,1,0:T(8,128)(2,1)} %refs_4_.9, ...), custom_call_target="tpu_custom_call" | custom-call | flops 1 | bytes 1 | tf_op jit(solution)/shard_map/gate_up/pallas_call | solution.py:48
  69.6 6.2 %gate_up.5 = (f32[12,128,384]{2,1,0:T(8,128)S(1)}, bf16[12,128,384]{2,1,0:T(8,128)(2,1)S(1)}, f32[8,128]{1,0:T(8,128)S(1)}) custom-call(bf16[256,640]{1,0:T(8,128)(2,1)S(1)} %get-tuple-element.131.refs_0_, bf16[2,640,3456]{2,1,0:T(8,128)(2,1)} %refs_2_.7, bf16[2,640,3456]{2,1,0:T(8,128)(2,1)} %refs_2_.7, bf16[2,640,3456]{2,1,0:T(8,128)(2,1)} %refs_4_.9, ...), custom_call_target="tpu_custom_call" | custom-call | flops 1 | bytes 1 | tf_op jit(solution)/shard_map/gate_up/pallas_call | solution.py:48
  76.6 6.2 %gate_up.6 = (f32[12,128,384]{2,1,0:T(8,128)S(1)}, bf16[12,128,384]{2,1,0:T(8,128)(2,1)S(1)}, f32[8,128]{1,0:T(8,128)S(1)}) custom-call(bf16[256,640]{1,0:T(8,128)(2,1)S(1)} %get-tuple-element.131.refs_0_, bf16[2,640,3456]{2,1,0:T(8,128)(2,1)} %refs_2_.7, bf16[2,640,3456]{2,1,0:T(8,128)(2,1)} %refs_2_.7, bf16[2,640,3456]{2,1,0:T(8,128)(2,1)} %refs_4_.9, ...), custom_call_target="tpu_custom_call" | custom-call | flops 1 | bytes 1 | tf_op jit(solution)/shard_map/gate_up/pallas_call | solution.py:48
  85.3 8.5 %collective-permute-done.23.refs_1_ = bf16[7,64,384]{2,1,0:T(8,128)(2,1)S(1)} collective-permute-done((bf16[7,64,384]{2,1,0:T(8,128)(2,1)S(1)}, bf16[7,64,384]{2,1,0:T(8,128)(2,1)S(1)}, u32[]{:S(2)}, u32[]{:S(2)}) %collective-permute-start.23) | collective-permute-done | bytes 344096 | tf_op jit(solution)/shard_map/ppermute | solution.py:66
  93.9 3.8 %gate_up.7 = (f32[6,128,384]{2,1,0:T(8,128)S(1)}, bf16[6,128,384]{2,1,0:T(8,128)(2,1)S(1)}, f32[8,128]{1,0:T(8,128)S(1)}) custom-call(bf16[256,640]{1,0:T(8,128)(2,1)S(1)} %get-tuple-element.131.refs_0_, bf16[2,640,3456]{2,1,0:T(8,128)(2,1)} %refs_2_.7, bf16[2,640,3456]{2,1,0:T(8,128)(2,1)} %refs_2_.7, bf16[2,640,3456]{2,1,0:T(8,128)(2,1)} %refs_4_.9, ...), custom_call_target="tpu_custom_call" | custom-call | flops 1 | bytes 1 | tf_op jit(solution)/shard_map/gate_up/pallas_call | solution.py:48
  100.7 8.6 %collective-permute-done.24.refs_1_ = bf16[7,32,384]{2,1,0:T(8,128)(2,1)S(1)} collective-permute-done((bf16[7,32,384]{2,1,0:T(8,128)(2,1)S(1)}, bf16[7,32,384]{2,1,0:T(8,128)(2,1)S(1)}, u32[]{:S(2)}, u32[]{:S(2)}) %collective-permute-start.24) | collective-permute-done | bytes 172064 | tf_op jit(solution)/shard_map/ppermute | solution.py:66
  113.2 16.1 %collective-permute-done.28.refs_1_ = bf16[32,1152]{1,0:T(8,128)(2,1)S(1)} collective-permute-done((bf16[32,1152]{1,0:T(8,128)(2,1)S(1)}, bf16[32,1152]{1,0:T(8,128)(2,1)S(1)}, u32[]{:S(2)}, u32[]{:S(2)}) %collective-permute-start.28) | collective-permute-done | bytes 73760 | tf_op jit(solution)/shard_map/ppermute | solution.py:66
  129.5 3.5 %collective-permute-start.30 = (bf16[6,64,384]{2,1,0:T(8,128)(2,1)S(1)}, bf16[6,64,384]{2,1,0:T(8,128)(2,1)S(1)}, u32[]{:S(2)}, u32[]{:S(2)}) collective-permute-start(bf16[6,64,384]{2,1,0:T(8,128)(2,1)S(1)} %get-tuple-element.166), channel_id=1, source_target_pairs={{0,2},{1,3},{2,0},{3,1},{4,6},{5,7},{6,4},{7,5},{8,10},{9,11},{10,... | collective-permute-start | bytes 884744 | tf_op jit(solution)/shard_map/ppermute | solution.py:66
  133.4 3.0 %collective-permute-start.35 = (bf16[12,32,384]{2,1,0:T(8,128)(2,1)S(1)}, bf16[12,32,384]{2,1,0:T(8,128)(2,1)S(1)}, u32[]{:S(2)}, u32[]{:S(2)}) collective-permute-start(bf16[12,32,384]{2,1,0:T(8,128)(2,1)S(1)} %get-tuple-element.177), channel_id=1, source_target_pairs={{0,4},{1,5},{2,6},{3,7},{4,0},{5,1},{6,2},{7,3},{8,12},{9,13},{10,... | collective-permute-start | bytes 884744 | tf_op jit(solution)/shard_map/ppermute | solution.py:66
  136.4 8.3 %collective-permute-done.30.refs_1_ = bf16[6,64,384]{2,1,0:T(8,128)(2,1)S(1)} collective-permute-done((bf16[6,64,384]{2,1,0:T(8,128)(2,1)S(1)}, bf16[6,64,384]{2,1,0:T(8,128)(2,1)S(1)}, u32[]{:S(2)}, u32[]{:S(2)}) %collective-permute-start.30) | collective-permute-done | bytes 294944 | tf_op jit(solution)/shard_map/ppermute | solution.py:66
  149.3 7.5 %collective-permute-done.35.refs_1_ = bf16[12,32,384]{2,1,0:T(8,128)(2,1)S(1)} collective-permute-done((bf16[12,32,384]{2,1,0:T(8,128)(2,1)S(1)}, bf16[12,32,384]{2,1,0:T(8,128)(2,1)S(1)}, u32[]{:S(2)}, u32[]{:S(2)}) %collective-permute-start.35) | collective-permute-done | bytes 294944 | tf_op jit(solution)/shard_map/ppermute | solution.py:66
  156.9 5.2 %collective-permute-done.34.refs_1_ = bf16[64,2304]{1,0:T(8,128)(2,1)S(1)} collective-permute-done((bf16[64,2304]{1,0:T(8,128)(2,1)S(1)}, bf16[64,2304]{1,0:T(8,128)(2,1)S(1)}, u32[]{:S(2)}, u32[]{:S(2)}) %collective-permute-start.34) | collective-permute-done | bytes 294944 | tf_op jit(solution)/shard_map/ppermute | solution.py:66
  166.0 7.2 %collective-permute-done.37.refs_1_ = bf16[32,2304]{1,0:T(8,128)(2,1)S(1)} collective-permute-done((bf16[32,2304]{1,0:T(8,128)(2,1)S(1)}, bf16[32,2304]{1,0:T(8,128)(2,1)S(1)}, u32[]{:S(2)}, u32[]{:S(2)}) %collective-permute-start.37) | collective-permute-done | bytes 147488 | tf_op jit(solution)/shard_map/ppermute | solution.py:66
  176.4 3.9 %collective-permute-done.39 = f32[4,640]{1,0:T(4,128)S(1)} collective-permute-done((f32[4,640]{1,0:T(4,128)S(1)}, f32[4,640]{1,0:T(4,128)S(1)}, u32[]{:S(2)}, u32[]{:S(2)}) %collective-permute-start.39) | collective-permute-done | bytes 10272 | tf_op jit(solution)/shard_map/ppermute | solution.py:66
  180.4 4.1 %down.3 = (f32[64,640]{1,0:T(8,128)S(1)}, bf16[64,640]{1,0:T(8,128)(2,1)S(1)}, bf16[64,640]{1,0:T(8,128)(2,1)S(1)}, bf16[64,640]{1,0:T(8,128)(2,1)S(1)}, f32[8,128]{1,0:T(8,128)S(1)}) custom-call(s32[8]{0:T(128)S(1)} %reshape.117.refs_0_, bf16[128,1152]{1,0:T(8,128)(2,1)S(1)} %get-tuple-element.195.refs_1_, ...), custom_call_target="tpu_custom_call" | custom-call | flops 1 | bytes 1 | tf_op jit(solution)/shard_map/down/pallas_call | solution.py:48
  184.6 3.3 %collective-permute-start.46 = (bf16[64,1152]{1,0:T(8,128)(2,1)S(1)}, bf16[64,1152]{1,0:T(8,128)(2,1)S(1)}, u32[]{:S(2)}, u32[]{:S(2)}) collective-permute-start(bf16[64,1152]{1,0:T(8,128)(2,1)S(1)} %get-tuple-element.202.refs_0_), channel_id=1, source_target_pairs={{0,2},{1,3},{2,0},{3,1},{4,6},{5,7},{6,4},{7,5},{8,10},{9,11},{10,... | collective-permute-start | bytes 442376 | tf_op jit(solution)/shard_map/ppermute | solution.py:66
  206.3 5.2 %collective-permute-done.51.refs_2_ = bf16[64,640]{1,0:T(8,128)(2,1)S(1)} collective-permute-done((bf16[64,640]{1,0:T(8,128)(2,1)S(1)}, bf16[64,640]{1,0:T(8,128)(2,1)S(1)}, u32[]{:S(2)}, u32[]{:S(2)}) %collective-permute-start.51) | collective-permute-done | bytes 81952 | tf_op jit(solution)/shard_map/ppermute | solution.py:66
  230.6 14.3 %head.2 = (f32[256,128]{1,0:T(8,128)S(1)}, f32[8,128]{1,0:T(8,128)S(1)}) custom-call(s32[8]{0:T(128)S(1)} %get-tuple-element.193.refs_0_, s32[4]{0:T(128)S(1)} %get-tuple-element.194.refs_1_, bf16[4,64,640]{2,1,0:T(8,128)(2,1)S(1)} %get-tuple-element.219.refs_2_, bf16[4,64,640]{2,1,0:T(8,128)(2,1)S(1)} %get-tuple-element.223.refs_3_, ...), custom_call_target="tpu_custom_call" | custom-call | flops 1 | bytes 1 | tf_op jit(solution)/shard_map/head/pallas_call | solution.py:48
  247.6 14.1 %head.3 = (f32[256,128]{1,0:T(8,128)S(1)}, f32[8,128]{1,0:T(8,128)}) custom-call(s32[8]{0:T(128)S(1)} %get-tuple-element.193.refs_0_, s32[4]{0:T(128)S(1)} %get-tuple-element.194.refs_1_, bf16[4,64,640]{2,1,0:T(8,128)(2,1)S(1)} %get-tuple-element.230.refs_2_, bf16[4,64,640]{2,1,0:T(8,128)(2,1)S(1)} %get-tuple-element.232.refs_3_, ...), custom_call_target="tpu_custom_call" | custom-call | flops 1 | bytes 1 | tf_op jit(solution)/shard_map/head/pallas_call | solution.py:48
  (241 shorter events, 122.9 us)
Async XLA Ops:
  19.4 12.4 %collective-permute-start.5 = (bf16[32,1920]{1,0:T(8,128)(2,1)S(1)}, bf16[32,1920]{1,0:T(8,128)(2,1)S(1)}, u32[]{:S(2)}, u32[]{:S(2)}) collective-permute-start(bf16[32,1920]{1,0:T(8,128)(2,1)S(1)} %get-tuple-element.125), channel_id=1, source_target_pairs={{0,4},{1,5},{2,6},{3,7},{4,0},{5,1},{6,2},{7,3},{8,12},{9,13},{10,... | collective-permute-start | bytes 368648 | tf_op jit(solution)/shard_map/ppermute | solution.py:66
  82.8 17.6 %collective-permute-start.25 = (bf16[12,128,384]{2,1,0:T(8,128)(2,1)S(1)}, bf16[12,128,384]{2,1,0:T(8,128)(2,1)S(1)}, u32[]{:S(2)}, u32[]{:S(2)}) collective-permute-start(bf16[12,128,384]{2,1,0:T(8,128)(2,1)S(1)} %get-tuple-element.150), channel_id=1, source_target_pairs={{0,1},{1,0},{2,3},{3,2},{4,5},{5,4},{6,7},{7,6},{8,9},{9,8},{10,11... | collective-permute-start | bytes 3538952 | tf_op jit(solution)/shard_map/ppermute | solution.py:66
  84.8 25.3 %collective-permute-start.22 = (bf16[12,64,384]{2,1,0:T(8,128)(2,1)S(1)}, bf16[12,64,384]{2,1,0:T(8,128)(2,1)S(1)}, u32[]{:S(2)}, u32[]{:S(2)}) collective-permute-start(bf16[12,64,384]{2,1,0:T(8,128)(2,1)S(1)} %get-tuple-element.143), channel_id=1, source_target_pairs={{0,2},{1,3},{2,0},{3,1},{4,6},{5,7},{6,4},{7,5},{8,10},{9,11},{10,... | collective-permute-start | bytes 1769480 | tf_op jit(solution)/shard_map/ppermute | solution.py:66
  97.6 31.7 %collective-permute-start.27 = (bf16[6,128,384]{2,1,0:T(8,128)(2,1)S(1)}, bf16[6,128,384]{2,1,0:T(8,128)(2,1)S(1)}, u32[]{:S(2)}, u32[]{:S(2)}) collective-permute-start(bf16[6,128,384]{2,1,0:T(8,128)(2,1)S(1)} %get-tuple-element.159), channel_id=1, source_target_pairs={{0,1},{1,0},{2,3},{3,2},{4,5},{5,4},{6,7},{7,6},{8,9},{9,8},{10,11... | collective-permute-start | bytes 1769480 | tf_op jit(solution)/shard_map/ppermute | solution.py:66
  100.5 32.7 %collective-permute-start.31 = (bf16[12,64,384]{2,1,0:T(8,128)(2,1)S(1)}, bf16[12,64,384]{2,1,0:T(8,128)(2,1)S(1)}, u32[]{:S(2)}, u32[]{:S(2)}) collective-permute-start(bf16[12,64,384]{2,1,0:T(8,128)(2,1)S(1)} %get-tuple-element.168), channel_id=1, source_target_pairs={{0,2},{1,3},{2,0},{3,1},{4,6},{5,7},{6,4},{7,5},{8,10},{9,11},{10,... | collective-permute-start | bytes 1769480 | tf_op jit(solution)/shard_map/ppermute | solution.py:66
  110.3 22.7 %collective-permute-start.26 = (bf16[12,32,384]{2,1,0:T(8,128)(2,1)S(1)}, bf16[12,32,384]{2,1,0:T(8,128)(2,1)S(1)}, u32[]{:S(2)}, u32[]{:S(2)}) collective-permute-start(bf16[12,32,384]{2,1,0:T(8,128)(2,1)S(1)} %get-tuple-element.156), channel_id=1, source_target_pairs={{0,4},{1,5},{2,6},{3,7},{4,0},{5,1},{6,2},{7,3},{8,12},{9,13},{10,... | collective-permute-start | bytes 884744 | tf_op jit(solution)/shard_map/ppermute | solution.py:66
  113.1 16.2 %collective-permute-start.28 = (bf16[32,1152]{1,0:T(8,128)(2,1)S(1)}, bf16[32,1152]{1,0:T(8,128)(2,1)S(1)}, u32[]{:S(2)}, u32[]{:S(2)}) collective-permute-start(bf16[32,1152]{1,0:T(8,128)(2,1)S(1)} %get-tuple-element.160.refs_0_), channel_id=1, source_target_pairs={{0,4},{1,5},{2,6},{3,7},{4,0},{5,1},{6,2},{7,3},{8,12},{9,13},{10,... | collective-permute-start | bytes 221192 | tf_op jit(solution)/shard_map/ppermute | solution.py:66
  129.5 15.2 %collective-permute-start.30 = (bf16[6,64,384]{2,1,0:T(8,128)(2,1)S(1)}, bf16[6,64,384]{2,1,0:T(8,128)(2,1)S(1)}, u32[]{:S(2)}, u32[]{:S(2)}) collective-permute-start(bf16[6,64,384]{2,1,0:T(8,128)(2,1)S(1)} %get-tuple-element.166), channel_id=1, source_target_pairs={{0,2},{1,3},{2,0},{3,1},{4,6},{5,7},{6,4},{7,5},{8,10},{9,11},{10,... | collective-permute-start | bytes 884744 | tf_op jit(solution)/shard_map/ppermute | solution.py:66
  133.1 11.6 %collective-permute-start.29 = (bf16[32,2304]{1,0:T(8,128)(2,1)S(1)}, bf16[32,2304]{1,0:T(8,128)(2,1)S(1)}, u32[]{:S(2)}, u32[]{:S(2)}) collective-permute-start(bf16[32,2304]{1,0:T(8,128)(2,1)S(1)} %get-tuple-element.164.refs_0_), channel_id=1, source_target_pairs={{0,4},{1,5},{2,6},{3,7},{4,0},{5,1},{6,2},{7,3},{8,12},{9,13},{10,... | collective-permute-start | bytes 442376 | tf_op jit(solution)/shard_map/ppermute | solution.py:66
  133.4 23.3 %collective-permute-start.35 = (bf16[12,32,384]{2,1,0:T(8,128)(2,1)S(1)}, bf16[12,32,384]{2,1,0:T(8,128)(2,1)S(1)}, u32[]{:S(2)}, u32[]{:S(2)}) collective-permute-start(bf16[12,32,384]{2,1,0:T(8,128)(2,1)S(1)} %get-tuple-element.177), channel_id=1, source_target_pairs={{0,4},{1,5},{2,6},{3,7},{4,0},{5,1},{6,2},{7,3},{8,12},{9,13},{10,... | collective-permute-start | bytes 884744 | tf_op jit(solution)/shard_map/ppermute | solution.py:66
  144.8 17.4 %collective-permute-start.34 = (bf16[64,2304]{1,0:T(8,128)(2,1)S(1)}, bf16[64,2304]{1,0:T(8,128)(2,1)S(1)}, u32[]{:S(2)}, u32[]{:S(2)}) collective-permute-start(bf16[64,2304]{1,0:T(8,128)(2,1)S(1)} %get-tuple-element.175.refs_0_), channel_id=1, source_target_pairs={{0,2},{1,3},{2,0},{3,1},{4,6},{5,7},{6,4},{7,5},{8,10},{9,11},{10,... | collective-permute-start | bytes 884744 | tf_op jit(solution)/shard_map/ppermute | solution.py:66
  146.2 17.5 %collective-permute-start.33 = (bf16[64,1152]{1,0:T(8,128)(2,1)S(1)}, bf16[64,1152]{1,0:T(8,128)(2,1)S(1)}, u32[]{:S(2)}, u32[]{:S(2)}) collective-permute-start(bf16[64,1152]{1,0:T(8,128)(2,1)S(1)} %get-tuple-element.174.refs_0_), channel_id=1, source_target_pairs={{0,2},{1,3},{2,0},{3,1},{4,6},{5,7},{6,4},{7,5},{8,10},{9,11},{10,... | collective-permute-start | bytes 442376 | tf_op jit(solution)/shard_map/ppermute | solution.py:66
  146.9 15.4 %collective-permute-start.32 = (f32[1,640]{1,0:T(1,128)S(1)}, f32[1,640]{1,0:T(1,128)S(1)}, u32[]{:S(2)}, u32[]{:S(2)}) collective-permute-start(f32[1,640]{1,0:T(1,128)S(1)} %get-tuple-element.173), channel_id=1, source_target_pairs={{0,1},{1,0},{2,3},{3,2},{4,5},{5,4},{6,7},{7,6},{8,9},{9,8},{10,11... | collective-permute-start | bytes 7688 | tf_op jit(solution)/shard_map/ppermute | solution.py:66
  147.0 17.5 %collective-permute-start.38 = (bf16[6,32,384]{2,1,0:T(8,128)(2,1)S(1)}, bf16[6,32,384]{2,1,0:T(8,128)(2,1)S(1)}, u32[]{:S(2)}, u32[]{:S(2)}) collective-permute-start(bf16[6,32,384]{2,1,0:T(8,128)(2,1)S(1)} %get-tuple-element.185), channel_id=1, source_target_pairs={{0,4},{1,5},{2,6},{3,7},{4,0},{5,1},{6,2},{7,3},{8,12},{9,13},{10,... | collective-permute-start | bytes 442376 | tf_op jit(solution)/shard_map/ppermute | solution.py:66
  162.2 18.2 %collective-permute-start.42 = (bf16[128,2304]{1,0:T(8,128)(2,1)S(1)}, bf16[128,2304]{1,0:T(8,128)(2,1)S(1)}, u32[]{:S(2)}, u32[]{:S(2)}) collective-permute-start(bf16[128,2304]{1,0:T(8,128)(2,1)S(1)} %get-tuple-element.196.refs_2_), channel_id=1, source_target_pairs={{0,1},{1,0},{2,3},{3,2},{4,5},{5,4},{6,7},{7,6},{8,9},{9,8},{10,11... | collective-permute-start | bytes 1769480 | tf_op jit(solution)/shard_map/ppermute | solution.py:66
  164.6 11.7 %collective-permute-start.40 = (bf16[32,1152]{1,0:T(8,128)(2,1)S(1)}, bf16[32,1152]{1,0:T(8,128)(2,1)S(1)}, u32[]{:S(2)}, u32[]{:S(2)}) collective-permute-start(bf16[32,1152]{1,0:T(8,128)(2,1)S(1)} %get-tuple-element.190.refs_0_), channel_id=1, source_target_pairs={{0,4},{1,5},{2,6},{3,7},{4,0},{5,1},{6,2},{7,3},{8,12},{9,13},{10,... | collective-permute-start | bytes 221192 | tf_op jit(solution)/shard_map/ppermute | solution.py:66
  166.0 14.3 %collective-permute-start.41 = (bf16[128,1152]{1,0:T(8,128)(2,1)S(1)}, bf16[128,1152]{1,0:T(8,128)(2,1)S(1)}, u32[]{:S(2)}, u32[]{:S(2)}) collective-permute-start(bf16[128,1152]{1,0:T(8,128)(2,1)S(1)} %get-tuple-element.195.refs_1_), channel_id=1, source_target_pairs={{0,1},{1,0},{2,3},{3,2},{4,5},{5,4},{6,7},{7,6},{8,9},{9,8},{10,11... | collective-permute-start | bytes 884744 | tf_op jit(solution)/shard_map/ppermute | solution.py:66
  211.5 14.8 %collective-permute-start.56 = (bf16[4,64,640]{2,1,0:T(8,128)(2,1)S(1)}, bf16[4,64,640]{2,1,0:T(8,128)(2,1)S(1)}, u32[]{:S(2)}, u32[]{:S(2)}) collective-permute-start(bf16[4,64,640]{2,1,0:T(8,128)(2,1)S(1)} %get-tuple-element.219.refs_2_), channel_id=1, source_target_pairs={{0,8},{8,0},{16,24},{24,16},{1,9},{9,1},{17,25},{25,17},{2,10},{10... | collective-permute-start | bytes 983048 | tf_op jit(solution)/shard_map/ppermute | solution.py:61
  212.7 13.7 %collective-permute-start.57 = (bf16[4,64,640]{2,1,0:T(8,128)(2,1)S(1)}, bf16[4,64,640]{2,1,0:T(8,128)(2,1)S(1)}, u32[]{:S(2)}, u32[]{:S(2)}) collective-permute-start(bf16[4,64,640]{2,1,0:T(8,128)(2,1)S(1)} %get-tuple-element.219.refs_2_), channel_id=1, source_target_pairs={{0,16},{8,24},{16,0},{24,8},{1,17},{9,25},{17,1},{25,9},{2,18},{10... | collective-permute-start | bytes 983048 | tf_op jit(solution)/shard_map/ppermute | solution.py:61
  213.8 12.6 %collective-permute-start.58 = (bf16[4,64,640]{2,1,0:T(8,128)(2,1)S(1)}, bf16[4,64,640]{2,1,0:T(8,128)(2,1)S(1)}, u32[]{:S(2)}, u32[]{:S(2)}) collective-permute-start(bf16[4,64,640]{2,1,0:T(8,128)(2,1)S(1)} %get-tuple-element.219.refs_2_), channel_id=1, source_target_pairs={{0,24},{8,16},{16,8},{24,0},{1,25},{9,17},{17,9},{25,1},{2,26},{10... | collective-permute-start | bytes 983048 | tf_op jit(solution)/shard_map/ppermute | solution.py:61
  227.1 17.8 %collective-permute-start.66 = (bf16[4,64,640]{2,1,0:T(8,128)(2,1)S(1)}, bf16[4,64,640]{2,1,0:T(8,128)(2,1)S(1)}, u32[]{:S(2)}, u32[]{:S(2)}) collective-permute-start(bf16[4,64,640]{2,1,0:T(8,128)(2,1)S(1)} %get-tuple-element.230.refs_2_), channel_id=1, source_target_pairs={{0,8},{8,0},{16,24},{24,16},{1,9},{9,1},{17,25},{25,17},{2,10},{10... | collective-permute-start | bytes 983048 | tf_op jit(solution)/shard_map/ppermute | solution.py:61
  228.1 16.8 %collective-permute-start.67 = (bf16[4,64,640]{2,1,0:T(8,128)(2,1)S(1)}, bf16[4,64,640]{2,1,0:T(8,128)(2,1)S(1)}, u32[]{:S(2)}, u32[]{:S(2)}) collective-permute-start(bf16[4,64,640]{2,1,0:T(8,128)(2,1)S(1)} %get-tuple-element.230.refs_2_), channel_id=1, source_target_pairs={{0,16},{8,24},{16,0},{24,8},{1,17},{9,25},{17,1},{25,9},{2,18},{10... | collective-permute-start | bytes 983048 | tf_op jit(solution)/shard_map/ppermute | solution.py:61
  229.3 15.7 %collective-permute-start.68 = (bf16[4,64,640]{2,1,0:T(8,128)(2,1)S(1)}, bf16[4,64,640]{2,1,0:T(8,128)(2,1)S(1)}, u32[]{:S(2)}, u32[]{:S(2)}) collective-permute-start(bf16[4,64,640]{2,1,0:T(8,128)(2,1)S(1)} %get-tuple-element.230.refs_2_), channel_id=1, source_target_pairs={{0,24},{8,16},{16,8},{24,0},{1,25},{9,17},{17,9},{25,1},{2,26},{10... | collective-permute-start | bytes 983048 | tf_op jit(solution)/shard_map/ppermute | solution.py:61
  230.6 15.3 %collective-permute-start.69 = (bf16[4,64,640]{2,1,0:T(8,128)(2,1)S(1)}, bf16[4,64,640]{2,1,0:T(8,128)(2,1)S(1)}, u32[]{:S(2)}, u32[]{:S(2)}) collective-permute-start(bf16[4,64,640]{2,1,0:T(8,128)(2,1)S(1)} %get-tuple-element.230.refs_2_), channel_id=1, source_target_pairs={{0,1},{1,0},{2,3},{3,2},{4,5},{5,4},{6,7},{7,6},{8,9},{9,8},{10,11... | collective-permute-start | bytes 983048 | tf_op jit(solution)/shard_map/ppermute | solution.py:66
  (65 other events, 524.5 us)
